TPU v7x, 256 devices: a whole 4x4x8 slice. The times are simulated.
256 devices in a mesh: tile: 32 (over y, x, core), rep: 8 (over z).
Axes of the slice: x: 4, y: 4, z: 8, core: 2. Of those that a mesh axis runs over, the one named last changes fastest.
Arguments:
- tile_data: bfloat16 [8, 128, 16, 16, 192], P('rep', 'tile'), may hold values from -6 to 6
- cotangent: bfloat16 [8, 128, 16, 16, 192], P('rep', 'tile'), may hold values from -6 to 6
- tile_place: int32 [8, 32, 4], P('rep', 'tile'), may hold values from 0 to 3, each once within a row
- tile_count: int32 [8, 32], P('rep', 'tile'), may hold values from 1 to 4, as said below
- kernel: float32 [7, 7, 192], replicated, may hold values from -0.875 to 0.875
- norm_gain: float32 [192], replicated, may hold values from 0.5 to 1.5
- expand_weight: bfloat16 [192, 768], P('rep'), may hold values from -0.4375 to 0.4375
- hidden_bias: float32 [768], replicated, may hold values from -3 to 3
- reduce_weight: bfloat16 [768, 192], P('rep'), may hold values from -0.21875 to 0.21875
Outputs:
- result_tiles: float32 [8, 128, 16, 16, 192], P('rep', 'tile')
- grad_tiles: float32 [8, 128, 16, 16, 192], P('rep', 'tile')
- grad_expand: float32 [192, 768], P('rep')
- grad_reduce: float32 [768, 192], P('rep')
- grad_kernel: float32 [7, 7, 192], replicated
Inputs may be any that keep to these rules, and one draw needn't show every extreme that they name: In every slide device d keeps its tiles in slots 0 to tile_count[d] - 1, and some device holds 4 tiles. `tile_place`: each row lists every block position once.
All inputs are finite; a program needn't handle non-finite values.
Results may differ from a plain program's by a relative error of at most 0.007.
Values may be sent and summed in bfloat16 or wider, within the bound.
No kernel may reach another device: no remote copies, remote signals or barrier semaphores. Data moves between devices by JAX's collectives and lax.ppermute only.
A program may use at most 64 MiB of HBM per device.

v0:
```python
import math

import jax
import jax.numpy as jnp
from jax import lax
from jax.sharding import PartitionSpec as P

REG_COLS = 4


conv_dims = ("NHWC", "HWIO", "NHWC")
inv_root_two = 0.7071067811865476
inv_root_two_pi = 0.3989422804014327


def from_behind(value, axis, by):
    count = lax.axis_size(axis)
    pairs = [(i, i + by) for i in range(count) if 0 <= i + by < count]
    return lax.ppermute(value, axis, pairs)


def depthwise(padded, kernel):
    output = lax.conv_general_dilated(
        padded[None],
        kernel[:, :, None, :],
        (1, 1),
        "VALID",
        dimension_numbers=conv_dims,
        feature_group_count=padded.shape[-1],
        precision=lax.Precision.HIGHEST,
    )
    return output[0]


def row_contract(left, right):
    return lax.dot_general(
        left, right, (((0,), (0,)), ((), ())), preferred_element_type=jnp.float32
    )


def right_contract(left, right):
    return lax.dot_general(
        left, right, (((1,), (1,)), ((), ())), preferred_element_type=jnp.float32
    )


def forward_backward(
    padded, live_mask, cotan_canvas, kernel, norm_gain, expand_weight, hidden_bias, reduce_weight
):
    row_count, col_count, channels = cotan_canvas.shape
    cell_count = row_count * col_count
    canvas = padded[3:-3, 3:-3, :].reshape(cell_count, channels)
    filtered = depthwise(padded.astype(jnp.float32), kernel).reshape(cell_count, channels)
    centre = jnp.mean(filtered, axis=1, keepdims=True)
    spread = filtered - centre
    inverse_spread = lax.rsqrt(jnp.mean(spread * spread, axis=1, keepdims=True) + 1e-06)
    normed = spread * inverse_spread
    scaled = (normed * norm_gain).astype(jnp.bfloat16)
    hidden_in = jnp.dot(scaled, expand_weight, preferred_element_type=jnp.float32) + hidden_bias
    normal_cdf = 0.5 * (1.0 + lax.erf(hidden_in * inv_root_two))
    active = (hidden_in * normal_cdf).astype(jnp.bfloat16)
    mixed = jnp.dot(active, reduce_weight, preferred_element_type=jnp.float32)
    mask_rows = live_mask.reshape(cell_count, 1)
    result = (canvas.astype(jnp.float32) + mixed) * mask_rows.astype(jnp.float32)
    upstream = cotan_canvas.reshape(cell_count, channels) * mask_rows
    grad_reduce = row_contract(active, upstream)
    grad_active = right_contract(upstream, reduce_weight)
    gelu_slope = normal_cdf + hidden_in * jnp.exp(-0.5 * hidden_in * hidden_in) * inv_root_two_pi
    grad_hidden = (grad_active * gelu_slope).astype(jnp.bfloat16)
    grad_expand = row_contract(scaled, grad_hidden)
    grad_scaled = right_contract(grad_hidden, expand_weight) * norm_gain
    grad_field = inverse_spread * (
        grad_scaled
        - jnp.mean(grad_scaled, axis=1, keepdims=True)
        - normed * jnp.mean(grad_scaled * normed, axis=1, keepdims=True)
    )
    grad_field = grad_field.astype(jnp.bfloat16).reshape(row_count, col_count, channels)
    return (
        result.reshape(row_count, col_count, channels),
        upstream.reshape(row_count, col_count, channels),
        grad_field,
        grad_expand,
        grad_reduce,
    )


def block_layout(tile_block, onehot):
    tile_side = tile_block.shape[1]
    placed = jnp.einsum(
        "jp,jxyc->pxyc", onehot, tile_block, preferred_element_type=jnp.float32
    ).astype(jnp.bfloat16)
    placed = placed.reshape(2, 2, tile_side, tile_side, -1).transpose(0, 2, 1, 3, 4)
    return placed.reshape(2 * tile_side, 2 * tile_side, -1)


def slot_layout(canvas, onehot):
    tile_side = canvas.shape[0] // 2
    blocks = (
        canvas.reshape(2, tile_side, 2, tile_side, -1)
        .transpose(0, 2, 1, 3, 4)
        .reshape(4, tile_side, tile_side, -1)
    )
    return jnp.einsum(
        "jp,pxyc->jxyc", onehot.astype(jnp.float32), blocks, preferred_element_type=jnp.float32
    )


def with_rims(canvas):
    height, breadth = (canvas.shape[0], canvas.shape[1])
    block_column = lax.axis_index("tile") % REG_COLS
    has_left = block_column > 0
    has_right = block_column < REG_COLS - 1
    west_side = from_behind(canvas[:, breadth - 3 :], "tile", 1)
    east_side = from_behind(canvas[:, :3], "tile", -1)
    west_side = jnp.where(has_left, west_side, jnp.zeros_like(west_side))
    east_side = jnp.where(has_right, east_side, jnp.zeros_like(east_side))
    widened = jnp.concatenate([west_side, canvas, east_side], axis=1)
    north_band = from_behind(widened[height - 3 :], "tile", REG_COLS)
    south_band = from_behind(widened[:3], "tile", -REG_COLS)
    return jnp.concatenate([north_band, widened, south_band], axis=0)


def per_device(
    tile_data,
    cotangent,
    tile_place,
    tile_count,
    kernel,
    norm_gain,
    expand_weight,
    hidden_bias,
    reduce_weight,
):
    expand_full, reduce_full = (
        lax.all_gather(expand_weight, "rep", axis=0, tiled=True),
        lax.all_gather(reduce_weight, "rep", axis=0, tiled=True),
    )
    slot_count = tile_place.shape[2]
    tile_side = tile_data.shape[2]
    positions = jnp.arange(slot_count)
    live_slots = (positions < tile_count[0, 0]).astype(jnp.int32)
    onehot = (
        (tile_place[0, 0][:, None] == positions[None, :]).astype(jnp.int32) * live_slots[:, None]
    ).astype(jnp.bfloat16)
    canvas = block_layout(tile_data[0], onehot)
    cotan_canvas = block_layout(cotangent[0], onehot)
    live_mask = block_layout(jnp.ones((slot_count, tile_side, tile_side, 1), jnp.bfloat16), onehot)
    padded = with_rims(canvas)
    result, upstream, grad_field, grad_expand, grad_reduce = forward_backward(
        padded, live_mask, cotan_canvas, kernel, norm_gain, expand_full, hidden_bias, reduce_full
    )
    grad_padded = with_rims(grad_field)
    grad_canvas = upstream.astype(jnp.float32) + depthwise(
        grad_padded.astype(jnp.float32), kernel[::-1, ::-1]
    )
    grad_canvas = grad_canvas * live_mask.astype(jnp.float32)
    grad_kern = depthwise(padded.astype(jnp.float32), grad_field.astype(jnp.float32))
    summed = lax.psum((grad_expand, grad_reduce), "tile")
    shares = (
        lax.psum_scatter(summed[0], "rep", scatter_dimension=0, tiled=True),
        lax.psum_scatter(summed[1], "rep", scatter_dimension=0, tiled=True),
    )
    kernel_total = lax.psum(grad_kern, ("tile", "rep"))
    factor = 1.0 / math.sqrt(
        lax.axis_size("rep") * lax.axis_size("tile") * slot_count * tile_side * tile_side
    )
    return (
        slot_layout(result, onehot)[None],
        slot_layout(grad_canvas, onehot)[None],
        shares[0] * factor,
        shares[1] * factor,
        kernel_total * factor,
    )


def solution(mesh):
    placed = (
        P("rep", "tile", None, None, None),
        P("rep", "tile", None, None, None),
        P("rep", "tile", None),
        P("rep", "tile"),
        P(),
        P(),
        P("rep", None),
        P(),
        P("rep", None),
    )
    return jax.shard_map(
        per_device,
        mesh=mesh,
        in_specs=placed,
        out_specs=(
            P("rep", "tile", None, None, None),
            P("rep", "tile", None, None, None),
            P("rep", None),
            P("rep", None),
            P(),
        ),
        check_vma=False,
    )
```

profile of v0, /device:TPU:1, one launch (start us, length us, event | category | flops | bytes accessed | tf_op | source)
XLA Modules:
  0.0 404.5 jit_solution(14529379989311913111)
XLA Ops:
  7.9 0.3 copy-done
  8.2 1.4 convolution_convert_fusion.1
  9.6 0.4 reshape.116
  10.0 0.1 copy.57
  10.2 4.5 %collective-permute-start = (bf16[32,3,192]{2,1,0:T(4,128)(2,1)S(1)}, bf16[32,3,192]{2,1,0:T(4,128)(2,1)S(1)}, u32[]{:S(2)}, u32[]{:S(2)}) collective-permute-start(bf16[32,3,192]{2,1,0:T(4,128)(2,1)S(1)} %get-tuple-element.30), channel_id=1, source_target_pairs={{0,8},{8,16},{16,24},{24,32},{32,40},{40,48},{48,56},{56,64},{64,7... | collective-permute-start | bytes 110600 | tf_op jit(solution)/shard_map/ppermute | solution.py:19
  14.7 1.9 collective-permute-start.1
  16.7 0.3 convolution_convert_fusion.2
  16.9 0.1 bitcast_convert_fusion
  17.1 0.1 reshape_reshape.10
  17.2 0.7 convolution_convert_fusion
  17.9 0.1 copy.90
  18.0 0.8 copy-done.1
  18.8 1.0 bitcast_multiply_fusion
  19.8 22.1 %all_gather.6 = bf16[192,768]{1,0:T(8,128)(2,1)S(1)} all-gather(bf16[24,768]{1,0:T(8,128)(2,1)S(1)} %copy-done.18), channel_id=1, replica_groups=mesh['tile'=32,'rep'=8] {'rep'}, dimensions={0}, use_global_device_ids=true | all-gather | bytes 331776 | tf_op jit(solution)/shard_map/all_gather | solution.py:135
  42.1 4.9 %collective-permute-start.2 = (bf16[3,38,192]{2,1,0:T(8,128)(2,1)S(1)}, bf16[3,38,192]{2,1,0:T(8,128)(2,1)S(1)}, u32[]{:S(2)}, u32[]{:S(2)}) collective-permute-start(bf16[3,38,192]{2,1,0:T(8,128)(2,1)S(1)} %get-tuple-element.26), channel_id=1, source_target_pairs={{0,32},{8,40},{16,48},{24,56},{32,64},{40,72},{48,80},{56,88},{64,... | collective-permute-start | bytes 131336 | tf_op jit(solution)/shard_map/ppermute | solution.py:19
  46.9 1.3 collective-permute-start.3
  48.2 21.1 %all_gather.7 = bf16[768,192]{1,0:T(8,128)(2,1)} all-gather(bf16[96,192]{1,0:T(8,128)(2,1)S(1)} %copy-done.17), channel_id=1, replica_groups=mesh['tile'=32,'rep'=8] {'rep'}, dimensions={0}, use_global_device_ids=true | all-gather | bytes 331776 | tf_op jit(solution)/shard_map/all_gather | solution.py:136
  69.3 0.6 convert_element_type.73
  69.9 0.6 copy.70
  70.5 0.7 rev.3
  71.2 1.2 copy.61
  72.4 0.4 maximum_bitcast_fusion
  72.8 19.5 %fusion.39 = (f32[32,32]{1,0:T(8,128)S(1)}, f32[1,32,32,192]{3,0,2,1:T(1,128)S(1)}) fusion(f32[7,7,1,192]{3,1,0,2:T(8,128)S(1)} %bitcast.94, bf16[1,38,38,192]{3,2,1,0:T(8,128)(2,1)S(1)} %maximum_bitcast_fusion), kind=kOutput, calls=%fused_computation.77 | convolution fusion | flops 115801088 | bytes 1382656 | tf_op jit(solution)/shard_map/conv_general_dilated | solution.py:23
  92.3 0.1 div.15
  92.3 15.3 %multiply_reduce_fusion = f32[32,32]{1,0:T(8,128)S(1)} fusion(f32[1,32,32,192]{3,0,2,1:T(1,128)S(1)} %get-tuple-element.35, f32[32,32]{1,0:T(8,128)S(1)} %broadcast_multiply_fusion.3), kind=kLoop, calls=%fused_computation.28 | loop fusion | flops 588800 | bytes 794624 | tf_op jit(solution)/shard_map/reduce_sum | solution.py:56
  107.6 0.1 copy.92
  107.7 0.3 copy.60
  108.1 0.1 copy-done.19
  108.3 2.3 multiply_convert_fusion
  110.7 1.2 copy-done.3
  111.8 1.5 fusion.40
  113.4 0.2 reduce-scatter.3.cloned.1.call-start
  113.6 3.3 fusion.5
  117.0 0.7 fusion.36
  117.7 1.0 multiply_convert_fusion.1
  118.6 1.2 copy.72
  119.8 10.5 %fusion.9 = f32[1,7,7,192]{3,0,2,1:T(1,128)S(1)} fusion(bf16[1,38,38,192]{3,2,1,0:T(8,128)(2,1)} %copy-done.7, bf16[32,32,1,192]{3,1,0,2:T(8,128)(2,1)S(1)} %bitcast.80), kind=kOutput, calls=%fused_computation.18 | convolution fusion | flops 19267584 | bytes 985344 | tf_op jit(solution)/shard_map/conv_general_dilated | solution.py:23
  130.3 92.0 %psum.23 = f32[7,7,192]{2,1,0:T(8,128)S(1)} all-reduce(f32[7,7,192]{2,1,0:T(8,128)S(1)} %bitcast.91), channel_id=1, replica_groups=mesh['tile'=32,'rep'=8] {'tile','rep'}, use_global_device_ids=true, to_apply=%region_8.9 | all-reduce | flops 9408 | bytes 75264 | tf_op jit(solution)/shard_map/psum | solution.py:163
  222.3 0.7 fusion.37
  223.0 2.3 collective-permute-start.4
  225.3 3.2 fusion.8
  228.5 1.3 fusion.34
  229.8 0.6 broadcast_multiply_fusion.2
  230.5 1.2 copy.64
  231.7 2.8 collective-permute-start.5
  234.5 0.9 broadcast_select_fusion.2
  235.4 1.9 collective-permute-done.5
  237.4 4.3 %collective-permute-start.6 = (bf16[3,38,192]{2,1,0:T(8,128)(2,1)S(1)}, bf16[3,38,192]{2,1,0:T(8,128)(2,1)S(1)}, u32[]{:S(2)}, u32[]{:S(2)}) collective-permute-start(bf16[3,38,192]{2,1,0:T(8,128)(2,1)S(1)} %get-tuple-element.24), channel_id=1, source_target_pairs={{0,32},{8,40},{16,48},{24,56},{32,64},{40,72},{48,80},{56,88},{64,... | collective-permute-start | bytes 131336 | tf_op jit(solution)/shard_map/ppermute | solution.py:19
  241.7 1.3 collective-permute-start.7
  243.0 0.5 convolution_bitcast_fusion.1
  243.6 1.2 copy.81
  244.8 0.3 all-reduce.3.cloned.1.call-start
  245.1 4.1 %collective-permute-done.7 = bf16[3,38,192]{2,1,0:T(8,128)(2,1)S(1)} collective-permute-done((bf16[3,38,192]{2,1,0:T(8,128)(2,1)S(1)}, bf16[3,38,192]{2,1,0:T(8,128)(2,1)S(1)}, u32[]{:S(2)}, u32[]{:S(2)}) %collective-permute-start.7) | collective-permute-done | bytes 43808 | tf_op jit(solution)/shard_map/ppermute | solution.py:19
  249.1 0.4 maximum_bitcast_fusion.1
  249.5 12.7 %fusion.6 = f32[1,32,32,192]{3,0,2,1:T(1,128)S(1)} fusion(bf16[1,38,38,192]{3,2,1,0:T(8,128)(2,1)S(1)} %maximum_bitcast_fusion.1, f32[7,7,1,192]{3,1,0,2:T(8,128)S(1)} %bitcast.95), kind=kOutput, calls=%fused_computation.9 | convolution fusion | flops 115605504 | bytes 1378560 | tf_op jit(solution)/shard_map/conv_general_dilated | solution.py:23
  262.2 0.1 copy.93
  262.3 0.9 copy-done.2
  263.2 0.4 fusion.15
  263.6 14.9 %reduce-scatter.3.cloned.1.call-done = f32[24,768]{1,0:T(8,128)} async-done(((f32[192,768]{1,0:T(8,128)}), f32[24,768]{1,0:T(8,128)}) %reduce-scatter.3.cloned.1.call-update) | async-done | bytes 73744 | tf_op jit(solution)/shard_map/reduce_scatter | solution.py:160
  278.6 0.5 convolution_bitcast_fusion
  279.1 1.2 copy.82
  280.3 114.6 %all-reduce.3.cloned.1.call-done = (f32[24,768]{1,0:T(8,128)}, f32[96,192]{1,0:T(8,128)}) async-done(((f32[24,768]{1,0:T(8,128)}, f32[96,192]{1,0:T(8,128)}), (f32[24,768]{1,0:T(8,128)}, f32[96,192]{1,0:T(8,128)})) %all-reduce.3.cloned.1.call-update) | async-done | bytes 147472 | tf_op jit(solution)/shard_map/psum | solution.py:158
  394.9 1.5 broadcast_multiply_fusion.1
  396.4 1.5 broadcast_multiply_fusion
  (76 shorter events, 0.7 us)
Async XLA Ops:
  7.2 1.1 copy-start
  7.2 256.4 %reduce-scatter.5.cloned.1.call-start = ((), (), s32[]{:S(2)}) async-start(), calls=%async_computation.3 | async-start | bytes 884736 | tf_op jit(solution)/shard_map/reduce_scatter | solution.py:161
  7.9 9.2 %copy-start.23 = (s32[4]{0:T(128)}, s32[4]{0:T(128)S(1)}, u32[]{:S(2)}) copy-start(s32[4]{0:T(128)S(1)} %compare_convert_fusion) | copy-start | bytes 52
  8.2 8.4 %copy-start.21 = (s32[1,1,4]{2,1,0:T(1,128)S(1)}, s32[1,1,4]{2,1,0:T(1,128)}, u32[]{:S(2)}) copy-start(s32[1,1,4]{2,1,0:T(1,128)} %param.11) | copy-start | bytes 52
  10.0 7.1 %copy-start.25 = (bf16[1,4,16,16,192]{4,3,2,1,0:T(8,128)(2,1)S(1)}, bf16[1,4,16,16,192]{4,3,2,1,0:T(8,128)(2,1)}, u32[]{:S(2)}) copy-start(bf16[1,4,16,16,192]{4,3,2,1,0:T(8,128)(2,1)} %param.10) | copy-start | bytes 1179652
  10.2 31.7 %collective-permute-start = (bf16[32,3,192]{2,1,0:T(4,128)(2,1)S(1)}, bf16[32,3,192]{2,1,0:T(4,128)(2,1)S(1)}, u32[]{:S(2)}, u32[]{:S(2)}) collective-permute-start(bf16[32,3,192]{2,1,0:T(4,128)(2,1)S(1)} %get-tuple-element.30), channel_id=1, source_target_pairs={{0,8},{8,16},{16,24},{24,32},{32,40},{40,48},{48,56},{56,64},{64,7... | collective-permute-start | bytes 110600 | tf_op jit(solution)/shard_map/ppermute | solution.py:19
  14.7 27.2 %collective-permute-start.1 = (bf16[32,3,192]{2,1,0:T(4,128)(2,1)S(1)}, bf16[32,3,192]{2,1,0:T(4,128)(2,1)S(1)}, u32[]{:S(2)}, u32[]{:S(2)}) collective-permute-start(bf16[32,3,192]{2,1,0:T(4,128)(2,1)S(1)} %get-tuple-element.31), channel_id=1, source_target_pairs={{8,0},{16,8},{24,16},{32,24},{40,32},{48,40},{56,48},{64,56},{72,6... | collective-permute-start | bytes 110600 | tf_op jit(solution)/shard_map/ppermute | solution.py:19
  17.9 2.0 copy-start.18
  17.9 0.8 copy-start.1
  18.7 29.5 %copy-start.17 = (bf16[96,192]{1,0:T(8,128)(2,1)S(1)}, bf16[96,192]{1,0:T(8,128)(2,1)}, u32[]{:S(2)}) copy-start(bf16[96,192]{1,0:T(8,128)(2,1)} %param.17) | copy-start | bytes 110596
  18.8 51.7 %copy-start.15 = (f32[7,7,192]{2,1,0:T(8,128)S(1)}, f32[7,7,192]{2,1,0:T(8,128)}, u32[]{:S(2)}) copy-start(f32[7,7,192]{2,1,0:T(8,128)} %param.13) | copy-start | bytes 112900
  41.9 66.2 %copy-start.5 = (bf16[192,768]{1,0:T(8,128)(2,1)}, bf16[192,768]{1,0:T(8,128)(2,1)S(1)}, u32[]{:S(2)}) copy-start(bf16[192,768]{1,0:T(8,128)(2,1)S(1)} %all_gather.6) | copy-start | bytes 884740
  42.1 30.3 %collective-permute-start.2 = (bf16[3,38,192]{2,1,0:T(8,128)(2,1)S(1)}, bf16[3,38,192]{2,1,0:T(8,128)(2,1)S(1)}, u32[]{:S(2)}, u32[]{:S(2)}) collective-permute-start(bf16[3,38,192]{2,1,0:T(8,128)(2,1)S(1)} %get-tuple-element.26), channel_id=1, source_target_pairs={{0,32},{8,40},{16,48},{24,56},{32,64},{40,72},{48,80},{56,88},{64,... | collective-permute-start | bytes 131336 | tf_op jit(solution)/shard_map/ppermute | solution.py:19
  46.9 25.5 %collective-permute-start.3 = (bf16[3,38,192]{2,1,0:T(8,128)(2,1)S(1)}, bf16[3,38,192]{2,1,0:T(8,128)(2,1)S(1)}, u32[]{:S(2)}, u32[]{:S(2)}) collective-permute-start(bf16[3,38,192]{2,1,0:T(8,128)(2,1)S(1)} %get-tuple-element.27), channel_id=1, source_target_pairs={{32,0},{40,8},{48,16},{56,24},{64,32},{72,40},{80,48},{88,56},{96,... | collective-permute-start | bytes 131336 | tf_op jit(solution)/shard_map/ppermute | solution.py:19
  72.8 19.5 %copy-start.7 = (bf16[1,38,38,192]{3,2,1,0:T(8,128)(2,1)}, bf16[1,38,38,192]{3,2,1,0:T(8,128)(2,1)S(1)}, u32[]{:S(2)}) copy-start(bf16[1,38,38,192]{3,2,1,0:T(8,128)(2,1)S(1)} %maximum_bitcast_fusion) | copy-start | bytes 1663492
  92.3 25.3 %copy-start.9 = (f32[1024]{0:T(1024)}, f32[1024]{0:T(1024)S(1)}, u32[]{:S(2)}) copy-start(f32[1024]{0:T(1024)S(1)} %div.15) | copy-start | bytes 12292
  107.6 0.7 copy-start.19
  107.6 0.7 copy-start.26
  108.3 9.4 %copy-start.11 = (f32[1024]{0:T(1024)}, f32[1024]{0:T(1024)S(1)}, u32[]{:S(2)}) copy-start(f32[1024]{0:T(1024)S(1)} %rsqrt.12) | copy-start | bytes 12292
  108.3 3.5 copy-start.8
  110.7 1.2 copy-start.3
  111.8 1.8 copy-start.4
  113.4 165.2 %reduce-scatter.3.cloned.1.call-start = ((), (), s32[]{:S(2)}) async-start(), calls=%async_computation.2 | async-start | bytes 663552 | tf_op jit(solution)/shard_map/reduce_scatter | solution.py:160
  113.6 3.3 copy-start.6
  223.0 5.4 %copy-start.10 = (f32[1024]{0:T(1024)S(1)}, f32[1024]{0:T(1024)}, u32[]{:S(2)}) copy-start(f32[1024]{0:T(1024)} %copy-done.9) | copy-start | bytes 12292
  223.0 5.4 %copy-start.12 = (f32[1024]{0:T(1024)S(1)}, f32[1024]{0:T(1024)}, u32[]{:S(2)}) copy-start(f32[1024]{0:T(1024)} %copy-done.11) | copy-start | bytes 12292
  223.0 5.4 %copy-start.20 = (f32[192]{0:T(256)S(1)}, f32[192]{0:T(256)}, u32[]{:S(2)}) copy-start(f32[192]{0:T(256)} %param.14) | copy-start | bytes 2308
  223.0 11.5 %collective-permute-start.4 = (bf16[32,3,192]{2,1,0:T(4,128)(2,1)}, bf16[32,3,192]{2,1,0:T(4,128)(2,1)}, u32[]{:S(2)}, u32[]{:S(2)}) collective-permute-start(bf16[32,3,192]{2,1,0:T(4,128)(2,1)} %get-tuple-element.28), channel_id=1, source_target_pairs={{0,8},{8,16},{16,24},{24,32},{32,40},{40,48},{48,56},{56,64},{64,7... | collective-permute-start | bytes 110600 | tf_op jit(solution)/shard_map/ppermute | solution.py:19
  229.8 1.9 copy-start.14
  229.8 13.2 %copy-start.22 = (s32[1,1,4]{2,1,0:T(1,128)S(1)}, s32[1,1,4]{2,1,0:T(1,128)}, u32[]{:S(2)}) copy-start(s32[1,1,4]{2,1,0:T(1,128)} %param.11) | copy-start | bytes 52
  229.8 13.2 %copy-start.24 = (s32[4]{0:T(128)S(1)}, s32[4]{0:T(128)}, u32[]{:S(2)}) copy-start(s32[4]{0:T(128)} %copy-done.23) | copy-start | bytes 52
  231.7 5.6 %collective-permute-start.5 = (bf16[32,3,192]{2,1,0:T(4,128)(2,1)S(1)}, bf16[32,3,192]{2,1,0:T(4,128)(2,1)S(1)}, u32[]{:S(2)}, u32[]{:S(2)}) collective-permute-start(bf16[32,3,192]{2,1,0:T(4,128)(2,1)S(1)} %copy-done.14), channel_id=1, source_target_pairs={{8,0},{16,8},{24,16},{32,24},{40,32},{48,40},{56,48},{64,56},{72,6... | collective-permute-start | bytes 110600 | tf_op jit(solution)/shard_map/ppermute | solution.py:19
  237.4 7.6 %collective-permute-start.6 = (bf16[3,38,192]{2,1,0:T(8,128)(2,1)S(1)}, bf16[3,38,192]{2,1,0:T(8,128)(2,1)S(1)}, u32[]{:S(2)}, u32[]{:S(2)}) collective-permute-start(bf16[3,38,192]{2,1,0:T(8,128)(2,1)S(1)} %get-tuple-element.24), channel_id=1, source_target_pairs={{0,32},{8,40},{16,48},{24,56},{32,64},{40,72},{48,80},{56,88},{64,... | collective-permute-start | bytes 131336 | tf_op jit(solution)/shard_map/ppermute | solution.py:19
  241.7 7.4 %collective-permute-start.7 = (bf16[3,38,192]{2,1,0:T(8,128)(2,1)S(1)}, bf16[3,38,192]{2,1,0:T(8,128)(2,1)S(1)}, u32[]{:S(2)}, u32[]{:S(2)}) collective-permute-start(bf16[3,38,192]{2,1,0:T(8,128)(2,1)S(1)} %get-tuple-element.25), channel_id=1, source_target_pairs={{32,0},{40,8},{48,16},{56,24},{64,32},{72,40},{80,48},{88,56},{96,... | collective-permute-start | bytes 131336 | tf_op jit(solution)/shard_map/ppermute | solution.py:19
  244.7 4.8 %copy-start.16 = (f32[7,7,192]{2,1,0:T(8,128)S(1)}, f32[7,7,192]{2,1,0:T(8,128)}, u32[]{:S(2)}) copy-start(f32[7,7,192]{2,1,0:T(8,128)} %rev.3) | copy-start | bytes 112900
  244.8 150.1 %all-reduce.3.cloned.1.call-start = ((), (), s32[]{:S(2)}) async-start(), calls=%async_computation.4 | async-start | bytes 344064 | tf_op jit(solution)/shard_map/psum | solution.py:158
  262.2 1.0 copy-start.2
  262.2 1.0 copy-start.13
Sparse Core Ops, SparseCore 0:
  113.5 46.8 reduce-scatter.4
  244.9 33.6 reduce-scatter.2
  282.3 112.5 all-reduce.2
where the time goes:
time: 405 us; the launch traced here: 404 us
  waiting for transfers between devices  136 us (34%)
  blocking collectives  135 us (33%)
  matrix products  58.4 us (14%)
  starting transfers between devices  23.8 us (6%)
  other arithmetic  23.8 us (6%)
  between operations  15 us (4%)
  local copies, waits for them, and re-layouts  12.8 us (3%)
    psum x1, waiting for transfers between devices, per_device(): summed = lax.psum((grad_expand, grad_reduce), 'tile')  115 us
    psum x1, blocking collectives, per_device(): kernel_total = lax.psum(grad_kern, ('tile', 'rep'))  92 us
    conv_general_dilated x3, matrix products, depthwise(): lax.conv_general_dilated(padded[None], kernel[:, :, None, :], (1, 1), 'VA...  42.6 us
    ppermute x8, starting transfers between devices, from_behind(): return lax.ppermute(value, axis, pairs)  23.2 us
    all_gather x1, blocking collectives, per_device(): lax.all_gather(expand_weight, 'rep', axis=0, tiled=True)  22.1 us
    all_gather x1, blocking collectives, per_device(): lax.all_gather(reduce_weight, 'rep', axis=0, tiled=True)  21.1 us
    reduce_sum x1, other arithmetic, forward_backward(): jnp.mean(spread * spread, axis=1, keepdims=True) + 1e-06  15.3 us
    reduce_scatter x1, waiting for transfers between devices, per_device(): lax.psum_scatter(summed[0], 'rep', scatter_dimension=0, tiled=True)  14.9 us
  transfers between devices with their start and end apart: 11, of which 4 were waited for; matrix products, arithmetic and copies ran while one was open for 12% of the time, Pallas kernels for 0%

commit v1 on v0

v1 whole, which is shorter than its diff:
```python
import math

import jax
import jax.numpy as jnp
from jax import lax
from jax.sharding import Mesh, PartitionSpec as P

conv_dims = ("NHWC", "HWIO", "NHWC")
inv_root_two = 0.7071067811865476
inv_root_two_pi = 0.3989422804014327
bf16 = jnp.bfloat16
f32 = jnp.float32
TILE = ("y", "x", "core")
SIZES = {"y": 4, "x": 4, "core": 2, "rep": 8}


def swap(value, axis, bit):
    return lax.ppermute(value, axis, [(i, i ^ bit) for i in range(SIZES[axis])])


def bit_of(axis, bit):
    return (lax.axis_index(axis) // bit) % 2


def depthwise(padded, kernel):
    output = lax.conv_general_dilated(
        padded[None],
        kernel[:, :, None, :],
        (1, 1),
        "VALID",
        dimension_numbers=conv_dims,
        feature_group_count=padded.shape[-1],
        precision=lax.Precision.HIGHEST,
    )
    return output[0]


def row_contract(left, right):
    return lax.dot_general(left, right, (((0,), (0,)), ((), ())), preferred_element_type=f32)


def right_contract(left, right):
    return lax.dot_general(left, right, (((1,), (1,)), ((), ())), preferred_element_type=f32)


def forward_backward(
    padded, live_mask, cotan_canvas, kernel, norm_gain, expand_weight, hidden_bias, reduce_weight
):
    row_count, col_count, channels = cotan_canvas.shape
    cell_count = row_count * col_count
    canvas = padded[3:-3, 3:-3, :].reshape(cell_count, channels)
    filtered = depthwise(padded.astype(f32), kernel).reshape(cell_count, channels)
    centre = jnp.mean(filtered, axis=1, keepdims=True)
    spread = filtered - centre
    inverse_spread = lax.rsqrt(jnp.mean(spread * spread, axis=1, keepdims=True) + 1e-06)
    normed = spread * inverse_spread
    scaled = (normed * norm_gain).astype(bf16)
    hidden_in = jnp.dot(scaled, expand_weight, preferred_element_type=f32) + hidden_bias
    normal_cdf = 0.5 * (1.0 + lax.erf(hidden_in * inv_root_two))
    active = (hidden_in * normal_cdf).astype(bf16)
    mixed = jnp.dot(active, reduce_weight, preferred_element_type=f32)
    mask_rows = live_mask.reshape(cell_count, 1)
    result = (canvas.astype(f32) + mixed) * mask_rows.astype(f32)
    upstream = cotan_canvas.reshape(cell_count, channels) * mask_rows
    grad_reduce = row_contract(active, upstream)
    grad_active = right_contract(upstream, reduce_weight)
    gelu_slope = normal_cdf + hidden_in * jnp.exp(-0.5 * hidden_in * hidden_in) * inv_root_two_pi
    grad_hidden = (grad_active * gelu_slope).astype(bf16)
    grad_expand = row_contract(scaled, grad_hidden)
    grad_scaled = right_contract(grad_hidden, expand_weight) * norm_gain
    grad_field = inverse_spread * (
        grad_scaled
        - jnp.mean(grad_scaled, axis=1, keepdims=True)
        - normed * jnp.mean(grad_scaled * normed, axis=1, keepdims=True)
    )
    grad_field = grad_field.astype(bf16).reshape(row_count, col_count, channels)
    return (
        result.reshape(row_count, col_count, channels),
        upstream.reshape(row_count, col_count, channels),
        grad_field,
        grad_expand,
        grad_reduce,
    )


def block_layout(tile_block, onehot):
    tile_side = tile_block.shape[1]
    placed = jnp.einsum(
        "jp,jxyc->pxyc", onehot, tile_block, preferred_element_type=f32
    ).astype(bf16)
    placed = placed.reshape(2, 2, tile_side, tile_side, -1).transpose(0, 2, 1, 3, 4)
    return placed.reshape(2 * tile_side, 2 * tile_side, -1)


def slot_layout(canvas, onehot):
    tile_side = canvas.shape[0] // 2
    blocks = (
        canvas.reshape(2, tile_side, 2, tile_side, -1)
        .transpose(0, 2, 1, 3, 4)
        .reshape(4, tile_side, tile_side, -1)
    )
    return jnp.einsum("jp,pxyc->jxyc", onehot.astype(f32), blocks, preferred_element_type=f32)


def with_rims(canvas):
    core = lax.axis_index("core")
    upper = lax.axis_index("x") // 2
    strips = canvas.transpose(1, 0, 2)
    west_edge, east_edge = strips[:3], strips[-3:]
    inner = swap(jnp.where(core == 0, east_edge, west_edge), "core", 1)
    outer = lax.ppermute(
        jnp.where(core == 0, west_edge, east_edge),
        ("x", "core"),
        [(1, 2), (2, 1), (5, 6), (6, 5)],
    )
    west = jnp.where(core == 0, outer, inner).transpose(1, 0, 2)
    east = jnp.where(core == 0, inner, outer).transpose(1, 0, 2)
    widened = jnp.concatenate([west, canvas, east], axis=1)
    north_edge, south_edge = widened[:3], widened[-3:]
    near = swap(jnp.where(upper == 0, south_edge, north_edge), "x", 2)
    pairs = [(4 * y + x, 4 * (y + 1) + x - 2) for y in range(3) for x in (2, 3)]
    far = lax.ppermute(
        jnp.where(upper == 0, north_edge, south_edge),
        ("y", "x"),
        pairs + [(b, a) for a, b in pairs],
    )
    north = jnp.where(upper == 0, far, near)
    south = jnp.where(upper == 0, near, far)
    return jnp.concatenate([north, widened, south], axis=0)


def gather_weights(expand_weight, reduce_weight):
    core = lax.axis_index("core")
    rows = jnp.where(core == 0, expand_weight.reshape(reduce_weight.shape), reduce_weight)
    held = rows[None]
    for step, bit in enumerate((4, 2, 1)):
        other = swap(held, "rep", bit)
        mine = bit_of("rep", bit)
        lower = jnp.where(mine == 0, held, other)
        higher = jnp.where(mine == 0, other, held)
        held = jnp.stack([lower, higher], axis=1).reshape(2 ** (step + 1), *rows.shape)
    whole = held.reshape(-1, rows.shape[1])
    other = swap(whole, "core", 1)
    expand_full = jnp.where(core == 0, whole, other)
    reduce_full = jnp.where(core == 0, other, whole)
    return expand_full.reshape(-1, expand_weight.shape[1]), reduce_full


def reduce_gradients(grad_expand, grad_reduce, grad_kern):
    core = lax.axis_index("core")
    width = grad_reduce.shape[1]
    shards = SIZES["rep"]
    expand = grad_expand.astype(bf16).reshape(-1, width)
    project = grad_reduce.astype(bf16)
    rows = expand.shape[0]
    taps = grad_kern.reshape(-1, width)
    tap_count = taps.shape[0]
    taps = jnp.pad(taps, ((0, 64 - tap_count), (0, 0))).astype(bf16)

    def exchange(keep, send, taps, axis, bit):
        got = swap(jnp.concatenate([send, taps], axis=0), axis, bit)
        count = send.shape[0]
        keep = keep.astype(f32) + got[:count].astype(f32)
        taps = (taps.astype(f32) + got[count:].astype(f32)).astype(bf16)
        return keep.astype(bf16), taps

    keep = jnp.where(core == 0, expand, project)
    send = jnp.where(core == 0, project, expand)
    held, taps = exchange(keep, send, taps, "core", 1)
    piece = rows // shards
    for bit in (1, 2, 4):
        parts = held.reshape(-1, 2, piece, width)
        mine = bit_of("rep", bit)
        keep = jnp.where(mine == 0, parts[:, 0], parts[:, 1]).reshape(-1, width)
        send = jnp.where(mine == 0, parts[:, 1], parts[:, 0]).reshape(-1, width)
        held, taps = exchange(keep, send, taps, "rep", bit)
    for axis in ("x", "y"):
        for bit in (1, 2):
            held, taps = exchange(held, held, taps, axis, bit)
    other = swap(held, "core", 1)
    expand = jnp.where(core == 0, held, other).astype(f32)
    project = jnp.where(core == 0, other, held).astype(f32)
    return (
        expand.reshape(-1, grad_expand.shape[1]),
        project,
        taps[:tap_count].astype(f32).reshape(grad_kern.shape),
    )


def per_device(
    tile_data,
    cotangent,
    tile_place,
    tile_count,
    kernel,
    norm_gain,
    expand_weight,
    hidden_bias,
    reduce_weight,
):
    expand_full, reduce_full = gather_weights(expand_weight, reduce_weight)
    slot_count = tile_place.shape[2]
    tile_side = tile_data.shape[2]
    positions = jnp.arange(slot_count)
    live_slots = (positions < tile_count[0, 0]).astype(jnp.int32)
    onehot = (
        (tile_place[0, 0][:, None] == positions[None, :]).astype(jnp.int32) * live_slots[:, None]
    ).astype(bf16)
    canvas = block_layout(tile_data[0], onehot)
    cotan_canvas = block_layout(cotangent[0], onehot)
    live_mask = block_layout(jnp.ones((slot_count, tile_side, tile_side, 1), bf16), onehot)
    padded = with_rims(canvas)
    result, upstream, grad_field, grad_expand, grad_reduce = forward_backward(
        padded, live_mask, cotan_canvas, kernel, norm_gain, expand_full, hidden_bias, reduce_full
    )
    grad_padded = with_rims(grad_field)
    grad_canvas = upstream.astype(f32) + depthwise(grad_padded.astype(f32), kernel[::-1, ::-1])
    grad_canvas = grad_canvas * live_mask.astype(f32)
    grad_kern = depthwise(padded.astype(f32), grad_field.astype(f32))
    sums = reduce_gradients(grad_expand, grad_reduce, grad_kern)
    factor = 1.0 / math.sqrt(SIZES["rep"] * 32 * slot_count * tile_side * tile_side)
    return (
        slot_layout(result, onehot)[None],
        slot_layout(grad_canvas, onehot)[None],
        sums[0] * factor,
        sums[1] * factor,
        sums[2] * factor,
    )


def solution(mesh):
    fine = Mesh(mesh.devices.reshape(4, 4, 2, 8), ("y", "x", "core", "rep"))
    placed = (
        P("rep", TILE, None, None, None),
        P("rep", TILE, None, None, None),
        P("rep", TILE, None),
        P("rep", TILE),
        P(),
        P(),
        P("rep", None),
        P(),
        P("rep", None),
    )
    return jax.shard_map(
        per_device,
        mesh=fine,
        in_specs=placed,
        out_specs=(
            P("rep", TILE, None, None, None),
            P("rep", TILE, None, None, None),
            P("rep", None),
            P("rep", None),
            P(),
        ),
        check_vma=False,
    )
```

time: 405 us -> 178 us (0.44)
  blocking collectives: 135 us -> 0 us
  waiting for transfers between devices: 136 us -> 23.3 us
  starting transfers between devices: 23.8 us -> 46.8 us
  between operations: 15 us -> 2.16 us
  local copies, waits for them, and re-layouts: 12.8 us -> 20.8 us
    psum x1 -> x0, waiting for transfers between devices: 115 us -> none  [per_device(): summed = lax.psum((grad_expand, grad_reduce), 'tile')]
    psum x1 -> x0, blocking collectives: 92 us -> none  [per_device(): kernel_total = lax.psum(grad_kern, ('tile', 'rep'))]
    all_gather x2 -> x0, blocking collectives: 43.2 us -> none  [the longest x1 22.1 us: per_device(): lax.all_gather(expand_weight, 'rep', axis=0, tiled=True)]
    ppermute x8 -> x21, starting transfers between devices: 23.2 us -> 46.8 us  [the longest x17 38.9 us: swap(): return lax.ppermute(value, axis, [(i, i ^ bit) for i in range(SIZES[axis])])]
    ppermute x8 -> x21, waiting for transfers between devices: 5.99 us -> 23.3 us  [the longest x17 23.2 us: swap(): return lax.ppermute(value, axis, [(i, i ^ bit) for i in range(SIZES[axis])])]
    reduce_scatter x2 -> x0, waiting for transfers between devices: 14.9 us -> none  [the longest x1 14.9 us: per_device(): lax.psum_scatter(summed[0], 'rep', scatter_dimension=0, tiled=True)]
    reshape x0 -> x3, local copies, waits for them, and re-layouts: none -> 4.14 us  [the longest x1 2.11 us: reduce_gradients(): expand = grad_expand.astype(bf16).reshape(-1, width)]
  transfers between devices with their start and end apart: 11 -> 21, of which waited for: 4 -> 9; matrix products, arithmetic and copies ran while one was open for 12% -> 39% of each run, Pallas kernels for 0% -> 0%
where the time goes in v1:
time: 178 us
  matrix products  58.7 us (33%)
  starting transfers between devices  46.8 us (26%)
  other arithmetic  26 us (15%)
  waiting for transfers between devices  23.3 us (13%)
  local copies, waits for them, and re-layouts  20.8 us (12%)
  between operations  2.16 us (1%)
    conv_general_dilated x3, matrix products, depthwise(): lax.conv_general_dilated(padded[None], kernel[:, :, None, :], (1, 1), 'VA...  41.3 us
    ppermute x17, starting transfers between devices, swap(): return lax.ppermute(value, axis, [(i, i ^ bit) for i in range(SIZES[axis])])  38.9 us
    ppermute x17, waiting for transfers between devices, swap(): return lax.ppermute(value, axis, [(i, i ^ bit) for i in range(SIZES[axis])])  23.2 us
    reduce_sum x1, other arithmetic, forward_backward(): jnp.mean(spread * spread, axis=1, keepdims=True) + 1e-06  15.9 us
    ppermute x2, starting transfers between devices, with_rims(): lax.ppermute(jnp.where(core == 0, west_edge, east_edge), ('x', 'core'), [...  6.58 us
    dot_general x2, matrix products, right_contract(): lax.dot_general(left, right, (((1,), (1,)), ((), ())), preferred_element_...  4.31 us
    unnamed x63, local copies, waits for them, and re-layouts  4.29 us
    dot_general x2, matrix products, row_contract(): lax.dot_general(left, right, (((0,), (0,)), ((), ())), preferred_element_...  4.03 us
  transfers between devices with their start and end apart: 21, of which 9 were waited for; matrix products, arithmetic and copies ran while one was open for 39% of the time, Pallas kernels for 0%

profile of v1, /device:TPU:1, one launch (start us, length us, event | category | flops | bytes accessed | tf_op | source)
XLA Modules:
  0.0 177.7 jit_solution(12758403507700678138)
XLA Ops:
  0.7 0.9 reshape.214
  1.6 0.8 select_bitcast_fusion.11
  2.4 7.7 %collective-permute-start.4 = (bf16[1,96,192]{2,1,0:T(8,128)(2,1)S(1)}, bf16[1,96,192]{2,1,0:T(8,128)(2,1)S(1)}, u32[]{:S(2)}, u32[]{:S(2)}) collective-permute-start(bf16[1,96,192]{2,1,0:T(8,128)(2,1)S(1)} %select_bitcast_fusion.11), channel_id=1, source_target_pairs={{0,4},{1,5},{2,6},{3,7},{4,0},{5,1},{6,2},{7,3},{8,12},{9,13},{10,... | collective-permute-start | bytes 110600 | tf_op jit(solution)/shard_map/ppermute | solution.py:18
  10.8 1.4 convolution_convert_fusion.1
  12.2 0.4 reshape.212
  12.8 3.3 %collective-permute-start = (bf16[3,32,192]{2,0,1:T(4,128)(2,1)S(1)}, bf16[3,32,192]{2,0,1:T(4,128)(2,1)S(1)}, u32[]{:S(2)}, u32[]{:S(2)}) collective-permute-start(bf16[3,32,192]{2,0,1:T(4,128)(2,1)S(1)} %get-tuple-element.35), channel_id=1, source_target_pairs={{8,16},{16,8},{40,48},{48,40},{9,17},{17,9},{41,49},{49,41},{10,18... | collective-permute-start | bytes 110600 | tf_op jit(solution)/shard_map/ppermute | solution.py:111
  16.7 1.7 convolution_convert_fusion
  18.5 1.0 bitcast_multiply_fusion
  19.5 0.6 convert_element_type.250
  20.1 0.6 copy.145
  20.7 0.6 copy.152
  21.4 0.6 rev.3
  22.0 1.2 copy.136
  23.4 2.5 %collective-permute-start.3 = (bf16[3,38,192]{2,1,0:T(8,128)(2,1)S(1)}, bf16[3,38,192]{2,1,0:T(8,128)(2,1)S(1)}, u32[]{:S(2)}, u32[]{:S(2)}) collective-permute-start(bf16[3,38,192]{2,1,0:T(8,128)(2,1)S(1)} %broadcast_select_fusion.19), channel_id=1, source_target_pairs={{0,32},{16,48},{32,0},{48,16},{1,33},{17,49},{33,1},{49,17},{2,34}... | collective-permute-start | bytes 131336 | tf_op jit(solution)/shard_map/ppermute | solution.py:18
  25.9 0.7 collective-permute-start.2
  26.6 1.3 collective-permute-start.5
  28.4 19.5 %fusion.47 = (f32[32,32]{1,0:T(8,128)S(1)}, f32[1,32,32,192]{3,0,2,1:T(1,128)S(1)}) fusion(f32[7,7,1,192]{3,1,0,2:T(8,128)S(1)} %bitcast.175, bf16[1,38,38,192]{3,2,1,0:T(8,128)(2,1)S(1)} %maximum_bitcast_fusion), kind=kOutput, calls=%fused_computation.141 | convolution fusion | flops 115801088 | bytes 1382656 | tf_op jit(solution)/shard_map/conv_general_dilated | solution.py:26
  48.0 15.9 %multiply_reduce_fusion = f32[32,32]{1,0:T(8,128)} fusion(f32[1,32,32,192]{3,0,2,1:T(1,128)S(1)} %get-tuple-element.60, f32[32,32]{1,0:T(8,128)S(1)} %broadcast_multiply_fusion), kind=kLoop, calls=%fused_computation.33 | loop fusion | flops 588800 | bytes 794624 | tf_op jit(solution)/shard_map/reduce_sum | solution.py:55
  63.8 0.7 div.53
  64.7 0.8 collective-permute-start.6
  65.6 0.6 add_rsqrt_fusion
  66.2 1.4 rsqrt.13
  67.5 1.8 %collective-permute-done.6 = bf16[4,96,192]{2,1,0:T(8,128)(2,1)S(1)} collective-permute-done((bf16[4,96,192]{2,1,0:T(8,128)(2,1)S(1)}, bf16[4,96,192]{2,1,0:T(8,128)(2,1)S(1)}, u32[]{:S(2)}, u32[]{:S(2)}) %collective-permute-start.6) | collective-permute-done | bytes 147488 | tf_op jit(solution)/shard_map/ppermute | solution.py:18
  69.5 0.8 copy.135
  70.2 2.8 %collective-permute-start.7 = (bf16[768,192]{1,0:T(8,128)(2,1)}, bf16[768,192]{1,0:T(8,128)(2,1)S(1)}, u32[]{:S(2)}, u32[]{:S(2)}) collective-permute-start(bf16[768,192]{1,0:T(8,128)(2,1)} %bitcast.25), channel_id=1, source_target_pairs={{0,8},{8,0},{1,9},{9,1},{2,10},{10,2},{3,11},{11,3},{4,12},{12,4},... | collective-permute-start | bytes 884744 | tf_op jit(solution)/shard_map/ppermute | solution.py:18
  73.0 2.5 %multiply_convert_fusion.1 = bf16[1,32,32,192]{3,0,2,1:T(2,128)(2,1)S(1)} fusion(f32[1,32,32,192]{3,0,2,1:T(1,128)S(1)} %get-tuple-element.60, f32[192]{0:T(256)S(1)} %copy-done.22, f32[32,32]{1,0:T(8,128)S(1)} %copy-done.13, f32[32,32]{1,0:T(8,128)S(1)} %broadcast_multiply_fusion), kind=kLoop, calls=%fused_computation.32 | loop fusion | flops 786432 | bytes 1188608 | tf_op jit(solution)/shard_map/convert_element_type | solution.py:57
  75.5 0.9 copy.174
  76.8 1.2 broadcast_select_fusion.2
  78.0 1.1 reshape.217
  79.1 2.2 %multiply_convert_fusion = (bf16[1024,768]{1,0:T(8,128)(2,1)S(1)}, f32[1024,768]{1,0:T(8,128)S(1)}) fusion(f32[768]{0:T(1024)S(1)} %copy-done.24, bf16[1024,192]{1,0:T(8,128)(2,1)} %bitcast.162, bf16[192,768]{1,0:T(8,128)(2,1)} %reshape.217), kind=kOutput, calls=%fused_computation.7 | convolution fusion | flops 306708480 | bytes 5409792 | tf_op jit(solution)/shard_map/dot_general | solution.py:58
  81.3 2.7 %fusion.5 = bf16[1024,768]{1,0:T(8,128)(2,1)S(1)} fusion(f32[1024,768]{1,0:T(8,128)S(1)} %get-tuple-element.62, bf16[1024,192]{1,0:T(8,128)(2,1)S(1)} %copy-done.10, f32[768]{0:T(1024)S(1)} %copy-done.24, bf16[768,192]{1,0:T(8,128)(2,1)S(1)} %copy-done.6, bf16[768,192]{1,0:T(8,128)(2,1)} %bitcast.25, pred[]{:T(512)S(6)} %eq.30), kind=kOutput, calls=%fused_computation.6 | convolution fusion | flops 310788096 | bytes 5704705 | tf_op jit(solution)/shard_map/dot_general | solution.py:43
  84.1 1.3 convolution_convert_fusion.3
  85.4 1.6 fusion.46
  87.0 2.4 %fusion.8 = bf16[1024,192]{0,1:T(8,128)(2,1)} fusion(f32[1024,192]{0,1:T(8,128)S(1)} %copy-done.1, bf16[1024,768]{1,0:T(8,128)(2,1)S(1)} %get-tuple-element.61, f32[1024]{0:T(1024)S(1)} %copy-done.21, bf16[768,192]{1,0:T(8,128)(2,1)S(1)} %copy-done.6, bf16[768,192]{1,0:T(8,128)(2,1)} %bitcast.25, pred[]{:T(512)S(6)} %eq.30), kind=kOutput, calls=%fused_computation.15 | convolution fusion | flops 302727168 | bytes 3346433 | tf_op jit(solution)/shard_map/dot_general | solution.py:61
  89.4 2.0 %copy.139 = bf16[1024,192]{1,0:T(8,128)(2,1)} copy(bf16[1024,192]{0,1:T(8,128)(2,1)} %fusion.8) | data formatting | bytes 786432 | tf_op jit(solution)/shard_map/mul | solution.py:63
  91.4 1.9 %copy.140 = bf16[2,2,16,16,192]{4,3,2,1,0:T(8,128)(2,1)} copy(bf16[2,2,16,16,192]{4,3,1,2,0:T(8,128)(2,1)} %bitcast.163) | data formatting | bytes 786432 | tf_op jit(solution)/shard_map/transpose | solution.py:99
  93.3 2.1 %reshape.223 = bf16[768,192]{1,0:T(8,128)(2,1)} reshape(bf16[192,768]{1,0:T(8,128)(2,1)} %convolution_convert_fusion.3) | data formatting | bytes 589824 | tf_op jit(solution)/shard_map/reshape | solution.py:153
  95.4 2.7 %broadcast_select_fusion = (bf16[768,192]{1,0:T(8,128)(2,1)}, bf16[768,192]{1,0:T(8,128)(2,1)}) fusion(bf16[768,192]{1,0:T(8,128)(2,1)} %reshape.223, pred[]{:T(512)S(6)} %eq.30, bf16[1024,768]{1,0:T(8,128)(2,1)S(1)} %get-tuple-element.61, bf16[1024,192]{1,0:T(8,128)(2,1)} %bitcast_multiply_fusion), kind=kOutput, calls=%fused_computation.52 | convolution fusion | flops 302284800 | bytes 2850817 | tf_op jit(solution)/shard_map/dot_general | solution.py:39
  98.6 0.7 copy-done.9
  99.3 9.2 %fusion.16 = bf16[7,7,192]{2,1,0:T(8,128)(2,1)S(1)} fusion(bf16[1,38,38,192]{3,2,1,0:T(8,128)(2,1)S(1)} %copy-done.9, bf16[32,32,1,192]{3,1,0,2:T(8,128)(2,1)S(1)} %bitcast.154), kind=kOutput, calls=%fused_computation.26 | convolution fusion | flops 19276992 | bytes 966528 | tf_op jit(solution)/shard_map/conv_general_dilated | solution.py:26
  108.8 3.3 %collective-permute-start.8 = (bf16[3,32,192]{2,0,1:T(4,128)(2,1)S(1)}, bf16[3,32,192]{2,0,1:T(4,128)(2,1)S(1)}, u32[]{:S(2)}, u32[]{:S(2)}) collective-permute-start(bf16[3,32,192]{2,0,1:T(4,128)(2,1)S(1)} %get-tuple-element.33), channel_id=1, source_target_pairs={{8,16},{16,8},{40,48},{48,40},{9,17},{17,9},{41,49},{49,41},{10,18... | collective-permute-start | bytes 110600 | tf_op jit(solution)/shard_map/ppermute | solution.py:111
  112.5 0.5 convolution_bitcast_fusion.1
  113.1 1.2 copy.162
  114.5 0.8 collective-permute-start.13
  115.5 5.8 %collective-permute-done.13 = bf16[448,192]{1,0:T(8,128)(2,1)S(1)} collective-permute-done((bf16[448,192]{1,0:T(8,128)(2,1)S(1)}, bf16[448,192]{1,0:T(8,128)(2,1)S(1)}, u32[]{:S(2)}, u32[]{:S(2)}) %collective-permute-start.13) | collective-permute-done | bytes 172064 | tf_op jit(solution)/shard_map/ppermute | solution.py:18
  121.4 1.3 collective-permute-start.14
  122.7 5.9 %collective-permute-start.11 = (bf16[3,38,192]{2,1,0:T(8,128)(2,1)S(1)}, bf16[3,38,192]{2,1,0:T(8,128)(2,1)S(1)}, u32[]{:S(2)}, u32[]{:S(2)}) collective-permute-start(bf16[3,38,192]{2,1,0:T(8,128)(2,1)S(1)} %broadcast_select_fusion.15), channel_id=1, source_target_pairs={{0,32},{16,48},{32,0},{48,16},{1,33},{17,49},{33,1},{49,17},{2,34}... | collective-permute-start | bytes 131336 | tf_op jit(solution)/shard_map/ppermute | solution.py:18
  128.6 0.7 collective-permute-start.10
  129.3 0.8 collective-permute-done.14
  130.4 8.4 %collective-permute-done.15 = bf16[160,192]{1,0:T(8,128)(2,1)S(1)} collective-permute-done((bf16[160,192]{1,0:T(8,128)(2,1)S(1)}, bf16[160,192]{1,0:T(8,128)(2,1)S(1)}, u32[]{:S(2)}, u32[]{:S(2)}) %collective-permute-start.15) | collective-permute-done | bytes 61472 | tf_op jit(solution)/shard_map/ppermute | solution.py:18
  139.0 0.4 maximum_bitcast_fusion.1
  139.3 2.9 %collective-permute-done.16 = bf16[160,192]{1,0:T(8,128)(2,1)S(1)} collective-permute-done((bf16[160,192]{1,0:T(8,128)(2,1)S(1)}, bf16[160,192]{1,0:T(8,128)(2,1)S(1)}, u32[]{:S(2)}, u32[]{:S(2)}) %collective-permute-start.16) | collective-permute-done | bytes 61472 | tf_op jit(solution)/shard_map/ppermute | solution.py:18
  142.3 5.9 %collective-permute-start.17 = (bf16[160,192]{1,0:T(8,128)(2,1)S(1)}, bf16[160,192]{1,0:T(8,128)(2,1)S(1)}, u32[]{:S(2)}, u32[]{:S(2)}) collective-permute-start(bf16[160,192]{1,0:T(8,128)(2,1)S(1)} %pad_maximum_fusion.7), channel_id=1, source_target_pairs={{0,32},{16,48},{32,0},{48,16},{1,33},{17,49},{33,1},{49,17},{2,34}... | collective-permute-start | bytes 184328 | tf_op jit(solution)/shard_map/ppermute | solution.py:18
  148.2 12.6 %fusion.6 = f32[1,32,32,192]{3,0,2,1:T(1,128)S(1)} fusion(bf16[1,38,38,192]{3,2,1,0:T(8,128)(2,1)S(1)} %maximum_bitcast_fusion.1, f32[7,7,1,192]{3,1,0,2:T(8,128)S(1)} %bitcast.176), kind=kOutput, calls=%fused_computation.9 | convolution fusion | flops 115605504 | bytes 1378560 | tf_op jit(solution)/shard_map/conv_general_dilated | solution.py:26
  161.0 1.4 collective-permute-start.18
  162.8 1.6 collective-permute-done.18
  164.5 1.7 collective-permute-start.19
  166.2 0.5 convolution_bitcast_fusion
  166.8 1.2 copy.163
  167.9 1.4 collective-permute-done.19
  169.4 6.1 %collective-permute-start.20 = (bf16[96,192]{1,0:T(8,128)(2,1)S(1)}, bf16[96,192]{1,0:T(8,128)(2,1)S(1)}, u32[]{:S(2)}, u32[]{:S(2)}) collective-permute-start(bf16[96,192]{1,0:T(8,128)(2,1)S(1)} %add_convert_fusion.1), channel_id=1, source_target_pairs={{0,8},{8,0},{1,9},{9,1},{2,10},{10,2},{3,11},{11,3},{4,12},{12,4},... | collective-permute-start | bytes 110600 | tf_op jit(solution)/shard_map/ppermute | solution.py:18
  175.5 0.6 mul.195
  176.3 0.7 convert_multiply_fusion
  177.0 0.7 mul.191
  (140 shorter events, 4.9 us)
Async XLA Ops:
  0.6 10.2 %copy-start = (bf16[1,4,16,16,192]{4,3,2,1,0:T(8,128)(2,1)S(1)}, bf16[1,4,16,16,192]{4,3,2,1,0:T(8,128)(2,1)}, u32[]{:S(2)}) copy-start(bf16[1,4,16,16,192]{4,3,2,1,0:T(8,128)(2,1)} %param.9) | copy-start | bytes 1179652
  2.4 24.2 %collective-permute-start.4 = (bf16[1,96,192]{2,1,0:T(8,128)(2,1)S(1)}, bf16[1,96,192]{2,1,0:T(8,128)(2,1)S(1)}, u32[]{:S(2)}, u32[]{:S(2)}) collective-permute-start(bf16[1,96,192]{2,1,0:T(8,128)(2,1)S(1)} %select_bitcast_fusion.11), channel_id=1, source_target_pairs={{0,4},{1,5},{2,6},{3,7},{4,0},{5,1},{6,2},{7,3},{8,12},{9,13},{10,... | collective-permute-start | bytes 110600 | tf_op jit(solution)/shard_map/ppermute | solution.py:18
  10.8 5.9 %copy-start.27 = (s32[4]{0:T(128)}, s32[4]{0:T(128)S(1)}, u32[]{:S(2)}) copy-start(s32[4]{0:T(128)S(1)} %compare_convert_fusion) | copy-start | bytes 52
  10.8 5.3 %copy-start.25 = (s32[1,1,4]{2,1,0:T(1,128)S(1)}, s32[1,1,4]{2,1,0:T(1,128)}, u32[]{:S(2)}) copy-start(s32[1,1,4]{2,1,0:T(1,128)} %param.11) | copy-start | bytes 52
  12.8 10.4 %collective-permute-start = (bf16[3,32,192]{2,0,1:T(4,128)(2,1)S(1)}, bf16[3,32,192]{2,0,1:T(4,128)(2,1)S(1)}, u32[]{:S(2)}, u32[]{:S(2)}) collective-permute-start(bf16[3,32,192]{2,0,1:T(4,128)(2,1)S(1)} %get-tuple-element.35), channel_id=1, source_target_pairs={{8,16},{16,8},{40,48},{48,40},{9,17},{17,9},{41,49},{49,41},{10,18... | collective-permute-start | bytes 110600 | tf_op jit(solution)/shard_map/ppermute | solution.py:111
  16.1 7.1 %collective-permute-start.1 = (bf16[3,32,192]{2,0,1:T(4,128)(2,1)S(1)}, bf16[3,32,192]{2,0,1:T(4,128)(2,1)S(1)}, u32[]{:S(2)}, u32[]{:S(2)}) collective-permute-start(bf16[3,32,192]{2,0,1:T(4,128)(2,1)S(1)} %get-tuple-element.36), channel_id=1, source_target_pairs={{0,8},{8,0},{1,9},{9,1},{2,10},{10,2},{3,11},{11,3},{4,12},{12,4},... | collective-permute-start | bytes 110600 | tf_op jit(solution)/shard_map/ppermute | solution.py:18
  18.4 3.0 %copy-start.19 = (f32[7,7,192]{2,1,0:T(8,128)S(1)}, f32[7,7,192]{2,1,0:T(8,128)}, u32[]{:S(2)}) copy-start(f32[7,7,192]{2,1,0:T(8,128)} %param.13) | copy-start | bytes 112900
  23.4 4.7 %collective-permute-start.3 = (bf16[3,38,192]{2,1,0:T(8,128)(2,1)S(1)}, bf16[3,38,192]{2,1,0:T(8,128)(2,1)S(1)}, u32[]{:S(2)}, u32[]{:S(2)}) collective-permute-start(bf16[3,38,192]{2,1,0:T(8,128)(2,1)S(1)} %broadcast_select_fusion.19), channel_id=1, source_target_pairs={{0,32},{16,48},{32,0},{48,16},{1,33},{17,49},{33,1},{49,17},{2,34}... | collective-permute-start | bytes 131336 | tf_op jit(solution)/shard_map/ppermute | solution.py:18
  25.9 2.1 %collective-permute-start.2 = (bf16[3,38,192]{2,1,0:T(8,128)(2,1)S(1)}, bf16[3,38,192]{2,1,0:T(8,128)(2,1)S(1)}, u32[]{:S(2)}, u32[]{:S(2)}) collective-permute-start(bf16[3,38,192]{2,1,0:T(8,128)(2,1)S(1)} %get-tuple-element.30), channel_id=1, source_target_pairs={{32,64},{48,80},{96,128},{112,144},{160,192},{176,208},{64,32},{80... | collective-permute-start | bytes 131336 | tf_op jit(solution)/shard_map/ppermute | solution.py:122
  26.6 38.0 %collective-permute-start.5 = (bf16[2,96,192]{2,1,0:T(8,128)(2,1)S(1)}, bf16[2,96,192]{2,1,0:T(8,128)(2,1)S(1)}, u32[]{:S(2)}, u32[]{:S(2)}) collective-permute-start(bf16[2,96,192]{2,1,0:T(8,128)(2,1)S(1)} %maximum_bitcast_fusion.2), channel_id=1, source_target_pairs={{0,2},{1,3},{2,0},{3,1},{4,6},{5,7},{6,4},{7,5},{8,10},{9,11},{10,... | collective-permute-start | bytes 221192 | tf_op jit(solution)/shard_map/ppermute | solution.py:18
  28.4 19.5 %copy-start.8 = (bf16[1,38,38,192]{3,2,1,0:T(8,128)(2,1)}, bf16[1,38,38,192]{3,2,1,0:T(8,128)(2,1)S(1)}, u32[]{:S(2)}) copy-start(bf16[1,38,38,192]{3,2,1,0:T(8,128)(2,1)S(1)} %maximum_bitcast_fusion) | copy-start | bytes 1663492
  64.5 1.0 copy-start.18
  64.7 4.6 %collective-permute-start.6 = (bf16[4,96,192]{2,1,0:T(8,128)(2,1)S(1)}, bf16[4,96,192]{2,1,0:T(8,128)(2,1)S(1)}, u32[]{:S(2)}, u32[]{:S(2)}) collective-permute-start(bf16[4,96,192]{2,1,0:T(8,128)(2,1)S(1)} %bitcast.170), channel_id=1, source_target_pairs={{0,1},{1,0},{2,3},{3,2},{4,5},{5,4},{6,7},{7,6},{8,9},{9,8},{10,11... | collective-permute-start | bytes 442376 | tf_op jit(solution)/shard_map/ppermute | solution.py:18
  67.5 5.5 %copy-start.13 = (f32[32,32]{1,0:T(8,128)S(1)}, f32[32,32]{1,0:T(8,128)}, u32[]{:S(2)}) copy-start(f32[32,32]{1,0:T(8,128)} %add_rsqrt_fusion) | copy-start | bytes 12292
  67.5 5.5 %copy-start.22 = (f32[192]{0:T(256)S(1)}, f32[192]{0:T(256)}, u32[]{:S(2)}) copy-start(f32[192]{0:T(256)} %param.14) | copy-start | bytes 2308
  70.2 6.5 %collective-permute-start.7 = (bf16[768,192]{1,0:T(8,128)(2,1)}, bf16[768,192]{1,0:T(8,128)(2,1)S(1)}, u32[]{:S(2)}, u32[]{:S(2)}) collective-permute-start(bf16[768,192]{1,0:T(8,128)(2,1)} %bitcast.25), channel_id=1, source_target_pairs={{0,8},{8,0},{1,9},{9,1},{2,10},{10,2},{3,11},{11,3},{4,12},{12,4},... | collective-permute-start | bytes 884744 | tf_op jit(solution)/shard_map/ppermute | solution.py:18
  76.4 2.6 %copy-start.24 = (f32[768]{0:T(1024)S(1)}, f32[768]{0:T(1024)}, u32[]{:S(2)}) copy-start(f32[768]{0:T(1024)} %param.16) | copy-start | bytes 9220
  76.8 2.3 %copy-start.5 = (bf16[768,192]{1,0:T(8,128)(2,1)}, bf16[768,192]{1,0:T(8,128)(2,1)S(1)}, u32[]{:S(2)}) copy-start(bf16[768,192]{1,0:T(8,128)(2,1)S(1)} %collective-permute-done.7) | copy-start | bytes 884740
  79.1 2.2 %copy-start.6 = (bf16[768,192]{1,0:T(8,128)(2,1)S(1)}, bf16[768,192]{1,0:T(8,128)(2,1)}, u32[]{:S(2)}) copy-start(bf16[768,192]{1,0:T(8,128)(2,1)} %copy-done.5) | copy-start | bytes 884740
  79.1 2.2 %copy-start.10 = (bf16[1024,192]{1,0:T(8,128)(2,1)S(1)}, bf16[1024,192]{1,0:T(8,128)(2,1)}, u32[]{:S(2)}) copy-start(bf16[1024,192]{1,0:T(8,128)(2,1)} %bitcast_multiply_fusion) | copy-start | bytes 1179652
  81.3 2.8 %copy-start.15 = (f32[1024]{0:T(1024)S(1)}, f32[1024]{0:T(1024)}, u32[]{:S(2)}) copy-start(f32[1024]{0:T(1024)} %div.53) | copy-start | bytes 12292
  81.3 2.8 %copy-start.16 = (f32[1024]{0:T(1024)S(1)}, f32[1024]{0:T(1024)}, u32[]{:S(2)}) copy-start(f32[1024]{0:T(1024)} %rsqrt.13) | copy-start | bytes 12292
  81.3 2.8 %copy-start.23 = (f32[192]{0:T(256)S(1)}, f32[192]{0:T(256)}, u32[]{:S(2)}) copy-start(f32[192]{0:T(256)} %param.14) | copy-start | bytes 2308
  84.1 1.3 copy-start.3
  85.4 1.6 copy-start.1
  85.4 1.6 copy-start.21
  95.4 2.8 %copy-start.2 = (f32[1024,192]{0,1:T(8,128)S(1)}, f32[1024,192]{0,1:T(8,128)}, u32[]{:S(2)}) copy-start(f32[1024,192]{0,1:T(8,128)} %get-tuple-element.63) | copy-start | bytes 2359300
  98.1 1.1 copy-start.9
  99.3 9.3 %copy-start.12 = (bf16[768,192]{1,0:T(8,128)(2,1)S(1)}, bf16[768,192]{1,0:T(8,128)(2,1)}, u32[]{:S(2)}) copy-start(bf16[768,192]{1,0:T(8,128)(2,1)} %get-tuple-element.64) | copy-start | bytes 884740
  99.3 13.2 %copy-start.26 = (s32[1,1,4]{2,1,0:T(1,128)S(1)}, s32[1,1,4]{2,1,0:T(1,128)}, u32[]{:S(2)}) copy-start(s32[1,1,4]{2,1,0:T(1,128)} %param.11) | copy-start | bytes 52
  99.3 13.2 %copy-start.28 = (s32[4]{0:T(128)S(1)}, s32[4]{0:T(128)}, u32[]{:S(2)}) copy-start(s32[4]{0:T(128)} %copy-done.27) | copy-start | bytes 52
  108.5 4.0 %copy-start.4 = (bf16[2,2,16,16,192]{4,3,2,1,0:T(8,128)(2,1)S(1)}, bf16[2,2,16,16,192]{4,3,2,1,0:T(8,128)(2,1)}, u32[]{:S(2)}) copy-start(bf16[2,2,16,16,192]{4,3,2,1,0:T(8,128)(2,1)} %copy.140) | copy-start | bytes 1179652
  108.6 5.6 %collective-permute-start.12 = (bf16[832,192]{1,0:T(8,128)(2,1)S(1)}, bf16[832,192]{1,0:T(8,128)(2,1)S(1)}, u32[]{:S(2)}, u32[]{:S(2)}) collective-permute-start(bf16[832,192]{1,0:T(8,128)(2,1)S(1)} %pad_maximum_fusion), channel_id=1, source_target_pairs={{0,8},{8,0},{1,9},{9,1},{2,10},{10,2},{3,11},{11,3},{4,12},{12,4},... | collective-permute-start | bytes 958472 | tf_op jit(solution)/shard_map/ppermute | solution.py:18
  108.8 6.5 %collective-permute-start.8 = (bf16[3,32,192]{2,0,1:T(4,128)(2,1)S(1)}, bf16[3,32,192]{2,0,1:T(4,128)(2,1)S(1)}, u32[]{:S(2)}, u32[]{:S(2)}) collective-permute-start(bf16[3,32,192]{2,0,1:T(4,128)(2,1)S(1)} %get-tuple-element.33), channel_id=1, source_target_pairs={{8,16},{16,8},{40,48},{48,40},{9,17},{17,9},{41,49},{49,41},{10,18... | collective-permute-start | bytes 110600 | tf_op jit(solution)/shard_map/ppermute | solution.py:111
  112.1 3.2 %collective-permute-start.9 = (bf16[3,32,192]{2,0,1:T(4,128)(2,1)S(1)}, bf16[3,32,192]{2,0,1:T(4,128)(2,1)S(1)}, u32[]{:S(2)}, u32[]{:S(2)}) collective-permute-start(bf16[3,32,192]{2,0,1:T(4,128)(2,1)S(1)} %get-tuple-element.34), channel_id=1, source_target_pairs={{0,8},{8,0},{1,9},{9,1},{2,10},{10,2},{3,11},{11,3},{4,12},{12,4},... | collective-permute-start | bytes 110600 | tf_op jit(solution)/shard_map/ppermute | solution.py:18
  112.5 1.7 copy-start.7
  112.5 1.7 copy-start.11
  114.5 6.8 %collective-permute-start.13 = (bf16[448,192]{1,0:T(8,128)(2,1)S(1)}, bf16[448,192]{1,0:T(8,128)(2,1)S(1)}, u32[]{:S(2)}, u32[]{:S(2)}) collective-permute-start(bf16[448,192]{1,0:T(8,128)(2,1)S(1)} %pad_maximum_fusion.2), channel_id=1, source_target_pairs={{0,1},{1,0},{2,3},{3,2},{4,5},{5,4},{6,7},{7,6},{8,9},{9,8},{10,11... | collective-permute-start | bytes 516104 | tf_op jit(solution)/shard_map/ppermute | solution.py:18
  121.4 8.7 %collective-permute-start.14 = (bf16[256,192]{1,0:T(8,128)(2,1)S(1)}, bf16[256,192]{1,0:T(8,128)(2,1)S(1)}, u32[]{:S(2)}, u32[]{:S(2)}) collective-permute-start(bf16[256,192]{1,0:T(8,128)(2,1)S(1)} %pad_maximum_fusion.4), channel_id=1, source_target_pairs={{0,2},{1,3},{2,0},{3,1},{4,6},{5,7},{6,4},{7,5},{8,10},{9,11},{10,... | collective-permute-start | bytes 294920 | tf_op jit(solution)/shard_map/ppermute | solution.py:18
  122.7 7.6 %collective-permute-start.11 = (bf16[3,38,192]{2,1,0:T(8,128)(2,1)S(1)}, bf16[3,38,192]{2,1,0:T(8,128)(2,1)S(1)}, u32[]{:S(2)}, u32[]{:S(2)}) collective-permute-start(bf16[3,38,192]{2,1,0:T(8,128)(2,1)S(1)} %broadcast_select_fusion.15), channel_id=1, source_target_pairs={{0,32},{16,48},{32,0},{48,16},{1,33},{17,49},{33,1},{49,17},{2,34}... | collective-permute-start | bytes 131336 | tf_op jit(solution)/shard_map/ppermute | solution.py:18
  128.6 1.7 collective-permute-start.10
  130.2 18.0 %copy-start.20 = (f32[7,7,192]{2,1,0:T(8,128)S(1)}, f32[7,7,192]{2,1,0:T(8,128)}, u32[]{:S(2)}) copy-start(f32[7,7,192]{2,1,0:T(8,128)} %rev.3) | copy-start | bytes 112900
  130.2 8.6 %collective-permute-start.15 = (bf16[160,192]{1,0:T(8,128)(2,1)S(1)}, bf16[160,192]{1,0:T(8,128)(2,1)S(1)}, u32[]{:S(2)}, u32[]{:S(2)}) collective-permute-start(bf16[160,192]{1,0:T(8,128)(2,1)S(1)} %pad_maximum_fusion.5), channel_id=1, source_target_pairs={{0,4},{1,5},{2,6},{3,7},{4,0},{5,1},{6,2},{7,3},{8,12},{9,13},{10,... | collective-permute-start | bytes 184328 | tf_op jit(solution)/shard_map/ppermute | solution.py:18
  138.9 3.4 %collective-permute-start.16 = (bf16[160,192]{1,0:T(8,128)(2,1)S(1)}, bf16[160,192]{1,0:T(8,128)(2,1)S(1)}, u32[]{:S(2)}, u32[]{:S(2)}) collective-permute-start(bf16[160,192]{1,0:T(8,128)(2,1)S(1)} %pad_maximum_fusion.6), channel_id=1, source_target_pairs={{0,16},{16,0},{32,48},{48,32},{1,17},{17,1},{33,49},{49,33},{2,18}... | collective-permute-start | bytes 184328 | tf_op jit(solution)/shard_map/ppermute | solution.py:18
  142.3 18.6 %collective-permute-start.17 = (bf16[160,192]{1,0:T(8,128)(2,1)S(1)}, bf16[160,192]{1,0:T(8,128)(2,1)S(1)}, u32[]{:S(2)}, u32[]{:S(2)}) collective-permute-start(bf16[160,192]{1,0:T(8,128)(2,1)S(1)} %pad_maximum_fusion.7), channel_id=1, source_target_pairs={{0,32},{16,48},{32,0},{48,16},{1,33},{17,49},{33,1},{49,17},{2,34}... | collective-permute-start | bytes 184328 | tf_op jit(solution)/shard_map/ppermute | solution.py:18
  160.8 1.6 copy-start.14
  160.8 1.6 copy-start.17
  161.0 3.4 %collective-permute-start.18 = (bf16[160,192]{1,0:T(8,128)(2,1)S(1)}, bf16[160,192]{1,0:T(8,128)(2,1)S(1)}, u32[]{:S(2)}, u32[]{:S(2)}) collective-permute-start(bf16[160,192]{1,0:T(8,128)(2,1)S(1)} %pad_maximum_fusion.8), channel_id=1, source_target_pairs={{0,64},{64,0},{128,192},{192,128},{1,65},{65,1},{129,193},{193,129... | collective-permute-start | bytes 184328 | tf_op jit(solution)/shard_map/ppermute | solution.py:18
  164.5 4.9 %collective-permute-start.19 = (bf16[160,192]{1,0:T(8,128)(2,1)S(1)}, bf16[160,192]{1,0:T(8,128)(2,1)S(1)}, u32[]{:S(2)}, u32[]{:S(2)}) collective-permute-start(bf16[160,192]{1,0:T(8,128)(2,1)S(1)} %pad_maximum_fusion.9), channel_id=1, source_target_pairs={{0,128},{64,192},{128,0},{192,64},{1,129},{65,193},{129,1},{193,65... | collective-permute-start | bytes 184328 | tf_op jit(solution)/shard_map/ppermute | solution.py:18
  169.4 7.0 %collective-permute-start.20 = (bf16[96,192]{1,0:T(8,128)(2,1)S(1)}, bf16[96,192]{1,0:T(8,128)(2,1)S(1)}, u32[]{:S(2)}, u32[]{:S(2)}) collective-permute-start(bf16[96,192]{1,0:T(8,128)(2,1)S(1)} %add_convert_fusion.1), channel_id=1, source_target_pairs={{0,8},{8,0},{1,9},{9,1},{2,10},{10,2},{3,11},{11,3},{4,12},{12,4},... | collective-permute-start | bytes 110600 | tf_op jit(solution)/shard_map/ppermute | solution.py:18

commit v2 on v1

v2 whole, which is shorter than its diff:
```python
import functools

import jax
import jax.numpy as jnp
from jax import lax
from jax.experimental import pallas as pl
from jax.experimental.pallas import tpu as pltpu
from jax.sharding import Mesh, PartitionSpec as P

inv_root_two = 0.7071067811865476
inv_root_two_pi = 0.3989422804014327
bf16 = jnp.bfloat16
f32 = jnp.float32
TILE = ("y", "x", "core")
SIZES = {"y": 4, "x": 4, "core": 2, "rep": 8}
C, FF, S, CAP, KS = 192, 768, 16, 4, 7
SIDE = 2 * S
TAPS = KS * KS
HALF = S + 6
WIDE = SIDE + 8
LANES = 128
TAIL = C - LANES
SHARD = C * FF // SIZES["rep"] // LANES
ROWS = SHARD * SIZES["rep"]
EROWS = C // SIZES["rep"]
RROWS = FF // SIZES["rep"]
GROWS = 48
FACTOR = 1.0 / 512.0
VMEM_LIMIT = 48 * 1024 * 1024


def swap(value, axis, bit):
    return lax.ppermute(value, axis, [(i, i ^ bit) for i in range(SIZES[axis])])


def bit_of(axis, bit):
    return (lax.axis_index(axis) // bit) % 2


def dot(left, right, contract):
    return lax.dot_general(left, right, ((contract[:1], contract[1:]), ((), ())), preferred_element_type=f32)


def place_kernel(place, count, tiles, canvas):
    canvas[...] = jnp.zeros_like(canvas)

    def body(j, carry):
        p = place[0, j]
        row = pl.multiple_of((p // 2) * S, S)
        col = pl.multiple_of((p % 2) * S, S)
        canvas[pl.ds(row, S), pl.ds(col, S), :] = tiles[j]
        return carry

    lax.fori_loop(0, count[0, 0], body, 0)


def fill_planes(padded, planes):
    planes[0] = padded[:HALF, :, :LANES]
    planes[2] = padded[S:, :, :LANES]
    planes[1] = jnp.concatenate([padded[:HALF, :, LANES:], padded[S:, :, LANES:]], axis=-1)


def conv_planes(planes, taps, out):
    def body(step, carry):
        t = step // 4
        col = pl.multiple_of((step % 4) * 8, 8)
        acc = jnp.zeros((S, 8, LANES), f32)
        for dx in range(KS):
            x = planes[t, :, pl.ds(col, 16), :][:, dx : dx + 8, :]
            for dy in range(KS):
                acc = acc + x[dy : dy + S] * taps[t % 2, dy * KS + dx]
        out[t, :, pl.ds(col, 8), :] = acc
        return carry

    lax.fori_loop(0, 12, body, 0)


def correlate_planes(planes, field, acc):
    acc[...] = jnp.zeros_like(acc)

    def body(step, carry):
        t = step // 4
        col = pl.multiple_of((step % 4) * 8, 8)
        g = field[t, :, pl.ds(col, 8), :]
        for dx in range(KS):
            x = planes[t, :, pl.ds(col, 16), :][:, dx : dx + 8, :]
            for dy in range(KS):
                acc[t, dy * KS + dx] += jnp.sum(x[dy : dy + S] * g, axis=0)
        return carry

    lax.fori_loop(0, 12, body, 0)


def tile_of(planes, p):
    lower = p // 2
    col = pl.multiple_of((p % 2) * S, S)
    main = planes[2 * lower, :, pl.ds(col, S), :].reshape(S * S, LANES)
    tail = planes[1, :, pl.ds(col, S), :].reshape(S * S, LANES)
    tail = jnp.where(lower == 1, pltpu.roll(tail, TAIL, 1), tail)
    return jnp.concatenate([main, tail[:, :TAIL]], axis=1)


def pack_expand(value):
    pieces = []
    for z in range(SIZES["rep"]):
        rows = value[z * EROWS : (z + 1) * EROWS]
        pieces += [rows[:, k * LANES : (k + 1) * LANES] for k in range(FF // LANES)]
    return jnp.concatenate(pieces, axis=0)


def pack_reduce(value):
    pieces = []
    for z in range(SIZES["rep"]):
        rows = value[z * RROWS : (z + 1) * RROWS]
        half = RROWS // 2
        pieces.append(rows[:, :LANES])
        pieces.append(jnp.concatenate([rows[:half, LANES:], rows[half:, LANES:]], axis=1))
    return jnp.concatenate(pieces, axis=0)


def unpack_expand(value):
    bands = []
    for z in range(value.shape[0] // SHARD):
        start = z * SHARD
        bands.append(
            jnp.concatenate(
                [value[start + k * EROWS : start + (k + 1) * EROWS] for k in range(FF // LANES)], axis=1
            )
        )
    return jnp.concatenate(bands, axis=0)


def unpack_reduce(value):
    bands = []
    for z in range(value.shape[0] // SHARD):
        start = z * SHARD
        tail = value[start + RROWS : start + SHARD]
        tails = jnp.concatenate([tail[:, :TAIL], tail[:, TAIL:]], axis=0)
        bands.append(jnp.concatenate([value[start : start + RROWS], tails], axis=1))
    return jnp.concatenate(bands, axis=0)


def split_high_low(value):
    high = value.astype(bf16)
    return high, (value - high.astype(f32)).astype(bf16)


def block_kernel(
    place, count, core, padded, tiles, cotan, taps, gain, bias, held, other,
    result, field_out, keep, send, keep_taps,
    planes, filtered, field, tap_acc, expand, project, hidden, active, grad_hidden, grad_e, grad_r,
):
    me = core[0, 0]
    fill_planes(padded, planes)
    conv_planes(planes, taps, filtered)
    mine, theirs = held[...].astype(f32), other[...].astype(f32)
    expand[...] = unpack_expand(jnp.where(me == 0, mine, theirs)).astype(bf16)
    project[...] = unpack_reduce(jnp.where(me == 0, theirs, mine)).astype(bf16)
    field[...] = jnp.zeros_like(field)
    field_out[...] = jnp.zeros_like(field_out)
    grad_e[...] = jnp.zeros_like(grad_e)
    grad_r[...] = jnp.zeros_like(grad_r)

    def blank(j, carry):
        result[j] = jnp.zeros_like(result[j])
        return carry

    lax.fori_loop(count[0, 0], CAP, blank, 0)

    def slot(j, carry):
        p = place[0, j]
        lower = p // 2
        row = pl.multiple_of(lower * S, S)
        col = pl.multiple_of((p % 2) * S, S)
        x = tile_of(filtered, p)
        spread = x - jnp.sum(x, axis=1, keepdims=True) * (1.0 / C)
        inverse = lax.rsqrt(jnp.sum(spread * spread, axis=1, keepdims=True) * (1.0 / C) + 1e-6)
        normed = spread * inverse
        scaled = (normed * gain[...]).astype(bf16)
        up = cotan[j].reshape(S * S, C)
        hidden[0] = dot(scaled, expand[...], (1, 0))
        hidden[1] = dot(up, project[...], (1, 1))

        def gelu(r, carry):
            rows = pl.ds(pl.multiple_of(r * 16, 16), 16)
            h = hidden[0, rows, :] + bias[...]
            cdf = 0.5 * (1.0 + lax.erf(h * inv_root_two))
            slope = cdf + h * jnp.exp(-0.5 * h * h) * inv_root_two_pi
            active[rows, :] = (h * cdf).astype(bf16)
            grad_hidden[rows, :] = (hidden[1, rows, :] * slope).astype(bf16)
            return carry

        lax.fori_loop(0, S, gelu, 0)
        a, gh = active[...], grad_hidden[...]
        mixed = dot(a, project[...], (1, 0))
        result[j] = tiles[j].astype(f32) + mixed.reshape(S, S, C)
        grad_e[...] += dot(scaled, gh, (0, 0))
        grad_r[...] += dot(up, a, (0, 0))
        q = dot(gh, expand[...], (1, 1)) * gain[...]
        mean_q = jnp.sum(q, axis=1, keepdims=True) * (1.0 / C)
        mean_qn = jnp.sum(q * normed, axis=1, keepdims=True) * (1.0 / C)
        g = (inverse * (q - mean_q - normed * mean_qn)).astype(bf16)
        field_out[pl.ds(row, S), pl.ds(col, S), :] = g.reshape(S, S, C)
        g = g.astype(f32)
        field[2 * lower, :, pl.ds(col, S), :] = g[:, :LANES].reshape(S, S, LANES)
        tail = jnp.concatenate([g[:, LANES:], g[:, LANES:]], axis=1).reshape(S, S, LANES)
        old = field[1, :, pl.ds(col, S), :]
        side = lax.broadcasted_iota(jnp.int32, (S, S, LANES), 2) // TAIL
        field[1, :, pl.ds(col, S), :] = jnp.where(side == lower, tail, old)
        return carry

    lax.fori_loop(0, count[0, 0], slot, 0)

    correlate_planes(planes, field, tap_acc)
    sums = jnp.sum(tap_acc[...], axis=2)
    main = sums[0] + sums[2]
    tail = sums[1] + pltpu.roll(sums[1], TAIL, 1)
    pad = jnp.zeros((7, LANES), f32)
    main = jnp.concatenate([main, pad], axis=0)
    tail = jnp.concatenate([tail, pad], axis=0)
    low_lane = lax.broadcasted_iota(jnp.int32, (16, LANES), 1) < TAIL
    halves = []
    for h in range(2):
        s = 24 * h
        tails = jnp.where(low_lane, tail[s : s + 16], tail[s + 16 : s + 32])
        halves.append(jnp.concatenate([main[s : s + 32], tails], axis=0))
    keep_taps[...] = jnp.where(me == 0, halves[0], halves[1])
    high, low = split_high_low(jnp.where(me == 0, halves[1], halves[0]))
    send[ROWS : ROWS + GROWS] = high
    send[ROWS + GROWS :] = low
    e = pack_expand(grad_e[...])
    r = pack_reduce(grad_r[...].T)
    keep[...] = jnp.where(me == 0, e, r).astype(bf16)
    send[:ROWS] = jnp.where(me == 0, r, e).astype(bf16)


def spread_kernel(place, count, padded, cotan, taps, out, planes, summed):
    fill_planes(padded, planes)
    conv_planes(planes, taps, summed)

    def blank(j, carry):
        out[j] = jnp.zeros_like(out[j])
        return carry

    lax.fori_loop(count[0, 0], CAP, blank, 0)

    def slot(j, carry):
        out[j] = cotan[j].astype(f32) + tile_of(summed, place[0, j]).reshape(S, S, C)
        return carry

    lax.fori_loop(0, count[0, 0], slot, 0)


def call(kernel, ins, outs, scratch=(), name=None):
    smem = pl.BlockSpec(memory_space=pltpu.SMEM)
    vmem = pl.BlockSpec(memory_space=pltpu.VMEM)
    specs = [smem if v.dtype == jnp.int32 else vmem for v in ins]
    return pl.pallas_call(
        kernel,
        out_shape=[jax.ShapeDtypeStruct(shape, dtype) for shape, dtype in outs],
        in_specs=specs,
        out_specs=[vmem for _ in outs],
        scratch_shapes=[pltpu.VMEM(shape, dtype) for shape, dtype in scratch],
        compiler_params=pltpu.CompilerParams(vmem_limit_bytes=VMEM_LIMIT),
        name=name,
    )(*ins)


def spread_taps(kernel):
    flat = kernel.reshape(TAPS, C)
    both = jnp.stack([flat[:, :LANES], jnp.concatenate([flat[:, LANES:], flat[:, LANES:]], axis=1)])
    return jnp.broadcast_to(both[:, :, None, :], (2, TAPS, 8, LANES))


def with_rims(canvas):
    core = lax.axis_index("core")
    upper = lax.axis_index("x") // 2
    west_edge = canvas[:, :3].transpose(1, 0, 2)
    east_edge = canvas[:, -3:].transpose(1, 0, 2)
    inner = swap(jnp.where(core == 0, east_edge, west_edge), "core", 1)
    outer = lax.ppermute(
        jnp.where(core == 0, west_edge, east_edge),
        ("x", "core"),
        [(1, 2), (2, 1), (5, 6), (6, 5)],
    )
    west = jnp.where(core == 0, outer, inner).transpose(1, 0, 2)
    east = jnp.where(core == 0, inner, outer).transpose(1, 0, 2)
    blank = jnp.zeros((SIDE, WIDE - SIDE - 6, C), canvas.dtype)
    widened = jnp.concatenate([west, canvas, east, blank], axis=1)
    north_edge, south_edge = widened[:3], widened[-3:]
    near = swap(jnp.where(upper == 0, south_edge, north_edge), "x", 2)
    pairs = [(4 * y + x, 4 * (y + 1) + x - 2) for y in range(3) for x in (2, 3)]
    far = lax.ppermute(
        jnp.where(upper == 0, north_edge, south_edge),
        ("y", "x"),
        pairs + [(b, a) for a, b in pairs],
    )
    north = jnp.where(upper == 0, far, near)
    south = jnp.where(upper == 0, near, far)
    return jnp.concatenate([north, widened, south], axis=0).astype(f32)


def gather_weights(expand_weight, reduce_weight):
    core = lax.axis_index("core")
    half = RROWS // 2
    expand = jnp.concatenate(
        [expand_weight[:, k * LANES : (k + 1) * LANES] for k in range(FF // LANES)], axis=0
    )
    tails = jnp.concatenate([reduce_weight[:half, LANES:], reduce_weight[half:, LANES:]], axis=1)
    project = jnp.concatenate([reduce_weight[:, :LANES], tails], axis=0)
    held = jnp.where(core == 0, expand, project)[None]
    for step, bit in enumerate((4, 2, 1)):
        other = swap(held, "rep", bit)
        mine = bit_of("rep", bit)
        lower = jnp.where(mine == 0, held, other)
        higher = jnp.where(mine == 0, other, held)
        held = jnp.stack([lower, higher], axis=1).reshape(2 ** (step + 1), SHARD, LANES)
    held = held.reshape(ROWS, LANES)
    return held, swap(held, "core", 1)


def reduce_gradients(keep, send, taps):
    got = swap(send, "core", 1)
    held = keep.astype(f32) + got[:ROWS].astype(f32)
    taps = taps + (got[ROWS : ROWS + GROWS].astype(f32) + got[ROWS + GROWS :].astype(f32))
    for bit in (1, 2, 4):
        parts = held.reshape(-1, 2, SHARD, LANES)
        mine = bit_of("rep", bit)
        keep = jnp.where(mine == 0, parts[:, 0], parts[:, 1]).reshape(-1, LANES)
        send = jnp.where(mine == 0, parts[:, 1], parts[:, 0]).reshape(-1, LANES).astype(bf16)
        high, low = split_high_low(taps)
        got = swap(jnp.concatenate([send, high, low], axis=0), "rep", bit)
        count = send.shape[0]
        held = keep + got[:count].astype(f32)
        taps = (high.astype(f32) + low.astype(f32)) + (
            got[count : count + GROWS].astype(f32) + got[count + GROWS :].astype(f32)
        )
    held = jnp.concatenate([held, taps], axis=0)
    for axis in ("x", "y"):
        for bit in (1, 2):
            held = held + swap(held, axis, bit)
    return held * FACTOR


def per_device(
    tile_data,
    cotangent,
    tile_place,
    tile_count,
    kernel,
    norm_gain,
    expand_weight,
    hidden_bias,
    reduce_weight,
):
    core = lax.axis_index("core")
    held, other = gather_weights(expand_weight, reduce_weight)
    tiles, cotan, place = tile_data[0], cotangent[0], tile_place[0]
    (canvas,) = call(place_kernel, (place, tile_count, tiles), [((SIDE, SIDE, C), bf16)], name="place")
    padded = with_rims(canvas)
    plane_shape, cell_shape = (3, HALF, WIDE, LANES), (3, S, SIDE, LANES)
    result, field, keep, send, taps = call(
        block_kernel,
        (
            place,
            tile_count,
            core.reshape(1, 1).astype(jnp.int32),
            padded,
            tiles,
            cotan,
            spread_taps(kernel),
            norm_gain.reshape(1, C),
            hidden_bias.reshape(1, FF),
            held,
            other,
        ),
        [
            ((CAP, S, S, C), f32),
            ((SIDE, SIDE, C), bf16),
            ((ROWS, LANES), bf16),
            ((ROWS + 2 * GROWS, LANES), bf16),
            ((GROWS, LANES), f32),
        ],
        [
            (plane_shape, f32),
            (cell_shape, f32),
            (cell_shape, f32),
            ((3, TAPS, 8, LANES), f32),
            ((C, FF), bf16),
            ((FF, C), bf16),
            ((2, S * S, FF), f32),
            ((S * S, FF), bf16),
            ((S * S, FF), bf16),
            ((C, FF), f32),
            ((C, FF), f32),
        ],
        name="block",
    )
    (grad_tiles,) = call(
        spread_kernel,
        (place, tile_count, with_rims(field), cotan, spread_taps(kernel[::-1, ::-1])),
        [((CAP, S, S, C), f32)],
        [(plane_shape, f32), (cell_shape, f32)],
        name="spread",
    )
    held = reduce_gradients(keep, send, taps)
    other = swap(held, "core", 1)
    first = jnp.where(core == 0, held, other)
    second = jnp.where(core == 0, other, held)
    halves = []
    for half in (first[SHARD:], second[SHARD:]):
        tails = jnp.concatenate([half[32:48, :TAIL], half[32:48, TAIL:]], axis=0)
        halves.append(jnp.concatenate([half[:32], tails], axis=1))
    grad_kernel = jnp.concatenate([halves[0][:24], halves[1][:25]], axis=0)
    return (
        result[None],
        grad_tiles[None],
        unpack_expand(first[:SHARD]),
        unpack_reduce(second[:SHARD]),
        grad_kernel.reshape(KS, KS, C),
    )


def solution(mesh):
    fine = Mesh(mesh.devices.reshape(4, 4, 2, 8), ("y", "x", "core", "rep"))
    tiles = P("rep", TILE, None, None, None)
    placed = (
        tiles,
        tiles,
        P("rep", TILE, None),
        P("rep", TILE),
        P(),
        P(),
        P("rep", None),
        P(),
        P("rep", None),
    )
    return jax.shard_map(
        per_device,
        mesh=fine,
        in_specs=placed,
        out_specs=(tiles, tiles, P("rep", None), P("rep", None), P()),
        check_vma=False,
    )
```

time: 178 us -> 127 us (0.71)
  matrix products: 58.7 us -> 0 us
  Pallas kernels: 0 us -> 32.8 us
  other arithmetic: 26 us -> 3.27 us
  local copies, waits for them, and re-layouts: 20.8 us -> 8.51 us
  starting transfers between devices: 46.8 us -> 54.4 us
  waiting for transfers between devices: 23.3 us -> 25.5 us
    conv_general_dilated x3 -> x0, matrix products: 41.3 us -> none  [depthwise(): lax.conv_general_dilated(padded[None], kernel[:, :, None, :], (1, 1), 'VA...]
    pallas_call x0 -> x3, Pallas kernels: none -> 32.8 us  [call(): pl.pallas_call(kernel, out_shape=[jax.ShapeDtypeStruct(shape, dtype) for...]
    dot_general x11 -> x0, matrix products: 17.4 us -> none  [the longest x2 4.31 us: right_contract(): lax.dot_general(left, right, (((1,), (1,)), ((), ())), preferred_element_...]
    reduce_sum x1 -> x0, other arithmetic: 15.9 us -> none  [forward_backward(): jnp.mean(spread * spread, axis=1, keepdims=True) + 1e-06]
    ppermute x17, starting transfers between devices: 38.9 us -> 47.2 us  [swap(): return lax.ppermute(value, axis, [(i, i ^ bit) for i in range(SIZES[axis])])]
    reshape x6 -> x4, local copies, waits for them, and re-layouts: 4.7 us -> 0.65 us  [the longest x1 0.63 us: per_device(): grad_kernel.reshape(KS, KS, C)]
    mul x4 -> x0, local copies, waits for them, and re-layouts: 3.94 us -> none  [the longest x1 1.99 us: forward_backward(): result = (canvas.astype(f32) + mixed) * mask_rows.astype(f32)]
    convert_element_type x21 -> x8, other arithmetic: 3.82 us -> 0.77 us  [the longest x2 0.67 us: with_rims(): return jnp.concatenate([north, widened, south], axis=0).astype(f32)]
  transfers between devices with their start and end apart: 21 -> 21, of which waited for: 9 -> 10; matrix products, arithmetic and copies ran while one was open for 39% -> 2% of each run, Pallas kernels for 0% -> 8%
where the time goes in v2:
time: 127 us; the launch traced here: 126 us
  starting transfers between devices  54.4 us (43%)
  Pallas kernels  32.8 us (26%)
  waiting for transfers between devices  25.5 us (20%)
  local copies, waits for them, and re-layouts  8.51 us (7%)
  other arithmetic  3.27 us (3%)
  between operations  1.96 us (2%)
    ppermute x17, starting transfers between devices, swap(): return lax.ppermute(value, axis, [(i, i ^ bit) for i in range(SIZES[axis])])  47.2 us
    pallas_call x3, Pallas kernels, call(): pl.pallas_call(kernel, out_shape=[jax.ShapeDtypeStruct(shape, dtype) for...  32.8 us
    ppermute x17, waiting for transfers between devices, swap(): return lax.ppermute(value, axis, [(i, i ^ bit) for i in range(SIZES[axis])])  25.3 us
    ppermute x2, starting transfers between devices, with_rims(): lax.ppermute(jnp.where(core == 0, west_edge, east_edge), ('x', 'core'), [...  5.86 us
    unnamed x32, local copies, waits for them, and re-layouts  5.24 us
  transfers between devices with their start and end apart: 21, of which 10 were waited for; matrix products, arithmetic and copies ran while one was open for 2% of the time, Pallas kernels for 8%

profile of v2, /device:TPU:1, one launch (start us, length us, event | category | flops | bytes accessed | tf_op | source)
XLA Modules:
  0.0 126.4 jit_solution(18165608415444223171)
XLA Ops:
  0.7 0.7 fusion.28
  1.4 0.7 slice_bitcast_fusion.6
  2.1 0.7 constant_dynamic-update-slice_fusion.5
  2.8 0.7 constant_dynamic-update-slice_fusion.4
  3.5 0.7 constant_dynamic-update-slice_fusion.3
  4.2 0.7 constant_dynamic-update-slice_fusion.2
  4.9 0.7 constant_dynamic-update-slice_fusion.1
  5.6 0.7 constant_dynamic-update-slice_fusion
  6.3 0.1 maximum_bitcast_fusion.3
  6.4 7.8 %collective-permute-start.4 = (bf16[1,144,128]{2,1,0:T(8,128)(2,1)S(1)}, bf16[1,144,128]{2,1,0:T(8,128)(2,1)S(1)}, u32[]{:S(2)}, u32[]{:S(2)}) collective-permute-start(bf16[1,144,128]{2,1,0:T(8,128)(2,1)S(1)} %maximum_select_fusion), channel_id=1, source_target_pairs={{0,4},{1,5},{2,6},{3,7},{4,0},{5,1},{6,2},{7,3},{8,12},{9,13},{10,... | collective-permute-start | bytes 110600 | tf_op jit(solution)/shard_map/ppermute | solution.py:33
  14.9 1.0 copy-done
  15.9 0.7 copy-done.3
  16.6 0.6 place.1
  17.2 0.1 select_bitcast_fusion.11
  17.3 3.9 %collective-permute-start = (bf16[3,32,192]{2,0,1:T(4,128)(2,1)S(1)}, bf16[3,32,192]{2,0,1:T(4,128)(2,1)S(1)}, u32[]{:S(2)}, u32[]{:S(2)}) collective-permute-start(bf16[3,32,192]{2,0,1:T(4,128)(2,1)S(1)} %get-tuple-element.27), channel_id=1, source_target_pairs={{8,16},{16,8},{40,48},{48,40},{9,17},{17,9},{41,49},{49,41},{10,18... | collective-permute-start | bytes 110600 | tf_op jit(solution)/shard_map/ppermute | solution.py:281
  21.3 0.1 collective-permute-start.1
  21.4 0.1 slice_bitcast_fusion.5
  21.6 0.1 rev.3
  21.8 1.3 collective-permute-start.5
  23.1 0.1 collective-permute-done
  23.2 0.1 select_bitcast_fusion.9
  23.3 0.4 pad_maximum_fusion.3
  23.7 4.4 %collective-permute-done.5 = bf16[2,144,128]{2,1,0:T(8,128)(2,1)S(1)} collective-permute-done((bf16[2,144,128]{2,1,0:T(8,128)(2,1)S(1)}, bf16[2,144,128]{2,1,0:T(8,128)(2,1)S(1)}, u32[]{:S(2)}, u32[]{:S(2)}) %collective-permute-start.5) | collective-permute-done | bytes 73760 | tf_op jit(solution)/shard_map/ppermute | solution.py:33
  28.1 0.1 collective-permute-start.6
  28.3 0.7 collective-permute-start.2
  28.9 5.3 %collective-permute-start.3 = (bf16[3,40,192]{2,1,0:T(8,128)(2,1)S(1)}, bf16[3,40,192]{2,1,0:T(8,128)(2,1)S(1)}, u32[]{:S(2)}, u32[]{:S(2)}) collective-permute-start(bf16[3,40,192]{2,1,0:T(8,128)(2,1)S(1)} %get-tuple-element.24), channel_id=1, source_target_pairs={{0,32},{16,48},{32,0},{48,16},{1,33},{17,49},{33,1},{49,17},{2,34}... | collective-permute-start | bytes 138248 | tf_op jit(solution)/shard_map/ppermute | solution.py:33
  34.4 0.0 copy-start.2
  34.4 1.6 %collective-permute-start.7 = (bf16[1152,128]{1,0:T(8,128)(2,1)S(1)}, bf16[1152,128]{1,0:T(8,128)(2,1)S(1)}, u32[]{:S(2)}, u32[]{:S(2)}) collective-permute-start(bf16[1152,128]{1,0:T(8,128)(2,1)S(1)} %bitcast.112), channel_id=1, source_target_pairs={{0,8},{8,0},{1,9},{9,1},{2,10},{10,2},{3,11},{11,3},{4,12},{12,4},... | collective-permute-start | bytes 884744 | tf_op jit(solution)/shard_map/ppermute | solution.py:33
  36.0 0.4 collective-permute-done.3
  36.4 0.3 fusion.2.padded
  36.7 0.5 collective-permute-done.7.other
  37.3 0.0 slice-start
  37.3 23.0 %block.1 = (f32[4,16,16,192]{3,2,1,0:T(8,128)}, bf16[32,32,192]{2,1,0:T(8,128)(2,1)S(1)}, bf16[1152,128]{1,0:T(8,128)(2,1)S(1)}, bf16[1248,128]{1,0:T(8,128)(2,1)S(1)}, f32[48,128]{1,0:T(8,128)S(1)}) custom-call(s32[1,4]{1,0:T(1,128)S(1)} %bitcast.115, s32[1,1]{1,0:T(1,128)S(6)} %copy.39.count, s32[1,1]{1,0:T(1,128)} %bitcast.1.core, ...), custom_call_target="tpu_custom_call" | custom-call | tf_op jit(solution)/shard_map/block/pallas_call | solution.py:258
  60.3 0.1 slice_bitcast_fusion.4
  60.4 0.1 select_bitcast_fusion.7
  60.5 1.9 %collective-permute-start.8 = (bf16[3,32,192]{2,0,1:T(4,128)(2,1)S(1)}, bf16[3,32,192]{2,0,1:T(4,128)(2,1)S(1)}, u32[]{:S(2)}, u32[]{:S(2)}) collective-permute-start(bf16[3,32,192]{2,0,1:T(4,128)(2,1)S(1)} %get-tuple-element.25), channel_id=1, source_target_pairs={{8,16},{16,8},{40,48},{48,40},{9,17},{17,9},{41,49},{49,41},{10,18... | collective-permute-start | bytes 110600 | tf_op jit(solution)/shard_map/ppermute | solution.py:281
  62.4 0.1 collective-permute-start.9
  62.5 0.1 convert_add_fusion
  62.6 3.4 %collective-permute-start.13 = (bf16[672,128]{1,0:T(8,128)(2,1)S(1)}, bf16[672,128]{1,0:T(8,128)(2,1)S(1)}, u32[]{:S(2)}, u32[]{:S(2)}) collective-permute-start(bf16[672,128]{1,0:T(8,128)(2,1)S(1)} %pad_maximum_fusion.5), channel_id=1, source_target_pairs={{0,1},{1,0},{2,3},{3,2},{4,5},{5,4},{6,7},{7,6},{8,9},{9,8},{10,11... | collective-permute-start | bytes 516104 | tf_op jit(solution)/shard_map/ppermute | solution.py:33
  66.1 4.3 %collective-permute-done.13 = bf16[672,128]{1,0:T(8,128)(2,1)S(1)} collective-permute-done((bf16[672,128]{1,0:T(8,128)(2,1)S(1)}, bf16[672,128]{1,0:T(8,128)(2,1)S(1)}, u32[]{:S(2)}, u32[]{:S(2)}) %collective-permute-start.13) | collective-permute-done | bytes 172064 | tf_op jit(solution)/shard_map/ppermute | solution.py:33
  70.5 2.4 %collective-permute-start.14 = (bf16[384,128]{1,0:T(8,128)(2,1)S(1)}, bf16[384,128]{1,0:T(8,128)(2,1)S(1)}, u32[]{:S(2)}, u32[]{:S(2)}) collective-permute-start(bf16[384,128]{1,0:T(8,128)(2,1)S(1)} %pad_maximum_fusion.7), channel_id=1, source_target_pairs={{0,2},{1,3},{2,0},{3,1},{4,6},{5,7},{6,4},{7,5},{8,10},{9,11},{10,... | collective-permute-start | bytes 294920 | tf_op jit(solution)/shard_map/ppermute | solution.py:33
  73.0 3.4 %collective-permute-done.14 = bf16[384,128]{1,0:T(8,128)(2,1)S(1)} collective-permute-done((bf16[384,128]{1,0:T(8,128)(2,1)S(1)}, bf16[384,128]{1,0:T(8,128)(2,1)S(1)}, u32[]{:S(2)}, u32[]{:S(2)}) %collective-permute-start.14) | collective-permute-done | bytes 98336 | tf_op jit(solution)/shard_map/ppermute | solution.py:33
  76.4 4.3 %collective-permute-start.15 = (bf16[240,128]{1,0:T(8,128)(2,1)S(1)}, bf16[240,128]{1,0:T(8,128)(2,1)S(1)}, u32[]{:S(2)}, u32[]{:S(2)}) collective-permute-start(bf16[240,128]{1,0:T(8,128)(2,1)S(1)} %pad_maximum_fusion.9), channel_id=1, source_target_pairs={{0,4},{1,5},{2,6},{3,7},{4,0},{5,1},{6,2},{7,3},{8,12},{9,13},{10,... | collective-permute-start | bytes 184328 | tf_op jit(solution)/shard_map/ppermute | solution.py:33
  80.8 0.1 select_bitcast_fusion.5
  80.8 2.7 %collective-permute-done.15 = bf16[240,128]{1,0:T(8,128)(2,1)S(1)} collective-permute-done((bf16[240,128]{1,0:T(8,128)(2,1)S(1)}, bf16[240,128]{1,0:T(8,128)(2,1)S(1)}, u32[]{:S(2)}, u32[]{:S(2)}) %collective-permute-start.15) | collective-permute-done | bytes 61472 | tf_op jit(solution)/shard_map/ppermute | solution.py:33
  83.5 0.3 collective-permute-start.16
  83.8 0.4 pad_maximum_fusion.2
  84.2 3.0 %collective-permute-done.16 = f32[192,128]{1,0:T(8,128)S(1)} collective-permute-done((f32[192,128]{1,0:T(8,128)S(1)}, f32[192,128]{1,0:T(8,128)S(1)}, u32[]{:S(2)}, u32[]{:S(2)}) %collective-permute-start.16) | collective-permute-done | bytes 98336 | tf_op jit(solution)/shard_map/ppermute | solution.py:33
  87.3 6.8 %collective-permute-start.17 = (f32[192,128]{1,0:T(8,128)S(1)}, f32[192,128]{1,0:T(8,128)S(1)}, u32[]{:S(2)}, u32[]{:S(2)}) collective-permute-start(f32[192,128]{1,0:T(8,128)S(1)} %fusion.21), channel_id=1, source_target_pairs={{0,32},{16,48},{32,0},{48,16},{1,33},{17,49},{33,1},{49,17},{2,34}... | collective-permute-start | bytes 294920 | tf_op jit(solution)/shard_map/ppermute | solution.py:33
  94.1 0.7 collective-permute-start.10
  94.8 2.3 %collective-permute-start.11 = (bf16[3,40,192]{2,1,0:T(8,128)(2,1)S(1)}, bf16[3,40,192]{2,1,0:T(8,128)(2,1)S(1)}, u32[]{:S(2)}, u32[]{:S(2)}) collective-permute-start(bf16[3,40,192]{2,1,0:T(8,128)(2,1)S(1)} %get-tuple-element.22), channel_id=1, source_target_pairs={{0,32},{16,48},{32,0},{48,16},{1,33},{17,49},{33,1},{49,17},{2,34}... | collective-permute-start | bytes 138248 | tf_op jit(solution)/shard_map/ppermute | solution.py:33
  97.1 4.0 %collective-permute-start.18 = (f32[192,128]{1,0:T(8,128)S(1)}, f32[192,128]{1,0:T(8,128)S(1)}, u32[]{:S(2)}, u32[]{:S(2)}) collective-permute-start(f32[192,128]{1,0:T(8,128)S(1)} %add.93), channel_id=1, source_target_pairs={{0,64},{64,0},{128,192},{192,128},{1,65},{65,1},{129,193},{193,129... | collective-permute-start | bytes 294920 | tf_op jit(solution)/shard_map/ppermute | solution.py:33
  101.1 2.0 %collective-permute-done.18 = f32[192,128]{1,0:T(8,128)S(1)} collective-permute-done((f32[192,128]{1,0:T(8,128)S(1)}, f32[192,128]{1,0:T(8,128)S(1)}, u32[]{:S(2)}, u32[]{:S(2)}) %collective-permute-start.18) | collective-permute-done | bytes 98336 | tf_op jit(solution)/shard_map/ppermute | solution.py:33
  103.1 0.3 collective-permute-start.19
  103.5 4.7 %collective-permute-done.19 = f32[192,128]{1,0:T(8,128)S(1)} collective-permute-done((f32[192,128]{1,0:T(8,128)S(1)}, f32[192,128]{1,0:T(8,128)S(1)}, u32[]{:S(2)}, u32[]{:S(2)}) %collective-permute-start.19) | collective-permute-done | bytes 98336 | tf_op jit(solution)/shard_map/ppermute | solution.py:33
  108.3 7.0 %collective-permute-start.20 = (f32[192,128]{1,0:T(8,128)S(1)}, f32[192,128]{1,0:T(8,128)S(1)}, u32[]{:S(2)}, u32[]{:S(2)}) collective-permute-start(f32[192,128]{1,0:T(8,128)S(1)} %add_multiply_fusion), channel_id=1, source_target_pairs={{0,8},{8,0},{1,9},{9,1},{2,10},{10,2},{3,11},{11,3},{4,12},{12,4},... | collective-permute-start | bytes 294920 | tf_op jit(solution)/shard_map/ppermute | solution.py:33
  115.2 0.3 fusion.5.padded
  115.6 9.2 %spread.1 = f32[4,16,16,192]{3,2,1,0:T(8,128)} custom-call(s32[1,4]{1,0:T(1,128)S(1)} %bitcast.116, s32[1,1]{1,0:T(1,128)S(6)} %copy.39.count, f32[38,40,192]{2,1,0:T(8,128)S(1)} %fusion.5.padded, bf16[4,16,16,192]{3,2,1,0:T(8,128)(2,1)S(1)} %bitcast.111, f32[2,49,8,128]{3,2,1,0:T(8,128)S(1)} %broadcast_in_dim.10.taps), custom_call_target="tpu_custom_call" | custom-call | tf_op jit(solution)/shard_map/spread/pallas_call | solution.py:258
  124.8 0.1 fusion.25
  124.9 0.1 fusion.26
  125.0 0.1 fusion.27
  125.1 0.6 reshape.205
  125.7 0.0 copy-start.10
  125.7 0.7 maximum_maximum_fusion
  (83 shorter events, 0.8 us)
Async XLA Ops:
  0.6 20.7 %copy-start.6 = (f32[7,7,192]{2,1,0:T(8,128)S(1)}, f32[7,7,192]{2,1,0:T(8,128)}, u32[]{:S(2)}) copy-start(f32[7,7,192]{2,1,0:T(8,128)} %param.13) | copy-start | bytes 112900
  0.6 21.1 %copy-start.9 = (f32[768]{0:T(1024)S(1)}, f32[768]{0:T(1024)}, u32[]{:S(2)}) copy-start(f32[768]{0:T(1024)} %param.16) | copy-start | bytes 9220
  6.4 15.3 %collective-permute-start.4 = (bf16[1,144,128]{2,1,0:T(8,128)(2,1)S(1)}, bf16[1,144,128]{2,1,0:T(8,128)(2,1)S(1)}, u32[]{:S(2)}, u32[]{:S(2)}) collective-permute-start(bf16[1,144,128]{2,1,0:T(8,128)(2,1)S(1)} %maximum_select_fusion), channel_id=1, source_target_pairs={{0,4},{1,5},{2,6},{3,7},{4,0},{5,1},{6,2},{7,3},{8,12},{9,13},{10,... | collective-permute-start | bytes 110600 | tf_op jit(solution)/shard_map/ppermute | solution.py:33
  14.9 1.0 copy-start
  15.9 0.7 copy-start.3
  17.3 5.9 %collective-permute-start = (bf16[3,32,192]{2,0,1:T(4,128)(2,1)S(1)}, bf16[3,32,192]{2,0,1:T(4,128)(2,1)S(1)}, u32[]{:S(2)}, u32[]{:S(2)}) collective-permute-start(bf16[3,32,192]{2,0,1:T(4,128)(2,1)S(1)} %get-tuple-element.27), channel_id=1, source_target_pairs={{8,16},{16,8},{40,48},{48,40},{9,17},{17,9},{41,49},{49,41},{10,18... | collective-permute-start | bytes 110600 | tf_op jit(solution)/shard_map/ppermute | solution.py:281
  21.3 1.9 %collective-permute-start.1 = (bf16[3,32,192]{2,0,1:T(4,128)(2,1)S(1)}, bf16[3,32,192]{2,0,1:T(4,128)(2,1)S(1)}, u32[]{:S(2)}, u32[]{:S(2)}) collective-permute-start(bf16[3,32,192]{2,0,1:T(4,128)(2,1)S(1)} %get-tuple-element.28), channel_id=1, source_target_pairs={{0,8},{8,0},{1,9},{9,1},{2,10},{10,2},{3,11},{11,3},{4,12},{12,4},... | collective-permute-start | bytes 110600 | tf_op jit(solution)/shard_map/ppermute | solution.py:33
  21.8 12.5 %copy-start.7 = (f32[49,192]{1,0:T(8,128)}, f32[49,192]{1,0:T(8,128)S(1)}, u32[]{:S(2)}) copy-start(f32[49,192]{1,0:T(8,128)S(1)} %reshape.201) | copy-start | bytes 112900
  21.8 6.3 %collective-permute-start.5 = (bf16[2,144,128]{2,1,0:T(8,128)(2,1)S(1)}, bf16[2,144,128]{2,1,0:T(8,128)(2,1)S(1)}, u32[]{:S(2)}, u32[]{:S(2)}) collective-permute-start(bf16[2,144,128]{2,1,0:T(8,128)(2,1)S(1)} %maximum_bitcast_fusion), channel_id=1, source_target_pairs={{0,2},{1,3},{2,0},{3,1},{4,6},{5,7},{6,4},{7,5},{8,10},{9,11},{10,... | collective-permute-start | bytes 221192 | tf_op jit(solution)/shard_map/ppermute | solution.py:33
  28.1 6.1 %collective-permute-start.6 = (bf16[4,144,128]{2,1,0:T(8,128)(2,1)S(1)}, bf16[4,144,128]{2,1,0:T(8,128)(2,1)S(1)}, u32[]{:S(2)}, u32[]{:S(2)}) collective-permute-start(bf16[4,144,128]{2,1,0:T(8,128)(2,1)S(1)} %bitcast.125), channel_id=1, source_target_pairs={{0,1},{1,0},{2,3},{3,2},{4,5},{5,4},{6,7},{7,6},{8,9},{9,8},{10,11... | collective-permute-start | bytes 442376 | tf_op jit(solution)/shard_map/ppermute | solution.py:33
  28.3 7.7 %collective-permute-start.2 = (bf16[3,40,192]{2,1,0:T(8,128)(2,1)S(1)}, bf16[3,40,192]{2,1,0:T(8,128)(2,1)S(1)}, u32[]{:S(2)}, u32[]{:S(2)}) collective-permute-start(bf16[3,40,192]{2,1,0:T(8,128)(2,1)S(1)} %get-tuple-element.23), channel_id=1, source_target_pairs={{32,64},{48,80},{96,128},{112,144},{160,192},{176,208},{64,32},{80... | collective-permute-start | bytes 138248 | tf_op jit(solution)/shard_map/ppermute | solution.py:293
  28.9 7.4 %collective-permute-start.3 = (bf16[3,40,192]{2,1,0:T(8,128)(2,1)S(1)}, bf16[3,40,192]{2,1,0:T(8,128)(2,1)S(1)}, u32[]{:S(2)}, u32[]{:S(2)}) collective-permute-start(bf16[3,40,192]{2,1,0:T(8,128)(2,1)S(1)} %get-tuple-element.24), channel_id=1, source_target_pairs={{0,32},{16,48},{32,0},{48,16},{1,33},{17,49},{33,1},{49,17},{2,34}... | collective-permute-start | bytes 138248 | tf_op jit(solution)/shard_map/ppermute | solution.py:33
  34.4 2.9 %copy-start.1 = (bf16[1,4,16,16,192]{4,3,2,1,0:T(8,128)(2,1)S(1)}, bf16[1,4,16,16,192]{4,3,2,1,0:T(8,128)(2,1)}, u32[]{:S(2)}) copy-start(bf16[1,4,16,16,192]{4,3,2,1,0:T(8,128)(2,1)} %param.9) | copy-start | bytes 1179652
  34.4 2.9 %copy-start.2 = (bf16[1,4,16,16,192]{4,3,2,1,0:T(8,128)(2,1)S(1)}, bf16[1,4,16,16,192]{4,3,2,1,0:T(8,128)(2,1)}, u32[]{:S(2)}) copy-start(bf16[1,4,16,16,192]{4,3,2,1,0:T(8,128)(2,1)} %param.10) | copy-start | bytes 1179652
  34.4 2.9 %copy-start.4 = (s32[1,1,4]{2,1,0:T(1,128)S(1)}, s32[1,1,4]{2,1,0:T(1,128)}, u32[]{:S(2)}) copy-start(s32[1,1,4]{2,1,0:T(1,128)} %param.11) | copy-start | bytes 52
  34.4 2.9 %copy-start.5 = (f32[192]{0:T(256)S(1)}, f32[192]{0:T(256)}, u32[]{:S(2)}) copy-start(f32[192]{0:T(256)} %param.14) | copy-start | bytes 2308
  34.4 2.8 %collective-permute-start.7 = (bf16[1152,128]{1,0:T(8,128)(2,1)S(1)}, bf16[1152,128]{1,0:T(8,128)(2,1)S(1)}, u32[]{:S(2)}, u32[]{:S(2)}) collective-permute-start(bf16[1152,128]{1,0:T(8,128)(2,1)S(1)} %bitcast.112), channel_id=1, source_target_pairs={{0,8},{8,0},{1,9},{9,1},{2,10},{10,2},{3,11},{11,3},{4,12},{12,4},... | collective-permute-start | bytes 884744 | tf_op jit(solution)/shard_map/ppermute | solution.py:33
  37.3 23.0 %copy-start.8 = (f32[49,192]{1,0:T(8,128)S(1)}, f32[49,192]{1,0:T(8,128)}, u32[]{:S(2)}) copy-start(f32[49,192]{1,0:T(8,128)} %copy-done.7) | copy-start | bytes 112900
  37.3 23.0 %slice-start = ((f32[49,192]{1,0:T(8,128)}), f32[49,64]{1,0:T(8,128)S(1)}, s32[]{:S(2)}) async-start(f32[49,192]{1,0:T(8,128)} %copy-done.7), calls=%async_computation | async-start | bytes 57344 | tf_op jit(solution)/shard_map/slice | solution.py:271
  60.3 2.2 %collective-permute-start.12 = (bf16[1248,128]{1,0:T(8,128)(2,1)S(1)}, bf16[1248,128]{1,0:T(8,128)(2,1)S(1)}, u32[]{:S(2)}, u32[]{:S(2)}) collective-permute-start(bf16[1248,128]{1,0:T(8,128)(2,1)S(1)} %get-tuple-element.13), channel_id=1, source_target_pairs={{0,8},{8,0},{1,9},{9,1},{2,10},{10,2},{3,11},{11,3},{4,12},{12,4},... | collective-permute-start | bytes 958472 | tf_op jit(solution)/shard_map/ppermute | solution.py:33
  60.5 20.3 %collective-permute-start.8 = (bf16[3,32,192]{2,0,1:T(4,128)(2,1)S(1)}, bf16[3,32,192]{2,0,1:T(4,128)(2,1)S(1)}, u32[]{:S(2)}, u32[]{:S(2)}) collective-permute-start(bf16[3,32,192]{2,0,1:T(4,128)(2,1)S(1)} %get-tuple-element.25), channel_id=1, source_target_pairs={{8,16},{16,8},{40,48},{48,40},{9,17},{17,9},{41,49},{49,41},{10,18... | collective-permute-start | bytes 110600 | tf_op jit(solution)/shard_map/ppermute | solution.py:281
  62.4 18.4 %collective-permute-start.9 = (bf16[3,32,192]{2,0,1:T(4,128)(2,1)S(1)}, bf16[3,32,192]{2,0,1:T(4,128)(2,1)S(1)}, u32[]{:S(2)}, u32[]{:S(2)}) collective-permute-start(bf16[3,32,192]{2,0,1:T(4,128)(2,1)S(1)} %get-tuple-element.26), channel_id=1, source_target_pairs={{0,8},{8,0},{1,9},{9,1},{2,10},{10,2},{3,11},{11,3},{4,12},{12,4},... | collective-permute-start | bytes 110600 | tf_op jit(solution)/shard_map/ppermute | solution.py:33
  62.6 7.8 %collective-permute-start.13 = (bf16[672,128]{1,0:T(8,128)(2,1)S(1)}, bf16[672,128]{1,0:T(8,128)(2,1)S(1)}, u32[]{:S(2)}, u32[]{:S(2)}) collective-permute-start(bf16[672,128]{1,0:T(8,128)(2,1)S(1)} %pad_maximum_fusion.5), channel_id=1, source_target_pairs={{0,1},{1,0},{2,3},{3,2},{4,5},{5,4},{6,7},{7,6},{8,9},{9,8},{10,11... | collective-permute-start | bytes 516104 | tf_op jit(solution)/shard_map/ppermute | solution.py:33
  70.5 5.8 %collective-permute-start.14 = (bf16[384,128]{1,0:T(8,128)(2,1)S(1)}, bf16[384,128]{1,0:T(8,128)(2,1)S(1)}, u32[]{:S(2)}, u32[]{:S(2)}) collective-permute-start(bf16[384,128]{1,0:T(8,128)(2,1)S(1)} %pad_maximum_fusion.7), channel_id=1, source_target_pairs={{0,2},{1,3},{2,0},{3,1},{4,6},{5,7},{6,4},{7,5},{8,10},{9,11},{10,... | collective-permute-start | bytes 294920 | tf_op jit(solution)/shard_map/ppermute | solution.py:33
  76.4 7.1 %collective-permute-start.15 = (bf16[240,128]{1,0:T(8,128)(2,1)S(1)}, bf16[240,128]{1,0:T(8,128)(2,1)S(1)}, u32[]{:S(2)}, u32[]{:S(2)}) collective-permute-start(bf16[240,128]{1,0:T(8,128)(2,1)S(1)} %pad_maximum_fusion.9), channel_id=1, source_target_pairs={{0,4},{1,5},{2,6},{3,7},{4,0},{5,1},{6,2},{7,3},{8,12},{9,13},{10,... | collective-permute-start | bytes 184328 | tf_op jit(solution)/shard_map/ppermute | solution.py:33
  83.5 3.7 %collective-permute-start.16 = (f32[192,128]{1,0:T(8,128)S(1)}, f32[192,128]{1,0:T(8,128)S(1)}, u32[]{:S(2)}, u32[]{:S(2)}) collective-permute-start(f32[192,128]{1,0:T(8,128)S(1)} %pad_maximum_fusion.8), channel_id=1, source_target_pairs={{0,16},{16,0},{32,48},{48,32},{1,17},{17,1},{33,49},{49,33},{2,18}... | collective-permute-start | bytes 294920 | tf_op jit(solution)/shard_map/ppermute | solution.py:33
  87.3 9.9 %collective-permute-start.17 = (f32[192,128]{1,0:T(8,128)S(1)}, f32[192,128]{1,0:T(8,128)S(1)}, u32[]{:S(2)}, u32[]{:S(2)}) collective-permute-start(f32[192,128]{1,0:T(8,128)S(1)} %fusion.21), channel_id=1, source_target_pairs={{0,32},{16,48},{32,0},{48,16},{1,33},{17,49},{33,1},{49,17},{2,34}... | collective-permute-start | bytes 294920 | tf_op jit(solution)/shard_map/ppermute | solution.py:33
  94.1 9.4 %collective-permute-start.10 = (bf16[3,40,192]{2,1,0:T(8,128)(2,1)S(1)}, bf16[3,40,192]{2,1,0:T(8,128)(2,1)S(1)}, u32[]{:S(2)}, u32[]{:S(2)}) collective-permute-start(bf16[3,40,192]{2,1,0:T(8,128)(2,1)S(1)} %get-tuple-element.21), channel_id=1, source_target_pairs={{32,64},{48,80},{96,128},{112,144},{160,192},{176,208},{64,32},{80... | collective-permute-start | bytes 138248 | tf_op jit(solution)/shard_map/ppermute | solution.py:293
  94.8 8.7 %collective-permute-start.11 = (bf16[3,40,192]{2,1,0:T(8,128)(2,1)S(1)}, bf16[3,40,192]{2,1,0:T(8,128)(2,1)S(1)}, u32[]{:S(2)}, u32[]{:S(2)}) collective-permute-start(bf16[3,40,192]{2,1,0:T(8,128)(2,1)S(1)} %get-tuple-element.22), channel_id=1, source_target_pairs={{0,32},{16,48},{32,0},{48,16},{1,33},{17,49},{33,1},{49,17},{2,34}... | collective-permute-start | bytes 138248 | tf_op jit(solution)/shard_map/ppermute | solution.py:33
  97.1 6.0 %collective-permute-start.18 = (f32[192,128]{1,0:T(8,128)S(1)}, f32[192,128]{1,0:T(8,128)S(1)}, u32[]{:S(2)}, u32[]{:S(2)}) collective-permute-start(f32[192,128]{1,0:T(8,128)S(1)} %add.93), channel_id=1, source_target_pairs={{0,64},{64,0},{128,192},{192,128},{1,65},{65,1},{129,193},{193,129... | collective-permute-start | bytes 294920 | tf_op jit(solution)/shard_map/ppermute | solution.py:33
  103.1 5.1 %collective-permute-start.19 = (f32[192,128]{1,0:T(8,128)S(1)}, f32[192,128]{1,0:T(8,128)S(1)}, u32[]{:S(2)}, u32[]{:S(2)}) collective-permute-start(f32[192,128]{1,0:T(8,128)S(1)} %add.94), channel_id=1, source_target_pairs={{0,128},{64,192},{128,0},{192,64},{1,129},{65,193},{129,1},{193,65... | collective-permute-start | bytes 294920 | tf_op jit(solution)/shard_map/ppermute | solution.py:33
  108.3 16.5 %collective-permute-start.20 = (f32[192,128]{1,0:T(8,128)S(1)}, f32[192,128]{1,0:T(8,128)S(1)}, u32[]{:S(2)}, u32[]{:S(2)}) collective-permute-start(f32[192,128]{1,0:T(8,128)S(1)} %add_multiply_fusion), channel_id=1, source_target_pairs={{0,8},{8,0},{1,9},{9,1},{2,10},{10,2},{3,11},{11,3},{4,12},{12,4},... | collective-permute-start | bytes 294920 | tf_op jit(solution)/shard_map/ppermute | solution.py:33
  125.7 0.7 copy-start.10

commit v3 on v2

v3 whole, which is shorter than its diff:
```python
import functools

import jax
import jax.numpy as jnp
from jax import lax
from jax.experimental import pallas as pl
from jax.experimental.pallas import tpu as pltpu
from jax.sharding import Mesh, PartitionSpec as P

inv_root_two = 0.7071067811865476
inv_root_two_pi = 0.3989422804014327
bf16 = jnp.bfloat16
f32 = jnp.float32
REP_ORDER = (0, 2, 4, 6, 1, 3, 5, 7)
TILE = ("y", "x", "core")
SIZES = {"y": 4, "x": 4, "core": 2, "rep": 8}
C, FF, S, CAP, KS = 192, 768, 16, 4, 7
SIDE = 2 * S
TAPS = KS * KS
HALF = S + 6
WIDE = SIDE + 8
LANES = 128
TAIL = C - LANES
SHARD = C * FF // SIZES["rep"] // LANES
ROWS = SHARD * SIZES["rep"]
EROWS = C // SIZES["rep"]
RROWS = FF // SIZES["rep"]
CHUNK = 40
GROWS = 64
PIECE = GROWS // 4
PART = CHUNK + PIECE
FACTOR = 1.0 / 512.0
VMEM_LIMIT = 48 * 1024 * 1024


def swap(value, axis, bit):
    return lax.ppermute(value, axis, [(i, i ^ bit) for i in range(SIZES[axis])])


def bit_of(axis, bit):
    return (lax.axis_index(axis) // bit) % 2


def dot(left, right, contract):
    return lax.dot_general(left, right, ((contract[:1], contract[1:]), ((), ())), preferred_element_type=f32)


CORE, AT_X, AT_REP, COUNT, PLACE = 0, 1, 2, 3, 4


def place_kernel(info, tiles, expand, project, canvas, packed, held_e, held_r, sems, tile_sems):
    weights = [
        pltpu.make_async_copy(expand, held_e, sems.at[0]),
        pltpu.make_async_copy(project, held_r, sems.at[1]),
    ]
    for copy in weights:
        copy.start()

    def tile_copy(j):
        p = info[0, PLACE + j]
        row = pl.multiple_of((p // 2) * S, S)
        col = pl.multiple_of((p % 2) * S, S)
        return row, col, pltpu.make_async_copy(
            tiles.at[j], canvas.at[pl.ds(row, S), pl.ds(col, S), :], tile_sems.at[j]
        )

    for j in range(CAP):
        row, col, copy = tile_copy(j)

        @pl.when(j < info[0, COUNT])
        def _():
            copy.start()

        @pl.when(j >= info[0, COUNT])
        def _():
            canvas[pl.ds(row, S), pl.ds(col, S), :] = jnp.zeros((S, S, C), bf16)

    for copy in weights:
        copy.wait()
    e, r = pack_expand(held_e[...].astype(f32)), pack_reduce(held_r[...].astype(f32))
    packed[...] = jnp.where(info[0, CORE] == 0, e, r).astype(bf16)
    for j in range(CAP):

        @pl.when(j < info[0, COUNT])
        def _():
            tile_copy(j)[2].wait()


def fill_taps(kernel, taps, flip):
    for dy in range(KS):
        for dx in range(KS):
            row = kernel[KS - 1 - dy, KS - 1 - dx : KS - dx] if flip else kernel[dy, dx : dx + 1]
            both = jnp.concatenate([row[:, LANES:], row[:, LANES:]], axis=1)
            taps[0, dy * KS + dx] = jnp.broadcast_to(row[:, :LANES], (8, LANES))
            taps[1, dy * KS + dx] = jnp.broadcast_to(both, (8, LANES))


def field_kernel(padded, kernel, planes, filtered, taps):
    fill_taps(kernel, taps, False)
    fill_planes(padded, planes)
    conv_planes(planes, taps, filtered)


def fill_planes(padded, planes):
    planes[0] = padded[:HALF, :, :LANES]
    planes[2] = padded[S:, :, :LANES]
    planes[1] = jnp.concatenate([padded[:HALF, :, LANES:], padded[S:, :, LANES:]], axis=-1)


def conv_planes(planes, taps, out):
    def body(step, carry):
        t = step // 4
        col = pl.multiple_of((step % 4) * 8, 8)
        acc = jnp.zeros((S, 8, LANES), f32)
        for dx in range(KS):
            x = planes[t, :, pl.ds(col + dx, 8), :]
            for dy in range(KS):
                acc = acc + x[dy : dy + S] * taps[t % 2, dy * KS + dx]
        out[t, :, pl.ds(col, 8), :] = acc
        return carry

    lax.fori_loop(0, 12, body, 0)


def correlate_planes(planes, field, acc):
    acc[...] = jnp.zeros_like(acc)

    def body(step, carry):
        t = step // 4
        col = pl.multiple_of((step % 4) * 8, 8)
        g = [field[t, row, pl.ds(col, 8), :] for row in range(S)]
        for dx in range(KS):
            sums = [None] * KS
            for row in range(HALF):
                x = planes[t, row, pl.ds(col + dx, 8), :]
                for dy in range(max(0, row - S + 1), min(KS, row + 1)):
                    term = x * g[row - dy]
                    sums[dy] = term if sums[dy] is None else sums[dy] + term
            for dy in range(KS):
                acc[t, dy * KS + dx] += sums[dy]
        return carry

    lax.fori_loop(0, 12, body, 0)


def tile_of(planes, p):
    lower = p // 2
    col = pl.multiple_of((p % 2) * S, S)
    main = planes[2 * lower, :, pl.ds(col, S), :].reshape(S * S, LANES)
    tail = planes[1, :, pl.ds(col, S), :].reshape(S * S, LANES)
    tail = jnp.where(lower == 1, pltpu.roll(tail, TAIL, 1), tail)
    return jnp.concatenate([main, tail[:, :TAIL]], axis=1)


def pack_expand(rows):
    return jnp.concatenate([rows[:, k * LANES : (k + 1) * LANES] for k in range(FF // LANES)], axis=0)


def pack_reduce(rows):
    half = RROWS // 2
    tails = jnp.concatenate([rows[:half, LANES:], rows[half:, LANES:]], axis=1)
    return jnp.concatenate([rows[:, :LANES], tails], axis=0)


def unpack_expand(value):
    return jnp.concatenate([value[k * EROWS : (k + 1) * EROWS] for k in range(FF // LANES)], axis=1)


def unpack_reduce(value):
    tail = value[RROWS:SHARD]
    tails = jnp.concatenate([tail[:, :TAIL], tail[:, TAIL:]], axis=0)
    return jnp.concatenate([value[:RROWS], tails], axis=1)


def split_high_low(value):
    high = value.astype(bf16)
    return high, (value - high.astype(f32)).astype(bf16)


def block_kernel(
    info, planes, filtered, tiles, cotan, gain, bias, held, other,
    result, field_out, keep, send, keep_taps,
    field, tap_acc, expand_wide, expand, project, hidden, active, grad_hidden,
    grad_e, grad_r, grad_rt, shards, tap_rows,
):
    me, my_x, my_z = info[0, CORE], info[0, AT_X], info[0, AT_REP]
    for k, s in enumerate(REP_ORDER):
        z = my_z ^ s
        mine, theirs = held[k].astype(f32), other[k].astype(f32)
        rows = pl.ds(pl.multiple_of(z * EROWS, 8), EROWS)
        expand_wide[rows, :] = unpack_expand(jnp.where(me == 0, mine, theirs))
        rows = pl.ds(pl.multiple_of(z * RROWS, RROWS), RROWS)
        project[rows, :] = unpack_reduce(jnp.where(me == 0, theirs, mine)).astype(bf16)
    expand[...] = expand_wide[...].astype(bf16)
    field[...] = jnp.zeros_like(field)
    field_out[...] = jnp.zeros_like(field_out)
    grad_e[...] = jnp.zeros_like(grad_e)
    grad_r[...] = jnp.zeros_like(grad_r)

    def blank(j, carry):
        result[j] = jnp.zeros_like(result[j])
        return carry

    lax.fori_loop(info[0, COUNT], CAP, blank, 0)

    def slot(j, carry):
        p = info[0, PLACE + j]
        lower = p // 2
        row = pl.multiple_of(lower * S, S)
        col = pl.multiple_of((p % 2) * S, S)
        x = tile_of(filtered, p)
        spread = x - jnp.sum(x, axis=1, keepdims=True) * (1.0 / C)
        inverse = lax.rsqrt(jnp.sum(spread * spread, axis=1, keepdims=True) * (1.0 / C) + 1e-6)
        normed = spread * inverse
        scaled = (normed * gain[...]).astype(bf16)
        up = cotan[j].reshape(S * S, C)
        hidden[0] = dot(scaled, expand[...], (1, 0))
        hidden[1] = dot(up, project[...], (1, 1))

        def gelu(r, carry):
            rows = pl.ds(pl.multiple_of(r * 16, 16), 16)
            h = hidden[0, rows, :] + bias[...]
            cdf = 0.5 * (1.0 + lax.erf(h * inv_root_two))
            slope = cdf + h * jnp.exp(-0.5 * h * h) * inv_root_two_pi
            active[rows, :] = (h * cdf).astype(bf16)
            grad_hidden[rows, :] = (hidden[1, rows, :] * slope).astype(bf16)
            return carry

        lax.fori_loop(0, S, gelu, 0)
        a, gh = active[...], grad_hidden[...]
        mixed = dot(a, project[...], (1, 0))
        result[j] = tiles[j].astype(f32) + mixed.reshape(S, S, C)
        grad_e[...] += dot(scaled, gh, (0, 0))
        grad_r[...] += dot(up, a, (0, 0))
        q = dot(gh, expand[...], (1, 1)) * gain[...]
        mean_q = jnp.sum(q, axis=1, keepdims=True) * (1.0 / C)
        mean_qn = jnp.sum(q * normed, axis=1, keepdims=True) * (1.0 / C)
        g = (inverse * (q - mean_q - normed * mean_qn)).astype(bf16)
        field_out[pl.ds(row, S), pl.ds(col, S), :] = g.reshape(S, S, C)
        g = g.astype(f32)
        field[2 * lower, :, pl.ds(col, S), :] = g[:, :LANES].reshape(S, S, LANES)
        tail = jnp.concatenate([g[:, LANES:], g[:, LANES:]], axis=1).reshape(S, S, LANES)
        old = field[1, :, pl.ds(col, S), :]
        side = lax.broadcasted_iota(jnp.int32, (S, S, LANES), 2) // TAIL
        field[1, :, pl.ds(col, S), :] = jnp.where(side == lower, tail, old)
        return carry

    lax.fori_loop(0, info[0, COUNT], slot, 0)

    correlate_planes(planes, field, tap_acc)
    sums = jnp.sum(tap_acc[...], axis=2)
    main = sums[0] + sums[2]
    tail = sums[1] + pltpu.roll(sums[1], TAIL, 1)
    pad = jnp.zeros((7, LANES), f32)
    main = jnp.concatenate([main, pad], axis=0)
    tail = jnp.concatenate([tail, pad], axis=0)
    low_lane = lax.broadcasted_iota(jnp.int32, (16, LANES), 1) < TAIL
    for h in range(2):
        s = 24 * h
        tails = jnp.where(low_lane, tail[s : s + 16], tail[s + 16 : s + 32])
        tap_rows[h] = jnp.concatenate([main[s : s + 32], tails, jnp.zeros((16, LANES), f32)], axis=0)
    for i in range(4):
        rows = pl.ds(pl.multiple_of((my_x ^ i) * PIECE, PIECE), PIECE)
        keep_taps[i] = tap_rows[me, rows, :]
        high, low = split_high_low(tap_rows[1 - me, rows, :])
        send[i, 8 * CHUNK : 8 * CHUNK + PIECE] = high
        send[i, 8 * CHUNK + PIECE :] = low
    grad_rt[...] = grad_r[...].T
    shards[:, SHARD:] = jnp.zeros((2, 4 * CHUNK - SHARD, LANES), f32)
    for k in range(8):
        z = my_z ^ k
        e = pack_expand(grad_e[pl.ds(pl.multiple_of(z * EROWS, 8), EROWS), :])
        r = pack_reduce(grad_rt[pl.ds(pl.multiple_of(z * RROWS, RROWS), RROWS), :])
        shards[0, :SHARD] = jnp.where(me == 0, e, r)
        shards[1, :SHARD] = jnp.where(me == 0, r, e)
        for i in range(4):
            rows = pl.ds(pl.multiple_of((my_x ^ i) * CHUNK, 8), CHUNK)
            keep[i, k * CHUNK : (k + 1) * CHUNK] = shards[0, rows, :]
            send[i, k * CHUNK : (k + 1) * CHUNK] = shards[1, rows, :].astype(bf16)


def finish_kernel(info, held, other, grad_e, grad_r, grad_k, shards, tap_rows):
    me, my_x = info[0, CORE], info[0, AT_X]
    for i in range(4):
        rows = pl.ds(pl.multiple_of((my_x ^ i) * CHUNK, 8), CHUNK)
        taps = pl.ds(pl.multiple_of((my_x ^ i) * PIECE, PIECE), PIECE)
        shards[me, rows, :] = held[i, :CHUNK]
        shards[1 - me, rows, :] = other[i, :CHUNK]
        tap_rows[me, taps, :] = held[i, CHUNK:]
        tap_rows[1 - me, taps, :] = other[i, CHUNK:]
    grad_e[...] = unpack_expand(shards[0]) * FACTOR
    grad_r[...] = unpack_reduce(shards[1]) * FACTOR
    halves = []
    for h in range(2):
        half = tap_rows[h]
        tails = jnp.concatenate([half[32:48, :TAIL], half[32:48, TAIL:]], axis=0)
        halves.append(jnp.concatenate([half[:32], tails], axis=1))
    whole = jnp.concatenate([halves[0][:24], halves[1]], axis=0) * FACTOR
    for dy in range(KS):
        grad_k[dy] = whole[dy * KS : (dy + 1) * KS]


def spread_kernel(info, padded, cotan, kernel, out, planes, summed, taps):
    fill_taps(kernel, taps, True)
    fill_planes(padded, planes)
    conv_planes(planes, taps, summed)

    def blank(j, carry):
        out[j] = jnp.zeros_like(out[j])
        return carry

    lax.fori_loop(info[0, COUNT], CAP, blank, 0)

    def slot(j, carry):
        out[j] = cotan[j].astype(f32) + tile_of(summed, info[0, PLACE + j]).reshape(S, S, C)
        return carry

    lax.fori_loop(0, info[0, COUNT], slot, 0)


def call(kernel, ins, outs, scratch=(), name=None, hbm=(), us=1):
    smem = pl.BlockSpec(memory_space=pltpu.SMEM)
    vmem = pl.BlockSpec(memory_space=pltpu.VMEM)
    specs = [smem if v.dtype == jnp.int32 else vmem for v in ins]
    for i in hbm:
        specs[i] = pl.BlockSpec(memory_space=pltpu.HBM)
    return pl.pallas_call(
        kernel,
        out_shape=[jax.ShapeDtypeStruct(shape, dtype) for shape, dtype in outs],
        in_specs=specs,
        out_specs=[vmem for _ in outs],
        scratch_shapes=[pltpu.VMEM(*s) if isinstance(s, tuple) else s for s in scratch],
        compiler_params=pltpu.CompilerParams(vmem_limit_bytes=VMEM_LIMIT),
        cost_estimate=pl.CostEstimate(flops=us * 10**9, bytes_accessed=us * 10**6, transcendentals=0),
        name=name,
    )(*ins)


TAP_PLANES = (2, TAPS, 8, LANES)
PLANES, CELLS = (3, HALF, WIDE, LANES), (3, S, SIDE, LANES)


def block_call(*ins):
    return call(
        block_kernel,
        ins,
        [
            ((CAP, S, S, C), f32),
            ((SIDE, SIDE, C), bf16),
            ((4, 8 * CHUNK, LANES), f32),
            ((4, 8 * CHUNK + 2 * PIECE, LANES), bf16),
            ((4, PIECE, LANES), f32),
        ],
        [
            (CELLS, f32),
            ((3, TAPS, 8, LANES), f32),
            ((C, FF), f32),
            ((C, FF), bf16),
            ((FF, C), bf16),
            ((2, S * S, FF), f32),
            ((S * S, FF), bf16),
            ((S * S, FF), bf16),
            ((C, FF), f32),
            ((C, FF), f32),
            ((FF, C), f32),
            ((2, 4 * CHUNK, LANES), f32),
            ((2, GROWS, LANES), f32),
        ],
        name="block",
        us=14,
    )


def side_rims(canvas):
    core = lax.axis_index("core")
    west_edge = canvas[:, :3].transpose(1, 0, 2)
    east_edge = canvas[:, -3:].transpose(1, 0, 2)
    inner = swap(jnp.where(core == 0, east_edge, west_edge), "core", 1)
    pairs = [(4 * i + a, 4 * i + 3 - a) for i in range(2) for a in range(4)]
    outer = lax.ppermute(jnp.where(core == 0, west_edge, east_edge), ("x", "core"), pairs)
    return inner, jnp.where(lax.axis_index("x") % 2 != core, outer, jnp.zeros_like(outer))


def widen(canvas, inner, outer):
    core = lax.axis_index("core")
    west = jnp.where(core == 0, outer, inner).transpose(1, 0, 2)
    east = jnp.where(core == 0, inner, outer).transpose(1, 0, 2)
    blank = jnp.zeros((SIDE, WIDE - SIDE - 6, C), canvas.dtype)
    return jnp.concatenate([west, canvas, east, blank], axis=1)


def end_rims(widened):
    upper = lax.axis_index("x") // 2
    north_edge, south_edge = widened[:3], widened[-3:]
    near = swap(jnp.where(upper == 0, south_edge, north_edge), "x", 2)
    pairs = [(4 * y + x, 4 * ((y + 1) % 4) + x - 2) for y in range(4) for x in (2, 3)]
    far = lax.ppermute(
        jnp.where(upper == 0, north_edge, south_edge),
        ("y", "x"),
        pairs + [(b, a) for a, b in pairs],
    )
    inside = jnp.where(upper == 0, lax.axis_index("y") > 0, lax.axis_index("y") < 3)
    return near, jnp.where(inside, far, jnp.zeros_like(far))


def pad_ends(widened, near, far):
    upper = lax.axis_index("x") // 2
    north = jnp.where(upper == 0, far, near)
    south = jnp.where(upper == 0, near, far)
    return jnp.concatenate([north, widened, south], axis=0).astype(f32)


def tie(value, *others):
    return lax.optimization_barrier((value, *others))


def rows_sum(own, got):
    return (own + got[0]) + (got[1] + got[2])


def join(value):
    return value[..., :PIECE, :].astype(f32) + value[..., PIECE:, :].astype(f32)


def per_device(
    tile_data,
    cotangent,
    tile_place,
    tile_count,
    kernel,
    norm_gain,
    expand_weight,
    hidden_bias,
    reduce_weight,
):
    scalars = [lax.axis_index(a) for a in ("core", "x", "rep")] + [tile_count[0, 0]]
    info = jnp.concatenate([jnp.stack(scalars).astype(jnp.int32), tile_place[0, 0]])[None]
    tiles, cotan = tile_data[0], cotangent[0]
    canvas, packed = call(
        place_kernel,
        (info, tiles, expand_weight, reduce_weight),
        [((SIDE, SIDE, C), bf16), ((SHARD, LANES), bf16)],
        [
            ((EROWS, FF), bf16),
            ((RROWS, C), bf16),
            pltpu.SemaphoreType.DMA((2,)),
            pltpu.SemaphoreType.DMA((CAP,)),
        ],
        name="place",
        hbm=(1, 2, 3),
        us=2,
    )
    inner, outer = side_rims(canvas)
    packed, inner = tie(packed, inner)
    held = jnp.stack([packed] + [swap(packed, "rep", bits) for bits in (2, 4, 6)])
    widened = widen(canvas, inner, outer)
    near, far = end_rims(widened)
    held = jnp.concatenate([held, swap(held, "rep", 1)])
    planes, filtered = call(
        field_kernel,
        (pad_ends(widened, near, far), kernel),
        [(PLANES, f32), (CELLS, f32)],
        [(TAP_PLANES, f32)],
        name="field",
        us=5,
    )
    other = swap(held, "core", 1)
    result, field, keep, send, taps = block_call(
        info,
        planes,
        filtered,
        tiles,
        cotan,
        norm_gain.reshape(1, C),
        hidden_bias.reshape(1, FF),
        held,
        other,
    )
    end, pair = 8 * CHUNK, 2 * CHUNK
    got = swap(send, "core", 1)
    inner, outer = side_rims(field)
    held = keep + got[:, :end].astype(f32)
    taps = taps + join(got[:, end:])
    high, low = split_high_low(taps)
    send = jnp.concatenate([held.astype(bf16), high, low], axis=1)
    got = [swap(send[i], "x", i) for i in (1, 2, 3)]
    widened = widen(field, inner, outer)
    near, far = end_rims(widened)
    held = rows_sum(held[0], [g[:end].astype(f32) for g in got])
    taps = rows_sum(taps[0], [join(g[end:]) for g in got])
    high, low = split_high_low(taps)
    sends = [
        jnp.concatenate([held[k * CHUNK : k * CHUNK + pair].astype(bf16), high, low]) for k in (2, 4, 6)
    ]
    *sends, near, far = tie(*sends, near, far)
    got = [swap(part, "rep", k) for part, k in zip(sends, (2, 4, 6))]
    (grad_tiles,) = call(
        spread_kernel,
        (info, pad_ends(widened, near, far), cotan, kernel),
        [((CAP, S, S, C), f32)],
        [(PLANES, f32), (CELLS, f32), (TAP_PLANES, f32)],
        name="spread",
        us=6,
    )
    held = rows_sum(held[:pair], [g[:pair].astype(f32) for g in got])
    taps = rows_sum(high.astype(f32) + low.astype(f32), [join(g[pair:]) for g in got])
    part, grad_tiles = tie(jnp.concatenate([held[CHUNK:], taps]), grad_tiles)
    held = jnp.concatenate([held[:CHUNK], taps]) + swap(part, "rep", 1)
    held = rows_sum(held, [swap(held, "y", i) for i in (1, 2, 3)])
    held = jnp.stack([held] + [swap(held, "x", i) for i in (1, 2, 3)])
    grad_expand, grad_reduce, grad_kernel = call(
        finish_kernel,
        (info, held, swap(held, "core", 1)),
        [((EROWS, FF), f32), ((RROWS, C), f32), ((KS, KS, C), f32)],
        [((2, 4 * CHUNK, LANES), f32), ((2, GROWS, LANES), f32)],
        name="finish",
    )
    return result[None], grad_tiles[None], grad_expand, grad_reduce, grad_kernel


def solution(mesh):
    fine = Mesh(mesh.devices.reshape(4, 4, 2, 8), ("y", "x", "core", "rep"))
    tiles = P("rep", TILE, None, None, None)
    placed = (
        tiles,
        tiles,
        P("rep", TILE, None),
        P("rep", TILE),
        P(),
        P(),
        P("rep", None),
        P(),
        P("rep", None),
    )
    return jax.shard_map(
        per_device,
        mesh=fine,
        in_specs=placed,
        out_specs=(tiles, tiles, P("rep", None), P("rep", None), P()),
        check_vma=False,
    )
```

time: 127 us -> 98.8 us (0.78)
  Pallas kernels: 32.8 us -> 20.7 us
  local copies, waits for them, and re-layouts: 8.51 us -> 3.46 us
  waiting for transfers between devices: 25.5 us -> 20.6 us
  starting transfers between devices: 54.4 us -> 49.9 us
    pallas_call x3 -> x5, Pallas kernels: 32.8 us -> 20.7 us  [call(): pl.pallas_call(kernel, out_shape=[jax.ShapeDtypeStruct(shape, dtype) for...]
    ppermute x17 -> x24, starting transfers between devices: 47.2 us -> 39.1 us  [swap(): return lax.ppermute(value, axis, [(i, i ^ bit) for i in range(SIZES[axis])])]
    ppermute x17 -> x24, waiting for transfers between devices: 25.3 us -> 17.8 us  [swap(): return lax.ppermute(value, axis, [(i, i ^ bit) for i in range(SIZES[axis])])]
    ppermute x4, starting transfers between devices: 7.19 us -> 10.8 us  [the longest x2 10.7 us: end_rims(): lax.ppermute(jnp.where(upper == 0, north_edge, south_edge), ('y', 'x'), p...]
    ppermute x4, waiting for transfers between devices: 0.15 us -> 2.83 us  [the longest x2 1.96 us: side_rims(): lax.ppermute(jnp.where(core == 0, west_edge, east_edge), ('x', 'core'), p...]
    unnamed x32 -> x20, local copies, waits for them, and re-layouts: 5.24 us -> 2.67 us
  transfers between devices with their start and end apart: 21 -> 28, of which waited for: 10 -> 12; matrix products, arithmetic and copies ran while one was open for 2% -> 2% of each run, Pallas kernels for 8% -> 9%
where the time goes in v3:
time: 98.8 us; the launch traced here: 98.4 us
  starting transfers between devices  49.9 us (51%)
  Pallas kernels  20.7 us (21%)
  waiting for transfers between devices  20.6 us (21%)
  local copies, waits for them, and re-layouts  3.46 us (4%)
  other arithmetic  2.11 us (2%)
  between operations  1.61 us (2%)
    ppermute x24, starting transfers between devices, swap(): return lax.ppermute(value, axis, [(i, i ^ bit) for i in range(SIZES[axis])])  39.1 us
    pallas_call x5, Pallas kernels, call(): pl.pallas_call(kernel, out_shape=[jax.ShapeDtypeStruct(shape, dtype) for...  20.7 us
    ppermute x24, waiting for transfers between devices, swap(): return lax.ppermute(value, axis, [(i, i ^ bit) for i in range(SIZES[axis])])  17.8 us
    ppermute x2, starting transfers between devices, end_rims(): lax.ppermute(jnp.where(upper == 0, north_edge, south_edge), ('y', 'x'), p...  10.7 us
    unnamed x20, local copies, waits for them, and re-layouts  2.67 us
  transfers between devices with their start and end apart: 28, of which 12 were waited for; matrix products, arithmetic and copies ran while one was open for 2% of the time, Pallas kernels for 9%

profile of v3, /device:TPU:1, one launch (start us, length us, event | category | flops | bytes accessed | tf_op | source)
XLA Modules:
  0.0 98.4 jit_solution(1293944665250990405)
XLA Ops:
  1.3 0.7 concatenate.37
  2.0 1.0 %copy-done = bf16[1,4,16,16,192]{4,3,2,1,0:T(8,128)(2,1)S(1)} copy-done((bf16[1,4,16,16,192]{4,3,2,1,0:T(8,128)(2,1)S(1)}, bf16[1,4,16,16,192]{4,3,2,1,0:T(8,128)(2,1)}, u32[]{:S(2)}) %copy-start) | copy-done | bytes 393240
  3.1 0.8 copy-done.4
  3.9 0.8 copy-done.5
  4.6 0.9 place.1
  5.5 0.1 select_bitcast_fusion.7
  5.6 3.3 %collective-permute-start.1 = (bf16[3,32,192]{2,0,1:T(4,128)(2,1)S(1)}, bf16[3,32,192]{2,0,1:T(4,128)(2,1)S(1)}, u32[]{:S(2)}, u32[]{:S(2)}) collective-permute-start(bf16[3,32,192]{2,0,1:T(4,128)(2,1)S(1)} %get-tuple-element.63), channel_id=1, source_target_pairs={{0,8},{8,0},{1,9},{9,1},{2,10},{10,2},{3,11},{11,3},{4,12},{12,4},... | collective-permute-start | bytes 110600 | tf_op jit(solution)/shard_map/ppermute | solution.py:37
  9.0 0.0 collective-permute-start
  9.0 0.9 collective-permute-done.1
  9.9 4.7 %collective-permute-start.6 = (bf16[144,128]{1,0:T(8,128)(2,1)S(1)}, bf16[144,128]{1,0:T(8,128)(2,1)S(1)}, u32[]{:S(2)}, u32[]{:S(2)}) collective-permute-start(bf16[144,128]{1,0:T(8,128)(2,1)S(1)} %get-tuple-element.31), channel_id=1, source_target_pairs={{0,6},{1,7},{2,4},{3,5},{4,2},{5,3},{6,0},{7,1},{8,14},{9,15},{10,... | collective-permute-start | bytes 110600 | tf_op jit(solution)/shard_map/ppermute | solution.py:37
  14.5 1.0 %collective-permute-start.5 = (bf16[144,128]{1,0:T(8,128)(2,1)S(1)}, bf16[144,128]{1,0:T(8,128)(2,1)S(1)}, u32[]{:S(2)}, u32[]{:S(2)}) collective-permute-start(bf16[144,128]{1,0:T(8,128)(2,1)S(1)} %get-tuple-element.31), channel_id=1, source_target_pairs={{0,4},{1,5},{2,6},{3,7},{4,0},{5,1},{6,2},{7,3},{8,12},{9,13},{10,... | collective-permute-start | bytes 110600 | tf_op jit(solution)/shard_map/ppermute | solution.py:37
  15.5 1.2 %collective-permute-start.4 = (bf16[144,128]{1,0:T(8,128)(2,1)S(1)}, bf16[144,128]{1,0:T(8,128)(2,1)S(1)}, u32[]{:S(2)}, u32[]{:S(2)}) collective-permute-start(bf16[144,128]{1,0:T(8,128)(2,1)S(1)} %get-tuple-element.31), channel_id=1, source_target_pairs={{0,2},{1,3},{2,0},{3,1},{4,6},{5,7},{6,4},{7,5},{8,10},{9,11},{10,... | collective-permute-start | bytes 110600 | tf_op jit(solution)/shard_map/ppermute | solution.py:37
  16.7 0.0 collective-permute-done
  16.7 0.1 select_bitcast_fusion.5
  16.8 0.4 pad_maximum_fusion.3
  17.3 5.0 %collective-permute-start.2 = (bf16[3,40,192]{2,1,0:T(8,128)(2,1)S(1)}, bf16[3,40,192]{2,1,0:T(8,128)(2,1)S(1)}, u32[]{:S(2)}, u32[]{:S(2)}) collective-permute-start(bf16[3,40,192]{2,1,0:T(8,128)(2,1)S(1)} %get-tuple-element.58), channel_id=1, source_target_pairs={{32,64},{48,80},{96,128},{112,144},{160,192},{176,208},{224,0},{24... | collective-permute-start | bytes 138248 | tf_op jit(solution)/shard_map/ppermute | solution.py:397
  22.2 0.0 collective-permute-start.3
  22.3 0.0 collective-permute-done.4
  22.3 0.0 copy-start.3
  22.3 0.8 collective-permute-start.7
  23.2 0.9 collective-permute-done.2
  24.0 2.8 %collective-permute-done.3 = bf16[3,40,192]{2,1,0:T(8,128)(2,1)S(1)} collective-permute-done((bf16[3,40,192]{2,1,0:T(8,128)(2,1)S(1)}, bf16[3,40,192]{2,1,0:T(8,128)(2,1)S(1)}, u32[]{:S(2)}, u32[]{:S(2)}) %collective-permute-start.3) | collective-permute-done | bytes 46112 | tf_op jit(solution)/shard_map/ppermute | solution.py:37
  26.8 0.3 fusion.2.padded
  27.2 0.0 copy-start.1
  27.2 0.0 copy-start.2
  27.2 0.0 copy-start.6
  27.3 2.5 %collective-permute-start.8 = (bf16[8,144,128]{2,1,0:T(8,128)(2,1)S(1)}, bf16[8,144,128]{2,1,0:T(8,128)(2,1)S(1)}, u32[]{:S(2)}, u32[]{:S(2)}) collective-permute-start(bf16[8,144,128]{2,1,0:T(8,128)(2,1)S(1)} %constant_dynamic-update-slice_fusion.held), channel_id=1, source_target_pairs={{0,8},{8,0},{1,9},{9,1},{2,10},{10,2},{3,11},{11,3},{4,12},{12,4},... | collective-permute-start | bytes 884744 | tf_op jit(solution)/shard_map/ppermute | solution.py:37
  29.8 3.7 %field.1 = (f32[3,22,40,128]{3,2,1,0:T(8,128)S(1)}, f32[3,16,32,128]{3,2,1,0:T(8,128)S(1)}) custom-call(f32[38,40,192]{2,1,0:T(8,128)S(1)} %fusion.2.padded, f32[7,7,192]{2,1,0:T(8,128)S(1)} %copy-done.3), custom_call_target="tpu_custom_call" | custom-call | flops 5000000000 | bytes 5000000 | tf_op jit(solution)/shard_map/field/pallas_call | solution.py:327
  33.5 0.0 collective-permute-done.8.other
  33.5 9.3 %block.1 = (f32[4,16,16,192]{3,2,1,0:T(8,128)}, bf16[32,32,192]{2,1,0:T(8,128)(2,1)S(1)}, f32[4,320,128]{2,1,0:T(8,128)S(1)}, bf16[4,352,128]{2,1,0:T(8,128)(2,1)S(1)}, f32[4,16,128]{2,1,0:T(8,128)S(1)}) custom-call(s32[1,8]{1,0:T(1,128)S(1)} %bitcast.62, f32[3,22,40,128]{3,2,1,0:T(8,128)S(1)} %get-tuple-element.29.planes, ...), custom_call_target="tpu_custom_call" | custom-call | flops 14000000000 | bytes 14000000 | tf_op jit(solution)/shard_map/block/pallas_call | solution.py:327
  42.8 0.1 select_bitcast_fusion.3
  42.9 0.1 collective-permute-start.13
  43.0 2.6 %collective-permute-start.14 = (bf16[3,32,192]{2,0,1:T(4,128)(2,1)S(1)}, bf16[3,32,192]{2,0,1:T(4,128)(2,1)S(1)}, u32[]{:S(2)}, u32[]{:S(2)}) collective-permute-start(bf16[3,32,192]{2,0,1:T(4,128)(2,1)S(1)} %get-tuple-element.61), channel_id=1, source_target_pairs={{0,8},{8,0},{1,9},{9,1},{2,10},{10,2},{3,11},{11,3},{4,12},{12,4},... | collective-permute-start | bytes 110600 | tf_op jit(solution)/shard_map/ppermute | solution.py:37
  45.6 2.0 %collective-permute-done.13 = bf16[3,32,192]{2,0,1:T(4,128)(2,1)S(1)} collective-permute-done((bf16[3,32,192]{2,0,1:T(4,128)(2,1)S(1)}, bf16[3,32,192]{2,0,1:T(4,128)(2,1)S(1)}, u32[]{:S(2)}, u32[]{:S(2)}) %collective-permute-start.13) | collective-permute-done | bytes 36896 | tf_op jit(solution)/shard_map/ppermute | solution.py:380
  47.5 0.1 select_bitcast_fusion.1
  47.6 0.4 pad_maximum_fusion.2
  48.0 5.7 %collective-permute-start.16 = (bf16[3,40,192]{2,1,0:T(8,128)(2,1)S(1)}, bf16[3,40,192]{2,1,0:T(8,128)(2,1)S(1)}, u32[]{:S(2)}, u32[]{:S(2)}) collective-permute-start(bf16[3,40,192]{2,1,0:T(8,128)(2,1)S(1)} %get-tuple-element.56), channel_id=1, source_target_pairs={{32,64},{48,80},{96,128},{112,144},{160,192},{176,208},{224,0},{24... | collective-permute-start | bytes 138248 | tf_op jit(solution)/shard_map/ppermute | solution.py:397
  53.7 0.0 collective-permute-start.15
  53.7 0.1 fusion.20
  53.9 0.1 collective-permute-start.10
  54.0 3.1 %collective-permute-start.11 = (bf16[352,128]{1,0:T(8,128)(2,1)S(1)}, bf16[352,128]{1,0:T(8,128)(2,1)S(1)}, u32[]{:S(2)}, u32[]{:S(2)}) collective-permute-start(bf16[352,128]{1,0:T(8,128)(2,1)S(1)} %get-tuple-element.65), channel_id=1, source_target_pairs={{0,32},{16,48},{32,0},{48,16},{1,33},{17,49},{33,1},{49,17},{2,34}... | collective-permute-start | bytes 270344 | tf_op jit(solution)/shard_map/ppermute | solution.py:37
  57.0 0.8 collective-permute-start.12
  57.8 0.0 collective-permute-done.10
  57.8 3.8 %collective-permute-done.11 = bf16[352,128]{1,0:T(8,128)(2,1)S(1)} collective-permute-done((bf16[352,128]{1,0:T(8,128)(2,1)S(1)}, bf16[352,128]{1,0:T(8,128)(2,1)S(1)}, u32[]{:S(2)}, u32[]{:S(2)}) %collective-permute-start.11) | collective-permute-done | bytes 90144 | tf_op jit(solution)/shard_map/ppermute | solution.py:37
  61.7 2.3 %collective-permute-done.12 = bf16[352,128]{1,0:T(8,128)(2,1)S(1)} collective-permute-done((bf16[352,128]{1,0:T(8,128)(2,1)S(1)}, bf16[352,128]{1,0:T(8,128)(2,1)S(1)}, u32[]{:S(2)}, u32[]{:S(2)}) %collective-permute-start.12) | collective-permute-done | bytes 90144 | tf_op jit(solution)/shard_map/ppermute | solution.py:37
  64.1 1.2 %collective-permute-start.17 = (bf16[112,128]{1,0:T(8,128)(2,1)S(1)}, bf16[112,128]{1,0:T(8,128)(2,1)S(1)}, u32[]{:S(2)}, u32[]{:S(2)}) collective-permute-start(bf16[112,128]{1,0:T(8,128)(2,1)S(1)} %get-tuple-element.37), channel_id=1, source_target_pairs={{0,2},{1,3},{2,0},{3,1},{4,6},{5,7},{6,4},{7,5},{8,10},{9,11},{10,... | collective-permute-start | bytes 86024 | tf_op jit(solution)/shard_map/ppermute | solution.py:37
  65.3 4.0 %collective-permute-start.18 = (bf16[112,128]{1,0:T(8,128)(2,1)S(1)}, bf16[112,128]{1,0:T(8,128)(2,1)S(1)}, u32[]{:S(2)}, u32[]{:S(2)}) collective-permute-start(bf16[112,128]{1,0:T(8,128)(2,1)S(1)} %get-tuple-element.38), channel_id=1, source_target_pairs={{0,4},{1,5},{2,6},{3,7},{4,0},{5,1},{6,2},{7,3},{8,12},{9,13},{10,... | collective-permute-start | bytes 86024 | tf_op jit(solution)/shard_map/ppermute | solution.py:37
  69.3 0.5 collective-permute-start.19
  69.8 0.3 fusion.5.padded
  70.2 5.5 %spread.1 = f32[4,16,16,192]{3,2,1,0:T(8,128)} custom-call(s32[1,8]{1,0:T(1,128)S(1)} %bitcast.63, f32[38,40,192]{2,1,0:T(8,128)S(1)} %fusion.5.padded, bf16[4,16,16,192]{3,2,1,0:T(8,128)(2,1)S(1)} %bitcast.68, f32[7,7,192]{2,1,0:T(8,128)S(1)} %copy-done.3), custom_call_target="tpu_custom_call" | custom-call | flops 6000000000 | bytes 6000000 | tf_op jit(solution)/shard_map/spread/pallas_call | solution.py:327
  75.7 1.3 %collective-permute-start.20 = (f32[56,128]{1,0:T(8,128)S(1)}, f32[56,128]{1,0:T(8,128)S(1)}, u32[]{:S(2)}, u32[]{:S(2)}) collective-permute-start(f32[56,128]{1,0:T(8,128)S(1)} %pad_maximum_fusion.15), channel_id=1, source_target_pairs={{0,1},{1,0},{2,3},{3,2},{4,5},{5,4},{6,7},{7,6},{8,9},{9,8},{10,11... | collective-permute-start | bytes 86024 | tf_op jit(solution)/shard_map/ppermute | solution.py:37
  77.0 1.5 %collective-permute-done.20 = f32[56,128]{1,0:T(8,128)S(1)} collective-permute-done((f32[56,128]{1,0:T(8,128)S(1)}, f32[56,128]{1,0:T(8,128)S(1)}, u32[]{:S(2)}, u32[]{:S(2)}) %collective-permute-start.20) | collective-permute-done | bytes 28704 | tf_op jit(solution)/shard_map/ppermute | solution.py:37
  78.5 2.5 %collective-permute-start.23 = (f32[56,128]{1,0:T(8,128)S(1)}, f32[56,128]{1,0:T(8,128)S(1)}, u32[]{:S(2)}, u32[]{:S(2)}) collective-permute-start(f32[56,128]{1,0:T(8,128)S(1)} %fusion.10), channel_id=1, source_target_pairs={{0,192},{64,128},{128,64},{192,0},{1,193},{65,129},{129,65},{193,1... | collective-permute-start | bytes 86024 | tf_op jit(solution)/shard_map/ppermute | solution.py:37
  81.0 0.8 collective-permute-start.21
  81.8 0.7 collective-permute-done.23
  82.5 2.8 %collective-permute-done.22 = f32[56,128]{1,0:T(8,128)S(1)} collective-permute-done((f32[56,128]{1,0:T(8,128)S(1)}, f32[56,128]{1,0:T(8,128)S(1)}, u32[]{:S(2)}, u32[]{:S(2)}) %collective-permute-start.22) | collective-permute-done | bytes 28704 | tf_op jit(solution)/shard_map/ppermute | solution.py:37
  85.3 1.2 %collective-permute-start.26 = (f32[56,128]{1,0:T(8,128)S(1)}, f32[56,128]{1,0:T(8,128)S(1)}, u32[]{:S(2)}, u32[]{:S(2)}) collective-permute-start(f32[56,128]{1,0:T(8,128)S(1)} %add_add_fusion.1), channel_id=1, source_target_pairs={{0,48},{16,32},{32,16},{48,0},{1,49},{17,33},{33,17},{49,1},{2,50}... | collective-permute-start | bytes 86024 | tf_op jit(solution)/shard_map/ppermute | solution.py:37
  86.4 1.1 %collective-permute-start.25 = (f32[56,128]{1,0:T(8,128)S(1)}, f32[56,128]{1,0:T(8,128)S(1)}, u32[]{:S(2)}, u32[]{:S(2)}) collective-permute-start(f32[56,128]{1,0:T(8,128)S(1)} %add_add_fusion.1), channel_id=1, source_target_pairs={{0,32},{16,48},{32,0},{48,16},{1,33},{17,49},{33,1},{49,17},{2,34}... | collective-permute-start | bytes 86024 | tf_op jit(solution)/shard_map/ppermute | solution.py:37
  87.5 1.1 %collective-permute-start.24 = (f32[56,128]{1,0:T(8,128)S(1)}, f32[56,128]{1,0:T(8,128)S(1)}, u32[]{:S(2)}, u32[]{:S(2)}) collective-permute-start(f32[56,128]{1,0:T(8,128)S(1)} %add_add_fusion.1), channel_id=1, source_target_pairs={{0,16},{16,0},{32,48},{48,32},{1,17},{17,1},{33,49},{49,33},{2,18}... | collective-permute-start | bytes 86024 | tf_op jit(solution)/shard_map/ppermute | solution.py:37
  88.6 0.7 collective-permute-done.26
  89.3 1.4 %collective-permute-done.25 = f32[56,128]{1,0:T(8,128)S(1)} collective-permute-done((f32[56,128]{1,0:T(8,128)S(1)}, f32[56,128]{1,0:T(8,128)S(1)}, u32[]{:S(2)}, u32[]{:S(2)}) %collective-permute-start.25) | collective-permute-done | bytes 28704 | tf_op jit(solution)/shard_map/ppermute | solution.py:37
  90.7 5.5 %collective-permute-start.27 = (f32[4,56,128]{2,1,0:T(8,128)S(1)}, f32[4,56,128]{2,1,0:T(8,128)S(1)}, u32[]{:S(2)}, u32[]{:S(2)}) collective-permute-start(f32[4,56,128]{2,1,0:T(8,128)S(1)} %pad_maximum_fusion.5.held), channel_id=1, source_target_pairs={{0,8},{8,0},{1,9},{9,1},{2,10},{10,2},{3,11},{11,3},{4,12},{12,4},... | collective-permute-start | bytes 344072 | tf_op jit(solution)/shard_map/ppermute | solution.py:37
  96.1 1.0 collective-permute-done.27.other
  97.1 1.3 %finish.1 = (f32[24,768]{1,0:T(8,128)}, f32[96,192]{1,0:T(8,128)}, f32[7,7,192]{2,1,0:T(8,128)}) custom-call(s32[1,8]{1,0:T(1,128)S(1)} %bitcast.64, f32[4,56,128]{2,1,0:T(8,128)S(1)} %pad_maximum_fusion.5.held, f32[4,56,128]{2,1,0:T(8,128)S(1)} %collective-permute-done.27.other), custom_call_target="tpu_custom_call" | custom-call | flops 1000000000 | bytes 1000000 | tf_op jit(solution)/shard_map/finish/pallas_call | solution.py:327
  (50 shorter events, 0.4 us)
Async XLA Ops:
  2.0 1.0 %copy-start = (bf16[1,4,16,16,192]{4,3,2,1,0:T(8,128)(2,1)S(1)}, bf16[1,4,16,16,192]{4,3,2,1,0:T(8,128)(2,1)}, u32[]{:S(2)}) copy-start(bf16[1,4,16,16,192]{4,3,2,1,0:T(8,128)(2,1)} %param.9) | copy-start | bytes 1179652
  3.1 0.8 copy-start.4
  3.9 0.8 copy-start.5
  4.6 4.3 %copy-start.7 = (f32[768]{0:T(1024)S(1)}, f32[768]{0:T(1024)}, u32[]{:S(2)}) copy-start(f32[768]{0:T(1024)} %param.16) | copy-start | bytes 9220
  5.6 4.2 %collective-permute-start.1 = (bf16[3,32,192]{2,0,1:T(4,128)(2,1)S(1)}, bf16[3,32,192]{2,0,1:T(4,128)(2,1)S(1)}, u32[]{:S(2)}, u32[]{:S(2)}) collective-permute-start(bf16[3,32,192]{2,0,1:T(4,128)(2,1)S(1)} %get-tuple-element.63), channel_id=1, source_target_pairs={{0,8},{8,0},{1,9},{9,1},{2,10},{10,2},{3,11},{11,3},{4,12},{12,4},... | collective-permute-start | bytes 110600 | tf_op jit(solution)/shard_map/ppermute | solution.py:37
  9.0 7.8 %collective-permute-start = (bf16[3,32,192]{2,0,1:T(4,128)(2,1)S(1)}, bf16[3,32,192]{2,0,1:T(4,128)(2,1)S(1)}, u32[]{:S(2)}, u32[]{:S(2)}) collective-permute-start(bf16[3,32,192]{2,0,1:T(4,128)(2,1)S(1)} %get-tuple-element.62), channel_id=1, source_target_pairs={{0,24},{8,16},{16,8},{24,0},{32,56},{40,48},{48,40},{56,32},{1,25}... | collective-permute-start | bytes 110600 | tf_op jit(solution)/shard_map/ppermute | solution.py:380
  9.9 12.4 %collective-permute-start.6 = (bf16[144,128]{1,0:T(8,128)(2,1)S(1)}, bf16[144,128]{1,0:T(8,128)(2,1)S(1)}, u32[]{:S(2)}, u32[]{:S(2)}) collective-permute-start(bf16[144,128]{1,0:T(8,128)(2,1)S(1)} %get-tuple-element.31), channel_id=1, source_target_pairs={{0,6},{1,7},{2,4},{3,5},{4,2},{5,3},{6,0},{7,1},{8,14},{9,15},{10,... | collective-permute-start | bytes 110600 | tf_op jit(solution)/shard_map/ppermute | solution.py:37
  14.5 7.7 %collective-permute-start.5 = (bf16[144,128]{1,0:T(8,128)(2,1)S(1)}, bf16[144,128]{1,0:T(8,128)(2,1)S(1)}, u32[]{:S(2)}, u32[]{:S(2)}) collective-permute-start(bf16[144,128]{1,0:T(8,128)(2,1)S(1)} %get-tuple-element.31), channel_id=1, source_target_pairs={{0,4},{1,5},{2,6},{3,7},{4,0},{5,1},{6,2},{7,3},{8,12},{9,13},{10,... | collective-permute-start | bytes 110600 | tf_op jit(solution)/shard_map/ppermute | solution.py:37
  15.5 6.7 %collective-permute-start.4 = (bf16[144,128]{1,0:T(8,128)(2,1)S(1)}, bf16[144,128]{1,0:T(8,128)(2,1)S(1)}, u32[]{:S(2)}, u32[]{:S(2)}) collective-permute-start(bf16[144,128]{1,0:T(8,128)(2,1)S(1)} %get-tuple-element.31), channel_id=1, source_target_pairs={{0,2},{1,3},{2,0},{3,1},{4,6},{5,7},{6,4},{7,5},{8,10},{9,11},{10,... | collective-permute-start | bytes 110600 | tf_op jit(solution)/shard_map/ppermute | solution.py:37
  17.3 6.8 %collective-permute-start.2 = (bf16[3,40,192]{2,1,0:T(8,128)(2,1)S(1)}, bf16[3,40,192]{2,1,0:T(8,128)(2,1)S(1)}, u32[]{:S(2)}, u32[]{:S(2)}) collective-permute-start(bf16[3,40,192]{2,1,0:T(8,128)(2,1)S(1)} %get-tuple-element.58), channel_id=1, source_target_pairs={{32,64},{48,80},{96,128},{112,144},{160,192},{176,208},{224,0},{24... | collective-permute-start | bytes 138248 | tf_op jit(solution)/shard_map/ppermute | solution.py:397
  22.2 4.6 %collective-permute-start.3 = (bf16[3,40,192]{2,1,0:T(8,128)(2,1)S(1)}, bf16[3,40,192]{2,1,0:T(8,128)(2,1)S(1)}, u32[]{:S(2)}, u32[]{:S(2)}) collective-permute-start(bf16[3,40,192]{2,1,0:T(8,128)(2,1)S(1)} %get-tuple-element.59), channel_id=1, source_target_pairs={{0,32},{16,48},{32,0},{48,16},{1,33},{17,49},{33,1},{49,17},{2,34}... | collective-permute-start | bytes 138248 | tf_op jit(solution)/shard_map/ppermute | solution.py:37
  22.3 7.5 %copy-start.3 = (f32[7,7,192]{2,1,0:T(8,128)S(1)}, f32[7,7,192]{2,1,0:T(8,128)}, u32[]{:S(2)}) copy-start(f32[7,7,192]{2,1,0:T(8,128)} %kernel.3) | copy-start | bytes 112900
  22.3 4.9 %collective-permute-start.7 = (bf16[4,144,128]{2,1,0:T(8,128)(2,1)S(1)}, bf16[4,144,128]{2,1,0:T(8,128)(2,1)S(1)}, u32[]{:S(2)}, u32[]{:S(2)}) collective-permute-start(bf16[4,144,128]{2,1,0:T(8,128)(2,1)S(1)} %pad_maximum_fusion.4), channel_id=1, source_target_pairs={{0,1},{1,0},{2,3},{3,2},{4,5},{5,4},{6,7},{7,6},{8,9},{9,8},{10,11... | collective-permute-start | bytes 442376 | tf_op jit(solution)/shard_map/ppermute | solution.py:37
  27.2 6.2 %copy-start.1 = (bf16[1,4,16,16,192]{4,3,2,1,0:T(8,128)(2,1)S(1)}, bf16[1,4,16,16,192]{4,3,2,1,0:T(8,128)(2,1)}, u32[]{:S(2)}) copy-start(bf16[1,4,16,16,192]{4,3,2,1,0:T(8,128)(2,1)} %param.9) | copy-start | bytes 1179652
  27.2 6.2 %copy-start.2 = (bf16[1,4,16,16,192]{4,3,2,1,0:T(8,128)(2,1)S(1)}, bf16[1,4,16,16,192]{4,3,2,1,0:T(8,128)(2,1)}, u32[]{:S(2)}) copy-start(bf16[1,4,16,16,192]{4,3,2,1,0:T(8,128)(2,1)} %param.10) | copy-start | bytes 1179652
  27.2 6.2 %copy-start.6 = (f32[192]{0:T(256)S(1)}, f32[192]{0:T(256)}, u32[]{:S(2)}) copy-start(f32[192]{0:T(256)} %param.14) | copy-start | bytes 2308
  27.3 6.2 %collective-permute-start.8 = (bf16[8,144,128]{2,1,0:T(8,128)(2,1)S(1)}, bf16[8,144,128]{2,1,0:T(8,128)(2,1)S(1)}, u32[]{:S(2)}, u32[]{:S(2)}) collective-permute-start(bf16[8,144,128]{2,1,0:T(8,128)(2,1)S(1)} %constant_dynamic-update-slice_fusion.held), channel_id=1, source_target_pairs={{0,8},{8,0},{1,9},{9,1},{2,10},{10,2},{3,11},{11,3},{4,12},{12,4},... | collective-permute-start | bytes 884744 | tf_op jit(solution)/shard_map/ppermute | solution.py:37
  42.9 4.6 %collective-permute-start.13 = (bf16[3,32,192]{2,0,1:T(4,128)(2,1)S(1)}, bf16[3,32,192]{2,0,1:T(4,128)(2,1)S(1)}, u32[]{:S(2)}, u32[]{:S(2)}) collective-permute-start(bf16[3,32,192]{2,0,1:T(4,128)(2,1)S(1)} %get-tuple-element.60), channel_id=1, source_target_pairs={{0,24},{8,16},{16,8},{24,0},{32,56},{40,48},{48,40},{56,32},{1,25}... | collective-permute-start | bytes 110600 | tf_op jit(solution)/shard_map/ppermute | solution.py:380
  43.0 4.5 %collective-permute-start.14 = (bf16[3,32,192]{2,0,1:T(4,128)(2,1)S(1)}, bf16[3,32,192]{2,0,1:T(4,128)(2,1)S(1)}, u32[]{:S(2)}, u32[]{:S(2)}) collective-permute-start(bf16[3,32,192]{2,0,1:T(4,128)(2,1)S(1)} %get-tuple-element.61), channel_id=1, source_target_pairs={{0,8},{8,0},{1,9},{9,1},{2,10},{10,2},{3,11},{11,3},{4,12},{12,4},... | collective-permute-start | bytes 110600 | tf_op jit(solution)/shard_map/ppermute | solution.py:37
  45.6 8.1 %collective-permute-start.9 = (bf16[4,352,128]{2,1,0:T(8,128)(2,1)S(1)}, bf16[4,352,128]{2,1,0:T(8,128)(2,1)S(1)}, u32[]{:S(2)}, u32[]{:S(2)}) collective-permute-start(bf16[4,352,128]{2,1,0:T(8,128)(2,1)S(1)} %get-tuple-element.34), channel_id=1, source_target_pairs={{0,8},{8,0},{1,9},{9,1},{2,10},{10,2},{3,11},{11,3},{4,12},{12,4},... | collective-permute-start | bytes 1081352 | tf_op jit(solution)/shard_map/ppermute | solution.py:37
  48.0 9.8 %collective-permute-start.16 = (bf16[3,40,192]{2,1,0:T(8,128)(2,1)S(1)}, bf16[3,40,192]{2,1,0:T(8,128)(2,1)S(1)}, u32[]{:S(2)}, u32[]{:S(2)}) collective-permute-start(bf16[3,40,192]{2,1,0:T(8,128)(2,1)S(1)} %get-tuple-element.56), channel_id=1, source_target_pairs={{32,64},{48,80},{96,128},{112,144},{160,192},{176,208},{224,0},{24... | collective-permute-start | bytes 138248 | tf_op jit(solution)/shard_map/ppermute | solution.py:397
  53.7 10.3 %collective-permute-start.15 = (bf16[3,40,192]{2,1,0:T(8,128)(2,1)S(1)}, bf16[3,40,192]{2,1,0:T(8,128)(2,1)S(1)}, u32[]{:S(2)}, u32[]{:S(2)}) collective-permute-start(bf16[3,40,192]{2,1,0:T(8,128)(2,1)S(1)} %get-tuple-element.57), channel_id=1, source_target_pairs={{0,32},{16,48},{32,0},{48,16},{1,33},{17,49},{33,1},{49,17},{2,34}... | collective-permute-start | bytes 138248 | tf_op jit(solution)/shard_map/ppermute | solution.py:37
  53.9 4.0 %collective-permute-start.10 = (bf16[352,128]{1,0:T(8,128)(2,1)S(1)}, bf16[352,128]{1,0:T(8,128)(2,1)S(1)}, u32[]{:S(2)}, u32[]{:S(2)}) collective-permute-start(bf16[352,128]{1,0:T(8,128)(2,1)S(1)} %get-tuple-element.64), channel_id=1, source_target_pairs={{0,16},{16,0},{32,48},{48,32},{1,17},{17,1},{33,49},{49,33},{2,18}... | collective-permute-start | bytes 270344 | tf_op jit(solution)/shard_map/ppermute | solution.py:37
  54.0 7.7 %collective-permute-start.11 = (bf16[352,128]{1,0:T(8,128)(2,1)S(1)}, bf16[352,128]{1,0:T(8,128)(2,1)S(1)}, u32[]{:S(2)}, u32[]{:S(2)}) collective-permute-start(bf16[352,128]{1,0:T(8,128)(2,1)S(1)} %get-tuple-element.65), channel_id=1, source_target_pairs={{0,32},{16,48},{32,0},{48,16},{1,33},{17,49},{33,1},{49,17},{2,34}... | collective-permute-start | bytes 270344 | tf_op jit(solution)/shard_map/ppermute | solution.py:37
  57.0 6.9 %collective-permute-start.12 = (bf16[352,128]{1,0:T(8,128)(2,1)S(1)}, bf16[352,128]{1,0:T(8,128)(2,1)S(1)}, u32[]{:S(2)}, u32[]{:S(2)}) collective-permute-start(bf16[352,128]{1,0:T(8,128)(2,1)S(1)} %get-tuple-element.66), channel_id=1, source_target_pairs={{0,48},{16,32},{32,16},{48,0},{1,49},{17,33},{33,17},{49,1},{2,50}... | collective-permute-start | bytes 270344 | tf_op jit(solution)/shard_map/ppermute | solution.py:37
  64.1 11.6 %collective-permute-start.17 = (bf16[112,128]{1,0:T(8,128)(2,1)S(1)}, bf16[112,128]{1,0:T(8,128)(2,1)S(1)}, u32[]{:S(2)}, u32[]{:S(2)}) collective-permute-start(bf16[112,128]{1,0:T(8,128)(2,1)S(1)} %get-tuple-element.37), channel_id=1, source_target_pairs={{0,2},{1,3},{2,0},{3,1},{4,6},{5,7},{6,4},{7,5},{8,10},{9,11},{10,... | collective-permute-start | bytes 86024 | tf_op jit(solution)/shard_map/ppermute | solution.py:37
  65.3 10.4 %collective-permute-start.18 = (bf16[112,128]{1,0:T(8,128)(2,1)S(1)}, bf16[112,128]{1,0:T(8,128)(2,1)S(1)}, u32[]{:S(2)}, u32[]{:S(2)}) collective-permute-start(bf16[112,128]{1,0:T(8,128)(2,1)S(1)} %get-tuple-element.38), channel_id=1, source_target_pairs={{0,4},{1,5},{2,6},{3,7},{4,0},{5,1},{6,2},{7,3},{8,12},{9,13},{10,... | collective-permute-start | bytes 86024 | tf_op jit(solution)/shard_map/ppermute | solution.py:37
  69.3 6.4 %collective-permute-start.19 = (bf16[112,128]{1,0:T(8,128)(2,1)S(1)}, bf16[112,128]{1,0:T(8,128)(2,1)S(1)}, u32[]{:S(2)}, u32[]{:S(2)}) collective-permute-start(bf16[112,128]{1,0:T(8,128)(2,1)S(1)} %get-tuple-element.39), channel_id=1, source_target_pairs={{0,6},{1,7},{2,4},{3,5},{4,2},{5,3},{6,0},{7,1},{8,14},{9,15},{10,... | collective-permute-start | bytes 86024 | tf_op jit(solution)/shard_map/ppermute | solution.py:37
  75.7 2.8 %collective-permute-start.20 = (f32[56,128]{1,0:T(8,128)S(1)}, f32[56,128]{1,0:T(8,128)S(1)}, u32[]{:S(2)}, u32[]{:S(2)}) collective-permute-start(f32[56,128]{1,0:T(8,128)S(1)} %pad_maximum_fusion.15), channel_id=1, source_target_pairs={{0,1},{1,0},{2,3},{3,2},{4,5},{5,4},{6,7},{7,6},{8,9},{9,8},{10,11... | collective-permute-start | bytes 86024 | tf_op jit(solution)/shard_map/ppermute | solution.py:37
  78.5 3.9 %collective-permute-start.23 = (f32[56,128]{1,0:T(8,128)S(1)}, f32[56,128]{1,0:T(8,128)S(1)}, u32[]{:S(2)}, u32[]{:S(2)}) collective-permute-start(f32[56,128]{1,0:T(8,128)S(1)} %fusion.10), channel_id=1, source_target_pairs={{0,192},{64,128},{128,64},{192,0},{1,193},{65,129},{129,65},{193,1... | collective-permute-start | bytes 86024 | tf_op jit(solution)/shard_map/ppermute | solution.py:37
  81.0 4.2 %collective-permute-start.22 = (f32[56,128]{1,0:T(8,128)S(1)}, f32[56,128]{1,0:T(8,128)S(1)}, u32[]{:S(2)}, u32[]{:S(2)}) collective-permute-start(f32[56,128]{1,0:T(8,128)S(1)} %fusion.10), channel_id=1, source_target_pairs={{0,128},{64,192},{128,0},{192,64},{1,129},{65,193},{129,1},{193,65... | collective-permute-start | bytes 86024 | tf_op jit(solution)/shard_map/ppermute | solution.py:37
  81.0 4.2 %collective-permute-start.21 = (f32[56,128]{1,0:T(8,128)S(1)}, f32[56,128]{1,0:T(8,128)S(1)}, u32[]{:S(2)}, u32[]{:S(2)}) collective-permute-start(f32[56,128]{1,0:T(8,128)S(1)} %fusion.10), channel_id=1, source_target_pairs={{0,64},{64,0},{128,192},{192,128},{1,65},{65,1},{129,193},{193,129... | collective-permute-start | bytes 86024 | tf_op jit(solution)/shard_map/ppermute | solution.py:37
  85.3 4.0 %collective-permute-start.26 = (f32[56,128]{1,0:T(8,128)S(1)}, f32[56,128]{1,0:T(8,128)S(1)}, u32[]{:S(2)}, u32[]{:S(2)}) collective-permute-start(f32[56,128]{1,0:T(8,128)S(1)} %add_add_fusion.1), channel_id=1, source_target_pairs={{0,48},{16,32},{32,16},{48,0},{1,49},{17,33},{33,17},{49,1},{2,50}... | collective-permute-start | bytes 86024 | tf_op jit(solution)/shard_map/ppermute | solution.py:37
  86.4 4.2 %collective-permute-start.25 = (f32[56,128]{1,0:T(8,128)S(1)}, f32[56,128]{1,0:T(8,128)S(1)}, u32[]{:S(2)}, u32[]{:S(2)}) collective-permute-start(f32[56,128]{1,0:T(8,128)S(1)} %add_add_fusion.1), channel_id=1, source_target_pairs={{0,32},{16,48},{32,0},{48,16},{1,33},{17,49},{33,1},{49,17},{2,34}... | collective-permute-start | bytes 86024 | tf_op jit(solution)/shard_map/ppermute | solution.py:37
  87.5 3.1 %collective-permute-start.24 = (f32[56,128]{1,0:T(8,128)S(1)}, f32[56,128]{1,0:T(8,128)S(1)}, u32[]{:S(2)}, u32[]{:S(2)}) collective-permute-start(f32[56,128]{1,0:T(8,128)S(1)} %add_add_fusion.1), channel_id=1, source_target_pairs={{0,16},{16,0},{32,48},{48,32},{1,17},{17,1},{33,49},{49,33},{2,18}... | collective-permute-start | bytes 86024 | tf_op jit(solution)/shard_map/ppermute | solution.py:37
  90.7 6.4 %collective-permute-start.27 = (f32[4,56,128]{2,1,0:T(8,128)S(1)}, f32[4,56,128]{2,1,0:T(8,128)S(1)}, u32[]{:S(2)}, u32[]{:S(2)}) collective-permute-start(f32[4,56,128]{2,1,0:T(8,128)S(1)} %pad_maximum_fusion.5.held), channel_id=1, source_target_pairs={{0,8},{8,0},{1,9},{9,1},{2,10},{10,2},{3,11},{11,3},{4,12},{12,4},... | collective-permute-start | bytes 344072 | tf_op jit(solution)/shard_map/ppermute | solution.py:37

commit v4 on v3

--- a/solution.py
+++ b/solution.py
@@ -11,7 +11,8 @@
 inv_root_two_pi = 0.3989422804014327
 bf16 = jnp.bfloat16
 f32 = jnp.float32
-REP_ORDER = (0, 2, 4, 6, 1, 3, 5, 7)
+REP_ORDER = (0, 7, 2, 5, 1, 6, 3, 4)
+SUM_ORDER = (0, 2, 1, 3, 6, 4, 7, 5)
 TILE = ("y", "x", "core")
 SIZES = {"y": 4, "x": 4, "core": 2, "rep": 8}
 C, FF, S, CAP, KS = 192, 768, 16, 4, 7
@@ -25,10 +26,7 @@
 ROWS = SHARD * SIZES["rep"]
 EROWS = C // SIZES["rep"]
 RROWS = FF // SIZES["rep"]
-CHUNK = 40
-GROWS = 64
-PIECE = GROWS // 4
-PART = CHUNK + PIECE
+GROWS = 48
 FACTOR = 1.0 / 512.0
 VMEM_LIMIT = 48 * 1024 * 1024
 
@@ -45,23 +43,16 @@
     return lax.dot_general(left, right, ((contract[:1], contract[1:]), ((), ())), preferred_element_type=f32)
 
 
-CORE, AT_X, AT_REP, COUNT, PLACE = 0, 1, 2, 3, 4
-
-
-def place_kernel(info, tiles, expand, project, canvas, packed, held_e, held_r, sems, tile_sems):
-    weights = [
-        pltpu.make_async_copy(expand, held_e, sems.at[0]),
-        pltpu.make_async_copy(project, held_r, sems.at[1]),
-    ]
-    for copy in weights:
-        copy.start()
-
+CORE, AT_REP, COUNT, PLACE = 0, 1, 2, 3
+
+
+def place_kernel(info, tiles, canvas, sems):
     def tile_copy(j):
         p = info[0, PLACE + j]
         row = pl.multiple_of((p // 2) * S, S)
         col = pl.multiple_of((p % 2) * S, S)
         return row, col, pltpu.make_async_copy(
-            tiles.at[j], canvas.at[pl.ds(row, S), pl.ds(col, S), :], tile_sems.at[j]
+            tiles.at[j], canvas.at[pl.ds(row, S), pl.ds(col, S), :], sems.at[j]
         )
 
     for j in range(CAP):
@@ -75,15 +66,16 @@
         def _():
             canvas[pl.ds(row, S), pl.ds(col, S), :] = jnp.zeros((S, S, C), bf16)
 
-    for copy in weights:
-        copy.wait()
-    e, r = pack_expand(held_e[...].astype(f32)), pack_reduce(held_r[...].astype(f32))
-    packed[...] = jnp.where(info[0, CORE] == 0, e, r).astype(bf16)
     for j in range(CAP):
 
         @pl.when(j < info[0, COUNT])
         def _():
             tile_copy(j)[2].wait()
+
+
+def pack_kernel(info, expand, project, packed):
+    e, r = pack_expand(expand[...].astype(f32)), pack_reduce(project[...].astype(f32))
+    packed[...] = jnp.where(info[0, CORE] == 0, e, r).astype(bf16)
 
 
 def fill_taps(kernel, taps, flip):
@@ -181,9 +173,9 @@
     info, planes, filtered, tiles, cotan, gain, bias, held, other,
     result, field_out, keep, send, keep_taps,
     field, tap_acc, expand_wide, expand, project, hidden, active, grad_hidden,
-    grad_e, grad_r, grad_rt, shards, tap_rows,
+    grad_e, grad_r, grad_rt,
 ):
-    me, my_x, my_z = info[0, CORE], info[0, AT_X], info[0, AT_REP]
+    me, my_z = info[0, CORE], info[0, AT_REP]
     for k, s in enumerate(REP_ORDER):
         z = my_z ^ s
         mine, theirs = held[k].astype(f32), other[k].astype(f32)
@@ -197,13 +189,8 @@
     grad_e[...] = jnp.zeros_like(grad_e)
     grad_r[...] = jnp.zeros_like(grad_r)
 
-    def blank(j, carry):
-        result[j] = jnp.zeros_like(result[j])
-        return carry
-
-    lax.fori_loop(info[0, COUNT], CAP, blank, 0)
-
-    def slot(j, carry):
+    def slot(j):
+        live = j < info[0, COUNT]
         p = info[0, PLACE + j]
         lower = p // 2
         row = pl.multiple_of(lower * S, S)
@@ -213,23 +200,23 @@
         inverse = lax.rsqrt(jnp.sum(spread * spread, axis=1, keepdims=True) * (1.0 / C) + 1e-6)
         normed = spread * inverse
         scaled = (normed * gain[...]).astype(bf16)
-        up = cotan[j].reshape(S * S, C)
-        hidden[0] = dot(scaled, expand[...], (1, 0))
-        hidden[1] = dot(up, project[...], (1, 1))
+        up = jnp.where(live, cotan[j].reshape(S * S, C), jnp.zeros((S * S, C), bf16))
+        hidden[j, 0] = dot(scaled, expand[...], (1, 0))
+        hidden[j, 1] = dot(up, project[...], (1, 1))
 
         def gelu(r, carry):
             rows = pl.ds(pl.multiple_of(r * 16, 16), 16)
-            h = hidden[0, rows, :] + bias[...]
+            h = hidden[j, 0, rows, :] + bias[...]
             cdf = 0.5 * (1.0 + lax.erf(h * inv_root_two))
             slope = cdf + h * jnp.exp(-0.5 * h * h) * inv_root_two_pi
-            active[rows, :] = (h * cdf).astype(bf16)
-            grad_hidden[rows, :] = (hidden[1, rows, :] * slope).astype(bf16)
+            active[j, rows, :] = (h * cdf).astype(bf16)
+            grad_hidden[j, rows, :] = (hidden[j, 1, rows, :] * slope).astype(bf16)
             return carry
 
-        lax.fori_loop(0, S, gelu, 0)
-        a, gh = active[...], grad_hidden[...]
+        lax.fori_loop(0, S, gelu, 0, unroll=S)
+        a, gh = active[j], grad_hidden[j]
         mixed = dot(a, project[...], (1, 0))
-        result[j] = tiles[j].astype(f32) + mixed.reshape(S, S, C)
+        result[j] = jnp.where(live, tiles[j].astype(f32) + mixed.reshape(S, S, C), jnp.zeros((S, S, C), f32))
         grad_e[...] += dot(scaled, gh, (0, 0))
         grad_r[...] += dot(up, a, (0, 0))
         q = dot(gh, expand[...], (1, 1)) * gain[...]
@@ -243,9 +230,9 @@
         old = field[1, :, pl.ds(col, S), :]
         side = lax.broadcasted_iota(jnp.int32, (S, S, LANES), 2) // TAIL
         field[1, :, pl.ds(col, S), :] = jnp.where(side == lower, tail, old)
-        return carry
-
-    lax.fori_loop(0, info[0, COUNT], slot, 0)
+
+    for j in range(CAP):
+        slot(j)
 
     correlate_planes(planes, field, tap_acc)
     sums = jnp.sum(tap_acc[...], axis=2)
@@ -255,45 +242,32 @@
     main = jnp.concatenate([main, pad], axis=0)
     tail = jnp.concatenate([tail, pad], axis=0)
     low_lane = lax.broadcasted_iota(jnp.int32, (16, LANES), 1) < TAIL
+    halves = []
     for h in range(2):
         s = 24 * h
         tails = jnp.where(low_lane, tail[s : s + 16], tail[s + 16 : s + 32])
-        tap_rows[h] = jnp.concatenate([main[s : s + 32], tails, jnp.zeros((16, LANES), f32)], axis=0)
-    for i in range(4):
-        rows = pl.ds(pl.multiple_of((my_x ^ i) * PIECE, PIECE), PIECE)
-        keep_taps[i] = tap_rows[me, rows, :]
-        high, low = split_high_low(tap_rows[1 - me, rows, :])
-        send[i, 8 * CHUNK : 8 * CHUNK + PIECE] = high
-        send[i, 8 * CHUNK + PIECE :] = low
+        halves.append(jnp.concatenate([main[s : s + 32], tails], axis=0))
+    keep_taps[...] = jnp.where(me == 0, halves[0], halves[1])
+    high, low = split_high_low(jnp.where(me == 0, halves[1], halves[0]))
+    send[ROWS : ROWS + GROWS] = high
+    send[ROWS + GROWS :] = low
     grad_rt[...] = grad_r[...].T
-    shards[:, SHARD:] = jnp.zeros((2, 4 * CHUNK - SHARD, LANES), f32)
-    for k in range(8):
-        z = my_z ^ k
+    for k, s in enumerate(SUM_ORDER):
+        z = my_z ^ s
         e = pack_expand(grad_e[pl.ds(pl.multiple_of(z * EROWS, 8), EROWS), :])
         r = pack_reduce(grad_rt[pl.ds(pl.multiple_of(z * RROWS, RROWS), RROWS), :])
-        shards[0, :SHARD] = jnp.where(me == 0, e, r)
-        shards[1, :SHARD] = jnp.where(me == 0, r, e)
-        for i in range(4):
-            rows = pl.ds(pl.multiple_of((my_x ^ i) * CHUNK, 8), CHUNK)
-            keep[i, k * CHUNK : (k + 1) * CHUNK] = shards[0, rows, :]
-            send[i, k * CHUNK : (k + 1) * CHUNK] = shards[1, rows, :].astype(bf16)
-
-
-def finish_kernel(info, held, other, grad_e, grad_r, grad_k, shards, tap_rows):
-    me, my_x = info[0, CORE], info[0, AT_X]
-    for i in range(4):
-        rows = pl.ds(pl.multiple_of((my_x ^ i) * CHUNK, 8), CHUNK)
-        taps = pl.ds(pl.multiple_of((my_x ^ i) * PIECE, PIECE), PIECE)
-        shards[me, rows, :] = held[i, :CHUNK]
-        shards[1 - me, rows, :] = other[i, :CHUNK]
-        tap_rows[me, taps, :] = held[i, CHUNK:]
-        tap_rows[1 - me, taps, :] = other[i, CHUNK:]
-    grad_e[...] = unpack_expand(shards[0]) * FACTOR
-    grad_r[...] = unpack_reduce(shards[1]) * FACTOR
+        keep[k * SHARD : (k + 1) * SHARD] = jnp.where(me == 0, e, r)
+        send[k * SHARD : (k + 1) * SHARD] = jnp.where(me == 0, r, e).astype(bf16)
+
+
+def finish_kernel(info, held, other, grad_e, grad_r, grad_k):
+    first = info[0, CORE] == 0
+    grad_e[...] = unpack_expand(jnp.where(first, held[:SHARD], other[:SHARD])) * FACTOR
+    grad_r[...] = unpack_reduce(jnp.where(first, other[:SHARD], held[:SHARD])) * FACTOR
+    a, b = held[SHARD:], other[SHARD:]
     halves = []
-    for h in range(2):
-        half = tap_rows[h]
-        tails = jnp.concatenate([half[32:48, :TAIL], half[32:48, TAIL:]], axis=0)
+    for half in (jnp.where(first, a, b), jnp.where(first, b, a)):
+        tails = jnp.concatenate([half[32:, :TAIL], half[32:, TAIL:]], axis=0)
         halves.append(jnp.concatenate([half[:32], tails], axis=1))
     whole = jnp.concatenate([halves[0][:24], halves[1]], axis=0) * FACTOR
     for dy in range(KS):
@@ -318,12 +292,10 @@
     lax.fori_loop(0, info[0, COUNT], slot, 0)
 
 
-def call(kernel, ins, outs, scratch=(), name=None, hbm=(), us=1):
+def call(kernel, ins, outs, scratch=(), name=None, us=1):
     smem = pl.BlockSpec(memory_space=pltpu.SMEM)
     vmem = pl.BlockSpec(memory_space=pltpu.VMEM)
     specs = [smem if v.dtype == jnp.int32 else vmem for v in ins]
-    for i in hbm:
-        specs[i] = pl.BlockSpec(memory_space=pltpu.HBM)
     return pl.pallas_call(
         kernel,
         out_shape=[jax.ShapeDtypeStruct(shape, dtype) for shape, dtype in outs],
@@ -347,9 +319,9 @@
         [
             ((CAP, S, S, C), f32),
             ((SIDE, SIDE, C), bf16),
-            ((4, 8 * CHUNK, LANES), f32),
-            ((4, 8 * CHUNK + 2 * PIECE, LANES), bf16),
-            ((4, PIECE, LANES), f32),
+            ((ROWS, LANES), f32),
+            ((ROWS + 2 * GROWS, LANES), bf16),
+            ((GROWS, LANES), f32),
         ],
         [
             (CELLS, f32),
@@ -357,14 +329,12 @@
             ((C, FF), f32),
             ((C, FF), bf16),
             ((FF, C), bf16),
-            ((2, S * S, FF), f32),
-            ((S * S, FF), bf16),
-            ((S * S, FF), bf16),
+            ((CAP, 2, S * S, FF), f32),
+            ((CAP, S * S, FF), bf16),
+            ((CAP, S * S, FF), bf16),
             ((C, FF), f32),
             ((C, FF), f32),
             ((FF, C), f32),
-            ((2, 4 * CHUNK, LANES), f32),
-            ((2, GROWS, LANES), f32),
         ],
         name="block",
         us=14,
@@ -414,12 +384,12 @@
     return lax.optimization_barrier((value, *others))
 
 
-def rows_sum(own, got):
-    return (own + got[0]) + (got[1] + got[2])
+def rows_sum(own, a, b, c):
+    return (own + a) + (b + c)
 
 
 def join(value):
-    return value[..., :PIECE, :].astype(f32) + value[..., PIECE:, :].astype(f32)
+    return value[:GROWS].astype(f32) + value[GROWS:].astype(f32)
 
 
 def per_device(
@@ -433,37 +403,36 @@
     hidden_bias,
     reduce_weight,
 ):
-    scalars = [lax.axis_index(a) for a in ("core", "x", "rep")] + [tile_count[0, 0]]
+    scalars = [lax.axis_index(a) for a in ("core", "rep")] + [tile_count[0, 0]]
     info = jnp.concatenate([jnp.stack(scalars).astype(jnp.int32), tile_place[0, 0]])[None]
     tiles, cotan = tile_data[0], cotangent[0]
-    canvas, packed = call(
+    (canvas,) = call(
         place_kernel,
-        (info, tiles, expand_weight, reduce_weight),
-        [((SIDE, SIDE, C), bf16), ((SHARD, LANES), bf16)],
-        [
-            ((EROWS, FF), bf16),
-            ((RROWS, C), bf16),
-            pltpu.SemaphoreType.DMA((2,)),
-            pltpu.SemaphoreType.DMA((CAP,)),
-        ],
+        (info, tiles),
+        [((SIDE, SIDE, C), bf16)],
+        [pltpu.SemaphoreType.DMA((CAP,))],
         name="place",
-        hbm=(1, 2, 3),
-        us=2,
     )
     inner, outer = side_rims(canvas)
-    packed, inner = tie(packed, inner)
-    held = jnp.stack([packed] + [swap(packed, "rep", bits) for bits in (2, 4, 6)])
+    shards, inner = tie(expand_weight, inner)
+    (packed,) = call(
+        pack_kernel, (info, shards, reduce_weight), [((SHARD, LANES), bf16)], name="pack", us=0
+    )
+    held = jnp.stack([packed, swap(packed, "rep", 7)])
     widened = widen(canvas, inner, outer)
     near, far = end_rims(widened)
-    held = jnp.concatenate([held, swap(held, "rep", 1)])
+    held = jnp.concatenate([held, swap(held, "rep", 2)])
+    held_got = swap(held, "rep", 1)
     planes, filtered = call(
         field_kernel,
         (pad_ends(widened, near, far), kernel),
         [(PLANES, f32), (CELLS, f32)],
         [(TAP_PLANES, f32)],
         name="field",
-        us=5,
-    )
+        us=0,
+    )
+    held_got, filtered = tie(held_got, filtered)
+    held = jnp.concatenate([held, held_got])
     other = swap(held, "core", 1)
     result, field, keep, send, taps = block_call(
         info,
@@ -476,43 +445,44 @@
         held,
         other,
     )
-    end, pair = 8 * CHUNK, 2 * CHUNK
+    pair = 2 * SHARD
     got = swap(send, "core", 1)
     inner, outer = side_rims(field)
-    held = keep + got[:, :end].astype(f32)
-    taps = taps + join(got[:, end:])
+    held = keep + got[:ROWS].astype(f32)
+    taps = taps + join(got[ROWS:])
     high, low = split_high_low(taps)
-    send = jnp.concatenate([held.astype(bf16), high, low], axis=1)
-    got = [swap(send[i], "x", i) for i in (1, 2, 3)]
+    got, inner = tie(got, inner)
     widened = widen(field, inner, outer)
     near, far = end_rims(widened)
-    held = rows_sum(held[0], [g[:end].astype(f32) for g in got])
-    taps = rows_sum(taps[0], [join(g[end:]) for g in got])
-    high, low = split_high_low(taps)
     sends = [
-        jnp.concatenate([held[k * CHUNK : k * CHUNK + pair].astype(bf16), high, low]) for k in (2, 4, 6)
+        jnp.concatenate([held[k * pair : (k + 1) * pair].astype(bf16), high, low]) for k in (1, 2, 3)
     ]
-    *sends, near, far = tie(*sends, near, far)
-    got = [swap(part, "rep", k) for part, k in zip(sends, (2, 4, 6))]
+    got = [swap(part, "rep", s) for part, s in zip(sends, (1, 6, 7))]
     (grad_tiles,) = call(
         spread_kernel,
         (info, pad_ends(widened, near, far), cotan, kernel),
         [((CAP, S, S, C), f32)],
         [(PLANES, f32), (CELLS, f32), (TAP_PLANES, f32)],
         name="spread",
-        us=6,
-    )
-    held = rows_sum(held[:pair], [g[:pair].astype(f32) for g in got])
-    taps = rows_sum(high.astype(f32) + low.astype(f32), [join(g[pair:]) for g in got])
-    part, grad_tiles = tie(jnp.concatenate([held[CHUNK:], taps]), grad_tiles)
-    held = jnp.concatenate([held[:CHUNK], taps]) + swap(part, "rep", 1)
-    held = rows_sum(held, [swap(held, "y", i) for i in (1, 2, 3)])
-    held = jnp.stack([held] + [swap(held, "x", i) for i in (1, 2, 3)])
+        us=0,
+    )
+    held = rows_sum(held[:pair], *[g[:pair].astype(f32) for g in got])
+    taps = rows_sum(high.astype(f32) + low.astype(f32), *[join(g[pair:]) for g in got])
+    high, low = split_high_low(taps)
+    part, grad_tiles = tie(jnp.concatenate([held[SHARD:].astype(bf16), high, low]), grad_tiles)
+    got = swap(part, "rep", 2)
+    held = held[:SHARD] + got[:SHARD].astype(f32)
+    taps = (high.astype(f32) + low.astype(f32)) + join(got[SHARD:])
+    for axis in ("x", "y"):
+        part = jnp.concatenate([held.astype(bf16), *split_high_low(taps)])
+        parts = [part] + [swap(part, axis, i) for i in (2, 1, 3)]
+        held = rows_sum(*[p[:SHARD].astype(f32) for p in parts])
+        taps = rows_sum(*[join(p[SHARD:]) for p in parts])
+    held = jnp.concatenate([held, taps])
     grad_expand, grad_reduce, grad_kernel = call(
         finish_kernel,
         (info, held, swap(held, "core", 1)),
         [((EROWS, FF), f32), ((RROWS, C), f32), ((KS, KS, C), f32)],
-        [((2, 4 * CHUNK, LANES), f32), ((2, GROWS, LANES), f32)],
         name="finish",
     )
     return result[None], grad_tiles[None], grad_expand, grad_reduce, grad_kernel

time: 98.8 us -> 88.6 us (0.90)
  starting transfers between devices: 49.9 us -> 41.2 us
  local copies, waits for them, and re-layouts: 3.46 us -> 1.13 us
    ppermute x24 -> x20, starting transfers between devices: 39.1 us -> 32.9 us  [swap(): return lax.ppermute(value, axis, [(i, i ^ bit) for i in range(SIZES[axis])])]
    ppermute x2, starting transfers between devices: 10.7 us -> 7.89 us  [end_rims(): lax.ppermute(jnp.where(upper == 0, north_edge, south_edge), ('y', 'x'), p...]
    unnamed x20 -> x16, local copies, waits for them, and re-layouts: 2.67 us -> 1.08 us
    ppermute x24 -> x20, waiting for transfers between devices: 17.8 us -> 18.5 us  [swap(): return lax.ppermute(value, axis, [(i, i ^ bit) for i in range(SIZES[axis])])]
    pallas_call x5 -> x6, Pallas kernels: 20.7 us -> 20.6 us  [call(): pl.pallas_call(kernel, out_shape=[jax.ShapeDtypeStruct(shape, dtype) for...]
  transfers between devices with their start and end apart: 28 -> 24, of which waited for: 12 -> 17; matrix products, arithmetic and copies ran while one was open for 2% -> 2% of each run, Pallas kernels for 9% -> 11%
where the time goes in v4:
time: 88.6 us; the launch traced here: 88.4 us
  starting transfers between devices  41.2 us (47%)
  waiting for transfers between devices  21 us (24%)
  Pallas kernels  20.6 us (23%)
  other arithmetic  2.94 us (3%)
  between operations  1.57 us (2%)
  local copies, waits for them, and re-layouts  1.13 us (1%)
    ppermute x20, starting transfers between devices, swap(): return lax.ppermute(value, axis, [(i, i ^ bit) for i in range(SIZES[axis])])  32.9 us
    pallas_call x6, Pallas kernels, call(): pl.pallas_call(kernel, out_shape=[jax.ShapeDtypeStruct(shape, dtype) for...  20.6 us
    ppermute x20, waiting for transfers between devices, swap(): return lax.ppermute(value, axis, [(i, i ^ bit) for i in range(SIZES[axis])])  18.5 us
    ppermute x2, starting transfers between devices, end_rims(): lax.ppermute(jnp.where(upper == 0, north_edge, south_edge), ('y', 'x'), p...  7.89 us
    ppermute x2, waiting for transfers between devices, side_rims(): lax.ppermute(jnp.where(core == 0, west_edge, east_edge), ('x', 'core'), p...  2.23 us
  transfers between devices with their start and end apart: 24, of which 17 were waited for; matrix products, arithmetic and copies ran while one was open for 2% of the time, Pallas kernels for 11%

profile of v4, /device:TPU:1, one launch (start us, length us, event | category | flops | bytes accessed | tf_op | source)
XLA Modules:
  0.0 88.4 jit_solution(11128259386215716743)
XLA Ops:
  1.3 0.7 add_bitcast_fusion.info
  2.0 1.0 %copy-done.4 = bf16[1,4,16,16,192]{4,3,2,1,0:T(8,128)(2,1)S(1)} copy-done((bf16[1,4,16,16,192]{4,3,2,1,0:T(8,128)(2,1)S(1)}, bf16[1,4,16,16,192]{4,3,2,1,0:T(8,128)(2,1)}, u32[]{:S(2)}) %copy-start.4) | copy-done | bytes 393240
  3.1 0.7 place.1
  3.8 0.1 select_bitcast_fusion.7
  3.9 3.3 %collective-permute-start.1 = (bf16[3,32,192]{2,0,1:T(4,128)(2,1)S(1)}, bf16[3,32,192]{2,0,1:T(4,128)(2,1)S(1)}, u32[]{:S(2)}, u32[]{:S(2)}) collective-permute-start(bf16[3,32,192]{2,0,1:T(4,128)(2,1)S(1)} %get-tuple-element.56), channel_id=1, source_target_pairs={{0,8},{8,0},{1,9},{9,1},{2,10},{10,2},{3,11},{11,3},{4,12},{12,4},... | collective-permute-start | bytes 110600 | tf_op jit(solution)/shard_map/ppermute | solution.py:35
  7.2 0.0 collective-permute-start
  7.2 0.9 %collective-permute-done.1 = bf16[3,32,192]{2,0,1:T(4,128)(2,1)S(1)} collective-permute-done((bf16[3,32,192]{2,0,1:T(4,128)(2,1)S(1)}, bf16[3,32,192]{2,0,1:T(4,128)(2,1)S(1)}, u32[]{:S(2)}, u32[]{:S(2)}) %collective-permute-start.1) | collective-permute-done | bytes 36896 | tf_op jit(solution)/shard_map/ppermute | solution.py:35
  8.1 0.6 pack.1
  8.7 4.2 %collective-permute-start.4 = (bf16[144,128]{1,0:T(8,128)(2,1)S(1)}, bf16[144,128]{1,0:T(8,128)(2,1)S(1)}, u32[]{:S(2)}, u32[]{:S(2)}) collective-permute-start(bf16[144,128]{1,0:T(8,128)(2,1)S(1)} %pack.1), channel_id=1, source_target_pairs={{0,7},{1,6},{2,5},{3,4},{4,3},{5,2},{6,1},{7,0},{8,15},{9,14},{10,... | collective-permute-start | bytes 110600 | tf_op jit(solution)/shard_map/ppermute | solution.py:35
  12.9 0.0 collective-permute-done
  12.9 0.1 select_bitcast_fusion.5
  13.0 0.4 pad_maximum_fusion.3
  13.4 0.0 copy-start.1
  13.4 5.0 %collective-permute-start.2 = (bf16[3,40,192]{2,1,0:T(8,128)(2,1)S(1)}, bf16[3,40,192]{2,1,0:T(8,128)(2,1)S(1)}, u32[]{:S(2)}, u32[]{:S(2)}) collective-permute-start(bf16[3,40,192]{2,1,0:T(8,128)(2,1)S(1)} %get-tuple-element.51), channel_id=1, source_target_pairs={{32,64},{48,80},{96,128},{112,144},{160,192},{176,208},{224,0},{24... | collective-permute-start | bytes 138248 | tf_op jit(solution)/shard_map/ppermute | solution.py:367
  18.4 0.0 collective-permute-done.4
  18.4 2.2 %collective-permute-start.5 = (bf16[2,144,128]{2,1,0:T(8,128)(2,1)S(1)}, bf16[2,144,128]{2,1,0:T(8,128)(2,1)S(1)}, u32[]{:S(2)}, u32[]{:S(2)}) collective-permute-start(bf16[2,144,128]{2,1,0:T(8,128)(2,1)S(1)} %pad_maximum_fusion.13), channel_id=1, source_target_pairs={{0,2},{1,3},{2,0},{3,1},{4,6},{5,7},{6,4},{7,5},{8,10},{9,11},{10,... | collective-permute-start | bytes 221192 | tf_op jit(solution)/shard_map/ppermute | solution.py:35
  20.6 2.4 %collective-permute-done.3 = bf16[3,40,192]{2,1,0:T(8,128)(2,1)S(1)} collective-permute-done((bf16[3,40,192]{2,1,0:T(8,128)(2,1)S(1)}, bf16[3,40,192]{2,1,0:T(8,128)(2,1)S(1)}, u32[]{:S(2)}, u32[]{:S(2)}) %collective-permute-start.3) | collective-permute-done | bytes 46112 | tf_op jit(solution)/shard_map/ppermute | solution.py:35
  23.0 0.0 collective-permute-done.5
  23.1 1.7 %collective-permute-start.6 = (bf16[4,144,128]{2,1,0:T(8,128)(2,1)S(1)}, bf16[4,144,128]{2,1,0:T(8,128)(2,1)S(1)}, u32[]{:S(2)}, u32[]{:S(2)}) collective-permute-start(bf16[4,144,128]{2,1,0:T(8,128)(2,1)S(1)} %pad_maximum_fusion.11), channel_id=1, source_target_pairs={{0,1},{1,0},{2,3},{3,2},{4,5},{5,4},{6,7},{7,6},{8,9},{9,8},{10,11... | collective-permute-start | bytes 442376 | tf_op jit(solution)/shard_map/ppermute | solution.py:35
  24.8 0.3 fusion.2.padded
  25.1 0.0 copy-start.7
  25.1 0.0 copy-start
  25.1 0.0 copy-start.5
  25.1 0.0 copy-start.6
  25.2 3.7 %field.1 = (f32[3,22,40,128]{3,2,1,0:T(8,128)S(1)}, f32[3,16,32,128]{3,2,1,0:T(8,128)S(1)}) custom-call(f32[38,40,192]{2,1,0:T(8,128)S(1)} %fusion.2.padded, f32[7,7,192]{2,1,0:T(8,128)S(1)} %copy-done.1), custom_call_target="tpu_custom_call" | custom-call | tf_op jit(solution)/shard_map/field/pallas_call | solution.py:299
  28.8 0.0 collective-permute-done.6
  28.9 2.7 %collective-permute-start.7 = (bf16[8,144,128]{2,1,0:T(8,128)(2,1)S(1)}, bf16[8,144,128]{2,1,0:T(8,128)(2,1)S(1)}, u32[]{:S(2)}, u32[]{:S(2)}) collective-permute-start(bf16[8,144,128]{2,1,0:T(8,128)(2,1)S(1)} %pad_maximum_fusion.4.held), channel_id=1, source_target_pairs={{0,8},{8,0},{1,9},{9,1},{2,10},{10,2},{3,11},{11,3},{4,12},{12,4},... | collective-permute-start | bytes 884744 | tf_op jit(solution)/shard_map/ppermute | solution.py:35
  31.6 1.2 %collective-permute-done.7.other = bf16[8,144,128]{2,1,0:T(8,128)(2,1)S(1)} collective-permute-done((bf16[8,144,128]{2,1,0:T(8,128)(2,1)S(1)}, bf16[8,144,128]{2,1,0:T(8,128)(2,1)S(1)}, u32[]{:S(2)}, u32[]{:S(2)}) %collective-permute-start.7) | collective-permute-done | bytes 294944 | tf_op jit(solution)/shard_map/ppermute | solution.py:35
  32.8 8.8 %block.1 = (f32[4,16,16,192]{3,2,1,0:T(8,128)}, bf16[32,32,192]{2,1,0:T(8,128)(2,1)S(1)}, f32[1152,128]{1,0:T(8,128)S(1)}, bf16[1248,128]{1,0:T(8,128)(2,1)S(1)}, f32[48,128]{1,0:T(8,128)S(1)}) custom-call(s32[1,7]{1,0:T(1,128)S(1)} %add_bitcast_fusion.info, f32[3,22,40,128]{3,2,1,0:T(8,128)S(1)} %get-tuple-element.23.planes, ...), custom_call_target="tpu_custom_call" | custom-call | flops 14000000000 | bytes 14000000 | tf_op jit(solution)/shard_map/block/pallas_call | solution.py:299
  41.6 0.4 collective-permute-start.8
  42.0 0.1 select_bitcast_fusion.3
  42.1 0.4 collective-permute-start.12
  42.5 0.4 collective-permute-start.13
  42.9 0.4 collective-permute-done.8
  43.2 0.1 fusion.24
  43.4 0.4 collective-permute-done.13
  43.8 2.2 %collective-permute-done.12 = bf16[3,32,192]{2,0,1:T(4,128)(2,1)S(1)} collective-permute-done((bf16[3,32,192]{2,0,1:T(4,128)(2,1)S(1)}, bf16[3,32,192]{2,0,1:T(4,128)(2,1)S(1)}, u32[]{:S(2)}, u32[]{:S(2)}) %collective-permute-start.12) | collective-permute-done | bytes 36896 | tf_op jit(solution)/shard_map/ppermute | solution.py:350
  46.0 0.1 select_bitcast_fusion.1
  46.1 0.4 pad_maximum_fusion.2
  46.5 2.9 %collective-permute-start.14 = (bf16[3,40,192]{2,1,0:T(8,128)(2,1)S(1)}, bf16[3,40,192]{2,1,0:T(8,128)(2,1)S(1)}, u32[]{:S(2)}, u32[]{:S(2)}) collective-permute-start(bf16[3,40,192]{2,1,0:T(8,128)(2,1)S(1)} %get-tuple-element.49), channel_id=1, source_target_pairs={{32,64},{48,80},{96,128},{112,144},{160,192},{176,208},{224,0},{24... | collective-permute-start | bytes 138248 | tf_op jit(solution)/shard_map/ppermute | solution.py:367
  49.4 0.0 collective-permute-start.15
  49.4 0.9 %collective-permute-start.9 = (bf16[384,128]{1,0:T(8,128)(2,1)S(1)}, bf16[384,128]{1,0:T(8,128)(2,1)S(1)}, u32[]{:S(2)}, u32[]{:S(2)}) collective-permute-start(bf16[384,128]{1,0:T(8,128)(2,1)S(1)} %get-tuple-element.68), channel_id=1, source_target_pairs={{0,1},{1,0},{2,3},{3,2},{4,5},{5,4},{6,7},{7,6},{8,9},{9,8},{10,11... | collective-permute-start | bytes 294920 | tf_op jit(solution)/shard_map/ppermute | solution.py:35
  50.3 2.5 %collective-permute-start.10 = (bf16[384,128]{1,0:T(8,128)(2,1)S(1)}, bf16[384,128]{1,0:T(8,128)(2,1)S(1)}, u32[]{:S(2)}, u32[]{:S(2)}) collective-permute-start(bf16[384,128]{1,0:T(8,128)(2,1)S(1)} %get-tuple-element.69), channel_id=1, source_target_pairs={{0,6},{1,7},{2,4},{3,5},{4,2},{5,3},{6,0},{7,1},{8,14},{9,15},{10,... | collective-permute-start | bytes 294920 | tf_op jit(solution)/shard_map/ppermute | solution.py:35
  52.8 0.6 collective-permute-start.11
  53.4 0.3 collective-permute-done.14
  53.7 0.6 collective-permute-done.15
  54.3 0.3 fusion.5.padded
  54.6 5.5 %spread.1 = f32[4,16,16,192]{3,2,1,0:T(8,128)} custom-call(s32[1,7]{1,0:T(1,128)S(1)} %add_bitcast_fusion.info, f32[38,40,192]{2,1,0:T(8,128)S(1)} %fusion.5.padded, bf16[4,16,16,192]{3,2,1,0:T(8,128)(2,1)S(1)} %bitcast.34, f32[7,7,192]{2,1,0:T(8,128)S(1)} %copy-done.1), custom_call_target="tpu_custom_call" | custom-call | tf_op jit(solution)/shard_map/spread/pallas_call | solution.py:299
  60.1 2.2 %collective-permute-done.11 = bf16[384,128]{1,0:T(8,128)(2,1)S(1)} collective-permute-done((bf16[384,128]{1,0:T(8,128)(2,1)S(1)}, bf16[384,128]{1,0:T(8,128)(2,1)S(1)}, u32[]{:S(2)}, u32[]{:S(2)}) %collective-permute-start.11) | collective-permute-done | bytes 98336 | tf_op jit(solution)/shard_map/ppermute | solution.py:35
  62.4 0.1 collective-permute-start.16
  62.5 4.0 %collective-permute-done.16 = bf16[240,128]{1,0:T(8,128)(2,1)S(1)} collective-permute-done((bf16[240,128]{1,0:T(8,128)(2,1)S(1)}, bf16[240,128]{1,0:T(8,128)(2,1)S(1)}, u32[]{:S(2)}, u32[]{:S(2)}) %collective-permute-start.16) | collective-permute-done | bytes 61472 | tf_op jit(solution)/shard_map/ppermute | solution.py:35
  66.5 2.6 %collective-permute-start.19 = (bf16[240,128]{1,0:T(8,128)(2,1)S(1)}, bf16[240,128]{1,0:T(8,128)(2,1)S(1)}, u32[]{:S(2)}, u32[]{:S(2)}) collective-permute-start(bf16[240,128]{1,0:T(8,128)(2,1)S(1)} %pad_maximum_fusion.15), channel_id=1, source_target_pairs={{0,48},{16,32},{32,16},{48,0},{1,49},{17,33},{33,17},{49,1},{2,50}... | collective-permute-start | bytes 184328 | tf_op jit(solution)/shard_map/ppermute | solution.py:35
  69.1 1.3 %collective-permute-start.17 = (bf16[240,128]{1,0:T(8,128)(2,1)S(1)}, bf16[240,128]{1,0:T(8,128)(2,1)S(1)}, u32[]{:S(2)}, u32[]{:S(2)}) collective-permute-start(bf16[240,128]{1,0:T(8,128)(2,1)S(1)} %pad_maximum_fusion.15), channel_id=1, source_target_pairs={{0,32},{16,48},{32,0},{48,16},{1,33},{17,49},{33,1},{49,17},{2,34}... | collective-permute-start | bytes 184328 | tf_op jit(solution)/shard_map/ppermute | solution.py:35
  70.4 0.4 collective-permute-done.19
  70.9 1.3 %collective-permute-done.18 = bf16[240,128]{1,0:T(8,128)(2,1)S(1)} collective-permute-done((bf16[240,128]{1,0:T(8,128)(2,1)S(1)}, bf16[240,128]{1,0:T(8,128)(2,1)S(1)}, u32[]{:S(2)}, u32[]{:S(2)}) %collective-permute-start.18) | collective-permute-done | bytes 61472 | tf_op jit(solution)/shard_map/ppermute | solution.py:35
  72.2 1.6 %collective-permute-done.17 = bf16[240,128]{1,0:T(8,128)(2,1)S(1)} collective-permute-done((bf16[240,128]{1,0:T(8,128)(2,1)S(1)}, bf16[240,128]{1,0:T(8,128)(2,1)S(1)}, u32[]{:S(2)}, u32[]{:S(2)}) %collective-permute-start.17) | collective-permute-done | bytes 61472 | tf_op jit(solution)/shard_map/ppermute | solution.py:35
  73.8 1.4 %collective-permute-start.22 = (bf16[240,128]{1,0:T(8,128)(2,1)S(1)}, bf16[240,128]{1,0:T(8,128)(2,1)S(1)}, u32[]{:S(2)}, u32[]{:S(2)}) collective-permute-start(bf16[240,128]{1,0:T(8,128)(2,1)S(1)} %pad_maximum_fusion.16), channel_id=1, source_target_pairs={{0,192},{64,128},{128,64},{192,0},{1,193},{65,129},{129,65},{193,1... | collective-permute-start | bytes 184328 | tf_op jit(solution)/shard_map/ppermute | solution.py:35
  75.2 2.5 %collective-permute-start.20 = (bf16[240,128]{1,0:T(8,128)(2,1)S(1)}, bf16[240,128]{1,0:T(8,128)(2,1)S(1)}, u32[]{:S(2)}, u32[]{:S(2)}) collective-permute-start(bf16[240,128]{1,0:T(8,128)(2,1)S(1)} %pad_maximum_fusion.16), channel_id=1, source_target_pairs={{0,128},{64,192},{128,0},{192,64},{1,129},{65,193},{129,1},{193,65... | collective-permute-start | bytes 184328 | tf_op jit(solution)/shard_map/ppermute | solution.py:35
  77.8 0.4 collective-permute-done.22
  78.2 0.1 collective-permute-done.21
  78.3 1.7 %collective-permute-done.20 = bf16[240,128]{1,0:T(8,128)(2,1)S(1)} collective-permute-done((bf16[240,128]{1,0:T(8,128)(2,1)S(1)}, bf16[240,128]{1,0:T(8,128)(2,1)S(1)}, u32[]{:S(2)}, u32[]{:S(2)}) %collective-permute-start.20) | collective-permute-done | bytes 61472 | tf_op jit(solution)/shard_map/ppermute | solution.py:35
  80.1 6.1 %collective-permute-start.23 = (f32[192,128]{1,0:T(8,128)S(1)}, f32[192,128]{1,0:T(8,128)S(1)}, u32[]{:S(2)}, u32[]{:S(2)}) collective-permute-start(f32[192,128]{1,0:T(8,128)S(1)} %pad_maximum_fusion.12.held), channel_id=1, source_target_pairs={{0,8},{8,0},{1,9},{9,1},{2,10},{10,2},{3,11},{11,3},{4,12},{12,4},... | collective-permute-start | bytes 294920 | tf_op jit(solution)/shard_map/ppermute | solution.py:35
  86.2 0.9 %collective-permute-done.23.other = f32[192,128]{1,0:T(8,128)S(1)} collective-permute-done((f32[192,128]{1,0:T(8,128)S(1)}, f32[192,128]{1,0:T(8,128)S(1)}, u32[]{:S(2)}, u32[]{:S(2)}) %collective-permute-start.23) | collective-permute-done | bytes 98336 | tf_op jit(solution)/shard_map/ppermute | solution.py:35
  87.1 1.3 %finish.1 = (f32[24,768]{1,0:T(8,128)}, f32[96,192]{1,0:T(8,128)}, f32[7,7,192]{2,1,0:T(8,128)}) custom-call(s32[1,7]{1,0:T(1,128)S(1)} %add_bitcast_fusion.info, f32[192,128]{1,0:T(8,128)S(1)} %pad_maximum_fusion.12.held, f32[192,128]{1,0:T(8,128)S(1)} %collective-permute-done.23.other), custom_call_target="tpu_custom_call" | custom-call | flops 1000000000 | bytes 1000000 | tf_op jit(solution)/shard_map/finish/pallas_call | solution.py:299
  (42 shorter events, 0.4 us)
Async XLA Ops:
  2.0 1.0 %copy-start.4 = (bf16[1,4,16,16,192]{4,3,2,1,0:T(8,128)(2,1)S(1)}, bf16[1,4,16,16,192]{4,3,2,1,0:T(8,128)(2,1)}, u32[]{:S(2)}) copy-start(bf16[1,4,16,16,192]{4,3,2,1,0:T(8,128)(2,1)} %param.9) | copy-start | bytes 1179652
  3.1 5.0 %copy-start.2 = (bf16[96,192]{1,0:T(8,128)(2,1)S(1)}, bf16[96,192]{1,0:T(8,128)(2,1)}, u32[]{:S(2)}) copy-start(bf16[96,192]{1,0:T(8,128)(2,1)} %project.1) | copy-start | bytes 110596
  3.1 5.0 %copy-start.3 = (bf16[24,768]{1,0:T(8,128)(2,1)S(1)}, bf16[24,768]{1,0:T(8,128)(2,1)}, u32[]{:S(2)}) copy-start(bf16[24,768]{1,0:T(8,128)(2,1)} %expand) | copy-start | bytes 110596
  3.9 4.2 %collective-permute-start.1 = (bf16[3,32,192]{2,0,1:T(4,128)(2,1)S(1)}, bf16[3,32,192]{2,0,1:T(4,128)(2,1)S(1)}, u32[]{:S(2)}, u32[]{:S(2)}) collective-permute-start(bf16[3,32,192]{2,0,1:T(4,128)(2,1)S(1)} %get-tuple-element.56), channel_id=1, source_target_pairs={{0,8},{8,0},{1,9},{9,1},{2,10},{10,2},{3,11},{11,3},{4,12},{12,4},... | collective-permute-start | bytes 110600 | tf_op jit(solution)/shard_map/ppermute | solution.py:35
  7.2 5.7 %collective-permute-start = (bf16[3,32,192]{2,0,1:T(4,128)(2,1)S(1)}, bf16[3,32,192]{2,0,1:T(4,128)(2,1)S(1)}, u32[]{:S(2)}, u32[]{:S(2)}) collective-permute-start(bf16[3,32,192]{2,0,1:T(4,128)(2,1)S(1)} %get-tuple-element.55), channel_id=1, source_target_pairs={{0,24},{8,16},{16,8},{24,0},{32,56},{40,48},{48,40},{56,32},{1,25}... | collective-permute-start | bytes 110600 | tf_op jit(solution)/shard_map/ppermute | solution.py:350
  8.7 9.7 %collective-permute-start.4 = (bf16[144,128]{1,0:T(8,128)(2,1)S(1)}, bf16[144,128]{1,0:T(8,128)(2,1)S(1)}, u32[]{:S(2)}, u32[]{:S(2)}) collective-permute-start(bf16[144,128]{1,0:T(8,128)(2,1)S(1)} %pack.1), channel_id=1, source_target_pairs={{0,7},{1,6},{2,5},{3,4},{4,3},{5,2},{6,1},{7,0},{8,15},{9,14},{10,... | collective-permute-start | bytes 110600 | tf_op jit(solution)/shard_map/ppermute | solution.py:35
  13.4 11.7 %copy-start.1 = (f32[7,7,192]{2,1,0:T(8,128)S(1)}, f32[7,7,192]{2,1,0:T(8,128)}, u32[]{:S(2)}) copy-start(f32[7,7,192]{2,1,0:T(8,128)} %kernel.3) | copy-start | bytes 112900
  13.4 7.2 %collective-permute-start.2 = (bf16[3,40,192]{2,1,0:T(8,128)(2,1)S(1)}, bf16[3,40,192]{2,1,0:T(8,128)(2,1)S(1)}, u32[]{:S(2)}, u32[]{:S(2)}) collective-permute-start(bf16[3,40,192]{2,1,0:T(8,128)(2,1)S(1)} %get-tuple-element.51), channel_id=1, source_target_pairs={{32,64},{48,80},{96,128},{112,144},{160,192},{176,208},{224,0},{24... | collective-permute-start | bytes 138248 | tf_op jit(solution)/shard_map/ppermute | solution.py:367
  18.4 4.6 %collective-permute-start.3 = (bf16[3,40,192]{2,1,0:T(8,128)(2,1)S(1)}, bf16[3,40,192]{2,1,0:T(8,128)(2,1)S(1)}, u32[]{:S(2)}, u32[]{:S(2)}) collective-permute-start(bf16[3,40,192]{2,1,0:T(8,128)(2,1)S(1)} %get-tuple-element.52), channel_id=1, source_target_pairs={{0,32},{16,48},{32,0},{48,16},{1,33},{17,49},{33,1},{49,17},{2,34}... | collective-permute-start | bytes 138248 | tf_op jit(solution)/shard_map/ppermute | solution.py:35
  18.4 4.6 %collective-permute-start.5 = (bf16[2,144,128]{2,1,0:T(8,128)(2,1)S(1)}, bf16[2,144,128]{2,1,0:T(8,128)(2,1)S(1)}, u32[]{:S(2)}, u32[]{:S(2)}) collective-permute-start(bf16[2,144,128]{2,1,0:T(8,128)(2,1)S(1)} %pad_maximum_fusion.13), channel_id=1, source_target_pairs={{0,2},{1,3},{2,0},{3,1},{4,6},{5,7},{6,4},{7,5},{8,10},{9,11},{10,... | collective-permute-start | bytes 221192 | tf_op jit(solution)/shard_map/ppermute | solution.py:35
  23.1 5.8 %collective-permute-start.6 = (bf16[4,144,128]{2,1,0:T(8,128)(2,1)S(1)}, bf16[4,144,128]{2,1,0:T(8,128)(2,1)S(1)}, u32[]{:S(2)}, u32[]{:S(2)}) collective-permute-start(bf16[4,144,128]{2,1,0:T(8,128)(2,1)S(1)} %pad_maximum_fusion.11), channel_id=1, source_target_pairs={{0,1},{1,0},{2,3},{3,2},{4,5},{5,4},{6,7},{7,6},{8,9},{9,8},{10,11... | collective-permute-start | bytes 442376 | tf_op jit(solution)/shard_map/ppermute | solution.py:35
  25.1 6.5 %copy-start.7 = (f32[768]{0:T(1024)S(1)}, f32[768]{0:T(1024)}, u32[]{:S(2)}) copy-start(f32[768]{0:T(1024)} %param.16) | copy-start | bytes 9220
  25.1 7.7 %copy-start = (bf16[1,4,16,16,192]{4,3,2,1,0:T(8,128)(2,1)S(1)}, bf16[1,4,16,16,192]{4,3,2,1,0:T(8,128)(2,1)}, u32[]{:S(2)}) copy-start(bf16[1,4,16,16,192]{4,3,2,1,0:T(8,128)(2,1)} %param.10) | copy-start | bytes 1179652
  25.1 7.7 %copy-start.5 = (bf16[1,4,16,16,192]{4,3,2,1,0:T(8,128)(2,1)S(1)}, bf16[1,4,16,16,192]{4,3,2,1,0:T(8,128)(2,1)}, u32[]{:S(2)}) copy-start(bf16[1,4,16,16,192]{4,3,2,1,0:T(8,128)(2,1)} %param.9) | copy-start | bytes 1179652
  25.1 7.7 %copy-start.6 = (f32[192]{0:T(256)S(1)}, f32[192]{0:T(256)}, u32[]{:S(2)}) copy-start(f32[192]{0:T(256)} %param.14) | copy-start | bytes 2308
  28.9 3.9 %collective-permute-start.7 = (bf16[8,144,128]{2,1,0:T(8,128)(2,1)S(1)}, bf16[8,144,128]{2,1,0:T(8,128)(2,1)S(1)}, u32[]{:S(2)}, u32[]{:S(2)}) collective-permute-start(bf16[8,144,128]{2,1,0:T(8,128)(2,1)S(1)} %pad_maximum_fusion.4.held), channel_id=1, source_target_pairs={{0,8},{8,0},{1,9},{9,1},{2,10},{10,2},{3,11},{11,3},{4,12},{12,4},... | collective-permute-start | bytes 884744 | tf_op jit(solution)/shard_map/ppermute | solution.py:35
  41.6 1.6 %collective-permute-start.8 = (bf16[1248,128]{1,0:T(8,128)(2,1)S(1)}, bf16[1248,128]{1,0:T(8,128)(2,1)S(1)}, u32[]{:S(2)}, u32[]{:S(2)}) collective-permute-start(bf16[1248,128]{1,0:T(8,128)(2,1)S(1)} %get-tuple-element.30), channel_id=1, source_target_pairs={{0,8},{8,0},{1,9},{9,1},{2,10},{10,2},{3,11},{11,3},{4,12},{12,4},... | collective-permute-start | bytes 958472 | tf_op jit(solution)/shard_map/ppermute | solution.py:35
  42.1 3.9 %collective-permute-start.12 = (bf16[3,32,192]{2,0,1:T(4,128)(2,1)S(1)}, bf16[3,32,192]{2,0,1:T(4,128)(2,1)S(1)}, u32[]{:S(2)}, u32[]{:S(2)}) collective-permute-start(bf16[3,32,192]{2,0,1:T(4,128)(2,1)S(1)} %get-tuple-element.53), channel_id=1, source_target_pairs={{0,24},{8,16},{16,8},{24,0},{32,56},{40,48},{48,40},{56,32},{1,25}... | collective-permute-start | bytes 110600 | tf_op jit(solution)/shard_map/ppermute | solution.py:350
  42.5 1.3 %collective-permute-start.13 = (bf16[3,32,192]{2,0,1:T(4,128)(2,1)S(1)}, bf16[3,32,192]{2,0,1:T(4,128)(2,1)S(1)}, u32[]{:S(2)}, u32[]{:S(2)}) collective-permute-start(bf16[3,32,192]{2,0,1:T(4,128)(2,1)S(1)} %get-tuple-element.54), channel_id=1, source_target_pairs={{0,8},{8,0},{1,9},{9,1},{2,10},{10,2},{3,11},{11,3},{4,12},{12,4},... | collective-permute-start | bytes 110600 | tf_op jit(solution)/shard_map/ppermute | solution.py:35
  46.5 7.2 %collective-permute-start.14 = (bf16[3,40,192]{2,1,0:T(8,128)(2,1)S(1)}, bf16[3,40,192]{2,1,0:T(8,128)(2,1)S(1)}, u32[]{:S(2)}, u32[]{:S(2)}) collective-permute-start(bf16[3,40,192]{2,1,0:T(8,128)(2,1)S(1)} %get-tuple-element.49), channel_id=1, source_target_pairs={{32,64},{48,80},{96,128},{112,144},{160,192},{176,208},{224,0},{24... | collective-permute-start | bytes 138248 | tf_op jit(solution)/shard_map/ppermute | solution.py:367
  49.4 4.9 %collective-permute-start.15 = (bf16[3,40,192]{2,1,0:T(8,128)(2,1)S(1)}, bf16[3,40,192]{2,1,0:T(8,128)(2,1)S(1)}, u32[]{:S(2)}, u32[]{:S(2)}) collective-permute-start(bf16[3,40,192]{2,1,0:T(8,128)(2,1)S(1)} %get-tuple-element.50), channel_id=1, source_target_pairs={{0,32},{16,48},{32,0},{48,16},{1,33},{17,49},{33,1},{49,17},{2,34}... | collective-permute-start | bytes 138248 | tf_op jit(solution)/shard_map/ppermute | solution.py:35
  49.4 10.7 %collective-permute-start.9 = (bf16[384,128]{1,0:T(8,128)(2,1)S(1)}, bf16[384,128]{1,0:T(8,128)(2,1)S(1)}, u32[]{:S(2)}, u32[]{:S(2)}) collective-permute-start(bf16[384,128]{1,0:T(8,128)(2,1)S(1)} %get-tuple-element.68), channel_id=1, source_target_pairs={{0,1},{1,0},{2,3},{3,2},{4,5},{5,4},{6,7},{7,6},{8,9},{9,8},{10,11... | collective-permute-start | bytes 294920 | tf_op jit(solution)/shard_map/ppermute | solution.py:35
  50.3 9.8 %collective-permute-start.10 = (bf16[384,128]{1,0:T(8,128)(2,1)S(1)}, bf16[384,128]{1,0:T(8,128)(2,1)S(1)}, u32[]{:S(2)}, u32[]{:S(2)}) collective-permute-start(bf16[384,128]{1,0:T(8,128)(2,1)S(1)} %get-tuple-element.69), channel_id=1, source_target_pairs={{0,6},{1,7},{2,4},{3,5},{4,2},{5,3},{6,0},{7,1},{8,14},{9,15},{10,... | collective-permute-start | bytes 294920 | tf_op jit(solution)/shard_map/ppermute | solution.py:35
  52.8 9.5 %collective-permute-start.11 = (bf16[384,128]{1,0:T(8,128)(2,1)S(1)}, bf16[384,128]{1,0:T(8,128)(2,1)S(1)}, u32[]{:S(2)}, u32[]{:S(2)}) collective-permute-start(bf16[384,128]{1,0:T(8,128)(2,1)S(1)} %get-tuple-element.70), channel_id=1, source_target_pairs={{0,7},{1,6},{2,5},{3,4},{4,3},{5,2},{6,1},{7,0},{8,15},{9,14},{10,... | collective-permute-start | bytes 294920 | tf_op jit(solution)/shard_map/ppermute | solution.py:35
  62.4 4.1 %collective-permute-start.16 = (bf16[240,128]{1,0:T(8,128)(2,1)S(1)}, bf16[240,128]{1,0:T(8,128)(2,1)S(1)}, u32[]{:S(2)}, u32[]{:S(2)}) collective-permute-start(bf16[240,128]{1,0:T(8,128)(2,1)S(1)} %pad_maximum_fusion.14), channel_id=1, source_target_pairs={{0,2},{1,3},{2,0},{3,1},{4,6},{5,7},{6,4},{7,5},{8,10},{9,11},{10,... | collective-permute-start | bytes 184328 | tf_op jit(solution)/shard_map/ppermute | solution.py:35
  66.5 4.4 %collective-permute-start.19 = (bf16[240,128]{1,0:T(8,128)(2,1)S(1)}, bf16[240,128]{1,0:T(8,128)(2,1)S(1)}, u32[]{:S(2)}, u32[]{:S(2)}) collective-permute-start(bf16[240,128]{1,0:T(8,128)(2,1)S(1)} %pad_maximum_fusion.15), channel_id=1, source_target_pairs={{0,48},{16,32},{32,16},{48,0},{1,49},{17,33},{33,17},{49,1},{2,50}... | collective-permute-start | bytes 184328 | tf_op jit(solution)/shard_map/ppermute | solution.py:35
  69.1 3.1 %collective-permute-start.18 = (bf16[240,128]{1,0:T(8,128)(2,1)S(1)}, bf16[240,128]{1,0:T(8,128)(2,1)S(1)}, u32[]{:S(2)}, u32[]{:S(2)}) collective-permute-start(bf16[240,128]{1,0:T(8,128)(2,1)S(1)} %pad_maximum_fusion.15), channel_id=1, source_target_pairs={{0,16},{16,0},{32,48},{48,32},{1,17},{17,1},{33,49},{49,33},{2,18}... | collective-permute-start | bytes 184328 | tf_op jit(solution)/shard_map/ppermute | solution.py:35
  69.1 4.6 %collective-permute-start.17 = (bf16[240,128]{1,0:T(8,128)(2,1)S(1)}, bf16[240,128]{1,0:T(8,128)(2,1)S(1)}, u32[]{:S(2)}, u32[]{:S(2)}) collective-permute-start(bf16[240,128]{1,0:T(8,128)(2,1)S(1)} %pad_maximum_fusion.15), channel_id=1, source_target_pairs={{0,32},{16,48},{32,0},{48,16},{1,33},{17,49},{33,1},{49,17},{2,34}... | collective-permute-start | bytes 184328 | tf_op jit(solution)/shard_map/ppermute | solution.py:35
  73.8 4.4 %collective-permute-start.22 = (bf16[240,128]{1,0:T(8,128)(2,1)S(1)}, bf16[240,128]{1,0:T(8,128)(2,1)S(1)}, u32[]{:S(2)}, u32[]{:S(2)}) collective-permute-start(bf16[240,128]{1,0:T(8,128)(2,1)S(1)} %pad_maximum_fusion.16), channel_id=1, source_target_pairs={{0,192},{64,128},{128,64},{192,0},{1,193},{65,129},{129,65},{193,1... | collective-permute-start | bytes 184328 | tf_op jit(solution)/shard_map/ppermute | solution.py:35
  75.2 3.1 %collective-permute-start.21 = (bf16[240,128]{1,0:T(8,128)(2,1)S(1)}, bf16[240,128]{1,0:T(8,128)(2,1)S(1)}, u32[]{:S(2)}, u32[]{:S(2)}) collective-permute-start(bf16[240,128]{1,0:T(8,128)(2,1)S(1)} %pad_maximum_fusion.16), channel_id=1, source_target_pairs={{0,64},{64,0},{128,192},{192,128},{1,65},{65,1},{129,193},{193,129... | collective-permute-start | bytes 184328 | tf_op jit(solution)/shard_map/ppermute | solution.py:35
  75.2 4.8 %collective-permute-start.20 = (bf16[240,128]{1,0:T(8,128)(2,1)S(1)}, bf16[240,128]{1,0:T(8,128)(2,1)S(1)}, u32[]{:S(2)}, u32[]{:S(2)}) collective-permute-start(bf16[240,128]{1,0:T(8,128)(2,1)S(1)} %pad_maximum_fusion.16), channel_id=1, source_target_pairs={{0,128},{64,192},{128,0},{192,64},{1,129},{65,193},{129,1},{193,65... | collective-permute-start | bytes 184328 | tf_op jit(solution)/shard_map/ppermute | solution.py:35
  80.1 7.0 %collective-permute-start.23 = (f32[192,128]{1,0:T(8,128)S(1)}, f32[192,128]{1,0:T(8,128)S(1)}, u32[]{:S(2)}, u32[]{:S(2)}) collective-permute-start(f32[192,128]{1,0:T(8,128)S(1)} %pad_maximum_fusion.12.held), channel_id=1, source_target_pairs={{0,8},{8,0},{1,9},{9,1},{2,10},{10,2},{3,11},{11,3},{4,12},{12,4},... | collective-permute-start | bytes 294920 | tf_op jit(solution)/shard_map/ppermute | solution.py:35

commit v5 on v4

--- a/solution.py
+++ b/solution.py
@@ -12,7 +12,6 @@
 bf16 = jnp.bfloat16
 f32 = jnp.float32
 REP_ORDER = (0, 7, 2, 5, 1, 6, 3, 4)
-SUM_ORDER = (0, 2, 1, 3, 6, 4, 7, 5)
 TILE = ("y", "x", "core")
 SIZES = {"y": 4, "x": 4, "core": 2, "rep": 8}
 C, FF, S, CAP, KS = 192, 768, 16, 4, 7
@@ -252,7 +251,7 @@
     send[ROWS : ROWS + GROWS] = high
     send[ROWS + GROWS :] = low
     grad_rt[...] = grad_r[...].T
-    for k, s in enumerate(SUM_ORDER):
+    for k, s in enumerate(REP_ORDER):
         z = my_z ^ s
         e = pack_expand(grad_e[pl.ds(pl.multiple_of(z * EROWS, 8), EROWS), :])
         r = pack_reduce(grad_rt[pl.ds(pl.multiple_of(z * RROWS, RROWS), RROWS), :])
@@ -445,19 +444,27 @@
         held,
         other,
     )
-    pair = 2 * SHARD
     got = swap(send, "core", 1)
     inner, outer = side_rims(field)
     held = keep + got[:ROWS].astype(f32)
     taps = taps + join(got[ROWS:])
-    high, low = split_high_low(taps)
+
+    def halve(held, taps, bits, *after):
+        half = held.shape[0] // 2
+        high, low = split_high_low(taps)
+        part = jnp.concatenate([held[half:].astype(bf16), high, low])
+        part = tie(part, *after)[0]
+        got = swap(part, "rep", bits)
+        return (
+            held[:half] + got[:half].astype(f32),
+            (high.astype(f32) + low.astype(f32)) + join(got[half:]),
+        )
+
     got, inner = tie(got, inner)
     widened = widen(field, inner, outer)
     near, far = end_rims(widened)
-    sends = [
-        jnp.concatenate([held[k * pair : (k + 1) * pair].astype(bf16), high, low]) for k in (1, 2, 3)
-    ]
-    got = [swap(part, "rep", s) for part, s in zip(sends, (1, 6, 7))]
+    held, taps = halve(held, taps, 1)
+    held, near = tie(held, near)
     (grad_tiles,) = call(
         spread_kernel,
         (info, pad_ends(widened, near, far), cotan, kernel),
@@ -466,13 +473,8 @@
         name="spread",
         us=0,
     )
-    held = rows_sum(held[:pair], *[g[:pair].astype(f32) for g in got])
-    taps = rows_sum(high.astype(f32) + low.astype(f32), *[join(g[pair:]) for g in got])
-    high, low = split_high_low(taps)
-    part, grad_tiles = tie(jnp.concatenate([held[SHARD:].astype(bf16), high, low]), grad_tiles)
-    got = swap(part, "rep", 2)
-    held = held[:SHARD] + got[:SHARD].astype(f32)
-    taps = (high.astype(f32) + low.astype(f32)) + join(got[SHARD:])
+    held, taps = halve(held, taps, 2)
+    held, taps = halve(held, taps, 7, grad_tiles)
     for axis in ("x", "y"):
         part = jnp.concatenate([held.astype(bf16), *split_high_low(taps)])
         parts = [part] + [swap(part, axis, i) for i in (2, 1, 3)]

time: 88.6 us -> 86.8 us (0.980)
  waiting for transfers between devices: 21 us -> 19.8 us
  starting transfers between devices: 41.2 us -> 40.2 us
    ppermute x20 -> x19, starting transfers between devices: 32.9 us -> 31.9 us  [swap(): return lax.ppermute(value, axis, [(i, i ^ bit) for i in range(SIZES[axis])])]
    ppermute x20 -> x19, waiting for transfers between devices: 18.5 us -> 18.2 us  [swap(): return lax.ppermute(value, axis, [(i, i ^ bit) for i in range(SIZES[axis])])]
  transfers between devices with their start and end apart: 24 -> 23, of which waited for: 17 -> 13; matrix products, arithmetic and copies ran while one was open for 2% -> 2% of each run, Pallas kernels for 11% -> 11%
where the time goes in v5:
time: 86.8 us; the launch traced here: 86.4 us
  starting transfers between devices  40.2 us (46%)
  Pallas kernels  20.7 us (24%)
  waiting for transfers between devices  19.8 us (23%)
  other arithmetic  2.93 us (3%)
  between operations  1.59 us (2%)
  local copies, waits for them, and re-layouts  1.14 us (1%)
    ppermute x19, starting transfers between devices, swap(): return lax.ppermute(value, axis, [(i, i ^ bit) for i in range(SIZES[axis])])  31.9 us
    pallas_call x6, Pallas kernels, call(): pl.pallas_call(kernel, out_shape=[jax.ShapeDtypeStruct(shape, dtype) for...  20.7 us
    ppermute x19, waiting for transfers between devices, swap(): return lax.ppermute(value, axis, [(i, i ^ bit) for i in range(SIZES[axis])])  18.2 us
    ppermute x2, starting transfers between devices, end_rims(): lax.ppermute(jnp.where(upper == 0, north_edge, south_edge), ('y', 'x'), p...  7.88 us
  transfers between devices with their start and end apart: 23, of which 13 were waited for; matrix products, arithmetic and copies ran while one was open for 2% of the time, Pallas kernels for 11%

profile of v5, /device:TPU:1, one launch (start us, length us, event | category | flops | bytes accessed | tf_op | source)
XLA Modules:
  0.0 86.4 jit_solution(13275931754401311708)
XLA Ops:
  1.3 0.7 add_bitcast_fusion.info
  2.0 1.0 %copy-done.4 = bf16[1,4,16,16,192]{4,3,2,1,0:T(8,128)(2,1)S(1)} copy-done((bf16[1,4,16,16,192]{4,3,2,1,0:T(8,128)(2,1)S(1)}, bf16[1,4,16,16,192]{4,3,2,1,0:T(8,128)(2,1)}, u32[]{:S(2)}) %copy-start.4) | copy-done | bytes 393240
  3.1 0.7 place.1
  3.8 0.1 select_bitcast_fusion.7
  3.9 3.3 %collective-permute-start.1 = (bf16[3,32,192]{2,0,1:T(4,128)(2,1)S(1)}, bf16[3,32,192]{2,0,1:T(4,128)(2,1)S(1)}, u32[]{:S(2)}, u32[]{:S(2)}) collective-permute-start(bf16[3,32,192]{2,0,1:T(4,128)(2,1)S(1)} %get-tuple-element.58), channel_id=1, source_target_pairs={{0,8},{8,0},{1,9},{9,1},{2,10},{10,2},{3,11},{11,3},{4,12},{12,4},... | collective-permute-start | bytes 110600 | tf_op jit(solution)/shard_map/ppermute | solution.py:34
  7.2 0.0 collective-permute-start
  7.2 0.9 %collective-permute-done.1 = bf16[3,32,192]{2,0,1:T(4,128)(2,1)S(1)} collective-permute-done((bf16[3,32,192]{2,0,1:T(4,128)(2,1)S(1)}, bf16[3,32,192]{2,0,1:T(4,128)(2,1)S(1)}, u32[]{:S(2)}, u32[]{:S(2)}) %collective-permute-start.1) | collective-permute-done | bytes 36896 | tf_op jit(solution)/shard_map/ppermute | solution.py:34
  8.1 0.6 pack.1
  8.7 4.2 %collective-permute-start.4 = (bf16[144,128]{1,0:T(8,128)(2,1)S(1)}, bf16[144,128]{1,0:T(8,128)(2,1)S(1)}, u32[]{:S(2)}, u32[]{:S(2)}) collective-permute-start(bf16[144,128]{1,0:T(8,128)(2,1)S(1)} %pack.1), channel_id=1, source_target_pairs={{0,7},{1,6},{2,5},{3,4},{4,3},{5,2},{6,1},{7,0},{8,15},{9,14},{10,... | collective-permute-start | bytes 110600 | tf_op jit(solution)/shard_map/ppermute | solution.py:34
  12.9 0.0 collective-permute-done
  12.9 0.1 select_bitcast_fusion.5
  13.0 0.4 pad_maximum_fusion.3
  13.4 0.0 copy-start.1
  13.4 5.0 %collective-permute-start.2 = (bf16[3,40,192]{2,1,0:T(8,128)(2,1)S(1)}, bf16[3,40,192]{2,1,0:T(8,128)(2,1)S(1)}, u32[]{:S(2)}, u32[]{:S(2)}) collective-permute-start(bf16[3,40,192]{2,1,0:T(8,128)(2,1)S(1)} %get-tuple-element.53), channel_id=1, source_target_pairs={{32,64},{48,80},{96,128},{112,144},{160,192},{176,208},{224,0},{24... | collective-permute-start | bytes 138248 | tf_op jit(solution)/shard_map/ppermute | solution.py:366
  18.4 0.0 collective-permute-start.3
  18.4 0.0 collective-permute-done.4
  18.4 2.2 %collective-permute-start.5 = (bf16[2,144,128]{2,1,0:T(8,128)(2,1)S(1)}, bf16[2,144,128]{2,1,0:T(8,128)(2,1)S(1)}, u32[]{:S(2)}, u32[]{:S(2)}) collective-permute-start(bf16[2,144,128]{2,1,0:T(8,128)(2,1)S(1)} %pad_maximum_fusion.9), channel_id=1, source_target_pairs={{0,2},{1,3},{2,0},{3,1},{4,6},{5,7},{6,4},{7,5},{8,10},{9,11},{10,... | collective-permute-start | bytes 221192 | tf_op jit(solution)/shard_map/ppermute | solution.py:34
  20.6 0.0 collective-permute-done.2
  20.6 2.4 %collective-permute-done.3 = bf16[3,40,192]{2,1,0:T(8,128)(2,1)S(1)} collective-permute-done((bf16[3,40,192]{2,1,0:T(8,128)(2,1)S(1)}, bf16[3,40,192]{2,1,0:T(8,128)(2,1)S(1)}, u32[]{:S(2)}, u32[]{:S(2)}) %collective-permute-start.3) | collective-permute-done | bytes 46112 | tf_op jit(solution)/shard_map/ppermute | solution.py:34
  23.0 0.0 collective-permute-done.5
  23.1 1.7 %collective-permute-start.6 = (bf16[4,144,128]{2,1,0:T(8,128)(2,1)S(1)}, bf16[4,144,128]{2,1,0:T(8,128)(2,1)S(1)}, u32[]{:S(2)}, u32[]{:S(2)}) collective-permute-start(bf16[4,144,128]{2,1,0:T(8,128)(2,1)S(1)} %pad_maximum_fusion.6), channel_id=1, source_target_pairs={{0,1},{1,0},{2,3},{3,2},{4,5},{5,4},{6,7},{7,6},{8,9},{9,8},{10,11... | collective-permute-start | bytes 442376 | tf_op jit(solution)/shard_map/ppermute | solution.py:34
  24.8 0.3 fusion.2.padded
  25.1 0.0 copy-start.7
  25.1 0.0 copy-start
  25.1 0.0 copy-start.5
  25.2 0.0 copy-start.6
  25.2 3.7 %field.1 = (f32[3,22,40,128]{3,2,1,0:T(8,128)S(1)}, f32[3,16,32,128]{3,2,1,0:T(8,128)S(1)}) custom-call(f32[38,40,192]{2,1,0:T(8,128)S(1)} %fusion.2.padded, f32[7,7,192]{2,1,0:T(8,128)S(1)} %copy-done.1), custom_call_target="tpu_custom_call" | custom-call | tf_op jit(solution)/shard_map/field/pallas_call | solution.py:298
  28.9 0.0 collective-permute-done.6
  28.9 2.7 %collective-permute-start.7 = (bf16[8,144,128]{2,1,0:T(8,128)(2,1)S(1)}, bf16[8,144,128]{2,1,0:T(8,128)(2,1)S(1)}, u32[]{:S(2)}, u32[]{:S(2)}) collective-permute-start(bf16[8,144,128]{2,1,0:T(8,128)(2,1)S(1)} %pad_maximum_fusion.4.held), channel_id=1, source_target_pairs={{0,8},{8,0},{1,9},{9,1},{2,10},{10,2},{3,11},{11,3},{4,12},{12,4},... | collective-permute-start | bytes 884744 | tf_op jit(solution)/shard_map/ppermute | solution.py:34
  31.6 1.2 %collective-permute-done.7.other = bf16[8,144,128]{2,1,0:T(8,128)(2,1)S(1)} collective-permute-done((bf16[8,144,128]{2,1,0:T(8,128)(2,1)S(1)}, bf16[8,144,128]{2,1,0:T(8,128)(2,1)S(1)}, u32[]{:S(2)}, u32[]{:S(2)}) %collective-permute-start.7) | collective-permute-done | bytes 294944 | tf_op jit(solution)/shard_map/ppermute | solution.py:34
  32.8 8.8 %block.1 = (f32[4,16,16,192]{3,2,1,0:T(8,128)}, bf16[32,32,192]{2,1,0:T(8,128)(2,1)S(1)}, f32[1152,128]{1,0:T(8,128)S(1)}, bf16[1248,128]{1,0:T(8,128)(2,1)S(1)}, f32[48,128]{1,0:T(8,128)S(1)}) custom-call(s32[1,7]{1,0:T(1,128)S(1)} %add_bitcast_fusion.info, f32[3,22,40,128]{3,2,1,0:T(8,128)S(1)} %get-tuple-element.24.planes, ...), custom_call_target="tpu_custom_call" | custom-call | flops 14000000000 | bytes 14000000 | tf_op jit(solution)/shard_map/block/pallas_call | solution.py:298
  41.6 0.3 collective-permute-start.9
  42.0 0.1 select_bitcast_fusion.3
  42.1 0.4 collective-permute-start.8
  42.5 0.4 collective-permute-start.10
  42.9 0.4 collective-permute-done.9
  43.3 0.1 convert_add_fusion
  43.4 0.4 collective-permute-done.10
  43.8 0.7 collective-permute-start.12
  44.5 1.6 %collective-permute-done.8 = bf16[3,32,192]{2,0,1:T(4,128)(2,1)S(1)} collective-permute-done((bf16[3,32,192]{2,0,1:T(4,128)(2,1)S(1)}, bf16[3,32,192]{2,0,1:T(4,128)(2,1)S(1)}, u32[]{:S(2)}, u32[]{:S(2)}) %collective-permute-start.8) | collective-permute-done | bytes 36896 | tf_op jit(solution)/shard_map/ppermute | solution.py:349
  46.0 0.1 select_bitcast_fusion.1
  46.1 0.4 pad_maximum_fusion.2
  46.5 2.9 %collective-permute-start.11 = (bf16[3,40,192]{2,1,0:T(8,128)(2,1)S(1)}, bf16[3,40,192]{2,1,0:T(8,128)(2,1)S(1)}, u32[]{:S(2)}, u32[]{:S(2)}) collective-permute-start(bf16[3,40,192]{2,1,0:T(8,128)(2,1)S(1)} %get-tuple-element.51), channel_id=1, source_target_pairs={{32,64},{48,80},{96,128},{112,144},{160,192},{176,208},{224,0},{24... | collective-permute-start | bytes 138248 | tf_op jit(solution)/shard_map/ppermute | solution.py:366
  49.4 0.0 collective-permute-start.13
  49.4 4.8 %collective-permute-done.13 = bf16[3,40,192]{2,1,0:T(8,128)(2,1)S(1)} collective-permute-done((bf16[3,40,192]{2,1,0:T(8,128)(2,1)S(1)}, bf16[3,40,192]{2,1,0:T(8,128)(2,1)S(1)}, u32[]{:S(2)}, u32[]{:S(2)}) %collective-permute-start.13) | collective-permute-done | bytes 46112 | tf_op jit(solution)/shard_map/ppermute | solution.py:34
  54.3 1.3 %collective-permute-start.14 = (bf16[384,128]{1,0:T(8,128)(2,1)S(1)}, bf16[384,128]{1,0:T(8,128)(2,1)S(1)}, u32[]{:S(2)}, u32[]{:S(2)}) collective-permute-start(bf16[384,128]{1,0:T(8,128)(2,1)S(1)} %pad_maximum_fusion.7), channel_id=1, source_target_pairs={{0,2},{1,3},{2,0},{3,1},{4,6},{5,7},{6,4},{7,5},{8,10},{9,11},{10,... | collective-permute-start | bytes 294920 | tf_op jit(solution)/shard_map/ppermute | solution.py:34
  55.6 0.3 fusion.5.padded
  56.0 5.6 %spread.1 = f32[4,16,16,192]{3,2,1,0:T(8,128)} custom-call(s32[1,7]{1,0:T(1,128)S(1)} %add_bitcast_fusion.info, f32[38,40,192]{2,1,0:T(8,128)S(1)} %fusion.5.padded, bf16[4,16,16,192]{3,2,1,0:T(8,128)(2,1)S(1)} %bitcast.34, f32[7,7,192]{2,1,0:T(8,128)S(1)} %copy-done.1), custom_call_target="tpu_custom_call" | custom-call | tf_op jit(solution)/shard_map/spread/pallas_call | solution.py:298
  61.6 1.7 %collective-permute-start.15 = (bf16[240,128]{1,0:T(8,128)(2,1)S(1)}, bf16[240,128]{1,0:T(8,128)(2,1)S(1)}, u32[]{:S(2)}, u32[]{:S(2)}) collective-permute-start(bf16[240,128]{1,0:T(8,128)(2,1)S(1)} %pad_maximum_fusion.10), channel_id=1, source_target_pairs={{0,7},{1,6},{2,5},{3,4},{4,3},{5,2},{6,1},{7,0},{8,15},{9,14},{10,... | collective-permute-start | bytes 184328 | tf_op jit(solution)/shard_map/ppermute | solution.py:34
  63.4 2.6 %collective-permute-done.15 = bf16[240,128]{1,0:T(8,128)(2,1)S(1)} collective-permute-done((bf16[240,128]{1,0:T(8,128)(2,1)S(1)}, bf16[240,128]{1,0:T(8,128)(2,1)S(1)}, u32[]{:S(2)}, u32[]{:S(2)}) %collective-permute-start.15) | collective-permute-done | bytes 61472 | tf_op jit(solution)/shard_map/ppermute | solution.py:34
  66.1 1.1 %collective-permute-start.18 = (bf16[240,128]{1,0:T(8,128)(2,1)S(1)}, bf16[240,128]{1,0:T(8,128)(2,1)S(1)}, u32[]{:S(2)}, u32[]{:S(2)}) collective-permute-start(bf16[240,128]{1,0:T(8,128)(2,1)S(1)} %pad_maximum_fusion.11), channel_id=1, source_target_pairs={{0,48},{16,32},{32,16},{48,0},{1,49},{17,33},{33,17},{49,1},{2,50}... | collective-permute-start | bytes 184328 | tf_op jit(solution)/shard_map/ppermute | solution.py:34
  67.1 0.0 collective-permute-start.17
  67.2 2.8 %collective-permute-start.16 = (bf16[240,128]{1,0:T(8,128)(2,1)S(1)}, bf16[240,128]{1,0:T(8,128)(2,1)S(1)}, u32[]{:S(2)}, u32[]{:S(2)}) collective-permute-start(bf16[240,128]{1,0:T(8,128)(2,1)S(1)} %pad_maximum_fusion.11), channel_id=1, source_target_pairs={{0,32},{16,48},{32,0},{48,16},{1,33},{17,49},{33,1},{49,17},{2,34}... | collective-permute-start | bytes 184328 | tf_op jit(solution)/shard_map/ppermute | solution.py:34
  70.0 0.4 collective-permute-done.18
  70.4 1.8 %collective-permute-done.16 = bf16[240,128]{1,0:T(8,128)(2,1)S(1)} collective-permute-done((bf16[240,128]{1,0:T(8,128)(2,1)S(1)}, bf16[240,128]{1,0:T(8,128)(2,1)S(1)}, u32[]{:S(2)}, u32[]{:S(2)}) %collective-permute-start.16) | collective-permute-done | bytes 61472 | tf_op jit(solution)/shard_map/ppermute | solution.py:34
  72.3 1.1 %collective-permute-start.21 = (bf16[240,128]{1,0:T(8,128)(2,1)S(1)}, bf16[240,128]{1,0:T(8,128)(2,1)S(1)}, u32[]{:S(2)}, u32[]{:S(2)}) collective-permute-start(bf16[240,128]{1,0:T(8,128)(2,1)S(1)} %pad_maximum_fusion.12), channel_id=1, source_target_pairs={{0,192},{64,128},{128,64},{192,0},{1,193},{65,129},{129,65},{193,1... | collective-permute-start | bytes 184328 | tf_op jit(solution)/shard_map/ppermute | solution.py:34
  73.4 0.0 collective-permute-start.20
  73.5 2.8 %collective-permute-start.19 = (bf16[240,128]{1,0:T(8,128)(2,1)S(1)}, bf16[240,128]{1,0:T(8,128)(2,1)S(1)}, u32[]{:S(2)}, u32[]{:S(2)}) collective-permute-start(bf16[240,128]{1,0:T(8,128)(2,1)S(1)} %pad_maximum_fusion.12), channel_id=1, source_target_pairs={{0,128},{64,192},{128,0},{192,64},{1,129},{65,193},{129,1},{193,65... | collective-permute-start | bytes 184328 | tf_op jit(solution)/shard_map/ppermute | solution.py:34
  76.3 0.4 collective-permute-done.21
  76.7 0.0 collective-permute-done.20
  76.7 1.8 %collective-permute-done.19 = bf16[240,128]{1,0:T(8,128)(2,1)S(1)} collective-permute-done((bf16[240,128]{1,0:T(8,128)(2,1)S(1)}, bf16[240,128]{1,0:T(8,128)(2,1)S(1)}, u32[]{:S(2)}, u32[]{:S(2)}) %collective-permute-start.19) | collective-permute-done | bytes 61472 | tf_op jit(solution)/shard_map/ppermute | solution.py:34
  78.6 5.5 %collective-permute-start.22 = (f32[192,128]{1,0:T(8,128)S(1)}, f32[192,128]{1,0:T(8,128)S(1)}, u32[]{:S(2)}, u32[]{:S(2)}) collective-permute-start(f32[192,128]{1,0:T(8,128)S(1)} %pad_maximum_fusion.8.held), channel_id=1, source_target_pairs={{0,8},{8,0},{1,9},{9,1},{2,10},{10,2},{3,11},{11,3},{4,12},{12,4},... | collective-permute-start | bytes 294920 | tf_op jit(solution)/shard_map/ppermute | solution.py:34
  84.2 0.9 %collective-permute-done.22.other = f32[192,128]{1,0:T(8,128)S(1)} collective-permute-done((f32[192,128]{1,0:T(8,128)S(1)}, f32[192,128]{1,0:T(8,128)S(1)}, u32[]{:S(2)}, u32[]{:S(2)}) %collective-permute-start.22) | collective-permute-done | bytes 98336 | tf_op jit(solution)/shard_map/ppermute | solution.py:34
  85.1 1.3 %finish.1 = (f32[24,768]{1,0:T(8,128)}, f32[96,192]{1,0:T(8,128)}, f32[7,7,192]{2,1,0:T(8,128)}) custom-call(s32[1,7]{1,0:T(1,128)S(1)} %add_bitcast_fusion.info, f32[192,128]{1,0:T(8,128)S(1)} %pad_maximum_fusion.8.held, f32[192,128]{1,0:T(8,128)S(1)} %collective-permute-done.22.other), custom_call_target="tpu_custom_call" | custom-call | flops 1000000000 | bytes 1000000 | tf_op jit(solution)/shard_map/finish/pallas_call | solution.py:298
  (44 shorter events, 0.5 us)
Async XLA Ops:
  2.0 1.0 %copy-start.4 = (bf16[1,4,16,16,192]{4,3,2,1,0:T(8,128)(2,1)S(1)}, bf16[1,4,16,16,192]{4,3,2,1,0:T(8,128)(2,1)}, u32[]{:S(2)}) copy-start(bf16[1,4,16,16,192]{4,3,2,1,0:T(8,128)(2,1)} %param.9) | copy-start | bytes 1179652
  3.1 5.0 %copy-start.2 = (bf16[96,192]{1,0:T(8,128)(2,1)S(1)}, bf16[96,192]{1,0:T(8,128)(2,1)}, u32[]{:S(2)}) copy-start(bf16[96,192]{1,0:T(8,128)(2,1)} %project.1) | copy-start | bytes 110596
  3.1 5.0 %copy-start.3 = (bf16[24,768]{1,0:T(8,128)(2,1)S(1)}, bf16[24,768]{1,0:T(8,128)(2,1)}, u32[]{:S(2)}) copy-start(bf16[24,768]{1,0:T(8,128)(2,1)} %expand) | copy-start | bytes 110596
  3.9 4.2 %collective-permute-start.1 = (bf16[3,32,192]{2,0,1:T(4,128)(2,1)S(1)}, bf16[3,32,192]{2,0,1:T(4,128)(2,1)S(1)}, u32[]{:S(2)}, u32[]{:S(2)}) collective-permute-start(bf16[3,32,192]{2,0,1:T(4,128)(2,1)S(1)} %get-tuple-element.58), channel_id=1, source_target_pairs={{0,8},{8,0},{1,9},{9,1},{2,10},{10,2},{3,11},{11,3},{4,12},{12,4},... | collective-permute-start | bytes 110600 | tf_op jit(solution)/shard_map/ppermute | solution.py:34
  7.2 5.7 %collective-permute-start = (bf16[3,32,192]{2,0,1:T(4,128)(2,1)S(1)}, bf16[3,32,192]{2,0,1:T(4,128)(2,1)S(1)}, u32[]{:S(2)}, u32[]{:S(2)}) collective-permute-start(bf16[3,32,192]{2,0,1:T(4,128)(2,1)S(1)} %get-tuple-element.57), channel_id=1, source_target_pairs={{0,24},{8,16},{16,8},{24,0},{32,56},{40,48},{48,40},{56,32},{1,25}... | collective-permute-start | bytes 110600 | tf_op jit(solution)/shard_map/ppermute | solution.py:349
  8.7 9.7 %collective-permute-start.4 = (bf16[144,128]{1,0:T(8,128)(2,1)S(1)}, bf16[144,128]{1,0:T(8,128)(2,1)S(1)}, u32[]{:S(2)}, u32[]{:S(2)}) collective-permute-start(bf16[144,128]{1,0:T(8,128)(2,1)S(1)} %pack.1), channel_id=1, source_target_pairs={{0,7},{1,6},{2,5},{3,4},{4,3},{5,2},{6,1},{7,0},{8,15},{9,14},{10,... | collective-permute-start | bytes 110600 | tf_op jit(solution)/shard_map/ppermute | solution.py:34
  13.4 11.7 %copy-start.1 = (f32[7,7,192]{2,1,0:T(8,128)S(1)}, f32[7,7,192]{2,1,0:T(8,128)}, u32[]{:S(2)}) copy-start(f32[7,7,192]{2,1,0:T(8,128)} %kernel.3) | copy-start | bytes 112900
  13.4 7.2 %collective-permute-start.2 = (bf16[3,40,192]{2,1,0:T(8,128)(2,1)S(1)}, bf16[3,40,192]{2,1,0:T(8,128)(2,1)S(1)}, u32[]{:S(2)}, u32[]{:S(2)}) collective-permute-start(bf16[3,40,192]{2,1,0:T(8,128)(2,1)S(1)} %get-tuple-element.53), channel_id=1, source_target_pairs={{32,64},{48,80},{96,128},{112,144},{160,192},{176,208},{224,0},{24... | collective-permute-start | bytes 138248 | tf_op jit(solution)/shard_map/ppermute | solution.py:366
  18.4 4.6 %collective-permute-start.3 = (bf16[3,40,192]{2,1,0:T(8,128)(2,1)S(1)}, bf16[3,40,192]{2,1,0:T(8,128)(2,1)S(1)}, u32[]{:S(2)}, u32[]{:S(2)}) collective-permute-start(bf16[3,40,192]{2,1,0:T(8,128)(2,1)S(1)} %get-tuple-element.54), channel_id=1, source_target_pairs={{0,32},{16,48},{32,0},{48,16},{1,33},{17,49},{33,1},{49,17},{2,34}... | collective-permute-start | bytes 138248 | tf_op jit(solution)/shard_map/ppermute | solution.py:34
  18.4 4.6 %collective-permute-start.5 = (bf16[2,144,128]{2,1,0:T(8,128)(2,1)S(1)}, bf16[2,144,128]{2,1,0:T(8,128)(2,1)S(1)}, u32[]{:S(2)}, u32[]{:S(2)}) collective-permute-start(bf16[2,144,128]{2,1,0:T(8,128)(2,1)S(1)} %pad_maximum_fusion.9), channel_id=1, source_target_pairs={{0,2},{1,3},{2,0},{3,1},{4,6},{5,7},{6,4},{7,5},{8,10},{9,11},{10,... | collective-permute-start | bytes 221192 | tf_op jit(solution)/shard_map/ppermute | solution.py:34
  23.1 5.8 %collective-permute-start.6 = (bf16[4,144,128]{2,1,0:T(8,128)(2,1)S(1)}, bf16[4,144,128]{2,1,0:T(8,128)(2,1)S(1)}, u32[]{:S(2)}, u32[]{:S(2)}) collective-permute-start(bf16[4,144,128]{2,1,0:T(8,128)(2,1)S(1)} %pad_maximum_fusion.6), channel_id=1, source_target_pairs={{0,1},{1,0},{2,3},{3,2},{4,5},{5,4},{6,7},{7,6},{8,9},{9,8},{10,11... | collective-permute-start | bytes 442376 | tf_op jit(solution)/shard_map/ppermute | solution.py:34
  25.1 6.5 %copy-start.7 = (f32[768]{0:T(1024)S(1)}, f32[768]{0:T(1024)}, u32[]{:S(2)}) copy-start(f32[768]{0:T(1024)} %param.16) | copy-start | bytes 9220
  25.1 7.7 %copy-start = (bf16[1,4,16,16,192]{4,3,2,1,0:T(8,128)(2,1)S(1)}, bf16[1,4,16,16,192]{4,3,2,1,0:T(8,128)(2,1)}, u32[]{:S(2)}) copy-start(bf16[1,4,16,16,192]{4,3,2,1,0:T(8,128)(2,1)} %param.10) | copy-start | bytes 1179652
  25.1 7.7 %copy-start.5 = (bf16[1,4,16,16,192]{4,3,2,1,0:T(8,128)(2,1)S(1)}, bf16[1,4,16,16,192]{4,3,2,1,0:T(8,128)(2,1)}, u32[]{:S(2)}) copy-start(bf16[1,4,16,16,192]{4,3,2,1,0:T(8,128)(2,1)} %param.9) | copy-start | bytes 1179652
  25.2 7.7 %copy-start.6 = (f32[192]{0:T(256)S(1)}, f32[192]{0:T(256)}, u32[]{:S(2)}) copy-start(f32[192]{0:T(256)} %param.14) | copy-start | bytes 2308
  28.9 3.9 %collective-permute-start.7 = (bf16[8,144,128]{2,1,0:T(8,128)(2,1)S(1)}, bf16[8,144,128]{2,1,0:T(8,128)(2,1)S(1)}, u32[]{:S(2)}, u32[]{:S(2)}) collective-permute-start(bf16[8,144,128]{2,1,0:T(8,128)(2,1)S(1)} %pad_maximum_fusion.4.held), channel_id=1, source_target_pairs={{0,8},{8,0},{1,9},{9,1},{2,10},{10,2},{3,11},{11,3},{4,12},{12,4},... | collective-permute-start | bytes 884744 | tf_op jit(solution)/shard_map/ppermute | solution.py:34
  41.6 1.6 %collective-permute-start.9 = (bf16[1248,128]{1,0:T(8,128)(2,1)S(1)}, bf16[1248,128]{1,0:T(8,128)(2,1)S(1)}, u32[]{:S(2)}, u32[]{:S(2)}) collective-permute-start(bf16[1248,128]{1,0:T(8,128)(2,1)S(1)} %get-tuple-element.31), channel_id=1, source_target_pairs={{0,8},{8,0},{1,9},{9,1},{2,10},{10,2},{3,11},{11,3},{4,12},{12,4},... | collective-permute-start | bytes 958472 | tf_op jit(solution)/shard_map/ppermute | solution.py:34
  42.1 4.0 %collective-permute-start.8 = (bf16[3,32,192]{2,0,1:T(4,128)(2,1)S(1)}, bf16[3,32,192]{2,0,1:T(4,128)(2,1)S(1)}, u32[]{:S(2)}, u32[]{:S(2)}) collective-permute-start(bf16[3,32,192]{2,0,1:T(4,128)(2,1)S(1)} %get-tuple-element.55), channel_id=1, source_target_pairs={{0,24},{8,16},{16,8},{24,0},{32,56},{40,48},{48,40},{56,32},{1,25}... | collective-permute-start | bytes 110600 | tf_op jit(solution)/shard_map/ppermute | solution.py:349
  42.5 1.3 %collective-permute-start.10 = (bf16[3,32,192]{2,0,1:T(4,128)(2,1)S(1)}, bf16[3,32,192]{2,0,1:T(4,128)(2,1)S(1)}, u32[]{:S(2)}, u32[]{:S(2)}) collective-permute-start(bf16[3,32,192]{2,0,1:T(4,128)(2,1)S(1)} %get-tuple-element.56), channel_id=1, source_target_pairs={{0,8},{8,0},{1,9},{9,1},{2,10},{10,2},{3,11},{11,3},{4,12},{12,4},... | collective-permute-start | bytes 110600 | tf_op jit(solution)/shard_map/ppermute | solution.py:34
  43.8 5.6 %collective-permute-start.12 = (bf16[672,128]{1,0:T(8,128)(2,1)S(1)}, bf16[672,128]{1,0:T(8,128)(2,1)S(1)}, u32[]{:S(2)}, u32[]{:S(2)}) collective-permute-start(bf16[672,128]{1,0:T(8,128)(2,1)S(1)} %pad_maximum_fusion.5), channel_id=1, source_target_pairs={{0,1},{1,0},{2,3},{3,2},{4,5},{5,4},{6,7},{7,6},{8,9},{9,8},{10,11... | collective-permute-start | bytes 516104 | tf_op jit(solution)/shard_map/ppermute | solution.py:34
  46.5 9.1 %collective-permute-start.11 = (bf16[3,40,192]{2,1,0:T(8,128)(2,1)S(1)}, bf16[3,40,192]{2,1,0:T(8,128)(2,1)S(1)}, u32[]{:S(2)}, u32[]{:S(2)}) collective-permute-start(bf16[3,40,192]{2,1,0:T(8,128)(2,1)S(1)} %get-tuple-element.51), channel_id=1, source_target_pairs={{32,64},{48,80},{96,128},{112,144},{160,192},{176,208},{224,0},{24... | collective-permute-start | bytes 138248 | tf_op jit(solution)/shard_map/ppermute | solution.py:366
  49.4 4.9 %collective-permute-start.13 = (bf16[3,40,192]{2,1,0:T(8,128)(2,1)S(1)}, bf16[3,40,192]{2,1,0:T(8,128)(2,1)S(1)}, u32[]{:S(2)}, u32[]{:S(2)}) collective-permute-start(bf16[3,40,192]{2,1,0:T(8,128)(2,1)S(1)} %get-tuple-element.52), channel_id=1, source_target_pairs={{0,32},{16,48},{32,0},{48,16},{1,33},{17,49},{33,1},{49,17},{2,34}... | collective-permute-start | bytes 138248 | tf_op jit(solution)/shard_map/ppermute | solution.py:34
  54.3 7.2 %collective-permute-start.14 = (bf16[384,128]{1,0:T(8,128)(2,1)S(1)}, bf16[384,128]{1,0:T(8,128)(2,1)S(1)}, u32[]{:S(2)}, u32[]{:S(2)}) collective-permute-start(bf16[384,128]{1,0:T(8,128)(2,1)S(1)} %pad_maximum_fusion.7), channel_id=1, source_target_pairs={{0,2},{1,3},{2,0},{3,1},{4,6},{5,7},{6,4},{7,5},{8,10},{9,11},{10,... | collective-permute-start | bytes 294920 | tf_op jit(solution)/shard_map/ppermute | solution.py:34
  61.6 4.4 %collective-permute-start.15 = (bf16[240,128]{1,0:T(8,128)(2,1)S(1)}, bf16[240,128]{1,0:T(8,128)(2,1)S(1)}, u32[]{:S(2)}, u32[]{:S(2)}) collective-permute-start(bf16[240,128]{1,0:T(8,128)(2,1)S(1)} %pad_maximum_fusion.10), channel_id=1, source_target_pairs={{0,7},{1,6},{2,5},{3,4},{4,3},{5,2},{6,1},{7,0},{8,15},{9,14},{10,... | collective-permute-start | bytes 184328 | tf_op jit(solution)/shard_map/ppermute | solution.py:34
  66.1 4.4 %collective-permute-start.18 = (bf16[240,128]{1,0:T(8,128)(2,1)S(1)}, bf16[240,128]{1,0:T(8,128)(2,1)S(1)}, u32[]{:S(2)}, u32[]{:S(2)}) collective-permute-start(bf16[240,128]{1,0:T(8,128)(2,1)S(1)} %pad_maximum_fusion.11), channel_id=1, source_target_pairs={{0,48},{16,32},{32,16},{48,0},{1,49},{17,33},{33,17},{49,1},{2,50}... | collective-permute-start | bytes 184328 | tf_op jit(solution)/shard_map/ppermute | solution.py:34
  67.1 3.3 %collective-permute-start.17 = (bf16[240,128]{1,0:T(8,128)(2,1)S(1)}, bf16[240,128]{1,0:T(8,128)(2,1)S(1)}, u32[]{:S(2)}, u32[]{:S(2)}) collective-permute-start(bf16[240,128]{1,0:T(8,128)(2,1)S(1)} %pad_maximum_fusion.11), channel_id=1, source_target_pairs={{0,16},{16,0},{32,48},{48,32},{1,17},{17,1},{33,49},{49,33},{2,18}... | collective-permute-start | bytes 184328 | tf_op jit(solution)/shard_map/ppermute | solution.py:34
  67.2 5.1 %collective-permute-start.16 = (bf16[240,128]{1,0:T(8,128)(2,1)S(1)}, bf16[240,128]{1,0:T(8,128)(2,1)S(1)}, u32[]{:S(2)}, u32[]{:S(2)}) collective-permute-start(bf16[240,128]{1,0:T(8,128)(2,1)S(1)} %pad_maximum_fusion.11), channel_id=1, source_target_pairs={{0,32},{16,48},{32,0},{48,16},{1,33},{17,49},{33,1},{49,17},{2,34}... | collective-permute-start | bytes 184328 | tf_op jit(solution)/shard_map/ppermute | solution.py:34
  72.3 4.4 %collective-permute-start.21 = (bf16[240,128]{1,0:T(8,128)(2,1)S(1)}, bf16[240,128]{1,0:T(8,128)(2,1)S(1)}, u32[]{:S(2)}, u32[]{:S(2)}) collective-permute-start(bf16[240,128]{1,0:T(8,128)(2,1)S(1)} %pad_maximum_fusion.12), channel_id=1, source_target_pairs={{0,192},{64,128},{128,64},{192,0},{1,193},{65,129},{129,65},{193,1... | collective-permute-start | bytes 184328 | tf_op jit(solution)/shard_map/ppermute | solution.py:34
  73.4 3.3 %collective-permute-start.20 = (bf16[240,128]{1,0:T(8,128)(2,1)S(1)}, bf16[240,128]{1,0:T(8,128)(2,1)S(1)}, u32[]{:S(2)}, u32[]{:S(2)}) collective-permute-start(bf16[240,128]{1,0:T(8,128)(2,1)S(1)} %pad_maximum_fusion.12), channel_id=1, source_target_pairs={{0,64},{64,0},{128,192},{192,128},{1,65},{65,1},{129,193},{193,129... | collective-permute-start | bytes 184328 | tf_op jit(solution)/shard_map/ppermute | solution.py:34
  73.5 5.1 %collective-permute-start.19 = (bf16[240,128]{1,0:T(8,128)(2,1)S(1)}, bf16[240,128]{1,0:T(8,128)(2,1)S(1)}, u32[]{:S(2)}, u32[]{:S(2)}) collective-permute-start(bf16[240,128]{1,0:T(8,128)(2,1)S(1)} %pad_maximum_fusion.12), channel_id=1, source_target_pairs={{0,128},{64,192},{128,0},{192,64},{1,129},{65,193},{129,1},{193,65... | collective-permute-start | bytes 184328 | tf_op jit(solution)/shard_map/ppermute | solution.py:34
  78.6 6.5 %collective-permute-start.22 = (f32[192,128]{1,0:T(8,128)S(1)}, f32[192,128]{1,0:T(8,128)S(1)}, u32[]{:S(2)}, u32[]{:S(2)}) collective-permute-start(f32[192,128]{1,0:T(8,128)S(1)} %pad_maximum_fusion.8.held), channel_id=1, source_target_pairs={{0,8},{8,0},{1,9},{9,1},{2,10},{10,2},{3,11},{11,3},{4,12},{12,4},... | collective-permute-start | bytes 294920 | tf_op jit(solution)/shard_map/ppermute | solution.py:34

commit v6 on v5

--- a/solution.py
+++ b/solution.py
@@ -98,7 +98,7 @@
     planes[1] = jnp.concatenate([padded[:HALF, :, LANES:], padded[S:, :, LANES:]], axis=-1)
 
 
-def conv_planes(planes, taps, out):
+def conv_planes(planes, taps, out, first=0, last=3):
     def body(step, carry):
         t = step // 4
         col = pl.multiple_of((step % 4) * 8, 8)
@@ -110,7 +110,7 @@
         out[t, :, pl.ds(col, 8), :] = acc
         return carry
 
-    lax.fori_loop(0, 12, body, 0)
+    lax.fori_loop(4 * first, 4 * last, body, 0)
 
 
 def correlate_planes(planes, field, acc):
@@ -273,10 +273,16 @@
         grad_k[dy] = whole[dy * KS : (dy + 1) * KS]
 
 
-def spread_kernel(info, padded, cotan, kernel, out, planes, summed, taps):
+def spread_kernel(padded, kernel, planes, summed, taps):
     fill_taps(kernel, taps, True)
     fill_planes(padded, planes)
-    conv_planes(planes, taps, summed)
+    conv_planes(planes, taps, summed, 0, 2)
+
+
+def emit_kernel(info, planes, partial, cotan, kernel, out, summed, taps):
+    fill_taps(kernel, taps, True)
+    summed[:2] = partial[:2]
+    conv_planes(planes, taps, summed, 2, 3)
 
     def blank(j, carry):
         out[j] = jnp.zeros_like(out[j])
@@ -464,17 +470,26 @@
     widened = widen(field, inner, outer)
     near, far = end_rims(widened)
     held, taps = halve(held, taps, 1)
-    held, near = tie(held, near)
-    (grad_tiles,) = call(
+    near = tie(near, held)[0]
+    planes, summed = call(
         spread_kernel,
-        (info, pad_ends(widened, near, far), cotan, kernel),
-        [((CAP, S, S, C), f32)],
-        [(PLANES, f32), (CELLS, f32), (TAP_PLANES, f32)],
+        (pad_ends(widened, near, far), kernel),
+        [(PLANES, f32), (CELLS, f32)],
+        [(TAP_PLANES, f32)],
         name="spread",
         us=0,
     )
     held, taps = halve(held, taps, 2)
-    held, taps = halve(held, taps, 7, grad_tiles)
+    held, taps = halve(held, taps, 7, summed)
+    (grad_tiles,) = call(
+        emit_kernel,
+        (info, planes, summed, cotan, kernel),
+        [((CAP, S, S, C), f32)],
+        [(CELLS, f32), (TAP_PLANES, f32)],
+        name="emit",
+        us=0,
+    )
+    taps, grad_tiles = tie(taps, grad_tiles)
     for axis in ("x", "y"):
         part = jnp.concatenate([held.astype(bf16), *split_high_low(taps)])
         parts = [part] + [swap(part, axis, i) for i in (2, 1, 3)]

time: 86.8 us -> 83.5 us (0.962)
  waiting for transfers between devices: 19.8 us -> 17.2 us
    ppermute x19, waiting for transfers between devices: 18.2 us -> 15.7 us  [swap(): return lax.ppermute(value, axis, [(i, i ^ bit) for i in range(SIZES[axis])])]
    pallas_call x6 -> x7, Pallas kernels: 20.7 us -> 20.6 us  [call(): pl.pallas_call(kernel, out_shape=[jax.ShapeDtypeStruct(shape, dtype) for...]
  transfers between devices with their start and end apart: 23 -> 23, of which waited for: 13 -> 13; matrix products, arithmetic and copies ran while one was open for 2% -> 2% of each run, Pallas kernels for 11% -> 12%
where the time goes in v6:
time: 83.5 us; the launch traced here: 83.4 us
  starting transfers between devices  39.9 us (48%)
  Pallas kernels  20.6 us (25%)
  waiting for transfers between devices  17.2 us (21%)
  other arithmetic  2.96 us (4%)
  between operations  1.6 us (2%)
  local copies, waits for them, and re-layouts  1.14 us (1%)
    ppermute x19, starting transfers between devices, swap(): return lax.ppermute(value, axis, [(i, i ^ bit) for i in range(SIZES[axis])])  31.6 us
    pallas_call x7, Pallas kernels, call(): pl.pallas_call(kernel, out_shape=[jax.ShapeDtypeStruct(shape, dtype) for...  20.6 us
    ppermute x19, waiting for transfers between devices, swap(): return lax.ppermute(value, axis, [(i, i ^ bit) for i in range(SIZES[axis])])  15.7 us
    ppermute x2, starting transfers between devices, end_rims(): lax.ppermute(jnp.where(upper == 0, north_edge, south_edge), ('y', 'x'), p...  7.85 us
  transfers between devices with their start and end apart: 23, of which 13 were waited for; matrix products, arithmetic and copies ran while one was open for 2% of the time, Pallas kernels for 12%

profile of v6, /device:TPU:1, one launch (start us, length us, event | category | flops | bytes accessed | tf_op | source)
XLA Modules:
  0.0 83.4 jit_solution(15272090868728868792)
XLA Ops:
  1.3 0.7 add_bitcast_fusion.info
  2.0 1.0 %copy-done.4 = bf16[1,4,16,16,192]{4,3,2,1,0:T(8,128)(2,1)S(1)} copy-done((bf16[1,4,16,16,192]{4,3,2,1,0:T(8,128)(2,1)S(1)}, bf16[1,4,16,16,192]{4,3,2,1,0:T(8,128)(2,1)}, u32[]{:S(2)}) %copy-start.4) | copy-done | bytes 393240
  3.1 0.7 place.1
  3.8 0.1 select_bitcast_fusion.7
  3.9 3.3 %collective-permute-start.1 = (bf16[3,32,192]{2,0,1:T(4,128)(2,1)S(1)}, bf16[3,32,192]{2,0,1:T(4,128)(2,1)S(1)}, u32[]{:S(2)}, u32[]{:S(2)}) collective-permute-start(bf16[3,32,192]{2,0,1:T(4,128)(2,1)S(1)} %get-tuple-element.62), channel_id=1, source_target_pairs={{0,8},{8,0},{1,9},{9,1},{2,10},{10,2},{3,11},{11,3},{4,12},{12,4},... | collective-permute-start | bytes 110600 | tf_op jit(solution)/shard_map/ppermute | solution.py:34
  7.2 0.0 collective-permute-start
  7.2 0.9 %collective-permute-done.1 = bf16[3,32,192]{2,0,1:T(4,128)(2,1)S(1)} collective-permute-done((bf16[3,32,192]{2,0,1:T(4,128)(2,1)S(1)}, bf16[3,32,192]{2,0,1:T(4,128)(2,1)S(1)}, u32[]{:S(2)}, u32[]{:S(2)}) %collective-permute-start.1) | collective-permute-done | bytes 36896 | tf_op jit(solution)/shard_map/ppermute | solution.py:34
  8.1 0.6 pack.1
  8.7 4.2 %collective-permute-start.4 = (bf16[144,128]{1,0:T(8,128)(2,1)S(1)}, bf16[144,128]{1,0:T(8,128)(2,1)S(1)}, u32[]{:S(2)}, u32[]{:S(2)}) collective-permute-start(bf16[144,128]{1,0:T(8,128)(2,1)S(1)} %pack.1), channel_id=1, source_target_pairs={{0,7},{1,6},{2,5},{3,4},{4,3},{5,2},{6,1},{7,0},{8,15},{9,14},{10,... | collective-permute-start | bytes 110600 | tf_op jit(solution)/shard_map/ppermute | solution.py:34
  12.9 0.0 collective-permute-done
  12.9 0.1 select_bitcast_fusion.5
  13.0 0.4 pad_maximum_fusion.3
  13.4 0.0 copy-start.1
  13.4 5.0 %collective-permute-start.2 = (bf16[3,40,192]{2,1,0:T(8,128)(2,1)S(1)}, bf16[3,40,192]{2,1,0:T(8,128)(2,1)S(1)}, u32[]{:S(2)}, u32[]{:S(2)}) collective-permute-start(bf16[3,40,192]{2,1,0:T(8,128)(2,1)S(1)} %get-tuple-element.57), channel_id=1, source_target_pairs={{32,64},{48,80},{96,128},{112,144},{160,192},{176,208},{224,0},{24... | collective-permute-start | bytes 138248 | tf_op jit(solution)/shard_map/ppermute | solution.py:372
  18.4 0.0 collective-permute-start.3
  18.4 0.0 collective-permute-done.4
  18.4 2.2 %collective-permute-start.5 = (bf16[2,144,128]{2,1,0:T(8,128)(2,1)S(1)}, bf16[2,144,128]{2,1,0:T(8,128)(2,1)S(1)}, u32[]{:S(2)}, u32[]{:S(2)}) collective-permute-start(bf16[2,144,128]{2,1,0:T(8,128)(2,1)S(1)} %pad_maximum_fusion.9), channel_id=1, source_target_pairs={{0,2},{1,3},{2,0},{3,1},{4,6},{5,7},{6,4},{7,5},{8,10},{9,11},{10,... | collective-permute-start | bytes 221192 | tf_op jit(solution)/shard_map/ppermute | solution.py:34
  20.6 2.4 %collective-permute-done.3 = bf16[3,40,192]{2,1,0:T(8,128)(2,1)S(1)} collective-permute-done((bf16[3,40,192]{2,1,0:T(8,128)(2,1)S(1)}, bf16[3,40,192]{2,1,0:T(8,128)(2,1)S(1)}, u32[]{:S(2)}, u32[]{:S(2)}) %collective-permute-start.3) | collective-permute-done | bytes 46112 | tf_op jit(solution)/shard_map/ppermute | solution.py:34
  23.1 1.7 %collective-permute-start.6 = (bf16[4,144,128]{2,1,0:T(8,128)(2,1)S(1)}, bf16[4,144,128]{2,1,0:T(8,128)(2,1)S(1)}, u32[]{:S(2)}, u32[]{:S(2)}) collective-permute-start(bf16[4,144,128]{2,1,0:T(8,128)(2,1)S(1)} %pad_maximum_fusion.6), channel_id=1, source_target_pairs={{0,1},{1,0},{2,3},{3,2},{4,5},{5,4},{6,7},{7,6},{8,9},{9,8},{10,11... | collective-permute-start | bytes 442376 | tf_op jit(solution)/shard_map/ppermute | solution.py:34
  24.8 0.3 fusion.2.padded
  25.1 0.0 copy-start.7
  25.1 0.0 copy-start
  25.1 0.0 copy-start.5
  25.1 0.0 copy-start.6
  25.2 3.7 %field.1 = (f32[3,22,40,128]{3,2,1,0:T(8,128)S(1)}, f32[3,16,32,128]{3,2,1,0:T(8,128)S(1)}) custom-call(f32[38,40,192]{2,1,0:T(8,128)S(1)} %fusion.2.padded, f32[7,7,192]{2,1,0:T(8,128)S(1)} %copy-done.1), custom_call_target="tpu_custom_call" | custom-call | tf_op jit(solution)/shard_map/field/pallas_call | solution.py:304
  28.8 0.0 collective-permute-done.6
  28.9 2.7 %collective-permute-start.7 = (bf16[8,144,128]{2,1,0:T(8,128)(2,1)S(1)}, bf16[8,144,128]{2,1,0:T(8,128)(2,1)S(1)}, u32[]{:S(2)}, u32[]{:S(2)}) collective-permute-start(bf16[8,144,128]{2,1,0:T(8,128)(2,1)S(1)} %pad_maximum_fusion.4.held), channel_id=1, source_target_pairs={{0,8},{8,0},{1,9},{9,1},{2,10},{10,2},{3,11},{11,3},{4,12},{12,4},... | collective-permute-start | bytes 884744 | tf_op jit(solution)/shard_map/ppermute | solution.py:34
  31.6 1.2 %collective-permute-done.7.other = bf16[8,144,128]{2,1,0:T(8,128)(2,1)S(1)} collective-permute-done((bf16[8,144,128]{2,1,0:T(8,128)(2,1)S(1)}, bf16[8,144,128]{2,1,0:T(8,128)(2,1)S(1)}, u32[]{:S(2)}, u32[]{:S(2)}) %collective-permute-start.7) | collective-permute-done | bytes 294944 | tf_op jit(solution)/shard_map/ppermute | solution.py:34
  32.8 8.8 %block.1 = (f32[4,16,16,192]{3,2,1,0:T(8,128)}, bf16[32,32,192]{2,1,0:T(8,128)(2,1)S(1)}, f32[1152,128]{1,0:T(8,128)S(1)}, bf16[1248,128]{1,0:T(8,128)(2,1)S(1)}, f32[48,128]{1,0:T(8,128)S(1)}) custom-call(s32[1,7]{1,0:T(1,128)S(1)} %add_bitcast_fusion.info, f32[3,22,40,128]{3,2,1,0:T(8,128)S(1)} %get-tuple-element.27.planes, ...), custom_call_target="tpu_custom_call" | custom-call | flops 14000000000 | bytes 14000000 | tf_op jit(solution)/shard_map/block/pallas_call | solution.py:304
  41.6 0.4 collective-permute-start.8
  42.0 0.1 select_bitcast_fusion.3
  42.1 0.4 collective-permute-start.11
  42.5 0.3 collective-permute-start.12
  42.8 0.4 collective-permute-done.8
  43.2 0.1 convert_add_fusion
  43.4 0.4 collective-permute-done.12
  43.8 0.7 collective-permute-start.9
  44.5 1.5 %collective-permute-done.11 = bf16[3,32,192]{2,0,1:T(4,128)(2,1)S(1)} collective-permute-done((bf16[3,32,192]{2,0,1:T(4,128)(2,1)S(1)}, bf16[3,32,192]{2,0,1:T(4,128)(2,1)S(1)}, u32[]{:S(2)}, u32[]{:S(2)}) %collective-permute-start.11) | collective-permute-done | bytes 36896 | tf_op jit(solution)/shard_map/ppermute | solution.py:355
  46.0 0.1 select_bitcast_fusion.1
  46.1 0.4 pad_maximum_fusion.2
  46.5 2.9 %collective-permute-start.13 = (bf16[3,40,192]{2,1,0:T(8,128)(2,1)S(1)}, bf16[3,40,192]{2,1,0:T(8,128)(2,1)S(1)}, u32[]{:S(2)}, u32[]{:S(2)}) collective-permute-start(bf16[3,40,192]{2,1,0:T(8,128)(2,1)S(1)} %get-tuple-element.55), channel_id=1, source_target_pairs={{32,64},{48,80},{96,128},{112,144},{160,192},{176,208},{224,0},{24... | collective-permute-start | bytes 138248 | tf_op jit(solution)/shard_map/ppermute | solution.py:372
  49.4 0.0 collective-permute-start.14
  49.4 0.0 collective-permute-done.9
  49.5 1.3 %collective-permute-start.10 = (bf16[384,128]{1,0:T(8,128)(2,1)S(1)}, bf16[384,128]{1,0:T(8,128)(2,1)S(1)}, u32[]{:S(2)}, u32[]{:S(2)}) collective-permute-start(bf16[384,128]{1,0:T(8,128)(2,1)S(1)} %pad_maximum_fusion.7), channel_id=1, source_target_pairs={{0,2},{1,3},{2,0},{3,1},{4,6},{5,7},{6,4},{7,5},{8,10},{9,11},{10,... | collective-permute-start | bytes 294920 | tf_op jit(solution)/shard_map/ppermute | solution.py:34
  50.8 3.4 %collective-permute-done.14 = bf16[3,40,192]{2,1,0:T(8,128)(2,1)S(1)} collective-permute-done((bf16[3,40,192]{2,1,0:T(8,128)(2,1)S(1)}, bf16[3,40,192]{2,1,0:T(8,128)(2,1)S(1)}, u32[]{:S(2)}, u32[]{:S(2)}) %collective-permute-start.14) | collective-permute-done | bytes 46112 | tf_op jit(solution)/shard_map/ppermute | solution.py:34
  54.2 0.0 collective-permute-done.13
  54.3 0.3 fusion.5.padded
  54.6 2.5 %spread.1 = (f32[3,22,40,128]{3,2,1,0:T(8,128)S(1)}, f32[3,16,32,128]{3,2,1,0:T(8,128)S(1)}) custom-call(f32[38,40,192]{2,1,0:T(8,128)S(1)} %fusion.5.padded, f32[7,7,192]{2,1,0:T(8,128)S(1)} %copy-done.1), custom_call_target="tpu_custom_call" | custom-call | tf_op jit(solution)/shard_map/spread/pallas_call | solution.py:304
  57.1 0.0 collective-permute-done.10
  57.2 2.0 %collective-permute-start.15 = (bf16[240,128]{1,0:T(8,128)(2,1)S(1)}, bf16[240,128]{1,0:T(8,128)(2,1)S(1)}, u32[]{:S(2)}, u32[]{:S(2)}) collective-permute-start(bf16[240,128]{1,0:T(8,128)(2,1)S(1)} %pad_maximum_fusion.10), channel_id=1, source_target_pairs={{0,7},{1,6},{2,5},{3,4},{4,3},{5,2},{6,1},{7,0},{8,15},{9,14},{10,... | collective-permute-start | bytes 184328 | tf_op jit(solution)/shard_map/ppermute | solution.py:34
  59.2 3.0 %emit.1 = f32[4,16,16,192]{3,2,1,0:T(8,128)} custom-call(s32[1,7]{1,0:T(1,128)S(1)} %add_bitcast_fusion.info, f32[3,22,40,128]{3,2,1,0:T(8,128)S(1)} %get-tuple-element.41.planes, f32[3,16,32,128]{3,2,1,0:T(8,128)S(1)} %get-tuple-element.39.partial, bf16[4,16,16,192]{3,2,1,0:T(8,128)(2,1)S(1)} %bitcast.34, f32[7,7,192]{2,1,0:T(8,128)S(1)} %copy-done.1), custom_call_target="tpu_custom_call" | custom-call | tf_op jit(solution)/shard_map/emit/pallas_call | solution.py:304
  62.2 2.6 %collective-permute-start.18 = (bf16[240,128]{1,0:T(8,128)(2,1)S(1)}, bf16[240,128]{1,0:T(8,128)(2,1)S(1)}, u32[]{:S(2)}, u32[]{:S(2)}) collective-permute-start(bf16[240,128]{1,0:T(8,128)(2,1)S(1)} %pad_maximum_fusion.11), channel_id=1, source_target_pairs={{0,48},{16,32},{32,16},{48,0},{1,49},{17,33},{33,17},{49,1},{2,50}... | collective-permute-start | bytes 184328 | tf_op jit(solution)/shard_map/ppermute | solution.py:34
  64.8 0.5 collective-permute-start.17
  65.2 0.9 %collective-permute-start.16 = (bf16[240,128]{1,0:T(8,128)(2,1)S(1)}, bf16[240,128]{1,0:T(8,128)(2,1)S(1)}, u32[]{:S(2)}, u32[]{:S(2)}) collective-permute-start(bf16[240,128]{1,0:T(8,128)(2,1)S(1)} %pad_maximum_fusion.11), channel_id=1, source_target_pairs={{0,32},{16,48},{32,0},{48,16},{1,33},{17,49},{33,1},{49,17},{2,34}... | collective-permute-start | bytes 184328 | tf_op jit(solution)/shard_map/ppermute | solution.py:34
  66.1 0.4 collective-permute-done.18
  66.6 1.3 %collective-permute-done.17 = bf16[240,128]{1,0:T(8,128)(2,1)S(1)} collective-permute-done((bf16[240,128]{1,0:T(8,128)(2,1)S(1)}, bf16[240,128]{1,0:T(8,128)(2,1)S(1)}, u32[]{:S(2)}, u32[]{:S(2)}) %collective-permute-start.17) | collective-permute-done | bytes 61472 | tf_op jit(solution)/shard_map/ppermute | solution.py:34
  67.9 2.1 %collective-permute-done.16 = bf16[240,128]{1,0:T(8,128)(2,1)S(1)} collective-permute-done((bf16[240,128]{1,0:T(8,128)(2,1)S(1)}, bf16[240,128]{1,0:T(8,128)(2,1)S(1)}, u32[]{:S(2)}, u32[]{:S(2)}) %collective-permute-start.16) | collective-permute-done | bytes 61472 | tf_op jit(solution)/shard_map/ppermute | solution.py:34
  70.0 1.3 %collective-permute-start.21 = (bf16[240,128]{1,0:T(8,128)(2,1)S(1)}, bf16[240,128]{1,0:T(8,128)(2,1)S(1)}, u32[]{:S(2)}, u32[]{:S(2)}) collective-permute-start(bf16[240,128]{1,0:T(8,128)(2,1)S(1)} %pad_maximum_fusion.12), channel_id=1, source_target_pairs={{0,192},{64,128},{128,64},{192,0},{1,193},{65,129},{129,65},{193,1... | collective-permute-start | bytes 184328 | tf_op jit(solution)/shard_map/ppermute | solution.py:34
  71.3 2.7 %collective-permute-start.19 = (bf16[240,128]{1,0:T(8,128)(2,1)S(1)}, bf16[240,128]{1,0:T(8,128)(2,1)S(1)}, u32[]{:S(2)}, u32[]{:S(2)}) collective-permute-start(bf16[240,128]{1,0:T(8,128)(2,1)S(1)} %pad_maximum_fusion.12), channel_id=1, source_target_pairs={{0,128},{64,192},{128,0},{192,64},{1,129},{65,193},{129,1},{193,65... | collective-permute-start | bytes 184328 | tf_op jit(solution)/shard_map/ppermute | solution.py:34
  73.9 0.4 collective-permute-done.21
  74.4 1.8 %collective-permute-done.19 = bf16[240,128]{1,0:T(8,128)(2,1)S(1)} collective-permute-done((bf16[240,128]{1,0:T(8,128)(2,1)S(1)}, bf16[240,128]{1,0:T(8,128)(2,1)S(1)}, u32[]{:S(2)}, u32[]{:S(2)}) %collective-permute-start.19) | collective-permute-done | bytes 61472 | tf_op jit(solution)/shard_map/ppermute | solution.py:34
  76.3 4.9 %collective-permute-start.22 = (f32[192,128]{1,0:T(8,128)S(1)}, f32[192,128]{1,0:T(8,128)S(1)}, u32[]{:S(2)}, u32[]{:S(2)}) collective-permute-start(f32[192,128]{1,0:T(8,128)S(1)} %pad_maximum_fusion.8.held), channel_id=1, source_target_pairs={{0,8},{8,0},{1,9},{9,1},{2,10},{10,2},{3,11},{11,3},{4,12},{12,4},... | collective-permute-start | bytes 294920 | tf_op jit(solution)/shard_map/ppermute | solution.py:34
  81.1 0.9 %collective-permute-done.22.other = f32[192,128]{1,0:T(8,128)S(1)} collective-permute-done((f32[192,128]{1,0:T(8,128)S(1)}, f32[192,128]{1,0:T(8,128)S(1)}, u32[]{:S(2)}, u32[]{:S(2)}) %collective-permute-start.22) | collective-permute-done | bytes 98336 | tf_op jit(solution)/shard_map/ppermute | solution.py:34
  82.1 1.3 %finish.1 = (f32[24,768]{1,0:T(8,128)}, f32[96,192]{1,0:T(8,128)}, f32[7,7,192]{2,1,0:T(8,128)}) custom-call(s32[1,7]{1,0:T(1,128)S(1)} %add_bitcast_fusion.info, f32[192,128]{1,0:T(8,128)S(1)} %pad_maximum_fusion.8.held, f32[192,128]{1,0:T(8,128)S(1)} %collective-permute-done.22.other), custom_call_target="tpu_custom_call" | custom-call | flops 1000000000 | bytes 1000000 | tf_op jit(solution)/shard_map/finish/pallas_call | solution.py:304
  (46 shorter events, 0.5 us)
Async XLA Ops:
  2.0 1.0 %copy-start.4 = (bf16[1,4,16,16,192]{4,3,2,1,0:T(8,128)(2,1)S(1)}, bf16[1,4,16,16,192]{4,3,2,1,0:T(8,128)(2,1)}, u32[]{:S(2)}) copy-start(bf16[1,4,16,16,192]{4,3,2,1,0:T(8,128)(2,1)} %param.9) | copy-start | bytes 1179652
  3.1 5.0 %copy-start.2 = (bf16[96,192]{1,0:T(8,128)(2,1)S(1)}, bf16[96,192]{1,0:T(8,128)(2,1)}, u32[]{:S(2)}) copy-start(bf16[96,192]{1,0:T(8,128)(2,1)} %project.1) | copy-start | bytes 110596
  3.1 5.0 %copy-start.3 = (bf16[24,768]{1,0:T(8,128)(2,1)S(1)}, bf16[24,768]{1,0:T(8,128)(2,1)}, u32[]{:S(2)}) copy-start(bf16[24,768]{1,0:T(8,128)(2,1)} %expand) | copy-start | bytes 110596
  3.9 4.2 %collective-permute-start.1 = (bf16[3,32,192]{2,0,1:T(4,128)(2,1)S(1)}, bf16[3,32,192]{2,0,1:T(4,128)(2,1)S(1)}, u32[]{:S(2)}, u32[]{:S(2)}) collective-permute-start(bf16[3,32,192]{2,0,1:T(4,128)(2,1)S(1)} %get-tuple-element.62), channel_id=1, source_target_pairs={{0,8},{8,0},{1,9},{9,1},{2,10},{10,2},{3,11},{11,3},{4,12},{12,4},... | collective-permute-start | bytes 110600 | tf_op jit(solution)/shard_map/ppermute | solution.py:34
  7.2 5.7 %collective-permute-start = (bf16[3,32,192]{2,0,1:T(4,128)(2,1)S(1)}, bf16[3,32,192]{2,0,1:T(4,128)(2,1)S(1)}, u32[]{:S(2)}, u32[]{:S(2)}) collective-permute-start(bf16[3,32,192]{2,0,1:T(4,128)(2,1)S(1)} %get-tuple-element.61), channel_id=1, source_target_pairs={{0,24},{8,16},{16,8},{24,0},{32,56},{40,48},{48,40},{56,32},{1,25}... | collective-permute-start | bytes 110600 | tf_op jit(solution)/shard_map/ppermute | solution.py:355
  8.7 9.7 %collective-permute-start.4 = (bf16[144,128]{1,0:T(8,128)(2,1)S(1)}, bf16[144,128]{1,0:T(8,128)(2,1)S(1)}, u32[]{:S(2)}, u32[]{:S(2)}) collective-permute-start(bf16[144,128]{1,0:T(8,128)(2,1)S(1)} %pack.1), channel_id=1, source_target_pairs={{0,7},{1,6},{2,5},{3,4},{4,3},{5,2},{6,1},{7,0},{8,15},{9,14},{10,... | collective-permute-start | bytes 110600 | tf_op jit(solution)/shard_map/ppermute | solution.py:34
  13.4 11.7 %copy-start.1 = (f32[7,7,192]{2,1,0:T(8,128)S(1)}, f32[7,7,192]{2,1,0:T(8,128)}, u32[]{:S(2)}) copy-start(f32[7,7,192]{2,1,0:T(8,128)} %kernel.5) | copy-start | bytes 112900
  13.4 7.2 %collective-permute-start.2 = (bf16[3,40,192]{2,1,0:T(8,128)(2,1)S(1)}, bf16[3,40,192]{2,1,0:T(8,128)(2,1)S(1)}, u32[]{:S(2)}, u32[]{:S(2)}) collective-permute-start(bf16[3,40,192]{2,1,0:T(8,128)(2,1)S(1)} %get-tuple-element.57), channel_id=1, source_target_pairs={{32,64},{48,80},{96,128},{112,144},{160,192},{176,208},{224,0},{24... | collective-permute-start | bytes 138248 | tf_op jit(solution)/shard_map/ppermute | solution.py:372
  18.4 4.6 %collective-permute-start.3 = (bf16[3,40,192]{2,1,0:T(8,128)(2,1)S(1)}, bf16[3,40,192]{2,1,0:T(8,128)(2,1)S(1)}, u32[]{:S(2)}, u32[]{:S(2)}) collective-permute-start(bf16[3,40,192]{2,1,0:T(8,128)(2,1)S(1)} %get-tuple-element.58), channel_id=1, source_target_pairs={{0,32},{16,48},{32,0},{48,16},{1,33},{17,49},{33,1},{49,17},{2,34}... | collective-permute-start | bytes 138248 | tf_op jit(solution)/shard_map/ppermute | solution.py:34
  18.4 4.6 %collective-permute-start.5 = (bf16[2,144,128]{2,1,0:T(8,128)(2,1)S(1)}, bf16[2,144,128]{2,1,0:T(8,128)(2,1)S(1)}, u32[]{:S(2)}, u32[]{:S(2)}) collective-permute-start(bf16[2,144,128]{2,1,0:T(8,128)(2,1)S(1)} %pad_maximum_fusion.9), channel_id=1, source_target_pairs={{0,2},{1,3},{2,0},{3,1},{4,6},{5,7},{6,4},{7,5},{8,10},{9,11},{10,... | collective-permute-start | bytes 221192 | tf_op jit(solution)/shard_map/ppermute | solution.py:34
  23.1 5.8 %collective-permute-start.6 = (bf16[4,144,128]{2,1,0:T(8,128)(2,1)S(1)}, bf16[4,144,128]{2,1,0:T(8,128)(2,1)S(1)}, u32[]{:S(2)}, u32[]{:S(2)}) collective-permute-start(bf16[4,144,128]{2,1,0:T(8,128)(2,1)S(1)} %pad_maximum_fusion.6), channel_id=1, source_target_pairs={{0,1},{1,0},{2,3},{3,2},{4,5},{5,4},{6,7},{7,6},{8,9},{9,8},{10,11... | collective-permute-start | bytes 442376 | tf_op jit(solution)/shard_map/ppermute | solution.py:34
  25.1 6.5 %copy-start.7 = (f32[768]{0:T(1024)S(1)}, f32[768]{0:T(1024)}, u32[]{:S(2)}) copy-start(f32[768]{0:T(1024)} %param.16) | copy-start | bytes 9220
  25.1 7.7 %copy-start = (bf16[1,4,16,16,192]{4,3,2,1,0:T(8,128)(2,1)S(1)}, bf16[1,4,16,16,192]{4,3,2,1,0:T(8,128)(2,1)}, u32[]{:S(2)}) copy-start(bf16[1,4,16,16,192]{4,3,2,1,0:T(8,128)(2,1)} %param.10) | copy-start | bytes 1179652
  25.1 7.7 %copy-start.5 = (bf16[1,4,16,16,192]{4,3,2,1,0:T(8,128)(2,1)S(1)}, bf16[1,4,16,16,192]{4,3,2,1,0:T(8,128)(2,1)}, u32[]{:S(2)}) copy-start(bf16[1,4,16,16,192]{4,3,2,1,0:T(8,128)(2,1)} %param.9) | copy-start | bytes 1179652
  25.1 7.7 %copy-start.6 = (f32[192]{0:T(256)S(1)}, f32[192]{0:T(256)}, u32[]{:S(2)}) copy-start(f32[192]{0:T(256)} %param.14) | copy-start | bytes 2308
  28.9 3.9 %collective-permute-start.7 = (bf16[8,144,128]{2,1,0:T(8,128)(2,1)S(1)}, bf16[8,144,128]{2,1,0:T(8,128)(2,1)S(1)}, u32[]{:S(2)}, u32[]{:S(2)}) collective-permute-start(bf16[8,144,128]{2,1,0:T(8,128)(2,1)S(1)} %pad_maximum_fusion.4.held), channel_id=1, source_target_pairs={{0,8},{8,0},{1,9},{9,1},{2,10},{10,2},{3,11},{11,3},{4,12},{12,4},... | collective-permute-start | bytes 884744 | tf_op jit(solution)/shard_map/ppermute | solution.py:34
  41.6 1.6 %collective-permute-start.8 = (bf16[1248,128]{1,0:T(8,128)(2,1)S(1)}, bf16[1248,128]{1,0:T(8,128)(2,1)S(1)}, u32[]{:S(2)}, u32[]{:S(2)}) collective-permute-start(bf16[1248,128]{1,0:T(8,128)(2,1)S(1)} %get-tuple-element.34), channel_id=1, source_target_pairs={{0,8},{8,0},{1,9},{9,1},{2,10},{10,2},{3,11},{11,3},{4,12},{12,4},... | collective-permute-start | bytes 958472 | tf_op jit(solution)/shard_map/ppermute | solution.py:34
  42.1 3.9 %collective-permute-start.11 = (bf16[3,32,192]{2,0,1:T(4,128)(2,1)S(1)}, bf16[3,32,192]{2,0,1:T(4,128)(2,1)S(1)}, u32[]{:S(2)}, u32[]{:S(2)}) collective-permute-start(bf16[3,32,192]{2,0,1:T(4,128)(2,1)S(1)} %get-tuple-element.59), channel_id=1, source_target_pairs={{0,24},{8,16},{16,8},{24,0},{32,56},{40,48},{48,40},{56,32},{1,25}... | collective-permute-start | bytes 110600 | tf_op jit(solution)/shard_map/ppermute | solution.py:355
  42.5 1.3 %collective-permute-start.12 = (bf16[3,32,192]{2,0,1:T(4,128)(2,1)S(1)}, bf16[3,32,192]{2,0,1:T(4,128)(2,1)S(1)}, u32[]{:S(2)}, u32[]{:S(2)}) collective-permute-start(bf16[3,32,192]{2,0,1:T(4,128)(2,1)S(1)} %get-tuple-element.60), channel_id=1, source_target_pairs={{0,8},{8,0},{1,9},{9,1},{2,10},{10,2},{3,11},{11,3},{4,12},{12,4},... | collective-permute-start | bytes 110600 | tf_op jit(solution)/shard_map/ppermute | solution.py:34
  43.8 5.6 %collective-permute-start.9 = (bf16[672,128]{1,0:T(8,128)(2,1)S(1)}, bf16[672,128]{1,0:T(8,128)(2,1)S(1)}, u32[]{:S(2)}, u32[]{:S(2)}) collective-permute-start(bf16[672,128]{1,0:T(8,128)(2,1)S(1)} %pad_maximum_fusion.5), channel_id=1, source_target_pairs={{0,1},{1,0},{2,3},{3,2},{4,5},{5,4},{6,7},{7,6},{8,9},{9,8},{10,11... | collective-permute-start | bytes 516104 | tf_op jit(solution)/shard_map/ppermute | solution.py:34
  46.5 7.7 %collective-permute-start.13 = (bf16[3,40,192]{2,1,0:T(8,128)(2,1)S(1)}, bf16[3,40,192]{2,1,0:T(8,128)(2,1)S(1)}, u32[]{:S(2)}, u32[]{:S(2)}) collective-permute-start(bf16[3,40,192]{2,1,0:T(8,128)(2,1)S(1)} %get-tuple-element.55), channel_id=1, source_target_pairs={{32,64},{48,80},{96,128},{112,144},{160,192},{176,208},{224,0},{24... | collective-permute-start | bytes 138248 | tf_op jit(solution)/shard_map/ppermute | solution.py:372
  49.4 4.9 %collective-permute-start.14 = (bf16[3,40,192]{2,1,0:T(8,128)(2,1)S(1)}, bf16[3,40,192]{2,1,0:T(8,128)(2,1)S(1)}, u32[]{:S(2)}, u32[]{:S(2)}) collective-permute-start(bf16[3,40,192]{2,1,0:T(8,128)(2,1)S(1)} %get-tuple-element.56), channel_id=1, source_target_pairs={{0,32},{16,48},{32,0},{48,16},{1,33},{17,49},{33,1},{49,17},{2,34}... | collective-permute-start | bytes 138248 | tf_op jit(solution)/shard_map/ppermute | solution.py:34
  49.5 7.7 %collective-permute-start.10 = (bf16[384,128]{1,0:T(8,128)(2,1)S(1)}, bf16[384,128]{1,0:T(8,128)(2,1)S(1)}, u32[]{:S(2)}, u32[]{:S(2)}) collective-permute-start(bf16[384,128]{1,0:T(8,128)(2,1)S(1)} %pad_maximum_fusion.7), channel_id=1, source_target_pairs={{0,2},{1,3},{2,0},{3,1},{4,6},{5,7},{6,4},{7,5},{8,10},{9,11},{10,... | collective-permute-start | bytes 294920 | tf_op jit(solution)/shard_map/ppermute | solution.py:34
  57.2 4.9 %collective-permute-start.15 = (bf16[240,128]{1,0:T(8,128)(2,1)S(1)}, bf16[240,128]{1,0:T(8,128)(2,1)S(1)}, u32[]{:S(2)}, u32[]{:S(2)}) collective-permute-start(bf16[240,128]{1,0:T(8,128)(2,1)S(1)} %pad_maximum_fusion.10), channel_id=1, source_target_pairs={{0,7},{1,6},{2,5},{3,4},{4,3},{5,2},{6,1},{7,0},{8,15},{9,14},{10,... | collective-permute-start | bytes 184328 | tf_op jit(solution)/shard_map/ppermute | solution.py:34
  62.2 4.4 %collective-permute-start.18 = (bf16[240,128]{1,0:T(8,128)(2,1)S(1)}, bf16[240,128]{1,0:T(8,128)(2,1)S(1)}, u32[]{:S(2)}, u32[]{:S(2)}) collective-permute-start(bf16[240,128]{1,0:T(8,128)(2,1)S(1)} %pad_maximum_fusion.11), channel_id=1, source_target_pairs={{0,48},{16,32},{32,16},{48,0},{1,49},{17,33},{33,17},{49,1},{2,50}... | collective-permute-start | bytes 184328 | tf_op jit(solution)/shard_map/ppermute | solution.py:34
  64.8 3.1 %collective-permute-start.17 = (bf16[240,128]{1,0:T(8,128)(2,1)S(1)}, bf16[240,128]{1,0:T(8,128)(2,1)S(1)}, u32[]{:S(2)}, u32[]{:S(2)}) collective-permute-start(bf16[240,128]{1,0:T(8,128)(2,1)S(1)} %pad_maximum_fusion.11), channel_id=1, source_target_pairs={{0,16},{16,0},{32,48},{48,32},{1,17},{17,1},{33,49},{49,33},{2,18}... | collective-permute-start | bytes 184328 | tf_op jit(solution)/shard_map/ppermute | solution.py:34
  65.2 4.7 %collective-permute-start.16 = (bf16[240,128]{1,0:T(8,128)(2,1)S(1)}, bf16[240,128]{1,0:T(8,128)(2,1)S(1)}, u32[]{:S(2)}, u32[]{:S(2)}) collective-permute-start(bf16[240,128]{1,0:T(8,128)(2,1)S(1)} %pad_maximum_fusion.11), channel_id=1, source_target_pairs={{0,32},{16,48},{32,0},{48,16},{1,33},{17,49},{33,1},{49,17},{2,34}... | collective-permute-start | bytes 184328 | tf_op jit(solution)/shard_map/ppermute | solution.py:34
  70.0 4.4 %collective-permute-start.21 = (bf16[240,128]{1,0:T(8,128)(2,1)S(1)}, bf16[240,128]{1,0:T(8,128)(2,1)S(1)}, u32[]{:S(2)}, u32[]{:S(2)}) collective-permute-start(bf16[240,128]{1,0:T(8,128)(2,1)S(1)} %pad_maximum_fusion.12), channel_id=1, source_target_pairs={{0,192},{64,128},{128,64},{192,0},{1,193},{65,129},{129,65},{193,1... | collective-permute-start | bytes 184328 | tf_op jit(solution)/shard_map/ppermute | solution.py:34
  71.3 3.1 %collective-permute-start.20 = (bf16[240,128]{1,0:T(8,128)(2,1)S(1)}, bf16[240,128]{1,0:T(8,128)(2,1)S(1)}, u32[]{:S(2)}, u32[]{:S(2)}) collective-permute-start(bf16[240,128]{1,0:T(8,128)(2,1)S(1)} %pad_maximum_fusion.12), channel_id=1, source_target_pairs={{0,64},{64,0},{128,192},{192,128},{1,65},{65,1},{129,193},{193,129... | collective-permute-start | bytes 184328 | tf_op jit(solution)/shard_map/ppermute | solution.py:34
  71.3 4.9 %collective-permute-start.19 = (bf16[240,128]{1,0:T(8,128)(2,1)S(1)}, bf16[240,128]{1,0:T(8,128)(2,1)S(1)}, u32[]{:S(2)}, u32[]{:S(2)}) collective-permute-start(bf16[240,128]{1,0:T(8,128)(2,1)S(1)} %pad_maximum_fusion.12), channel_id=1, source_target_pairs={{0,128},{64,192},{128,0},{192,64},{1,129},{65,193},{129,1},{193,65... | collective-permute-start | bytes 184328 | tf_op jit(solution)/shard_map/ppermute | solution.py:34
  76.3 5.8 %collective-permute-start.22 = (f32[192,128]{1,0:T(8,128)S(1)}, f32[192,128]{1,0:T(8,128)S(1)}, u32[]{:S(2)}, u32[]{:S(2)}) collective-permute-start(f32[192,128]{1,0:T(8,128)S(1)} %pad_maximum_fusion.8.held), channel_id=1, source_target_pairs={{0,8},{8,0},{1,9},{9,1},{2,10},{10,2},{3,11},{11,3},{4,12},{12,4},... | collective-permute-start | bytes 294920 | tf_op jit(solution)/shard_map/ppermute | solution.py:34

commit v7 on v6

--- a/solution.py
+++ b/solution.py
@@ -492,7 +492,7 @@
     taps, grad_tiles = tie(taps, grad_tiles)
     for axis in ("x", "y"):
         part = jnp.concatenate([held.astype(bf16), *split_high_low(taps)])
-        parts = [part] + [swap(part, axis, i) for i in (2, 1, 3)]
+        parts = [part] + [swap(part, axis, i) for i in (1, 3, 2)]
         held = rows_sum(*[p[:SHARD].astype(f32) for p in parts])
         taps = rows_sum(*[join(p[SHARD:]) for p in parts])
     held = jnp.concatenate([held, taps])

time: 83.5 us -> 83.8 us (level)
  waiting for transfers between devices: 17.2 us -> 19.2 us
  starting transfers between devices: 39.9 us -> 38.2 us
    ppermute x19, waiting for transfers between devices: 15.7 us -> 17.6 us  [swap(): return lax.ppermute(value, axis, [(i, i ^ bit) for i in range(SIZES[axis])])]
    ppermute x19, starting transfers between devices: 31.6 us -> 29.8 us  [swap(): return lax.ppermute(value, axis, [(i, i ^ bit) for i in range(SIZES[axis])])]
where the time goes in v7:
time: 83.8 us; the launch traced here: 83.6 us
  starting transfers between devices  38.2 us (46%)
  Pallas kernels  20.6 us (25%)
  waiting for transfers between devices  19.2 us (23%)
  other arithmetic  2.96 us (4%)
  between operations  1.6 us (2%)
  local copies, waits for them, and re-layouts  1.14 us (1%)
    ppermute x19, starting transfers between devices, swap(): return lax.ppermute(value, axis, [(i, i ^ bit) for i in range(SIZES[axis])])  29.8 us
    pallas_call x7, Pallas kernels, call(): pl.pallas_call(kernel, out_shape=[jax.ShapeDtypeStruct(shape, dtype) for...  20.6 us
    ppermute x19, waiting for transfers between devices, swap(): return lax.ppermute(value, axis, [(i, i ^ bit) for i in range(SIZES[axis])])  17.6 us
    ppermute x2, starting transfers between devices, end_rims(): lax.ppermute(jnp.where(upper == 0, north_edge, south_edge), ('y', 'x'), p...  7.9 us
  transfers between devices with their start and end apart: 23, of which 13 were waited for; matrix products, arithmetic and copies ran while one was open for 2% of the time, Pallas kernels for 12%

profile of v7, /device:TPU:1, one launch (start us, length us, event | category | flops | bytes accessed | tf_op | source)
XLA Modules:
  0.0 83.6 jit_solution(9992517085603953024)
XLA Ops:
  1.3 0.7 add_bitcast_fusion.info
  2.0 1.0 %copy-done.4 = bf16[1,4,16,16,192]{4,3,2,1,0:T(8,128)(2,1)S(1)} copy-done((bf16[1,4,16,16,192]{4,3,2,1,0:T(8,128)(2,1)S(1)}, bf16[1,4,16,16,192]{4,3,2,1,0:T(8,128)(2,1)}, u32[]{:S(2)}) %copy-start.4) | copy-done | bytes 393240
  3.1 0.7 place.1
  3.8 0.1 select_bitcast_fusion.7
  3.9 3.3 %collective-permute-start.1 = (bf16[3,32,192]{2,0,1:T(4,128)(2,1)S(1)}, bf16[3,32,192]{2,0,1:T(4,128)(2,1)S(1)}, u32[]{:S(2)}, u32[]{:S(2)}) collective-permute-start(bf16[3,32,192]{2,0,1:T(4,128)(2,1)S(1)} %get-tuple-element.62), channel_id=1, source_target_pairs={{0,8},{8,0},{1,9},{9,1},{2,10},{10,2},{3,11},{11,3},{4,12},{12,4},... | collective-permute-start | bytes 110600 | tf_op jit(solution)/shard_map/ppermute | solution.py:34
  7.2 0.0 collective-permute-start
  7.2 0.9 %collective-permute-done.1 = bf16[3,32,192]{2,0,1:T(4,128)(2,1)S(1)} collective-permute-done((bf16[3,32,192]{2,0,1:T(4,128)(2,1)S(1)}, bf16[3,32,192]{2,0,1:T(4,128)(2,1)S(1)}, u32[]{:S(2)}, u32[]{:S(2)}) %collective-permute-start.1) | collective-permute-done | bytes 36896 | tf_op jit(solution)/shard_map/ppermute | solution.py:34
  8.1 0.6 pack.1
  8.7 4.2 %collective-permute-start.4 = (bf16[144,128]{1,0:T(8,128)(2,1)S(1)}, bf16[144,128]{1,0:T(8,128)(2,1)S(1)}, u32[]{:S(2)}, u32[]{:S(2)}) collective-permute-start(bf16[144,128]{1,0:T(8,128)(2,1)S(1)} %pack.1), channel_id=1, source_target_pairs={{0,7},{1,6},{2,5},{3,4},{4,3},{5,2},{6,1},{7,0},{8,15},{9,14},{10,... | collective-permute-start | bytes 110600 | tf_op jit(solution)/shard_map/ppermute | solution.py:34
  12.9 0.0 collective-permute-done
  12.9 0.1 select_bitcast_fusion.5
  13.0 0.4 pad_maximum_fusion.3
  13.4 0.0 copy-start.1
  13.4 5.0 %collective-permute-start.2 = (bf16[3,40,192]{2,1,0:T(8,128)(2,1)S(1)}, bf16[3,40,192]{2,1,0:T(8,128)(2,1)S(1)}, u32[]{:S(2)}, u32[]{:S(2)}) collective-permute-start(bf16[3,40,192]{2,1,0:T(8,128)(2,1)S(1)} %get-tuple-element.57), channel_id=1, source_target_pairs={{32,64},{48,80},{96,128},{112,144},{160,192},{176,208},{224,0},{24... | collective-permute-start | bytes 138248 | tf_op jit(solution)/shard_map/ppermute | solution.py:372
  18.4 0.0 collective-permute-start.3
  18.4 2.2 %collective-permute-start.5 = (bf16[2,144,128]{2,1,0:T(8,128)(2,1)S(1)}, bf16[2,144,128]{2,1,0:T(8,128)(2,1)S(1)}, u32[]{:S(2)}, u32[]{:S(2)}) collective-permute-start(bf16[2,144,128]{2,1,0:T(8,128)(2,1)S(1)} %pad_maximum_fusion.9), channel_id=1, source_target_pairs={{0,2},{1,3},{2,0},{3,1},{4,6},{5,7},{6,4},{7,5},{8,10},{9,11},{10,... | collective-permute-start | bytes 221192 | tf_op jit(solution)/shard_map/ppermute | solution.py:34
  20.6 0.0 collective-permute-done.2
  20.6 2.4 %collective-permute-done.3 = bf16[3,40,192]{2,1,0:T(8,128)(2,1)S(1)} collective-permute-done((bf16[3,40,192]{2,1,0:T(8,128)(2,1)S(1)}, bf16[3,40,192]{2,1,0:T(8,128)(2,1)S(1)}, u32[]{:S(2)}, u32[]{:S(2)}) %collective-permute-start.3) | collective-permute-done | bytes 46112 | tf_op jit(solution)/shard_map/ppermute | solution.py:34
  23.0 0.0 collective-permute-done.5
  23.1 1.7 %collective-permute-start.6 = (bf16[4,144,128]{2,1,0:T(8,128)(2,1)S(1)}, bf16[4,144,128]{2,1,0:T(8,128)(2,1)S(1)}, u32[]{:S(2)}, u32[]{:S(2)}) collective-permute-start(bf16[4,144,128]{2,1,0:T(8,128)(2,1)S(1)} %pad_maximum_fusion.6), channel_id=1, source_target_pairs={{0,1},{1,0},{2,3},{3,2},{4,5},{5,4},{6,7},{7,6},{8,9},{9,8},{10,11... | collective-permute-start | bytes 442376 | tf_op jit(solution)/shard_map/ppermute | solution.py:34
  24.8 0.3 fusion.2.padded
  25.1 0.0 copy-start.7
  25.1 0.0 copy-start
  25.1 0.0 copy-start.5
  25.2 0.0 copy-start.6
  25.2 3.7 %field.1 = (f32[3,22,40,128]{3,2,1,0:T(8,128)S(1)}, f32[3,16,32,128]{3,2,1,0:T(8,128)S(1)}) custom-call(f32[38,40,192]{2,1,0:T(8,128)S(1)} %fusion.2.padded, f32[7,7,192]{2,1,0:T(8,128)S(1)} %copy-done.1), custom_call_target="tpu_custom_call" | custom-call | tf_op jit(solution)/shard_map/field/pallas_call | solution.py:304
  28.9 0.0 collective-permute-done.6
  28.9 2.7 %collective-permute-start.7 = (bf16[8,144,128]{2,1,0:T(8,128)(2,1)S(1)}, bf16[8,144,128]{2,1,0:T(8,128)(2,1)S(1)}, u32[]{:S(2)}, u32[]{:S(2)}) collective-permute-start(bf16[8,144,128]{2,1,0:T(8,128)(2,1)S(1)} %pad_maximum_fusion.4.held), channel_id=1, source_target_pairs={{0,8},{8,0},{1,9},{9,1},{2,10},{10,2},{3,11},{11,3},{4,12},{12,4},... | collective-permute-start | bytes 884744 | tf_op jit(solution)/shard_map/ppermute | solution.py:34
  31.6 1.2 %collective-permute-done.7.other = bf16[8,144,128]{2,1,0:T(8,128)(2,1)S(1)} collective-permute-done((bf16[8,144,128]{2,1,0:T(8,128)(2,1)S(1)}, bf16[8,144,128]{2,1,0:T(8,128)(2,1)S(1)}, u32[]{:S(2)}, u32[]{:S(2)}) %collective-permute-start.7) | collective-permute-done | bytes 294944 | tf_op jit(solution)/shard_map/ppermute | solution.py:34
  32.8 8.8 %block.1 = (f32[4,16,16,192]{3,2,1,0:T(8,128)}, bf16[32,32,192]{2,1,0:T(8,128)(2,1)S(1)}, f32[1152,128]{1,0:T(8,128)S(1)}, bf16[1248,128]{1,0:T(8,128)(2,1)S(1)}, f32[48,128]{1,0:T(8,128)S(1)}) custom-call(s32[1,7]{1,0:T(1,128)S(1)} %add_bitcast_fusion.info, f32[3,22,40,128]{3,2,1,0:T(8,128)S(1)} %get-tuple-element.27.planes, ...), custom_call_target="tpu_custom_call" | custom-call | flops 14000000000 | bytes 14000000 | tf_op jit(solution)/shard_map/block/pallas_call | solution.py:304
  41.6 0.4 collective-permute-start.8
  42.0 0.1 select_bitcast_fusion.3
  42.1 0.4 collective-permute-start.11
  42.5 0.4 collective-permute-start.12
  42.9 0.4 collective-permute-done.8
  43.2 0.1 convert_add_fusion
  43.4 0.4 collective-permute-done.12
  43.8 0.7 collective-permute-start.9
  44.5 1.6 %collective-permute-done.11 = bf16[3,32,192]{2,0,1:T(4,128)(2,1)S(1)} collective-permute-done((bf16[3,32,192]{2,0,1:T(4,128)(2,1)S(1)}, bf16[3,32,192]{2,0,1:T(4,128)(2,1)S(1)}, u32[]{:S(2)}, u32[]{:S(2)}) %collective-permute-start.11) | collective-permute-done | bytes 36896 | tf_op jit(solution)/shard_map/ppermute | solution.py:355
  46.0 0.1 select_bitcast_fusion.1
  46.1 0.4 pad_maximum_fusion.2
  46.5 2.9 %collective-permute-start.13 = (bf16[3,40,192]{2,1,0:T(8,128)(2,1)S(1)}, bf16[3,40,192]{2,1,0:T(8,128)(2,1)S(1)}, u32[]{:S(2)}, u32[]{:S(2)}) collective-permute-start(bf16[3,40,192]{2,1,0:T(8,128)(2,1)S(1)} %get-tuple-element.55), channel_id=1, source_target_pairs={{32,64},{48,80},{96,128},{112,144},{160,192},{176,208},{224,0},{24... | collective-permute-start | bytes 138248 | tf_op jit(solution)/shard_map/ppermute | solution.py:372
  49.4 0.0 collective-permute-start.14
  49.5 1.3 %collective-permute-start.10 = (bf16[384,128]{1,0:T(8,128)(2,1)S(1)}, bf16[384,128]{1,0:T(8,128)(2,1)S(1)}, u32[]{:S(2)}, u32[]{:S(2)}) collective-permute-start(bf16[384,128]{1,0:T(8,128)(2,1)S(1)} %pad_maximum_fusion.7), channel_id=1, source_target_pairs={{0,2},{1,3},{2,0},{3,1},{4,6},{5,7},{6,4},{7,5},{8,10},{9,11},{10,... | collective-permute-start | bytes 294920 | tf_op jit(solution)/shard_map/ppermute | solution.py:34
  50.8 3.5 %collective-permute-done.14 = bf16[3,40,192]{2,1,0:T(8,128)(2,1)S(1)} collective-permute-done((bf16[3,40,192]{2,1,0:T(8,128)(2,1)S(1)}, bf16[3,40,192]{2,1,0:T(8,128)(2,1)S(1)}, u32[]{:S(2)}, u32[]{:S(2)}) %collective-permute-start.14) | collective-permute-done | bytes 46112 | tf_op jit(solution)/shard_map/ppermute | solution.py:34
  54.3 0.3 fusion.5.padded
  54.6 2.5 %spread.1 = (f32[3,22,40,128]{3,2,1,0:T(8,128)S(1)}, f32[3,16,32,128]{3,2,1,0:T(8,128)S(1)}) custom-call(f32[38,40,192]{2,1,0:T(8,128)S(1)} %fusion.5.padded, f32[7,7,192]{2,1,0:T(8,128)S(1)} %copy-done.1), custom_call_target="tpu_custom_call" | custom-call | tf_op jit(solution)/shard_map/spread/pallas_call | solution.py:304
  57.2 0.0 collective-permute-done.10
  57.3 2.1 %collective-permute-start.15 = (bf16[240,128]{1,0:T(8,128)(2,1)S(1)}, bf16[240,128]{1,0:T(8,128)(2,1)S(1)}, u32[]{:S(2)}, u32[]{:S(2)}) collective-permute-start(bf16[240,128]{1,0:T(8,128)(2,1)S(1)} %pad_maximum_fusion.10), channel_id=1, source_target_pairs={{0,7},{1,6},{2,5},{3,4},{4,3},{5,2},{6,1},{7,0},{8,15},{9,14},{10,... | collective-permute-start | bytes 184328 | tf_op jit(solution)/shard_map/ppermute | solution.py:34
  59.4 3.0 %emit.1 = f32[4,16,16,192]{3,2,1,0:T(8,128)} custom-call(s32[1,7]{1,0:T(1,128)S(1)} %add_bitcast_fusion.info, f32[3,22,40,128]{3,2,1,0:T(8,128)S(1)} %get-tuple-element.41.planes, f32[3,16,32,128]{3,2,1,0:T(8,128)S(1)} %get-tuple-element.39.partial, bf16[4,16,16,192]{3,2,1,0:T(8,128)(2,1)S(1)} %bitcast.34, f32[7,7,192]{2,1,0:T(8,128)S(1)} %copy-done.1), custom_call_target="tpu_custom_call" | custom-call | tf_op jit(solution)/shard_map/emit/pallas_call | solution.py:304
  62.3 0.0 collective-permute-done.15
  62.4 3.1 %collective-permute-start.18 = (bf16[240,128]{1,0:T(8,128)(2,1)S(1)}, bf16[240,128]{1,0:T(8,128)(2,1)S(1)}, u32[]{:S(2)}, u32[]{:S(2)}) collective-permute-start(bf16[240,128]{1,0:T(8,128)(2,1)S(1)} %pad_maximum_fusion.11), channel_id=1, source_target_pairs={{0,32},{16,48},{32,0},{48,16},{1,33},{17,49},{33,1},{49,17},{2,34}... | collective-permute-start | bytes 184328 | tf_op jit(solution)/shard_map/ppermute | solution.py:34
  65.5 0.0 collective-permute-start.17
  65.5 0.1 collective-permute-start.16
  65.6 1.5 %collective-permute-done.18 = bf16[240,128]{1,0:T(8,128)(2,1)S(1)} collective-permute-done((bf16[240,128]{1,0:T(8,128)(2,1)S(1)}, bf16[240,128]{1,0:T(8,128)(2,1)S(1)}, u32[]{:S(2)}, u32[]{:S(2)}) %collective-permute-start.18) | collective-permute-done | bytes 61472 | tf_op jit(solution)/shard_map/ppermute | solution.py:34
  67.1 3.0 %collective-permute-done.17 = bf16[240,128]{1,0:T(8,128)(2,1)S(1)} collective-permute-done((bf16[240,128]{1,0:T(8,128)(2,1)S(1)}, bf16[240,128]{1,0:T(8,128)(2,1)S(1)}, u32[]{:S(2)}, u32[]{:S(2)}) %collective-permute-start.17) | collective-permute-done | bytes 61472 | tf_op jit(solution)/shard_map/ppermute | solution.py:34
  70.3 0.1 collective-permute-start.21
  70.4 3.2 %collective-permute-start.20 = (bf16[240,128]{1,0:T(8,128)(2,1)S(1)}, bf16[240,128]{1,0:T(8,128)(2,1)S(1)}, u32[]{:S(2)}, u32[]{:S(2)}) collective-permute-start(bf16[240,128]{1,0:T(8,128)(2,1)S(1)} %pad_maximum_fusion.12), channel_id=1, source_target_pairs={{0,192},{64,128},{128,64},{192,0},{1,193},{65,129},{129,65},{193,1... | collective-permute-start | bytes 184328 | tf_op jit(solution)/shard_map/ppermute | solution.py:34
  73.6 1.4 %collective-permute-done.21 = bf16[240,128]{1,0:T(8,128)(2,1)S(1)} collective-permute-done((bf16[240,128]{1,0:T(8,128)(2,1)S(1)}, bf16[240,128]{1,0:T(8,128)(2,1)S(1)}, u32[]{:S(2)}, u32[]{:S(2)}) %collective-permute-start.21) | collective-permute-done | bytes 61472 | tf_op jit(solution)/shard_map/ppermute | solution.py:34
  75.0 0.6 collective-permute-done.20
  75.6 1.4 %collective-permute-done.19 = bf16[240,128]{1,0:T(8,128)(2,1)S(1)} collective-permute-done((bf16[240,128]{1,0:T(8,128)(2,1)S(1)}, bf16[240,128]{1,0:T(8,128)(2,1)S(1)}, u32[]{:S(2)}, u32[]{:S(2)}) %collective-permute-start.19) | collective-permute-done | bytes 61472 | tf_op jit(solution)/shard_map/ppermute | solution.py:34
  77.0 4.4 %collective-permute-start.22 = (f32[192,128]{1,0:T(8,128)S(1)}, f32[192,128]{1,0:T(8,128)S(1)}, u32[]{:S(2)}, u32[]{:S(2)}) collective-permute-start(f32[192,128]{1,0:T(8,128)S(1)} %pad_maximum_fusion.8.held), channel_id=1, source_target_pairs={{0,8},{8,0},{1,9},{9,1},{2,10},{10,2},{3,11},{11,3},{4,12},{12,4},... | collective-permute-start | bytes 294920 | tf_op jit(solution)/shard_map/ppermute | solution.py:34
  81.4 0.9 %collective-permute-done.22.other = f32[192,128]{1,0:T(8,128)S(1)} collective-permute-done((f32[192,128]{1,0:T(8,128)S(1)}, f32[192,128]{1,0:T(8,128)S(1)}, u32[]{:S(2)}, u32[]{:S(2)}) %collective-permute-start.22) | collective-permute-done | bytes 98336 | tf_op jit(solution)/shard_map/ppermute | solution.py:34
  82.3 1.3 %finish.1 = (f32[24,768]{1,0:T(8,128)}, f32[96,192]{1,0:T(8,128)}, f32[7,7,192]{2,1,0:T(8,128)}) custom-call(s32[1,7]{1,0:T(1,128)S(1)} %add_bitcast_fusion.info, f32[192,128]{1,0:T(8,128)S(1)} %pad_maximum_fusion.8.held, f32[192,128]{1,0:T(8,128)S(1)} %collective-permute-done.22.other), custom_call_target="tpu_custom_call" | custom-call | flops 1000000000 | bytes 1000000 | tf_op jit(solution)/shard_map/finish/pallas_call | solution.py:304
  (46 shorter events, 0.5 us)
Async XLA Ops:
  2.0 1.0 %copy-start.4 = (bf16[1,4,16,16,192]{4,3,2,1,0:T(8,128)(2,1)S(1)}, bf16[1,4,16,16,192]{4,3,2,1,0:T(8,128)(2,1)}, u32[]{:S(2)}) copy-start(bf16[1,4,16,16,192]{4,3,2,1,0:T(8,128)(2,1)} %param.9) | copy-start | bytes 1179652
  3.1 5.0 %copy-start.2 = (bf16[96,192]{1,0:T(8,128)(2,1)S(1)}, bf16[96,192]{1,0:T(8,128)(2,1)}, u32[]{:S(2)}) copy-start(bf16[96,192]{1,0:T(8,128)(2,1)} %project.1) | copy-start | bytes 110596
  3.1 5.0 %copy-start.3 = (bf16[24,768]{1,0:T(8,128)(2,1)S(1)}, bf16[24,768]{1,0:T(8,128)(2,1)}, u32[]{:S(2)}) copy-start(bf16[24,768]{1,0:T(8,128)(2,1)} %expand) | copy-start | bytes 110596
  3.9 4.2 %collective-permute-start.1 = (bf16[3,32,192]{2,0,1:T(4,128)(2,1)S(1)}, bf16[3,32,192]{2,0,1:T(4,128)(2,1)S(1)}, u32[]{:S(2)}, u32[]{:S(2)}) collective-permute-start(bf16[3,32,192]{2,0,1:T(4,128)(2,1)S(1)} %get-tuple-element.62), channel_id=1, source_target_pairs={{0,8},{8,0},{1,9},{9,1},{2,10},{10,2},{3,11},{11,3},{4,12},{12,4},... | collective-permute-start | bytes 110600 | tf_op jit(solution)/shard_map/ppermute | solution.py:34
  7.2 5.7 %collective-permute-start = (bf16[3,32,192]{2,0,1:T(4,128)(2,1)S(1)}, bf16[3,32,192]{2,0,1:T(4,128)(2,1)S(1)}, u32[]{:S(2)}, u32[]{:S(2)}) collective-permute-start(bf16[3,32,192]{2,0,1:T(4,128)(2,1)S(1)} %get-tuple-element.61), channel_id=1, source_target_pairs={{0,24},{8,16},{16,8},{24,0},{32,56},{40,48},{48,40},{56,32},{1,25}... | collective-permute-start | bytes 110600 | tf_op jit(solution)/shard_map/ppermute | solution.py:355
  8.7 9.7 %collective-permute-start.4 = (bf16[144,128]{1,0:T(8,128)(2,1)S(1)}, bf16[144,128]{1,0:T(8,128)(2,1)S(1)}, u32[]{:S(2)}, u32[]{:S(2)}) collective-permute-start(bf16[144,128]{1,0:T(8,128)(2,1)S(1)} %pack.1), channel_id=1, source_target_pairs={{0,7},{1,6},{2,5},{3,4},{4,3},{5,2},{6,1},{7,0},{8,15},{9,14},{10,... | collective-permute-start | bytes 110600 | tf_op jit(solution)/shard_map/ppermute | solution.py:34
  13.4 11.7 %copy-start.1 = (f32[7,7,192]{2,1,0:T(8,128)S(1)}, f32[7,7,192]{2,1,0:T(8,128)}, u32[]{:S(2)}) copy-start(f32[7,7,192]{2,1,0:T(8,128)} %kernel.5) | copy-start | bytes 112900
  13.4 7.2 %collective-permute-start.2 = (bf16[3,40,192]{2,1,0:T(8,128)(2,1)S(1)}, bf16[3,40,192]{2,1,0:T(8,128)(2,1)S(1)}, u32[]{:S(2)}, u32[]{:S(2)}) collective-permute-start(bf16[3,40,192]{2,1,0:T(8,128)(2,1)S(1)} %get-tuple-element.57), channel_id=1, source_target_pairs={{32,64},{48,80},{96,128},{112,144},{160,192},{176,208},{224,0},{24... | collective-permute-start | bytes 138248 | tf_op jit(solution)/shard_map/ppermute | solution.py:372
  18.4 4.6 %collective-permute-start.3 = (bf16[3,40,192]{2,1,0:T(8,128)(2,1)S(1)}, bf16[3,40,192]{2,1,0:T(8,128)(2,1)S(1)}, u32[]{:S(2)}, u32[]{:S(2)}) collective-permute-start(bf16[3,40,192]{2,1,0:T(8,128)(2,1)S(1)} %get-tuple-element.58), channel_id=1, source_target_pairs={{0,32},{16,48},{32,0},{48,16},{1,33},{17,49},{33,1},{49,17},{2,34}... | collective-permute-start | bytes 138248 | tf_op jit(solution)/shard_map/ppermute | solution.py:34
  18.4 4.6 %collective-permute-start.5 = (bf16[2,144,128]{2,1,0:T(8,128)(2,1)S(1)}, bf16[2,144,128]{2,1,0:T(8,128)(2,1)S(1)}, u32[]{:S(2)}, u32[]{:S(2)}) collective-permute-start(bf16[2,144,128]{2,1,0:T(8,128)(2,1)S(1)} %pad_maximum_fusion.9), channel_id=1, source_target_pairs={{0,2},{1,3},{2,0},{3,1},{4,6},{5,7},{6,4},{7,5},{8,10},{9,11},{10,... | collective-permute-start | bytes 221192 | tf_op jit(solution)/shard_map/ppermute | solution.py:34
  23.1 5.8 %collective-permute-start.6 = (bf16[4,144,128]{2,1,0:T(8,128)(2,1)S(1)}, bf16[4,144,128]{2,1,0:T(8,128)(2,1)S(1)}, u32[]{:S(2)}, u32[]{:S(2)}) collective-permute-start(bf16[4,144,128]{2,1,0:T(8,128)(2,1)S(1)} %pad_maximum_fusion.6), channel_id=1, source_target_pairs={{0,1},{1,0},{2,3},{3,2},{4,5},{5,4},{6,7},{7,6},{8,9},{9,8},{10,11... | collective-permute-start | bytes 442376 | tf_op jit(solution)/shard_map/ppermute | solution.py:34
  25.1 6.5 %copy-start.7 = (f32[768]{0:T(1024)S(1)}, f32[768]{0:T(1024)}, u32[]{:S(2)}) copy-start(f32[768]{0:T(1024)} %param.16) | copy-start | bytes 9220
  25.1 7.7 %copy-start = (bf16[1,4,16,16,192]{4,3,2,1,0:T(8,128)(2,1)S(1)}, bf16[1,4,16,16,192]{4,3,2,1,0:T(8,128)(2,1)}, u32[]{:S(2)}) copy-start(bf16[1,4,16,16,192]{4,3,2,1,0:T(8,128)(2,1)} %param.10) | copy-start | bytes 1179652
  25.1 7.7 %copy-start.5 = (bf16[1,4,16,16,192]{4,3,2,1,0:T(8,128)(2,1)S(1)}, bf16[1,4,16,16,192]{4,3,2,1,0:T(8,128)(2,1)}, u32[]{:S(2)}) copy-start(bf16[1,4,16,16,192]{4,3,2,1,0:T(8,128)(2,1)} %param.9) | copy-start | bytes 1179652
  25.2 7.7 %copy-start.6 = (f32[192]{0:T(256)S(1)}, f32[192]{0:T(256)}, u32[]{:S(2)}) copy-start(f32[192]{0:T(256)} %param.14) | copy-start | bytes 2308
  28.9 3.9 %collective-permute-start.7 = (bf16[8,144,128]{2,1,0:T(8,128)(2,1)S(1)}, bf16[8,144,128]{2,1,0:T(8,128)(2,1)S(1)}, u32[]{:S(2)}, u32[]{:S(2)}) collective-permute-start(bf16[8,144,128]{2,1,0:T(8,128)(2,1)S(1)} %pad_maximum_fusion.4.held), channel_id=1, source_target_pairs={{0,8},{8,0},{1,9},{9,1},{2,10},{10,2},{3,11},{11,3},{4,12},{12,4},... | collective-permute-start | bytes 884744 | tf_op jit(solution)/shard_map/ppermute | solution.py:34
  41.6 1.6 %collective-permute-start.8 = (bf16[1248,128]{1,0:T(8,128)(2,1)S(1)}, bf16[1248,128]{1,0:T(8,128)(2,1)S(1)}, u32[]{:S(2)}, u32[]{:S(2)}) collective-permute-start(bf16[1248,128]{1,0:T(8,128)(2,1)S(1)} %get-tuple-element.34), channel_id=1, source_target_pairs={{0,8},{8,0},{1,9},{9,1},{2,10},{10,2},{3,11},{11,3},{4,12},{12,4},... | collective-permute-start | bytes 958472 | tf_op jit(solution)/shard_map/ppermute | solution.py:34
  42.1 3.9 %collective-permute-start.11 = (bf16[3,32,192]{2,0,1:T(4,128)(2,1)S(1)}, bf16[3,32,192]{2,0,1:T(4,128)(2,1)S(1)}, u32[]{:S(2)}, u32[]{:S(2)}) collective-permute-start(bf16[3,32,192]{2,0,1:T(4,128)(2,1)S(1)} %get-tuple-element.59), channel_id=1, source_target_pairs={{0,24},{8,16},{16,8},{24,0},{32,56},{40,48},{48,40},{56,32},{1,25}... | collective-permute-start | bytes 110600 | tf_op jit(solution)/shard_map/ppermute | solution.py:355
  42.5 1.3 %collective-permute-start.12 = (bf16[3,32,192]{2,0,1:T(4,128)(2,1)S(1)}, bf16[3,32,192]{2,0,1:T(4,128)(2,1)S(1)}, u32[]{:S(2)}, u32[]{:S(2)}) collective-permute-start(bf16[3,32,192]{2,0,1:T(4,128)(2,1)S(1)} %get-tuple-element.60), channel_id=1, source_target_pairs={{0,8},{8,0},{1,9},{9,1},{2,10},{10,2},{3,11},{11,3},{4,12},{12,4},... | collective-permute-start | bytes 110600 | tf_op jit(solution)/shard_map/ppermute | solution.py:34
  43.8 5.7 %collective-permute-start.9 = (bf16[672,128]{1,0:T(8,128)(2,1)S(1)}, bf16[672,128]{1,0:T(8,128)(2,1)S(1)}, u32[]{:S(2)}, u32[]{:S(2)}) collective-permute-start(bf16[672,128]{1,0:T(8,128)(2,1)S(1)} %pad_maximum_fusion.5), channel_id=1, source_target_pairs={{0,1},{1,0},{2,3},{3,2},{4,5},{5,4},{6,7},{7,6},{8,9},{9,8},{10,11... | collective-permute-start | bytes 516104 | tf_op jit(solution)/shard_map/ppermute | solution.py:34
  46.5 7.8 %collective-permute-start.13 = (bf16[3,40,192]{2,1,0:T(8,128)(2,1)S(1)}, bf16[3,40,192]{2,1,0:T(8,128)(2,1)S(1)}, u32[]{:S(2)}, u32[]{:S(2)}) collective-permute-start(bf16[3,40,192]{2,1,0:T(8,128)(2,1)S(1)} %get-tuple-element.55), channel_id=1, source_target_pairs={{32,64},{48,80},{96,128},{112,144},{160,192},{176,208},{224,0},{24... | collective-permute-start | bytes 138248 | tf_op jit(solution)/shard_map/ppermute | solution.py:372
  49.4 4.9 %collective-permute-start.14 = (bf16[3,40,192]{2,1,0:T(8,128)(2,1)S(1)}, bf16[3,40,192]{2,1,0:T(8,128)(2,1)S(1)}, u32[]{:S(2)}, u32[]{:S(2)}) collective-permute-start(bf16[3,40,192]{2,1,0:T(8,128)(2,1)S(1)} %get-tuple-element.56), channel_id=1, source_target_pairs={{0,32},{16,48},{32,0},{48,16},{1,33},{17,49},{33,1},{49,17},{2,34}... | collective-permute-start | bytes 138248 | tf_op jit(solution)/shard_map/ppermute | solution.py:34
  49.5 7.7 %collective-permute-start.10 = (bf16[384,128]{1,0:T(8,128)(2,1)S(1)}, bf16[384,128]{1,0:T(8,128)(2,1)S(1)}, u32[]{:S(2)}, u32[]{:S(2)}) collective-permute-start(bf16[384,128]{1,0:T(8,128)(2,1)S(1)} %pad_maximum_fusion.7), channel_id=1, source_target_pairs={{0,2},{1,3},{2,0},{3,1},{4,6},{5,7},{6,4},{7,5},{8,10},{9,11},{10,... | collective-permute-start | bytes 294920 | tf_op jit(solution)/shard_map/ppermute | solution.py:34
  57.3 5.0 %collective-permute-start.15 = (bf16[240,128]{1,0:T(8,128)(2,1)S(1)}, bf16[240,128]{1,0:T(8,128)(2,1)S(1)}, u32[]{:S(2)}, u32[]{:S(2)}) collective-permute-start(bf16[240,128]{1,0:T(8,128)(2,1)S(1)} %pad_maximum_fusion.10), channel_id=1, source_target_pairs={{0,7},{1,6},{2,5},{3,4},{4,3},{5,2},{6,1},{7,0},{8,15},{9,14},{10,... | collective-permute-start | bytes 184328 | tf_op jit(solution)/shard_map/ppermute | solution.py:34
  62.4 4.7 %collective-permute-start.18 = (bf16[240,128]{1,0:T(8,128)(2,1)S(1)}, bf16[240,128]{1,0:T(8,128)(2,1)S(1)}, u32[]{:S(2)}, u32[]{:S(2)}) collective-permute-start(bf16[240,128]{1,0:T(8,128)(2,1)S(1)} %pad_maximum_fusion.11), channel_id=1, source_target_pairs={{0,32},{16,48},{32,0},{48,16},{1,33},{17,49},{33,1},{49,17},{2,34}... | collective-permute-start | bytes 184328 | tf_op jit(solution)/shard_map/ppermute | solution.py:34
  65.5 4.7 %collective-permute-start.17 = (bf16[240,128]{1,0:T(8,128)(2,1)S(1)}, bf16[240,128]{1,0:T(8,128)(2,1)S(1)}, u32[]{:S(2)}, u32[]{:S(2)}) collective-permute-start(bf16[240,128]{1,0:T(8,128)(2,1)S(1)} %pad_maximum_fusion.11), channel_id=1, source_target_pairs={{0,48},{16,32},{32,16},{48,0},{1,49},{17,33},{33,17},{49,1},{2,50}... | collective-permute-start | bytes 184328 | tf_op jit(solution)/shard_map/ppermute | solution.py:34
  65.5 4.7 %collective-permute-start.16 = (bf16[240,128]{1,0:T(8,128)(2,1)S(1)}, bf16[240,128]{1,0:T(8,128)(2,1)S(1)}, u32[]{:S(2)}, u32[]{:S(2)}) collective-permute-start(bf16[240,128]{1,0:T(8,128)(2,1)S(1)} %pad_maximum_fusion.11), channel_id=1, source_target_pairs={{0,16},{16,0},{32,48},{48,32},{1,17},{17,1},{33,49},{49,33},{2,18}... | collective-permute-start | bytes 184328 | tf_op jit(solution)/shard_map/ppermute | solution.py:34
  70.3 4.7 %collective-permute-start.21 = (bf16[240,128]{1,0:T(8,128)(2,1)S(1)}, bf16[240,128]{1,0:T(8,128)(2,1)S(1)}, u32[]{:S(2)}, u32[]{:S(2)}) collective-permute-start(bf16[240,128]{1,0:T(8,128)(2,1)S(1)} %pad_maximum_fusion.12), channel_id=1, source_target_pairs={{0,128},{64,192},{128,0},{192,64},{1,129},{65,193},{129,1},{193,65... | collective-permute-start | bytes 184328 | tf_op jit(solution)/shard_map/ppermute | solution.py:34
  70.4 5.2 %collective-permute-start.20 = (bf16[240,128]{1,0:T(8,128)(2,1)S(1)}, bf16[240,128]{1,0:T(8,128)(2,1)S(1)}, u32[]{:S(2)}, u32[]{:S(2)}) collective-permute-start(bf16[240,128]{1,0:T(8,128)(2,1)S(1)} %pad_maximum_fusion.12), channel_id=1, source_target_pairs={{0,192},{64,128},{128,64},{192,0},{1,193},{65,129},{129,65},{193,1... | collective-permute-start | bytes 184328 | tf_op jit(solution)/shard_map/ppermute | solution.py:34
  73.6 3.4 %collective-permute-start.19 = (bf16[240,128]{1,0:T(8,128)(2,1)S(1)}, bf16[240,128]{1,0:T(8,128)(2,1)S(1)}, u32[]{:S(2)}, u32[]{:S(2)}) collective-permute-start(bf16[240,128]{1,0:T(8,128)(2,1)S(1)} %pad_maximum_fusion.12), channel_id=1, source_target_pairs={{0,64},{64,0},{128,192},{192,128},{1,65},{65,1},{129,193},{193,129... | collective-permute-start | bytes 184328 | tf_op jit(solution)/shard_map/ppermute | solution.py:34
  77.0 5.3 %collective-permute-start.22 = (f32[192,128]{1,0:T(8,128)S(1)}, f32[192,128]{1,0:T(8,128)S(1)}, u32[]{:S(2)}, u32[]{:S(2)}) collective-permute-start(f32[192,128]{1,0:T(8,128)S(1)} %pad_maximum_fusion.8.held), channel_id=1, source_target_pairs={{0,8},{8,0},{1,9},{9,1},{2,10},{10,2},{3,11},{11,3},{4,12},{12,4},... | collective-permute-start | bytes 294920 | tf_op jit(solution)/shard_map/ppermute | solution.py:34

commit v8 on v6

--- a/solution.py
+++ b/solution.py
@@ -110,7 +110,7 @@
         out[t, :, pl.ds(col, 8), :] = acc
         return carry
 
-    lax.fori_loop(4 * first, 4 * last, body, 0)
+    lax.fori_loop(4 * first, 4 * last, body, 0, unroll=4)
 
 
 def correlate_planes(planes, field, acc):
@@ -131,7 +131,7 @@
                 acc[t, dy * KS + dx] += sums[dy]
         return carry
 
-    lax.fori_loop(0, 12, body, 0)
+    lax.fori_loop(0, 12, body, 0, unroll=2)
 
 
 def tile_of(planes, p):

time: 83.5 us -> 83.2 us (level)
  transfers between devices with their start and end apart: 23 -> 23, of which waited for: 13 -> 14; matrix products, arithmetic and copies ran while one was open for 2% -> 2% of each run, Pallas kernels for 12% -> 11%
where the time goes in v8:
time: 83.2 us; the launch traced here: 83.1 us
  starting transfers between devices  40.2 us (48%)
  Pallas kernels  19.8 us (24%)
  waiting for transfers between devices  17.4 us (21%)
  other arithmetic  2.96 us (4%)
  between operations  1.61 us (2%)
  local copies, waits for them, and re-layouts  1.14 us (1%)
    ppermute x19, starting transfers between devices, swap(): return lax.ppermute(value, axis, [(i, i ^ bit) for i in range(SIZES[axis])])  32 us
    pallas_call x7, Pallas kernels, call(): pl.pallas_call(kernel, out_shape=[jax.ShapeDtypeStruct(shape, dtype) for...  19.8 us
    ppermute x19, waiting for transfers between devices, swap(): return lax.ppermute(value, axis, [(i, i ^ bit) for i in range(SIZES[axis])])  15.6 us
    ppermute x2, starting transfers between devices, end_rims(): lax.ppermute(jnp.where(upper == 0, north_edge, south_edge), ('y', 'x'), p...  7.7 us
    ppermute x2, waiting for transfers between devices, side_rims(): lax.ppermute(jnp.where(core == 0, west_edge, east_edge), ('x', 'core'), p...  1.75 us
  transfers between devices with their start and end apart: 23, of which 14 were waited for; matrix products, arithmetic and copies ran while one was open for 2% of the time, Pallas kernels for 11%

profile of v8, /device:TPU:1, one launch (start us, length us, event | category | flops | bytes accessed | tf_op | source)
XLA Modules:
  0.0 83.1 jit_solution(13626806550042396191)
XLA Ops:
  1.3 0.7 add_bitcast_fusion.info
  2.0 1.0 %copy-done.4 = bf16[1,4,16,16,192]{4,3,2,1,0:T(8,128)(2,1)S(1)} copy-done((bf16[1,4,16,16,192]{4,3,2,1,0:T(8,128)(2,1)S(1)}, bf16[1,4,16,16,192]{4,3,2,1,0:T(8,128)(2,1)}, u32[]{:S(2)}) %copy-start.4) | copy-done | bytes 393240
  3.1 0.7 place.1
  3.8 0.1 select_bitcast_fusion.7
  3.9 3.3 %collective-permute-start.1 = (bf16[3,32,192]{2,0,1:T(4,128)(2,1)S(1)}, bf16[3,32,192]{2,0,1:T(4,128)(2,1)S(1)}, u32[]{:S(2)}, u32[]{:S(2)}) collective-permute-start(bf16[3,32,192]{2,0,1:T(4,128)(2,1)S(1)} %get-tuple-element.62), channel_id=1, source_target_pairs={{0,8},{8,0},{1,9},{9,1},{2,10},{10,2},{3,11},{11,3},{4,12},{12,4},... | collective-permute-start | bytes 110600 | tf_op jit(solution)/shard_map/ppermute | solution.py:34
  7.2 0.0 collective-permute-start
  7.2 0.9 %collective-permute-done.1 = bf16[3,32,192]{2,0,1:T(4,128)(2,1)S(1)} collective-permute-done((bf16[3,32,192]{2,0,1:T(4,128)(2,1)S(1)}, bf16[3,32,192]{2,0,1:T(4,128)(2,1)S(1)}, u32[]{:S(2)}, u32[]{:S(2)}) %collective-permute-start.1) | collective-permute-done | bytes 36896 | tf_op jit(solution)/shard_map/ppermute | solution.py:34
  8.1 0.6 pack.1
  8.7 4.2 %collective-permute-start.4 = (bf16[144,128]{1,0:T(8,128)(2,1)S(1)}, bf16[144,128]{1,0:T(8,128)(2,1)S(1)}, u32[]{:S(2)}, u32[]{:S(2)}) collective-permute-start(bf16[144,128]{1,0:T(8,128)(2,1)S(1)} %pack.1), channel_id=1, source_target_pairs={{0,7},{1,6},{2,5},{3,4},{4,3},{5,2},{6,1},{7,0},{8,15},{9,14},{10,... | collective-permute-start | bytes 110600 | tf_op jit(solution)/shard_map/ppermute | solution.py:34
  12.9 0.0 collective-permute-done
  12.9 0.1 select_bitcast_fusion.5
  13.0 0.4 pad_maximum_fusion.3
  13.4 0.0 copy-start.1
  13.4 5.0 %collective-permute-start.2 = (bf16[3,40,192]{2,1,0:T(8,128)(2,1)S(1)}, bf16[3,40,192]{2,1,0:T(8,128)(2,1)S(1)}, u32[]{:S(2)}, u32[]{:S(2)}) collective-permute-start(bf16[3,40,192]{2,1,0:T(8,128)(2,1)S(1)} %get-tuple-element.57), channel_id=1, source_target_pairs={{32,64},{48,80},{96,128},{112,144},{160,192},{176,208},{224,0},{24... | collective-permute-start | bytes 138248 | tf_op jit(solution)/shard_map/ppermute | solution.py:372
  18.4 2.1 %collective-permute-start.5 = (bf16[2,144,128]{2,1,0:T(8,128)(2,1)S(1)}, bf16[2,144,128]{2,1,0:T(8,128)(2,1)S(1)}, u32[]{:S(2)}, u32[]{:S(2)}) collective-permute-start(bf16[2,144,128]{2,1,0:T(8,128)(2,1)S(1)} %pad_maximum_fusion.9), channel_id=1, source_target_pairs={{0,2},{1,3},{2,0},{3,1},{4,6},{5,7},{6,4},{7,5},{8,10},{9,11},{10,... | collective-permute-start | bytes 221192 | tf_op jit(solution)/shard_map/ppermute | solution.py:34
  20.6 2.4 %collective-permute-done.3 = bf16[3,40,192]{2,1,0:T(8,128)(2,1)S(1)} collective-permute-done((bf16[3,40,192]{2,1,0:T(8,128)(2,1)S(1)}, bf16[3,40,192]{2,1,0:T(8,128)(2,1)S(1)}, u32[]{:S(2)}, u32[]{:S(2)}) %collective-permute-start.3) | collective-permute-done | bytes 46112 | tf_op jit(solution)/shard_map/ppermute | solution.py:34
  23.0 0.0 collective-permute-done.5
  23.1 1.7 %collective-permute-start.6 = (bf16[4,144,128]{2,1,0:T(8,128)(2,1)S(1)}, bf16[4,144,128]{2,1,0:T(8,128)(2,1)S(1)}, u32[]{:S(2)}, u32[]{:S(2)}) collective-permute-start(bf16[4,144,128]{2,1,0:T(8,128)(2,1)S(1)} %pad_maximum_fusion.6), channel_id=1, source_target_pairs={{0,1},{1,0},{2,3},{3,2},{4,5},{5,4},{6,7},{7,6},{8,9},{9,8},{10,11... | collective-permute-start | bytes 442376 | tf_op jit(solution)/shard_map/ppermute | solution.py:34
  24.8 0.3 fusion.2.padded
  25.1 0.0 copy-start.7
  25.1 0.0 copy-start
  25.1 0.0 copy-start.5
  25.2 0.0 copy-start.6
  25.2 3.5 %field.1 = (f32[3,22,40,128]{3,2,1,0:T(8,128)S(1)}, f32[3,16,32,128]{3,2,1,0:T(8,128)S(1)}) custom-call(f32[38,40,192]{2,1,0:T(8,128)S(1)} %fusion.2.padded, f32[7,7,192]{2,1,0:T(8,128)S(1)} %copy-done.1), custom_call_target="tpu_custom_call" | custom-call | tf_op jit(solution)/shard_map/field/pallas_call | solution.py:304
  28.6 0.0 collective-permute-done.6
  28.7 2.9 %collective-permute-start.7 = (bf16[8,144,128]{2,1,0:T(8,128)(2,1)S(1)}, bf16[8,144,128]{2,1,0:T(8,128)(2,1)S(1)}, u32[]{:S(2)}, u32[]{:S(2)}) collective-permute-start(bf16[8,144,128]{2,1,0:T(8,128)(2,1)S(1)} %pad_maximum_fusion.4.held), channel_id=1, source_target_pairs={{0,8},{8,0},{1,9},{9,1},{2,10},{10,2},{3,11},{11,3},{4,12},{12,4},... | collective-permute-start | bytes 884744 | tf_op jit(solution)/shard_map/ppermute | solution.py:34
  31.6 1.2 %collective-permute-done.7.other = bf16[8,144,128]{2,1,0:T(8,128)(2,1)S(1)} collective-permute-done((bf16[8,144,128]{2,1,0:T(8,128)(2,1)S(1)}, bf16[8,144,128]{2,1,0:T(8,128)(2,1)S(1)}, u32[]{:S(2)}, u32[]{:S(2)}) %collective-permute-start.7) | collective-permute-done | bytes 294944 | tf_op jit(solution)/shard_map/ppermute | solution.py:34
  32.8 8.6 %block.1 = (f32[4,16,16,192]{3,2,1,0:T(8,128)}, bf16[32,32,192]{2,1,0:T(8,128)(2,1)S(1)}, f32[1152,128]{1,0:T(8,128)S(1)}, bf16[1248,128]{1,0:T(8,128)(2,1)S(1)}, f32[48,128]{1,0:T(8,128)S(1)}) custom-call(s32[1,7]{1,0:T(1,128)S(1)} %add_bitcast_fusion.info, f32[3,22,40,128]{3,2,1,0:T(8,128)S(1)} %get-tuple-element.27.planes, ...), custom_call_target="tpu_custom_call" | custom-call | flops 14000000000 | bytes 14000000 | tf_op jit(solution)/shard_map/block/pallas_call | solution.py:304
  41.5 0.4 collective-permute-start.8
  41.9 0.1 select_bitcast_fusion.3
  42.0 0.4 collective-permute-start.11
  42.4 0.4 collective-permute-start.12
  42.8 0.4 collective-permute-done.8
  43.1 0.1 convert_add_fusion
  43.3 0.4 collective-permute-done.12
  43.7 0.5 collective-permute-start.9
  44.1 1.7 %collective-permute-done.11 = bf16[3,32,192]{2,0,1:T(4,128)(2,1)S(1)} collective-permute-done((bf16[3,32,192]{2,0,1:T(4,128)(2,1)S(1)}, bf16[3,32,192]{2,0,1:T(4,128)(2,1)S(1)}, u32[]{:S(2)}, u32[]{:S(2)}) %collective-permute-start.11) | collective-permute-done | bytes 36896 | tf_op jit(solution)/shard_map/ppermute | solution.py:355
  45.9 0.1 select_bitcast_fusion.1
  45.9 0.4 pad_maximum_fusion.2
  46.4 2.7 %collective-permute-start.13 = (bf16[3,40,192]{2,1,0:T(8,128)(2,1)S(1)}, bf16[3,40,192]{2,1,0:T(8,128)(2,1)S(1)}, u32[]{:S(2)}, u32[]{:S(2)}) collective-permute-start(bf16[3,40,192]{2,1,0:T(8,128)(2,1)S(1)} %get-tuple-element.55), channel_id=1, source_target_pairs={{32,64},{48,80},{96,128},{112,144},{160,192},{176,208},{224,0},{24... | collective-permute-start | bytes 138248 | tf_op jit(solution)/shard_map/ppermute | solution.py:372
  49.1 0.2 collective-permute-done.9
  49.4 1.3 %collective-permute-start.10 = (bf16[384,128]{1,0:T(8,128)(2,1)S(1)}, bf16[384,128]{1,0:T(8,128)(2,1)S(1)}, u32[]{:S(2)}, u32[]{:S(2)}) collective-permute-start(bf16[384,128]{1,0:T(8,128)(2,1)S(1)} %pad_maximum_fusion.7), channel_id=1, source_target_pairs={{0,2},{1,3},{2,0},{3,1},{4,6},{5,7},{6,4},{7,5},{8,10},{9,11},{10,... | collective-permute-start | bytes 294920 | tf_op jit(solution)/shard_map/ppermute | solution.py:34
  50.7 3.2 %collective-permute-done.14 = bf16[3,40,192]{2,1,0:T(8,128)(2,1)S(1)} collective-permute-done((bf16[3,40,192]{2,1,0:T(8,128)(2,1)S(1)}, bf16[3,40,192]{2,1,0:T(8,128)(2,1)S(1)}, u32[]{:S(2)}, u32[]{:S(2)}) %collective-permute-start.14) | collective-permute-done | bytes 46112 | tf_op jit(solution)/shard_map/ppermute | solution.py:34
  53.9 0.0 collective-permute-done.13
  54.0 0.3 fusion.5.padded
  54.3 2.4 %spread.1 = (f32[3,22,40,128]{3,2,1,0:T(8,128)S(1)}, f32[3,16,32,128]{3,2,1,0:T(8,128)S(1)}) custom-call(f32[38,40,192]{2,1,0:T(8,128)S(1)} %fusion.5.padded, f32[7,7,192]{2,1,0:T(8,128)S(1)} %copy-done.1), custom_call_target="tpu_custom_call" | custom-call | tf_op jit(solution)/shard_map/spread/pallas_call | solution.py:304
  56.8 2.5 %collective-permute-start.15 = (bf16[240,128]{1,0:T(8,128)(2,1)S(1)}, bf16[240,128]{1,0:T(8,128)(2,1)S(1)}, u32[]{:S(2)}, u32[]{:S(2)}) collective-permute-start(bf16[240,128]{1,0:T(8,128)(2,1)S(1)} %pad_maximum_fusion.10), channel_id=1, source_target_pairs={{0,7},{1,6},{2,5},{3,4},{4,3},{5,2},{6,1},{7,0},{8,15},{9,14},{10,... | collective-permute-start | bytes 184328 | tf_op jit(solution)/shard_map/ppermute | solution.py:34
  59.3 2.7 %emit.1 = f32[4,16,16,192]{3,2,1,0:T(8,128)} custom-call(s32[1,7]{1,0:T(1,128)S(1)} %add_bitcast_fusion.info, f32[3,22,40,128]{3,2,1,0:T(8,128)S(1)} %get-tuple-element.41.planes, f32[3,16,32,128]{3,2,1,0:T(8,128)S(1)} %get-tuple-element.39.partial, bf16[4,16,16,192]{3,2,1,0:T(8,128)(2,1)S(1)} %bitcast.34, f32[7,7,192]{2,1,0:T(8,128)S(1)} %copy-done.1), custom_call_target="tpu_custom_call" | custom-call | tf_op jit(solution)/shard_map/emit/pallas_call | solution.py:304
  62.0 0.0 collective-permute-done.15
  62.0 2.6 %collective-permute-start.18 = (bf16[240,128]{1,0:T(8,128)(2,1)S(1)}, bf16[240,128]{1,0:T(8,128)(2,1)S(1)}, u32[]{:S(2)}, u32[]{:S(2)}) collective-permute-start(bf16[240,128]{1,0:T(8,128)(2,1)S(1)} %pad_maximum_fusion.11), channel_id=1, source_target_pairs={{0,48},{16,32},{32,16},{48,0},{1,49},{17,33},{33,17},{49,1},{2,50}... | collective-permute-start | bytes 184328 | tf_op jit(solution)/shard_map/ppermute | solution.py:34
  64.6 0.4 collective-permute-start.17
  65.0 1.0 %collective-permute-start.16 = (bf16[240,128]{1,0:T(8,128)(2,1)S(1)}, bf16[240,128]{1,0:T(8,128)(2,1)S(1)}, u32[]{:S(2)}, u32[]{:S(2)}) collective-permute-start(bf16[240,128]{1,0:T(8,128)(2,1)S(1)} %pad_maximum_fusion.11), channel_id=1, source_target_pairs={{0,32},{16,48},{32,0},{48,16},{1,33},{17,49},{33,1},{49,17},{2,34}... | collective-permute-start | bytes 184328 | tf_op jit(solution)/shard_map/ppermute | solution.py:34
  66.0 0.4 collective-permute-done.18
  66.4 1.3 %collective-permute-done.17 = bf16[240,128]{1,0:T(8,128)(2,1)S(1)} collective-permute-done((bf16[240,128]{1,0:T(8,128)(2,1)S(1)}, bf16[240,128]{1,0:T(8,128)(2,1)S(1)}, u32[]{:S(2)}, u32[]{:S(2)}) %collective-permute-start.17) | collective-permute-done | bytes 61472 | tf_op jit(solution)/shard_map/ppermute | solution.py:34
  67.7 2.0 %collective-permute-done.16 = bf16[240,128]{1,0:T(8,128)(2,1)S(1)} collective-permute-done((bf16[240,128]{1,0:T(8,128)(2,1)S(1)}, bf16[240,128]{1,0:T(8,128)(2,1)S(1)}, u32[]{:S(2)}, u32[]{:S(2)}) %collective-permute-start.16) | collective-permute-done | bytes 61472 | tf_op jit(solution)/shard_map/ppermute | solution.py:34
  69.7 1.1 %collective-permute-start.21 = (bf16[240,128]{1,0:T(8,128)(2,1)S(1)}, bf16[240,128]{1,0:T(8,128)(2,1)S(1)}, u32[]{:S(2)}, u32[]{:S(2)}) collective-permute-start(bf16[240,128]{1,0:T(8,128)(2,1)S(1)} %pad_maximum_fusion.12), channel_id=1, source_target_pairs={{0,192},{64,128},{128,64},{192,0},{1,193},{65,129},{129,65},{193,1... | collective-permute-start | bytes 184328 | tf_op jit(solution)/shard_map/ppermute | solution.py:34
  70.9 0.3 collective-permute-start.20
  71.2 2.5 %collective-permute-start.19 = (bf16[240,128]{1,0:T(8,128)(2,1)S(1)}, bf16[240,128]{1,0:T(8,128)(2,1)S(1)}, u32[]{:S(2)}, u32[]{:S(2)}) collective-permute-start(bf16[240,128]{1,0:T(8,128)(2,1)S(1)} %pad_maximum_fusion.12), channel_id=1, source_target_pairs={{0,128},{64,192},{128,0},{192,64},{1,129},{65,193},{129,1},{193,65... | collective-permute-start | bytes 184328 | tf_op jit(solution)/shard_map/ppermute | solution.py:34
  73.7 0.4 collective-permute-done.21
  74.1 0.0 collective-permute-done.20
  74.1 1.8 %collective-permute-done.19 = bf16[240,128]{1,0:T(8,128)(2,1)S(1)} collective-permute-done((bf16[240,128]{1,0:T(8,128)(2,1)S(1)}, bf16[240,128]{1,0:T(8,128)(2,1)S(1)}, u32[]{:S(2)}, u32[]{:S(2)}) %collective-permute-start.19) | collective-permute-done | bytes 61472 | tf_op jit(solution)/shard_map/ppermute | solution.py:34
  76.0 4.8 %collective-permute-start.22 = (f32[192,128]{1,0:T(8,128)S(1)}, f32[192,128]{1,0:T(8,128)S(1)}, u32[]{:S(2)}, u32[]{:S(2)}) collective-permute-start(f32[192,128]{1,0:T(8,128)S(1)} %pad_maximum_fusion.8.held), channel_id=1, source_target_pairs={{0,8},{8,0},{1,9},{9,1},{2,10},{10,2},{3,11},{11,3},{4,12},{12,4},... | collective-permute-start | bytes 294920 | tf_op jit(solution)/shard_map/ppermute | solution.py:34
  80.8 0.9 %collective-permute-done.22.other = f32[192,128]{1,0:T(8,128)S(1)} collective-permute-done((f32[192,128]{1,0:T(8,128)S(1)}, f32[192,128]{1,0:T(8,128)S(1)}, u32[]{:S(2)}, u32[]{:S(2)}) %collective-permute-start.22) | collective-permute-done | bytes 98336 | tf_op jit(solution)/shard_map/ppermute | solution.py:34
  81.8 1.3 %finish.1 = (f32[24,768]{1,0:T(8,128)}, f32[96,192]{1,0:T(8,128)}, f32[7,7,192]{2,1,0:T(8,128)}) custom-call(s32[1,7]{1,0:T(1,128)S(1)} %add_bitcast_fusion.info, f32[192,128]{1,0:T(8,128)S(1)} %pad_maximum_fusion.8.held, f32[192,128]{1,0:T(8,128)S(1)} %collective-permute-done.22.other), custom_call_target="tpu_custom_call" | custom-call | flops 1000000000 | bytes 1000000 | tf_op jit(solution)/shard_map/finish/pallas_call | solution.py:304
  (46 shorter events, 0.5 us)
Async XLA Ops:
  2.0 1.0 %copy-start.4 = (bf16[1,4,16,16,192]{4,3,2,1,0:T(8,128)(2,1)S(1)}, bf16[1,4,16,16,192]{4,3,2,1,0:T(8,128)(2,1)}, u32[]{:S(2)}) copy-start(bf16[1,4,16,16,192]{4,3,2,1,0:T(8,128)(2,1)} %param.9) | copy-start | bytes 1179652
  3.1 5.0 %copy-start.2 = (bf16[96,192]{1,0:T(8,128)(2,1)S(1)}, bf16[96,192]{1,0:T(8,128)(2,1)}, u32[]{:S(2)}) copy-start(bf16[96,192]{1,0:T(8,128)(2,1)} %project.1) | copy-start | bytes 110596
  3.1 5.0 %copy-start.3 = (bf16[24,768]{1,0:T(8,128)(2,1)S(1)}, bf16[24,768]{1,0:T(8,128)(2,1)}, u32[]{:S(2)}) copy-start(bf16[24,768]{1,0:T(8,128)(2,1)} %expand) | copy-start | bytes 110596
  3.9 4.2 %collective-permute-start.1 = (bf16[3,32,192]{2,0,1:T(4,128)(2,1)S(1)}, bf16[3,32,192]{2,0,1:T(4,128)(2,1)S(1)}, u32[]{:S(2)}, u32[]{:S(2)}) collective-permute-start(bf16[3,32,192]{2,0,1:T(4,128)(2,1)S(1)} %get-tuple-element.62), channel_id=1, source_target_pairs={{0,8},{8,0},{1,9},{9,1},{2,10},{10,2},{3,11},{11,3},{4,12},{12,4},... | collective-permute-start | bytes 110600 | tf_op jit(solution)/shard_map/ppermute | solution.py:34
  7.2 5.7 %collective-permute-start = (bf16[3,32,192]{2,0,1:T(4,128)(2,1)S(1)}, bf16[3,32,192]{2,0,1:T(4,128)(2,1)S(1)}, u32[]{:S(2)}, u32[]{:S(2)}) collective-permute-start(bf16[3,32,192]{2,0,1:T(4,128)(2,1)S(1)} %get-tuple-element.61), channel_id=1, source_target_pairs={{0,24},{8,16},{16,8},{24,0},{32,56},{40,48},{48,40},{56,32},{1,25}... | collective-permute-start | bytes 110600 | tf_op jit(solution)/shard_map/ppermute | solution.py:355
  8.7 9.7 %collective-permute-start.4 = (bf16[144,128]{1,0:T(8,128)(2,1)S(1)}, bf16[144,128]{1,0:T(8,128)(2,1)S(1)}, u32[]{:S(2)}, u32[]{:S(2)}) collective-permute-start(bf16[144,128]{1,0:T(8,128)(2,1)S(1)} %pack.1), channel_id=1, source_target_pairs={{0,7},{1,6},{2,5},{3,4},{4,3},{5,2},{6,1},{7,0},{8,15},{9,14},{10,... | collective-permute-start | bytes 110600 | tf_op jit(solution)/shard_map/ppermute | solution.py:34
  13.4 11.7 %copy-start.1 = (f32[7,7,192]{2,1,0:T(8,128)S(1)}, f32[7,7,192]{2,1,0:T(8,128)}, u32[]{:S(2)}) copy-start(f32[7,7,192]{2,1,0:T(8,128)} %kernel.5) | copy-start | bytes 112900
  13.4 7.2 %collective-permute-start.2 = (bf16[3,40,192]{2,1,0:T(8,128)(2,1)S(1)}, bf16[3,40,192]{2,1,0:T(8,128)(2,1)S(1)}, u32[]{:S(2)}, u32[]{:S(2)}) collective-permute-start(bf16[3,40,192]{2,1,0:T(8,128)(2,1)S(1)} %get-tuple-element.57), channel_id=1, source_target_pairs={{32,64},{48,80},{96,128},{112,144},{160,192},{176,208},{224,0},{24... | collective-permute-start | bytes 138248 | tf_op jit(solution)/shard_map/ppermute | solution.py:372
  18.4 4.6 %collective-permute-start.3 = (bf16[3,40,192]{2,1,0:T(8,128)(2,1)S(1)}, bf16[3,40,192]{2,1,0:T(8,128)(2,1)S(1)}, u32[]{:S(2)}, u32[]{:S(2)}) collective-permute-start(bf16[3,40,192]{2,1,0:T(8,128)(2,1)S(1)} %get-tuple-element.58), channel_id=1, source_target_pairs={{0,32},{16,48},{32,0},{48,16},{1,33},{17,49},{33,1},{49,17},{2,34}... | collective-permute-start | bytes 138248 | tf_op jit(solution)/shard_map/ppermute | solution.py:34
  18.4 4.6 %collective-permute-start.5 = (bf16[2,144,128]{2,1,0:T(8,128)(2,1)S(1)}, bf16[2,144,128]{2,1,0:T(8,128)(2,1)S(1)}, u32[]{:S(2)}, u32[]{:S(2)}) collective-permute-start(bf16[2,144,128]{2,1,0:T(8,128)(2,1)S(1)} %pad_maximum_fusion.9), channel_id=1, source_target_pairs={{0,2},{1,3},{2,0},{3,1},{4,6},{5,7},{6,4},{7,5},{8,10},{9,11},{10,... | collective-permute-start | bytes 221192 | tf_op jit(solution)/shard_map/ppermute | solution.py:34
  23.1 5.6 %collective-permute-start.6 = (bf16[4,144,128]{2,1,0:T(8,128)(2,1)S(1)}, bf16[4,144,128]{2,1,0:T(8,128)(2,1)S(1)}, u32[]{:S(2)}, u32[]{:S(2)}) collective-permute-start(bf16[4,144,128]{2,1,0:T(8,128)(2,1)S(1)} %pad_maximum_fusion.6), channel_id=1, source_target_pairs={{0,1},{1,0},{2,3},{3,2},{4,5},{5,4},{6,7},{7,6},{8,9},{9,8},{10,11... | collective-permute-start | bytes 442376 | tf_op jit(solution)/shard_map/ppermute | solution.py:34
  25.1 6.5 %copy-start.7 = (f32[768]{0:T(1024)S(1)}, f32[768]{0:T(1024)}, u32[]{:S(2)}) copy-start(f32[768]{0:T(1024)} %param.16) | copy-start | bytes 9220
  25.1 7.7 %copy-start = (bf16[1,4,16,16,192]{4,3,2,1,0:T(8,128)(2,1)S(1)}, bf16[1,4,16,16,192]{4,3,2,1,0:T(8,128)(2,1)}, u32[]{:S(2)}) copy-start(bf16[1,4,16,16,192]{4,3,2,1,0:T(8,128)(2,1)} %param.10) | copy-start | bytes 1179652
  25.1 7.7 %copy-start.5 = (bf16[1,4,16,16,192]{4,3,2,1,0:T(8,128)(2,1)S(1)}, bf16[1,4,16,16,192]{4,3,2,1,0:T(8,128)(2,1)}, u32[]{:S(2)}) copy-start(bf16[1,4,16,16,192]{4,3,2,1,0:T(8,128)(2,1)} %param.9) | copy-start | bytes 1179652
  25.2 7.7 %copy-start.6 = (f32[192]{0:T(256)S(1)}, f32[192]{0:T(256)}, u32[]{:S(2)}) copy-start(f32[192]{0:T(256)} %param.14) | copy-start | bytes 2308
  28.7 4.2 %collective-permute-start.7 = (bf16[8,144,128]{2,1,0:T(8,128)(2,1)S(1)}, bf16[8,144,128]{2,1,0:T(8,128)(2,1)S(1)}, u32[]{:S(2)}, u32[]{:S(2)}) collective-permute-start(bf16[8,144,128]{2,1,0:T(8,128)(2,1)S(1)} %pad_maximum_fusion.4.held), channel_id=1, source_target_pairs={{0,8},{8,0},{1,9},{9,1},{2,10},{10,2},{3,11},{11,3},{4,12},{12,4},... | collective-permute-start | bytes 884744 | tf_op jit(solution)/shard_map/ppermute | solution.py:34
  41.5 1.6 %collective-permute-start.8 = (bf16[1248,128]{1,0:T(8,128)(2,1)S(1)}, bf16[1248,128]{1,0:T(8,128)(2,1)S(1)}, u32[]{:S(2)}, u32[]{:S(2)}) collective-permute-start(bf16[1248,128]{1,0:T(8,128)(2,1)S(1)} %get-tuple-element.34), channel_id=1, source_target_pairs={{0,8},{8,0},{1,9},{9,1},{2,10},{10,2},{3,11},{11,3},{4,12},{12,4},... | collective-permute-start | bytes 958472 | tf_op jit(solution)/shard_map/ppermute | solution.py:34
  42.0 3.9 %collective-permute-start.11 = (bf16[3,32,192]{2,0,1:T(4,128)(2,1)S(1)}, bf16[3,32,192]{2,0,1:T(4,128)(2,1)S(1)}, u32[]{:S(2)}, u32[]{:S(2)}) collective-permute-start(bf16[3,32,192]{2,0,1:T(4,128)(2,1)S(1)} %get-tuple-element.59), channel_id=1, source_target_pairs={{0,24},{8,16},{16,8},{24,0},{32,56},{40,48},{48,40},{56,32},{1,25}... | collective-permute-start | bytes 110600 | tf_op jit(solution)/shard_map/ppermute | solution.py:355
  42.4 1.3 %collective-permute-start.12 = (bf16[3,32,192]{2,0,1:T(4,128)(2,1)S(1)}, bf16[3,32,192]{2,0,1:T(4,128)(2,1)S(1)}, u32[]{:S(2)}, u32[]{:S(2)}) collective-permute-start(bf16[3,32,192]{2,0,1:T(4,128)(2,1)S(1)} %get-tuple-element.60), channel_id=1, source_target_pairs={{0,8},{8,0},{1,9},{9,1},{2,10},{10,2},{3,11},{11,3},{4,12},{12,4},... | collective-permute-start | bytes 110600 | tf_op jit(solution)/shard_map/ppermute | solution.py:34
  43.7 5.6 %collective-permute-start.9 = (bf16[672,128]{1,0:T(8,128)(2,1)S(1)}, bf16[672,128]{1,0:T(8,128)(2,1)S(1)}, u32[]{:S(2)}, u32[]{:S(2)}) collective-permute-start(bf16[672,128]{1,0:T(8,128)(2,1)S(1)} %pad_maximum_fusion.5), channel_id=1, source_target_pairs={{0,1},{1,0},{2,3},{3,2},{4,5},{5,4},{6,7},{7,6},{8,9},{9,8},{10,11... | collective-permute-start | bytes 516104 | tf_op jit(solution)/shard_map/ppermute | solution.py:34
  46.4 7.6 %collective-permute-start.13 = (bf16[3,40,192]{2,1,0:T(8,128)(2,1)S(1)}, bf16[3,40,192]{2,1,0:T(8,128)(2,1)S(1)}, u32[]{:S(2)}, u32[]{:S(2)}) collective-permute-start(bf16[3,40,192]{2,1,0:T(8,128)(2,1)S(1)} %get-tuple-element.55), channel_id=1, source_target_pairs={{32,64},{48,80},{96,128},{112,144},{160,192},{176,208},{224,0},{24... | collective-permute-start | bytes 138248 | tf_op jit(solution)/shard_map/ppermute | solution.py:372
  49.1 4.9 %collective-permute-start.14 = (bf16[3,40,192]{2,1,0:T(8,128)(2,1)S(1)}, bf16[3,40,192]{2,1,0:T(8,128)(2,1)S(1)}, u32[]{:S(2)}, u32[]{:S(2)}) collective-permute-start(bf16[3,40,192]{2,1,0:T(8,128)(2,1)S(1)} %get-tuple-element.56), channel_id=1, source_target_pairs={{0,32},{16,48},{32,0},{48,16},{1,33},{17,49},{33,1},{49,17},{2,34}... | collective-permute-start | bytes 138248 | tf_op jit(solution)/shard_map/ppermute | solution.py:34
  49.4 7.3 %collective-permute-start.10 = (bf16[384,128]{1,0:T(8,128)(2,1)S(1)}, bf16[384,128]{1,0:T(8,128)(2,1)S(1)}, u32[]{:S(2)}, u32[]{:S(2)}) collective-permute-start(bf16[384,128]{1,0:T(8,128)(2,1)S(1)} %pad_maximum_fusion.7), channel_id=1, source_target_pairs={{0,2},{1,3},{2,0},{3,1},{4,6},{5,7},{6,4},{7,5},{8,10},{9,11},{10,... | collective-permute-start | bytes 294920 | tf_op jit(solution)/shard_map/ppermute | solution.py:34
  56.8 5.2 %collective-permute-start.15 = (bf16[240,128]{1,0:T(8,128)(2,1)S(1)}, bf16[240,128]{1,0:T(8,128)(2,1)S(1)}, u32[]{:S(2)}, u32[]{:S(2)}) collective-permute-start(bf16[240,128]{1,0:T(8,128)(2,1)S(1)} %pad_maximum_fusion.10), channel_id=1, source_target_pairs={{0,7},{1,6},{2,5},{3,4},{4,3},{5,2},{6,1},{7,0},{8,15},{9,14},{10,... | collective-permute-start | bytes 184328 | tf_op jit(solution)/shard_map/ppermute | solution.py:34
  62.0 4.4 %collective-permute-start.18 = (bf16[240,128]{1,0:T(8,128)(2,1)S(1)}, bf16[240,128]{1,0:T(8,128)(2,1)S(1)}, u32[]{:S(2)}, u32[]{:S(2)}) collective-permute-start(bf16[240,128]{1,0:T(8,128)(2,1)S(1)} %pad_maximum_fusion.11), channel_id=1, source_target_pairs={{0,48},{16,32},{32,16},{48,0},{1,49},{17,33},{33,17},{49,1},{2,50}... | collective-permute-start | bytes 184328 | tf_op jit(solution)/shard_map/ppermute | solution.py:34
  64.6 3.1 %collective-permute-start.17 = (bf16[240,128]{1,0:T(8,128)(2,1)S(1)}, bf16[240,128]{1,0:T(8,128)(2,1)S(1)}, u32[]{:S(2)}, u32[]{:S(2)}) collective-permute-start(bf16[240,128]{1,0:T(8,128)(2,1)S(1)} %pad_maximum_fusion.11), channel_id=1, source_target_pairs={{0,16},{16,0},{32,48},{48,32},{1,17},{17,1},{33,49},{49,33},{2,18}... | collective-permute-start | bytes 184328 | tf_op jit(solution)/shard_map/ppermute | solution.py:34
  65.0 4.7 %collective-permute-start.16 = (bf16[240,128]{1,0:T(8,128)(2,1)S(1)}, bf16[240,128]{1,0:T(8,128)(2,1)S(1)}, u32[]{:S(2)}, u32[]{:S(2)}) collective-permute-start(bf16[240,128]{1,0:T(8,128)(2,1)S(1)} %pad_maximum_fusion.11), channel_id=1, source_target_pairs={{0,32},{16,48},{32,0},{48,16},{1,33},{17,49},{33,1},{49,17},{2,34}... | collective-permute-start | bytes 184328 | tf_op jit(solution)/shard_map/ppermute | solution.py:34
  69.7 4.4 %collective-permute-start.21 = (bf16[240,128]{1,0:T(8,128)(2,1)S(1)}, bf16[240,128]{1,0:T(8,128)(2,1)S(1)}, u32[]{:S(2)}, u32[]{:S(2)}) collective-permute-start(bf16[240,128]{1,0:T(8,128)(2,1)S(1)} %pad_maximum_fusion.12), channel_id=1, source_target_pairs={{0,192},{64,128},{128,64},{192,0},{1,193},{65,129},{129,65},{193,1... | collective-permute-start | bytes 184328 | tf_op jit(solution)/shard_map/ppermute | solution.py:34
  70.9 3.2 %collective-permute-start.20 = (bf16[240,128]{1,0:T(8,128)(2,1)S(1)}, bf16[240,128]{1,0:T(8,128)(2,1)S(1)}, u32[]{:S(2)}, u32[]{:S(2)}) collective-permute-start(bf16[240,128]{1,0:T(8,128)(2,1)S(1)} %pad_maximum_fusion.12), channel_id=1, source_target_pairs={{0,64},{64,0},{128,192},{192,128},{1,65},{65,1},{129,193},{193,129... | collective-permute-start | bytes 184328 | tf_op jit(solution)/shard_map/ppermute | solution.py:34
  71.2 4.8 %collective-permute-start.19 = (bf16[240,128]{1,0:T(8,128)(2,1)S(1)}, bf16[240,128]{1,0:T(8,128)(2,1)S(1)}, u32[]{:S(2)}, u32[]{:S(2)}) collective-permute-start(bf16[240,128]{1,0:T(8,128)(2,1)S(1)} %pad_maximum_fusion.12), channel_id=1, source_target_pairs={{0,128},{64,192},{128,0},{192,64},{1,129},{65,193},{129,1},{193,65... | collective-permute-start | bytes 184328 | tf_op jit(solution)/shard_map/ppermute | solution.py:34
  76.0 5.8 %collective-permute-start.22 = (f32[192,128]{1,0:T(8,128)S(1)}, f32[192,128]{1,0:T(8,128)S(1)}, u32[]{:S(2)}, u32[]{:S(2)}) collective-permute-start(f32[192,128]{1,0:T(8,128)S(1)} %pad_maximum_fusion.8.held), channel_id=1, source_target_pairs={{0,8},{8,0},{1,9},{9,1},{2,10},{10,2},{3,11},{11,3},{4,12},{12,4},... | collective-permute-start | bytes 294920 | tf_op jit(solution)/shard_map/ppermute | solution.py:34
